TPU v7x, 128 devices: a whole 4x4x4 slice. The times are simulated.
128 devices in a mesh: seq: 64 (over x, z, y), head: 2 (over core).
Axes of the slice: x: 4, y: 4, z: 4, core: 2. Of those that a mesh axis runs over, the one named last changes fastest.
Arguments:
- layer_in: bfloat16 [16384, 1536], P('seq'), may hold values from -6 to 6
- norm_first: float32 [1536], replicated, may hold values from 0.5 to 1.5
- mixer_in: bfloat16 [1536, 2, 3072], P('seq', None, 'head'), may hold values from -0.15625 to 0.15625
- state_proj: bfloat16 [1536, 256], P('seq'), may hold values from -0.15625 to 0.15625
- step_proj: bfloat16 [1536, 48], P('seq', 'head'), may hold values from -0.15625 to 0.15625
- step_bias: float32 [48], P('head'), may hold values from -2 to 0
- conv_main: float32 [4, 3072], P(None, 'head'), may hold values from -3 to 3
- conv_state: float32 [4, 256], replicated, may hold values from -3 to 3
- decay_rate: float32 [48], P('head'), may hold values from 3.0517578e-05 to 0.05
- skip_gain: float32 [48], P('head'), may hold values from 0.25 to 1.75
- gate_gain: float32 [3072], P('head'), may hold values from 0.5 to 1.5
- mixer_out: bfloat16 [1536, 3072], P('seq', 'head'), may hold values from -0.109375 to 0.109375
- norm_second: float32 [1536], replicated, may hold values from 0.5 to 1.5
- shared_gate_up: bfloat16 [1536, 2, 1024], P('seq', None, 'head'), may hold values from -0.15625 to 0.15625
- shared_down: bfloat16 [1536, 1024], P('seq', 'head'), may hold values from -0.1875 to 0.1875
- expert_gate_up: bfloat16 [64, 1536, 2, 512], P('seq', None, None, 'head'), may hold values from -0.15625 to 0.15625
- expert_down: bfloat16 [64, 512, 1536], P('seq', 'head'), may hold values from -0.25 to 0.25
- routes: int32 [16384, 6], P('seq'), may hold values from 0 to 63, all different within a row; in each aligned block of 256 rows (0 to 255, 256 to 511, ...) at most 32 rows name the same one
- route_weights: float32 [16384, 6], P('seq'), may hold values from 0.3 to 0.9
- grad_out: bfloat16 [16384, 1536], P('seq'), may hold values from -6 to 6
Outputs:
- layer_out: bfloat16 [16384, 1536], P('seq')
- input_grad: float32 [16384, 1536], P('seq')
- norm_first_grad: float32 [1536], replicated
- mixer_in_grad: float32 [1536, 2, 3072], P('seq', None, 'head')
- state_proj_grad: float32 [1536, 256], P('seq')
- step_proj_grad: float32 [1536, 48], P('seq', 'head')
- step_bias_grad: float32 [48], P('head')
- conv_main_grad: float32 [4, 3072], P(None, 'head')
- conv_state_grad: float32 [4, 256], replicated
- decay_rate_grad: float32 [48], P('head')
- skip_gain_grad: float32 [48], P('head')
- gate_gain_grad: float32 [3072], P('head')
- mixer_out_grad: float32 [1536, 3072], P('seq', 'head')
- norm_second_grad: float32 [1536], replicated
- shared_gate_up_grad: float32 [1536, 2, 1024], P('seq', None, 'head')
- shared_down_grad: float32 [1536, 1024], P('seq', 'head')
- expert_gate_up_grad: float32 [64, 1536, 2, 512], P('seq', None, None, 'head')
- expert_down_grad: float32 [64, 512, 1536], P('seq', 'head')
Inputs may be any that keep to these rules, and one draw needn't show every extreme that they name: `routes`: in each aligned block of 256 rows (the rows of one device) no expert is named in more than 32 rows; each row names 6 different experts.
All inputs are finite; a program needn't handle non-finite values.
Results may differ from a plain program's by a relative error of at most 0.015.
Values may be sent and summed in bfloat16 or wider, within the bound.
A program may use at most 320 MiB of HBM per device.

v0:
```python
import jax
import jax.numpy as jnp
from jax import lax
from jax.sharding import PartitionSpec as P

HIGHEST = lax.Precision.HIGHEST
EPSILON = 1e-05


def shifted(value, axis, steps):
    count = lax.axis_size(axis)
    leading, last = (max(0, -steps), min(count, count - steps))
    return lax.ppermute(value, axis, [(source, source + steps) for source in range(leading, last)])


def carried_in(array, axis, combine, identity, reverse):
    peers, here = (lax.axis_size(axis), lax.axis_index(axis))
    everything = jax.tree.map(lambda part: lax.all_gather(part, axis), array)
    start = jax.tree.map(
        lambda part, zero: jnp.broadcast_to(jnp.asarray(zero, part.dtype), part.shape),
        array,
        identity,
    )

    def step(k, before):
        at = peers - 1 - k if reverse else k
        reached = at > here if reverse else at < here
        new = combine(before, jax.tree.map(lambda part: part[at], everything))
        return jax.tree.map(lambda a, b: jnp.where(reached, a, b), new, before)

    return lax.fori_loop(0, peers, step, start)


def product(left_side, right_side):
    return jnp.dot(left_side, right_side, preferred_element_type=jnp.float32)


def product_nt(left_side, right_side):
    return lax.dot_general(
        left_side, right_side, (((1,), (1,)), ((), ())), preferred_element_type=jnp.float32
    )


def product_tn(left_side, right_side):
    return lax.dot_general(
        left_side, right_side, (((0,), (0,)), ((), ())), preferred_element_type=jnp.float32
    )


def silu(operand):
    return operand * jax.nn.sigmoid(operand)


def silu_slope(operand):
    sig_part = jax.nn.sigmoid(operand)
    return sig_part * (1.0 + operand * (1.0 - sig_part))


def rms_scale(operand):
    return lax.rsqrt(jnp.mean(operand * operand, axis=-1, keepdims=True) + EPSILON)


def norm_back(operand, row_scale, gain_vec, grad_rows):
    gain_grad = jnp.sum(grad_rows * operand * row_scale, axis=0)
    inner_mean = jnp.mean(operand * gain_vec * grad_rows, axis=-1, keepdims=True)
    return (gain_grad, row_scale * gain_vec * grad_rows - operand * row_scale**3 * inner_mean)


def group_state(heads_x, state_in, step_size, decay_rate):
    cum_decay = jnp.cumsum(-step_size * decay_rate[None, :], axis=0)
    tail_decay = cum_decay[-1]
    tok_weight = jnp.exp(tail_decay[None, :] - cum_decay) * step_size
    state_new = jnp.einsum("th,thp,tn->hpn", tok_weight, heads_x, state_in, precision=HIGHEST)
    return (jnp.exp(tail_decay), state_new)


def group_out(heads_x, state_in, state_read, step_size, decay_rate, state_start, skip_gain):
    length_rows = heads_x.shape[0]
    cum_decay = jnp.cumsum(-step_size * decay_rate[None, :], axis=0)
    causal = (jnp.arange(length_rows)[:, None] >= jnp.arange(length_rows)[None, :])[:, :, None]
    gap_decay = cum_decay[:, None, :] - cum_decay[None, :, :]
    decay_mat = jnp.where(causal, jnp.exp(jnp.where(causal, gap_decay, 0.0)), 0.0)
    scores = jnp.dot(state_read, state_in.T, precision=HIGHEST)
    mixing = decay_mat * scores[:, :, None] * step_size[None, :, :]
    within_part = jnp.einsum("tsh,shp->thp", mixing, heads_x, precision=HIGHEST)
    carried_part = jnp.exp(cum_decay)[:, :, None] * jnp.einsum(
        "tn,hpn->thp", state_read, state_start, precision=HIGHEST
    )
    return within_part + carried_part + skip_gain[None, :, None] * heads_x


def combine_states(earlier, following):
    first_decay, first_state = earlier
    next_decay, next_state = following
    return (first_decay * next_decay, next_decay[:, None, None] * first_state + next_state)


def head_total(operand):
    return lax.psum(operand, "head")


def gate_stat(operand):
    return lax.psum(operand, "head")


def to_experts(operand):
    return lax.all_to_all(operand, "seq", split_axis=1, concat_axis=1, tiled=True)


def to_home(operand):
    return lax.all_to_all(operand, "seq", split_axis=1, concat_axis=1, tiled=True)


def per_device(
    layer_in,
    norm_first,
    mixer_in,
    state_proj,
    step_proj,
    step_bias,
    conv_main,
    conv_state,
    decay_rate,
    skip_gain,
    gate_gain,
    mixer_out,
    norm_second,
    shared_gate_up,
    shared_down,
    expert_gate_up,
    expert_down,
    routes,
    route_weights,
    grad_out,
):
    tokens = layer_in.shape[0]
    model_width = layer_in.shape[1]
    inner_dev = mixer_in.shape[2]
    inner_all = inner_dev * lax.axis_size("head")
    state_size = state_proj.shape[1] // 2
    heads_dev = step_proj.shape[1]
    head_size = inner_dev // heads_dev
    conv_taps = conv_main.shape[0]
    shared_dev = shared_down.shape[1]
    local_experts = expert_gate_up.shape[0]
    seq_devices = lax.axis_size("seq")
    experts_all = local_experts * seq_devices
    choices_per = routes.shape[1]
    capacity = max(2, tokens * choices_per * 4 // (3 * experts_all))
    slot_count = local_experts * seq_devices * capacity
    gathered = (
        lax.all_gather(mixer_in, "seq", axis=0, tiled=True),
        lax.all_gather(state_proj, "seq", axis=0, tiled=True),
        lax.all_gather(step_proj, "seq", axis=0, tiled=True),
        lax.all_gather(mixer_out, "seq", axis=0, tiled=True),
        lax.all_gather(shared_gate_up, "seq", axis=0, tiled=True),
        lax.all_gather(shared_down, "seq", axis=0, tiled=True),
    )
    full_in, full_state, full_step, full_out, full_shared, full_down = gathered
    resid_in = layer_in.astype(jnp.float32)
    scale_first = rms_scale(resid_in)
    normed = (resid_in * scale_first * norm_first).astype(jnp.bfloat16)
    zx_both = product(normed, full_in.reshape(model_width, 2 * inner_dev))
    gate_z = zx_both[:, :inner_dev]
    pre_x = zx_both[:, inner_dev:]
    pre_bc = product(normed, full_state)
    step_raw = product(normed, full_step) + step_bias
    conv_input = jnp.concatenate([pre_x, pre_bc], axis=1)
    edge_rows = shifted(conv_input[tokens - (conv_taps - 1) :], "seq", 1)
    padded = jnp.concatenate([edge_rows, conv_input], axis=0)
    kernel = jnp.concatenate([conv_main, conv_state], axis=1)
    conv_sum = kernel[0] * padded[0:tokens]
    for tap_index in range(1, conv_taps):
        conv_sum = conv_sum + kernel[tap_index] * padded[tap_index : tap_index + tokens]
    active = silu(conv_sum)
    heads_x = active[:, :inner_dev].reshape(tokens, heads_dev, head_size)
    state_in = active[:, inner_dev : inner_dev + state_size]
    state_read = active[:, inner_dev + state_size :]
    step_size = jax.nn.softplus(step_raw)
    decay_total, state_local = group_state(heads_x, state_in, step_size, decay_rate)
    identity = (jnp.ones_like(decay_total), jnp.zeros_like(state_local))
    prefix = carried_in((decay_total, state_local), "seq", combine_states, identity, False)
    state_start = prefix[1]
    ssd = group_out(
        heads_x, state_in, state_read, step_size, decay_rate, state_start, skip_gain
    ).reshape(tokens, inner_dev)
    gate_act = silu(gate_z)
    gated_ssd = ssd * gate_act
    gate_scale = lax.rsqrt(gate_stat(jnp.sum(gated_ssd * gated_ssd, axis=1)) / inner_all + EPSILON)[
        :, None
    ]
    normed_gate = (gated_ssd * gate_scale * gate_gain).astype(jnp.bfloat16)
    mixer_sum = head_total(product_nt(normed_gate, full_out))
    residual = resid_in + mixer_sum
    scale_second = rms_scale(residual)
    normed_second = (residual * scale_second * norm_second).astype(jnp.bfloat16)
    shared_flat = full_shared.reshape(model_width, 2 * shared_dev)
    shared_both = product(normed_second, shared_flat)
    shared_gate = shared_both[:, :shared_dev]
    shared_up = shared_both[:, shared_dev:]
    shared_hid = (silu(shared_gate) * shared_up).astype(jnp.bfloat16)
    shared_part = product_nt(shared_hid, full_down)
    flat_routes = routes.reshape(-1)
    one_hot = (flat_routes[:, None] == jnp.arange(experts_all, dtype=jnp.int32)[None, :]).astype(
        jnp.int32
    )
    position = jnp.sum((jnp.cumsum(one_hot, axis=0) - one_hot) * one_hot, axis=1)
    slot_row = (
        flat_routes % local_experts * (seq_devices * capacity)
        + flat_routes // local_experts * capacity
        + position
    )
    owner_mask = (slot_row[None, :] == jnp.arange(slot_count, dtype=jnp.int32)[:, None]).reshape(
        slot_count, tokens, choices_per
    )
    picker = jnp.any(owner_mask, axis=2).astype(jnp.bfloat16)
    send_rows = (
        product(picker, normed_second)
        .astype(jnp.bfloat16)
        .reshape(local_experts, seq_devices * capacity, model_width)
    )
    slot_in = to_experts(send_rows)
    gate_up_res = jnp.einsum(
        "erd,edkf->erkf", slot_in, expert_gate_up, preferred_element_type=jnp.float32
    )
    expert_gate = gate_up_res[:, :, 0]
    expert_up = gate_up_res[:, :, 1]
    expert_hid = (silu(expert_gate) * expert_up).astype(jnp.bfloat16)
    expert_res = jnp.einsum(
        "erf,efd->erd", expert_hid, expert_down, preferred_element_type=jnp.float32
    ).astype(jnp.bfloat16)
    home_rows = to_home(expert_res).reshape(slot_count, model_width)
    picked = home_rows[slot_row].astype(jnp.float32).reshape(tokens, choices_per, model_width)
    expert_mix = jnp.sum(picked * route_weights[:, :, None], axis=1)
    branch_sum = head_total(shared_part + expert_mix)
    layer_out = (residual + branch_sum).astype(jnp.bfloat16)
    gathered = (
        lax.all_gather(mixer_in, "seq", axis=0, tiled=True),
        lax.all_gather(state_proj, "seq", axis=0, tiled=True),
        lax.all_gather(step_proj, "seq", axis=0, tiled=True),
        lax.all_gather(mixer_out, "seq", axis=0, tiled=True),
        lax.all_gather(shared_gate_up, "seq", axis=0, tiled=True),
        lax.all_gather(shared_down, "seq", axis=0, tiled=True),
    )
    full_in, full_state, full_step, full_out, full_shared, full_down = gathered
    shared_flat = full_shared.reshape(model_width, 2 * shared_dev)
    grad_float = grad_out.astype(jnp.float32)
    slot_weight = jnp.zeros((slot_count,), jnp.float32).at[slot_row].set(route_weights.reshape(-1))
    grad_send = (product(picker, grad_out) * slot_weight[:, None]).astype(jnp.bfloat16)
    grad_slots = to_experts(grad_send.reshape(local_experts, seq_devices * capacity, model_width))
    grad_hid = jnp.einsum(
        "erd,efd->erf", grad_slots, expert_down, preferred_element_type=jnp.float32
    )
    grad_expert_gate = grad_hid * expert_up * silu_slope(expert_gate)
    grad_expert_up = grad_hid * silu(expert_gate)
    grad_gate_up = jnp.stack([grad_expert_gate, grad_expert_up], axis=2).astype(jnp.bfloat16)
    expert_down_grad = jnp.einsum(
        "erf,erd->efd", expert_hid, grad_slots, preferred_element_type=jnp.float32
    )
    expert_gate_up_grad = jnp.einsum(
        "erd,erkf->edkf", slot_in, grad_gate_up, preferred_element_type=jnp.float32
    )
    grad_slot_in = jnp.einsum(
        "erkf,edkf->erd", grad_gate_up, expert_gate_up, preferred_element_type=jnp.float32
    ).astype(jnp.bfloat16)
    grad_home = to_home(grad_slot_in).reshape(slot_count, model_width)
    expert_grad_rows = jnp.sum(
        grad_home[slot_row].astype(jnp.float32).reshape(tokens, choices_per, model_width), axis=1
    )
    grad_shared_hid = product(grad_out, full_down)
    grad_shared_gate = grad_shared_hid * shared_up * silu_slope(shared_gate)
    grad_shared_up = grad_shared_hid * silu(shared_gate)
    grad_shared_both = jnp.concatenate([grad_shared_gate, grad_shared_up], axis=1).astype(
        jnp.bfloat16
    )
    shared_down_grad = product_tn(grad_out, shared_hid)
    shared_gate_up_grad = product_tn(normed_second, grad_shared_both).reshape(
        model_width, 2, shared_dev
    )
    grad_normed_second = head_total(product_nt(grad_shared_both, shared_flat) + expert_grad_rows)
    norm_second_grad, grad_resid_norm = norm_back(
        residual, scale_second, norm_second, grad_normed_second
    )
    grad_resid = grad_float + grad_resid_norm
    grad_mix = grad_resid.astype(jnp.bfloat16)
    mixer_out_grad = product_tn(grad_mix, normed_gate)
    grad_normed_gate = product(grad_mix, full_out)
    weighted = grad_normed_gate * gate_gain
    inner_dot = gate_stat(jnp.sum(weighted * gated_ssd, axis=1))[:, None]
    grad_gated = gate_scale * weighted - gated_ssd * gate_scale**3 * inner_dot / inner_all
    gate_gain_grad = jnp.sum(grad_normed_gate * gated_ssd * gate_scale, axis=0)
    grad_ssd = grad_gated * gate_act
    grad_gate_z = grad_gated * ssd * silu_slope(gate_z)
    _, pull_out = jax.vjp(
        group_out, heads_x, state_in, state_read, step_size, decay_rate, state_start, skip_gain
    )
    (
        grad_x_first,
        grad_in_first,
        grad_read,
        grad_step_first,
        grad_rate_first,
        grad_start,
        skip_gain_grad,
    ) = pull_out(grad_ssd.reshape(tokens, heads_dev, head_size))
    suffix = carried_in((decay_total, grad_start), "seq", combine_states, identity, True)
    grad_next = suffix[1]
    grad_decay = jnp.sum(grad_next * state_start, axis=(1, 2))
    _, pull_state = jax.vjp(group_state, heads_x, state_in, step_size, decay_rate)
    grad_x_second, grad_in_second, grad_step_second, grad_rate_second = pull_state(
        (grad_decay, grad_next)
    )
    decay_rate_grad = grad_rate_first + grad_rate_second
    grad_bc = lax.psum(
        jnp.concatenate([grad_in_first + grad_in_second, grad_read], axis=1).astype(jnp.bfloat16),
        "head",
    ).astype(jnp.float32)
    grad_active = jnp.concatenate(
        [(grad_x_first + grad_x_second).reshape(tokens, inner_dev), grad_bc], axis=1
    )
    grad_conv = grad_active * silu_slope(conv_sum)
    grad_padded = jnp.pad(kernel[0] * grad_conv, ((0, conv_taps - 1), (0, 0)))
    for tap_index in range(1, conv_taps):
        grad_padded = grad_padded + jnp.pad(
            kernel[tap_index] * grad_conv, ((tap_index, conv_taps - 1 - tap_index), (0, 0))
        )
    kernel_grad = jnp.stack(
        [
            jnp.sum(grad_conv * padded[tap_index : tap_index + tokens], axis=0)
            for tap_index in range(conv_taps)
        ]
    )
    spill_rows = shifted(grad_padded[: conv_taps - 1], "seq", -1)
    grad_pre = grad_padded[conv_taps - 1 :]
    grad_pre = jnp.concatenate(
        [grad_pre[: tokens - (conv_taps - 1)], grad_pre[tokens - (conv_taps - 1) :] + spill_rows],
        axis=0,
    )
    grad_step_raw = (grad_step_first + grad_step_second) * jax.nn.sigmoid(step_raw)
    step_bias_grad = jnp.sum(grad_step_raw, axis=0)
    grad_zx = jnp.concatenate([grad_gate_z, grad_pre[:, :inner_dev]], axis=1).astype(jnp.bfloat16)
    grad_bc_low = grad_pre[:, inner_dev:].astype(jnp.bfloat16)
    grad_step_low = grad_step_raw.astype(jnp.bfloat16)
    in_partial = product_nt(grad_zx, full_in.reshape(model_width, 2 * inner_dev)) + product_nt(
        grad_step_low, full_step
    )
    grad_normed = head_total(in_partial) + product_nt(grad_bc_low, full_state)
    mixer_in_grad = product_tn(normed, grad_zx).reshape(model_width, 2, inner_dev)
    state_proj_grad = product_tn(normed, grad_bc_low)
    step_proj_grad = product_tn(normed, grad_step_low)
    norm_first_grad, grad_in_norm = norm_back(resid_in, scale_first, norm_first, grad_normed)
    input_grad = grad_resid + grad_in_norm
    weight_sums = (
        lax.psum_scatter(mixer_in_grad, "seq", scatter_dimension=0, tiled=True),
        lax.psum_scatter(state_proj_grad, "seq", scatter_dimension=0, tiled=True),
        lax.psum_scatter(step_proj_grad, "seq", scatter_dimension=0, tiled=True),
        lax.psum_scatter(mixer_out_grad, "seq", scatter_dimension=0, tiled=True),
        lax.psum_scatter(shared_gate_up_grad, "seq", scatter_dimension=0, tiled=True),
        lax.psum_scatter(shared_down_grad, "seq", scatter_dimension=0, tiled=True),
    )
    small_sums = lax.psum(
        (
            norm_first_grad,
            norm_second_grad,
            step_bias_grad,
            kernel_grad[:, :inner_dev],
            kernel_grad[:, inner_dev:],
            decay_rate_grad,
            skip_gain_grad,
            gate_gain_grad,
        ),
        "seq",
    )
    return (
        layer_out,
        input_grad,
        small_sums[0],
        weight_sums[0],
        weight_sums[1],
        weight_sums[2],
        small_sums[2],
        small_sums[3],
        small_sums[4],
        small_sums[5],
        small_sums[6],
        small_sums[7],
        weight_sums[3],
        small_sums[1],
        weight_sums[4],
        weight_sums[5],
        expert_gate_up_grad,
        expert_down_grad,
    )


def solution(mesh):
    placed = (
        P("seq", None),
        P(),
        P("seq", None, "head"),
        P("seq", None),
        P("seq", "head"),
        P("head"),
        P(None, "head"),
        P(),
        P("head"),
        P("head"),
        P("head"),
        P("seq", "head"),
        P(),
        P("seq", None, "head"),
        P("seq", "head"),
        P("seq", None, None, "head"),
        P("seq", "head", None),
        P("seq", None),
        P("seq", None),
        P("seq", None),
    )
    return jax.shard_map(
        per_device,
        mesh=mesh,
        in_specs=placed,
        out_specs=(
            P("seq", None),
            P("seq", None),
            P(),
            P("seq", None, "head"),
            P("seq", None),
            P("seq", "head"),
            P("head"),
            P(None, "head"),
            P(),
            P("head"),
            P("head"),
            P("head"),
            P("seq", "head"),
            P(),
            P("seq", None, "head"),
            P("seq", "head"),
            P("seq", None, None, "head"),
            P("seq", "head", None),
        ),
        check_vma=False,
    )
```

profile of v0, /device:TPU:1, one launch (start us, length us, event | category | flops | bytes accessed | tf_op | source)
XLA Modules:
  0.0 3446.3 jit_solution(5210682948415158954)
XLA Ops:
  8.1 154.4 %all_gather.44 = bf16[1536,24]{1,0:T(8,128)(2,1)S(1)} all-gather(bf16[24,24]{1,0:T(8,128)(2,1)} %param.28), channel_id=1, replica_groups=mesh['seq'=64,'head'=2] {'seq'}, dimensions={0}, use_global_device_ids=true | all-gather | bytes 74880 | tf_op jit(solution)/shard_map/all_gather | solution.py:154
  168.6 145.8 %all_gather.43 = bf16[1536,256]{1,0:T(8,128)(2,1)S(1)} all-gather(bf16[24,256]{1,0:T(8,128)(2,1)S(1)} %copy-done.99), channel_id=1, replica_groups=mesh['seq'=64,'head'=2] {'seq'}, dimensions={0}, use_global_device_ids=true | all-gather | bytes 798720 | tf_op jit(solution)/shard_map/all_gather | solution.py:153
  410.8 69.3 %copy.286 = bf16[1,2048,1536]{2,0,1:T(2,128)(2,1)} copy(bf16[1,2048,1536]{2,1,0:T(8,128)(2,1)S(1)} %fusion.5) | data formatting | bytes 12582912 | tf_op jit(solution)/shard_map/reshape | solution.py:250
  480.6 41.9 %reduce.26 = bf16[2048,1536]{1,0:T(8,128)(2,1)} reduce(bf16[2048,1,1536]{2,1,0:T(2,128)(2,1)} %bitcast.407, bf16[]{:T(256)} %broadcast.341), dimensions={1}, to_apply=%bitcast.386.reduce_sub_computation | reduce | bytes 12582914
  544.7 222.8 %all-gather.2 = f32[64,1,24]{2,1,0:T(1,128)S(1)} all-gather(f32[1,1,24]{2,1,0:T(1,128)S(1)} %bitcast.443), channel_id=1, replica_groups=mesh['seq'=64,'head'=2] {'seq'}, dimensions={0}, use_global_device_ids=true | all-gather | bytes 6240 | tf_op jit(solution)/shard_map/all_gather | solution.py:18
  768.9 86.3 %while.30 = (s32[]{:T(128)}, f32[24,64,128]{2,1,0:T(8,128)S(1)}, s32[]{:T(128)}, f32[64,24]{1,0:T(8,128)S(1)}, f32[64,24,64,128]{3,2,1,0:T(8,128)}, /*index=5*/s32[]{:T(128)}, s32[]{:T(128)}) while((s32[]{:T(128)}, f32[24,64,128]{2,1,0:T(8,128)S(1)}, s32[]{:T(128)}, f32[64,24]{1,0:T(8,128)S(1)}, f32[64,24,64,128]{3,2,1,0:T(8,128)}, ...), condition=%wide.region_4.5_spmd.clone, body=%wide.region_3.4_spmd.clone.sunk | while | flops 786436 | bytes 2359697 | solution.py:31
  873.2 73.7 %psum.105 = f32[256]{0:T(256)S(1)} all-reduce(f32[256]{0:T(256)S(1)} %get-tuple-element.435), channel_id=1, replica_groups=mesh['seq'=64,'head'=2] {'head'}, use_global_device_ids=true, to_apply=%region_6.7 | all-reduce | flops 256 | bytes 2048 | tf_op jit(solution)/shard_map/psum | solution.py:103
  977.8 69.3 %copy.288 = bf16[1,2048,1536]{2,0,1:T(2,128)(2,1)} copy(bf16[1,2048,1536]{2,1,0:T(8,128)(2,1)S(1)} %fusion.3) | data formatting | bytes 12582912 | tf_op jit(solution)/shard_map/reshape | solution.py:220
  1047.1 41.6 %reduce.24 = bf16[2048,1536]{1,0:T(8,128)(2,1)} reduce(bf16[2048,1,1536]{2,1,0:T(2,128)(2,1)} %bitcast.409, bf16[]{:T(256)} %broadcast.341), dimensions={1}, to_apply=%bitcast.388.reduce_sub_computation | reduce | bytes 12582914
  1151.9 44.9 %all-to-all-done = bf16[64,2,24576]{2,1,0:T(2,128)(2,1)} async-done(((bf16[64,2,24576]{2,1,0:T(2,128)(2,1)}), bf16[64,2,24576]{2,1,0:T(2,128)(2,1)}, u32[]{:S(2)}, u32[]{:S(2)}) %all-to-all-start) | async-done | bytes 6291488 | tf_op jit(solution)/shard_map/all_to_all | solution.py:107
  1248.4 69.3 %copy.285 = bf16[1,2048,1536]{2,0,1:T(2,128)(2,1)} copy(bf16[1,2048,1536]{2,1,0:T(8,128)(2,1)S(1)} %fusion.6) | data formatting | bytes 12582912 | tf_op jit(solution)/shard_map/convert_element_type | solution.py:265
  1317.7 41.8 %reduce.27 = bf16[2048,1536]{1,0:T(8,128)(2,1)} reduce(bf16[2048,1,1536]{2,1,0:T(2,128)(2,1)} %bitcast.410, bf16[]{:T(256)} %broadcast.341), dimensions={1}, to_apply=%bitcast.385.reduce_sub_computation | reduce | bytes 12582914
  1399.1 113.6 %all-gather.16.cloned.1.call-done = bf16[1536,512]{1,0:T(8,128)(2,1)} async-done(((bf16[24,512]{1,0:T(8,128)(2,1)}), bf16[1536,512]{1,0:T(8,128)(2,1)}) %all-gather.16.cloned.1.call-update) | async-done | bytes 1572880 | tf_op jit(solution)/shard_map/all_gather | solution.py:157
  1515.5 37.2 %reshape.447 = bf16[2048,1,1536]{2,1,0:T(2,128)(2,1)} reshape(bf16[64,2,24576]{2,1,0:T(2,128)(2,1)} %all-to-all-done.3) | data formatting | bytes 12582912
  1650.8 69.3 %copy.287 = bf16[1,2048,1536]{2,0,1:T(2,128)(2,1)} copy(bf16[1,2048,1536]{2,1,0:T(8,128)(2,1)S(1)} %fusion.4) | data formatting | bytes 12582912 | tf_op jit(solution)/shard_map/convert_element_type | solution.py:231
  1720.0 41.7 %reduce.25 = bf16[2048,1536]{1,0:T(8,128)(2,1)} reduce(bf16[2048,1,1536]{2,1,0:T(2,128)(2,1)} %bitcast.408, bf16[]{:T(256)} %broadcast.341), dimensions={1}, to_apply=%bitcast.387.reduce_sub_computation | reduce | bytes 12582914
  1787.7 138.4 %all-to-all-done.1 = bf16[64,2,24576]{2,1,0:T(2,128)(2,1)} async-done(((bf16[64,2,24576]{2,1,0:T(2,128)(2,1)}), bf16[64,2,24576]{2,1,0:T(2,128)(2,1)}, u32[]{:S(2)}, u32[]{:S(2)}) %all-to-all-start.1) | async-done | bytes 6291488 | tf_op jit(solution)/shard_map/all_to_all | solution.py:111
  1926.1 37.3 %reshape.443 = bf16[2048,1,1536]{2,1,0:T(2,128)(2,1)} reshape(bf16[64,2,24576]{2,1,0:T(2,128)(2,1)} %all-to-all-done.1) | data formatting | bytes 12582912
  2029.8 129.6 %while.31 = (s32[]{:T(128)}, f32[24,64,128]{2,1,0:T(8,128)S(1)}, s32[]{:T(128)}, f32[64,24]{1,0:T(8,128)}, f32[64,24,64,128]{3,2,1,0:T(8,128)}, /*index=5*/s32[]{:T(128)}, s32[]{:T(128)}, s32[]{:T(128)}, s32[]{:T(128)}) while((s32[]{:T(128)}, f32[24,64,128]{2,1,0:T(8,128)S(1)}, s32[]{:T(128)}, f32[64,24]{1,0:T(8,128)}, ...), condition=%wide.region_22.23_spmd.clone, body=%wide.region_21.22_spmd.clone.sunk | while | flops 786440 | bytes 2359759 | solution.py:31
  2349.5 296.6 %all-reduce.8 = (f32[1536]{0:T(1024)}, f32[24]{0:T(128)}, f32[4,1536]{1,0:T(4,128)}, f32[4,256]{1,0:T(4,128)}, f32[24]{0:T(128)}, /*index=5*/f32[24]{0:T(128)}, f32[1536]{0:T(1024)}, f32[1536]{0:T(1024)}) all-reduce(f32[1536]{0:T(1024)S(1)} %get-tuple-element.383, ...), channel_id=1, replica_groups=mesh['seq'=64,'head'=2] {'seq'}, use_global_device_ids=true, to_apply=%region_38.39 | all-reduce | flops 11848 | bytes 94784 | tf_op jit(solution)/shard_map/psum | solution.py:361
  2653.6 114.8 %reduce-scatter.13.cloned.1.call-done = f32[24,512]{1,0:T(8,128)} async-done(((f32[1536,512]{1,0:T(8,128)}), f32[24,512]{1,0:T(8,128)}) %reduce-scatter.13.cloned.1.call-update) | async-done | bytes 49168
  2768.4 229.6 %reduce-scatter.11.cloned.1.call-done = f32[24,1536]{1,0:T(8,128)} async-done(((f32[1536,1536]{1,0:T(8,128)}), f32[24,1536]{1,0:T(8,128)}) %reduce-scatter.11.cloned.1.call-update) | async-done | bytes 147472 | tf_op jit(solution)/shard_map/reduce_scatter | solution.py:357
  2998.0 220.6 %reduce-scatter.15.cloned.1.call-done = f32[24,24]{1,0:T(8,128)} async-done(((f32[1536,24]{1,0:T(8,128)}), f32[24,24]{1,0:T(8,128)}) %reduce-scatter.15.cloned.1.call-update) | async-done | bytes 2320
  3218.6 221.0 %reduce-scatter.9.cloned.1.call-done = f32[24,256]{1,0:T(8,128)} async-done(((f32[1536,256]{1,0:T(8,128)}), f32[24,256]{1,0:T(8,128)}) %reduce-scatter.9.cloned.1.call-update) | async-done | bytes 24592 | tf_op jit(solution)/shard_map/reduce_scatter | solution.py:355
  (717 shorter events, 931.1 us)
Async XLA Ops:
  7.2 1226.4 %copy-start = (bf16[1,1536,2,256]{3,2,1,0:T(2,128)(2,1)S(1)}, bf16[1,1536,2,256]{3,2,1,0:T(2,128)(2,1)}, u32[]{:S(2)}) copy-start(bf16[1,1536,2,256]{3,2,1,0:T(2,128)(2,1)} %param.39) | copy-start | bytes 4718596
  7.2 308.5 %all-gather.10.cloned.1.call-start = ((), (), s32[]{:S(2)}) async-start(), calls=%async_computation.8 | async-start | bytes 9584640 | tf_op jit(solution)/shard_map/all_gather | solution.py:152
  8.0 760.9 %all-gather.18.cloned.1.call-start = ((), (), s32[]{:S(2)}) async-start(), calls=%async_computation.17 | async-start | bytes 51118080 | tf_op jit(solution)/shard_map/all_gather | solution.py:18
  332.6 4.5 collective-permute-start
  538.0 566.2 %all-to-all-start.2 = ((bf16[64,2,24576]{2,1,0:T(2,128)(2,1)}), bf16[64,2,24576]{2,1,0:T(2,128)(2,1)}, u32[]{:S(2)}, u32[]{:S(2)}) async-start(bf16[64,2,24576]{2,1,0:T(2,128)(2,1)} %reshape.444), calls=%async_computation.2 | async-start | bytes 12582912 | tf_op jit(solution)/shard_map/all_to_all | solution.py:107
  543.9 403.1 %all-gather.12.cloned.1.call-start = ((), (), s32[]{:S(2)}) async-start(), calls=%async_computation.9 | async-start | bytes 4792320 | tf_op jit(solution)/shard_map/all_gather | solution.py:155
  544.6 428.3 %all-reduce.17.cloned.1.call-start = ((), (), s32[]{:S(2)}) async-start(), calls=%async_computation.10 | async-start | bytes 3145728 | tf_op jit(solution)/shard_map/psum | solution.py:99
  946.9 688.5 %copy-start.100 = (f32[256]{0:T(256)}, f32[256]{0:T(256)S(1)}, u32[]{:S(2)}) copy-start(f32[256]{0:T(256)S(1)} %get-tuple-element.459) | copy-start | bytes 3076
  1104.2 92.6 %all-to-all-start = ((bf16[64,2,24576]{2,1,0:T(2,128)(2,1)}), bf16[64,2,24576]{2,1,0:T(2,128)(2,1)}, u32[]{:S(2)}, u32[]{:S(2)}) async-start(bf16[64,2,24576]{2,1,0:T(2,128)(2,1)} %reshape.440), calls=%async_computation | async-start | bytes 12582912 | tf_op jit(solution)/shard_map/all_to_all | solution.py:107
  1114.6 279.1 %all-gather.14.cloned.1.call-start = ((), (), s32[]{:S(2)}) async-start(), calls=%async_computation.11 | async-start | bytes 3194880 | tf_op jit(solution)/shard_map/all_gather | solution.py:156
  1375.0 140.5 %all-to-all-start.3 = ((bf16[64,2,24576]{2,1,0:T(2,128)(2,1)}), bf16[64,2,24576]{2,1,0:T(2,128)(2,1)}, u32[]{:S(2)}, u32[]{:S(2)}) async-start(bf16[64,2,24576]{2,1,0:T(2,128)(2,1)} %reshape.446), calls=%async_computation.3 | async-start | bytes 12582912 | tf_op jit(solution)/shard_map/all_to_all | solution.py:111
  1393.1 119.6 %all-gather.16.cloned.1.call-start = ((), (), s32[]{:S(2)}) async-start(), calls=%async_computation.12 | async-start | bytes 1597440 | tf_op jit(solution)/shard_map/all_gather | solution.py:157
  1393.6 229.0 %all-reduce.19.cloned.1.call-start = ((), (), s32[]{:S(2)}) async-start(), calls=%async_computation.13 | async-start | bytes 3145728 | tf_op jit(solution)/shard_map/psum | solution.py:99
  1597.2 432.6 %all-gather.20.cloned.1.call-start = ((), (), s32[]{:S(2)}) async-start(), calls=%async_computation.18 | async-start | bytes 51118080 | tf_op jit(solution)/shard_map/all_gather | solution.py:18
  1777.3 148.8 %all-to-all-start.1 = ((bf16[64,2,24576]{2,1,0:T(2,128)(2,1)}), bf16[64,2,24576]{2,1,0:T(2,128)(2,1)}, u32[]{:S(2)}, u32[]{:S(2)}) async-start(bf16[64,2,24576]{2,1,0:T(2,128)(2,1)} %reshape.442), calls=%async_computation.1 | async-start | bytes 12582912 | tf_op jit(solution)/shard_map/all_to_all | solution.py:111
  1787.7 419.0 %all-reduce.21.cloned.1.call-start = ((), (), s32[]{:S(2)}) async-start(), calls=%async_computation.14 | async-start | bytes 262144 | tf_op jit(solution)/shard_map/psum | solution.py:314
  2182.0 164.0 %all-reduce.25.cloned.1.call-start = ((), (), s32[]{:S(2)}) async-start(), calls=%async_computation.22 | async-start | bytes 6291456 | tf_op jit(solution)/shard_map/psum | solution.py:99
  2211.2 4.6 collective-permute-start.1
  2221.5 428.9 %all-reduce.23.cloned.1.call-start = ((), (), s32[]{:S(2)}) async-start(), calls=%async_computation.21 | async-start | bytes 50331648
  2270.4 498.0 %reduce-scatter.13.cloned.1.call-start = ((), (), s32[]{:S(2)}) async-start(), calls=%async_computation.19 | async-start | bytes 3194880
  2277.4 720.7 %reduce-scatter.11.cloned.1.call-start = ((), (), s32[]{:S(2)}) async-start(), calls=%async_computation.16 | async-start | bytes 9584640 | tf_op jit(solution)/shard_map/reduce_scatter | solution.py:357
  2285.7 932.9 %reduce-scatter.15.cloned.1.call-start = ((), (), s32[]{:S(2)}) async-start(), calls=%async_computation.20 | async-start | bytes 798720
  2318.9 1120.7 %reduce-scatter.9.cloned.1.call-start = ((), (), s32[]{:S(2)}) async-start(), calls=%async_computation.15 | async-start | bytes 1597440 | tf_op jit(solution)/shard_map/reduce_scatter | solution.py:355
  2648.7 790.9 %copy-start.1 = (bf16[1,1536,2,256]{3,2,1,0:T(2,128)(2,1)S(1)}, bf16[1,1536,2,256]{3,2,1,0:T(2,128)(2,1)}, u32[]{:S(2)}) copy-start(bf16[1,1536,2,256]{3,2,1,0:T(2,128)(2,1)} %param.39) | copy-start | bytes 4718596
  (121 other events, 3767.7 us)
Sparse Core Ops, SparseCore 0:
  10.8 85.6 all-gather.9
  348.9 336.5 all-gather.17
  688.3 72.9 all-gather.11
  952.5 20.3 all-reduce.16
  1118.3 121.1 all-gather.13
  1396.8 115.8 all-gather.15
  1597.4 25.2 all-reduce.18
  1645.2 286.7 all-gather.19
  2182.1 24.6 all-reduce.20
  2221.6 34.9 all-reduce.24
  2270.5 275.4 all-reduce.22
  2550.8 217.5 reduce-scatter.12
  2773.6 224.4 reduce-scatter.10
  3003.4 215.2 reduce-scatter.14
  3224.0 215.6 reduce-scatter.8
where the time goes:
time: 3480 us; the launch traced here: 3450 us
  waiting for transfers between devices  1150 us (33%)
  blocking collectives  896 us (26%)
  local copies, waits for them, and re-layouts  749 us (22%)
  other arithmetic  435 us (12%)
  matrix products  149 us (4%)
  starting transfers between devices  50.2 us (1%)
    unnamed x18, waiting for transfers between devices  338 us
    psum x1, blocking collectives, per_device(): lax.psum((norm_first_grad, norm_second_grad, step_bias_grad, kernel_grad[...  297 us
    unnamed x269, local copies, waits for them, and re-layouts  276 us
    reduce_scatter x1, waiting for transfers between devices, per_device(): lax.psum_scatter(mixer_out_grad, 'seq', scatter_dimension=0, tiled=True)  230 us
    all_gather x1, blocking collectives, carried_in(): everything = jax.tree.map(lambda part: lax.all_gather(part, axis), array)  223 us
    reduce_scatter x1, waiting for transfers between devices, per_device(): lax.psum_scatter(state_proj_grad, 'seq', scatter_dimension=0, tiled=True)  221 us
    unnamed x8, other arithmetic  168 us
    select_n x128, other arithmetic, step(): return jax.tree.map(lambda a, b: jnp.where(reached, a, b), new, before)  167 us
  transfers between devices with their start and end apart: 21, of which 12 were waited for; matrix products, arithmetic and copies ran while one was open for 30% of the time, Pallas kernels for 0%

commit v1 on v0

--- a/solution.py
+++ b/solution.py
@@ -1,7 +1,690 @@
+import functools
 import jax
 import jax.numpy as jnp
 from jax import lax
+from jax.experimental import pallas as pl
+from jax.experimental.pallas import tpu as pltpu
 from jax.sharding import PartitionSpec as P
+
+ORDERS = ((0, 1, 2), (1, 2, 0), (2, 0, 1))
+MIB = 1 << 20
+
+
+def coordinates():
+    me = lax.axis_index("seq")
+    return me, [me // 16, (me // 4) % 4, me % 4]
+
+
+def seq_of(at):
+    return at[0] * 16 + at[1] * 4 + at[2]
+
+
+def moved(at, axis, by):
+    return [(c + by) % 4 if i == axis else c for i, c in enumerate(at)]
+
+
+def greet_neighbours(at):
+    barrier = pltpu.get_barrier_semaphore()
+    for axis in range(3):
+        for by in (1, 3):
+            pl.semaphore_signal(barrier, inc=1, device_id={"seq": seq_of(moved(at, axis, by))})
+    pl.semaphore_wait(barrier, 6)
+
+
+def greet_all(me):
+    barrier = pltpu.get_barrier_semaphore()
+
+    @pl.loop(1, 64)
+    def _(k):
+        pl.semaphore_signal(barrier, inc=1, device_id={"seq": (me + k) % 64})
+
+    pl.semaphore_wait(barrier, 63)
+
+
+def parts_of(columns):
+    third = columns // 3
+    tiles = third // 128
+    half = tiles // 2 * 128
+    return third, half
+
+
+def region(at, order, phase, value, cols):
+    index = [None] * 3
+    for i in range(3):
+        if i < phase:
+            index[order[i]] = slice(None)
+        elif i == phase:
+            index[order[i]] = value
+        else:
+            index[order[i]] = at[order[i]]
+    return tuple(index) + (slice(None), cols)
+
+
+def gather_kernel(columns, x_ref, out_ref, local_sem, send, recv):
+    me, at = coordinates()
+    third, half = parts_of(columns)
+    own = pltpu.make_async_copy(x_ref, out_ref.at[at[0], at[1], at[2]], local_sem)
+    own.start()
+    greet_neighbours(at)
+    for phase in range(3):
+        firsts, seconds = [], []
+        for p, order in enumerate(ORDERS):
+            axis = order[phase]
+            cols = pl.ds(p * third, third)
+            here = region(at, order, phase, at[axis], cols)
+            source = x_ref.at[:, cols] if phase == 0 else out_ref.at[here]
+            for kind, by in enumerate((1, 3)):
+                copy = pltpu.make_async_remote_copy(
+                    src_ref=source,
+                    dst_ref=out_ref.at[here],
+                    send_sem=send.at[phase, p, kind],
+                    recv_sem=recv.at[phase, p, kind],
+                    device_id={"seq": seq_of(moved(at, axis, by))},
+                )
+                copy.start()
+                firsts.append(copy)
+        if phase == 0:
+            own.wait()
+        for p, order in enumerate(ORDERS):
+            axis = order[phase]
+            for kind, by in enumerate((1, 3)):
+                cols = pl.ds(p * third, half) if kind == 0 else pl.ds(p * third + half, third - half)
+                there = region(at, order, phase, (at[axis] - by) % 4, cols)
+                firsts[p * 2 + kind].wait_recv()
+                copy = pltpu.make_async_remote_copy(
+                    src_ref=out_ref.at[there],
+                    dst_ref=out_ref.at[there],
+                    send_sem=send.at[phase, p, 2 + kind],
+                    recv_sem=recv.at[phase, p, 2 + kind],
+                    device_id={"seq": seq_of(moved(at, axis, by))},
+                )
+                copy.start()
+                seconds.append(copy)
+        for copy in seconds:
+            copy.wait_recv()
+        for copy in firsts + seconds:
+            copy.wait_send()
+
+
+def gather_rows(x, collective):
+    rows, columns = x.shape
+    out = pl.pallas_call(
+        functools.partial(gather_kernel, columns),
+        out_shape=jax.ShapeDtypeStruct((4, 4, 4, rows, columns), x.dtype),
+        in_specs=[pl.BlockSpec(memory_space=pl.ANY)],
+        out_specs=pl.BlockSpec(memory_space=pl.ANY),
+        scratch_shapes=[
+            pltpu.SemaphoreType.DMA,
+            pltpu.SemaphoreType.DMA((3, 3, 4)),
+            pltpu.SemaphoreType.DMA((3, 3, 4)),
+        ],
+        compiler_params=pltpu.CompilerParams(collective_id=collective, has_side_effects=True),
+        name="gather_rows",
+    )(x)
+    return out
+
+
+def exchange_kernel(x_ref, out_ref, local_sem, send, recv):
+    me, at = coordinates()
+    own = pltpu.make_async_copy(x_ref.at[me], out_ref.at[me], local_sem)
+    own.start()
+    greet_all(me)
+
+    @pl.loop(1, 64)
+    def _(k):
+        target = ((at[0] + k // 16) % 4) * 16 + ((at[1] + k // 4) % 4) * 4 + (at[2] + k) % 4
+        pltpu.make_async_remote_copy(
+            src_ref=x_ref.at[target],
+            dst_ref=out_ref.at[me],
+            send_sem=send,
+            recv_sem=recv,
+            device_id={"seq": target},
+        ).start()
+
+    own.wait()
+    whole = pltpu.make_async_copy(x_ref.at[pl.ds(0, 63)], out_ref.at[pl.ds(0, 63)], send)
+    whole.wait()
+    whole = pltpu.make_async_copy(x_ref.at[pl.ds(0, 63)], out_ref.at[pl.ds(0, 63)], recv)
+    whole.wait()
+
+
+def exchange(x, collective):
+    return pl.pallas_call(
+        exchange_kernel,
+        out_shape=jax.ShapeDtypeStruct(x.shape, x.dtype),
+        in_specs=[pl.BlockSpec(memory_space=pl.ANY)],
+        out_specs=pl.BlockSpec(memory_space=pl.ANY),
+        scratch_shapes=[pltpu.SemaphoreType.DMA] * 3,
+        compiler_params=pltpu.CompilerParams(collective_id=collective, has_side_effects=True),
+        name="exchange",
+    )(x)
+
+
+def scatter_kernel(columns, x_ref, out_ref, buf, rest, in_sem, send, recv):
+    me, at = coordinates()
+    third, half = parts_of(columns)
+    loads = []
+    for p in range(3):
+        cols = pl.ds(p * third, third)
+        load = pltpu.make_async_copy(
+            x_ref.at[:, :, :, :, cols], buf.at[:, :, :, :, cols], in_sem.at[p]
+        )
+        load.start()
+        loads.append(load)
+    greet_neighbours(at)
+
+    def spans(p):
+        return pl.ds(p * third, half), pl.ds(p * third + half, third - half)
+
+    for phase in (2, 1, 0):
+        copies = {}
+        room = rest[phase]
+
+        def send_to(p, order, by, value, cols, slot, kind):
+            axis = order[phase]
+            lead = (slice(None),) * phase
+            copy = pltpu.make_async_remote_copy(
+                src_ref=buf.at[region(at, order, phase, value, cols)],
+                dst_ref=room.at[(slot,) + lead + (slice(None), cols)],
+                send_sem=send.at[phase, p, kind],
+                recv_sem=recv.at[phase, p, kind],
+                device_id={"seq": seq_of(moved(at, axis, by))},
+            )
+            copy.start()
+            copies[p, kind] = copy
+
+        def added(p, order, value, cols, slots):
+            lead = 4**phase
+
+            @pl.loop(0, lead)
+            def _(i):
+                free = ((), (i,), (i // 4, i % 4))[phase]
+                index = list(region(at, order, phase, value, cols))
+                for n, axis in enumerate(sorted(order[:phase])):
+                    index[axis] = free[n]
+                index = tuple(index)
+                total = buf[index].astype(jnp.float32)
+                for slot in slots:
+                    total = total + room[(slot,) + free + (slice(None), cols)].astype(jnp.float32)
+                if phase == 0 and len(slots) == 2:
+                    out_ref[:, cols] = total
+                else:
+                    buf[index] = total.astype(jnp.bfloat16)
+
+        for p, order in enumerate(ORDERS):
+            if phase == 2:
+                loads[p].wait()
+            c = at[order[phase]]
+            low, high = spans(p)
+            send_to(p, order, 1, (c + 2) % 4, low, 2, 0)
+            send_to(p, order, 3, (c + 2) % 4, high, 2, 1)
+            send_to(p, order, 1, (c + 1) % 4, high, 0, 2)
+            send_to(p, order, 3, (c + 3) % 4, low, 1, 3)
+        for p, order in enumerate(ORDERS):
+            c = at[order[phase]]
+            low, high = spans(p)
+            copies[p, 0].wait_recv()
+            added(p, order, (c + 1) % 4, low, (2,))
+            send_to(p, order, 1, (c + 1) % 4, low, 0, 4)
+            copies[p, 1].wait_recv()
+            added(p, order, (c + 3) % 4, high, (2,))
+            send_to(p, order, 3, (c + 3) % 4, high, 1, 5)
+        for p, order in enumerate(ORDERS):
+            c = at[order[phase]]
+            low, high = spans(p)
+            copies[p, 2].wait_recv()
+            copies[p, 5].wait_recv()
+            added(p, order, c, high, (0, 1))
+            copies[p, 3].wait_recv()
+            copies[p, 4].wait_recv()
+            added(p, order, c, low, (0, 1))
+        for copy in copies.values():
+            copy.wait_send()
+
+
+def scatter_rows(x, collective):
+    rows, columns = x.shape[3:]
+    return pl.pallas_call(
+        functools.partial(scatter_kernel, columns),
+        out_shape=jax.ShapeDtypeStruct((rows, columns), jnp.float32),
+        in_specs=[pl.BlockSpec(memory_space=pl.ANY)],
+        out_specs=pl.BlockSpec(memory_space=pltpu.VMEM),
+        scratch_shapes=[
+            pltpu.VMEM((4, 4, 4, rows, columns), x.dtype),
+            [
+                pltpu.VMEM((3,) + (4,) * phase + (rows, columns), x.dtype)
+                for phase in range(3)
+            ],
+            pltpu.SemaphoreType.DMA((3,)),
+            pltpu.SemaphoreType.DMA((3, 3, 6)),
+            pltpu.SemaphoreType.DMA((3, 3, 6)),
+        ],
+        compiler_params=pltpu.CompilerParams(
+            collective_id=collective, has_side_effects=True, vmem_limit_bytes=60 * MIB
+        ),
+        name="scatter_rows",
+    )(x)
+
+
+def torus_target(at, k):
+    return ((at[0] + k // 16) % 4) * 16 + ((at[1] + k // 4) % 4) * 4 + (at[2] + k) % 4
+
+
+def params(collective, **more):
+    return pltpu.CompilerParams(collective_id=collective, has_side_effects=True, **more)
+
+
+def greet_all_and_sibling(me):
+    barrier = pltpu.get_barrier_semaphore()
+
+    @pl.loop(1, 64)
+    def _(k):
+        pl.semaphore_signal(barrier, inc=1, device_id={"seq": (me + k) % 64})
+
+    pl.semaphore_signal(barrier, inc=1, device_id={"head": 1 - lax.axis_index("head")})
+    pl.semaphore_wait(barrier, 64)
+
+
+def greet_sibling():
+    barrier = pltpu.get_barrier_semaphore()
+    pl.semaphore_signal(barrier, inc=1, device_id={"head": 1 - lax.axis_index("head")})
+    pl.semaphore_wait(barrier, 1)
+
+
+def dispatch_kernel(x_ref, out_ref, local_sem, send, recv, pair_send, pair_recv):
+    me, at = coordinates()
+    head = lax.axis_index("head")
+    own = pltpu.make_async_copy(x_ref.at[me], out_ref.at[me, head], local_sem)
+    own.start()
+    greet_all_and_sibling(me)
+
+    @pl.loop(1, 64)
+    def _(k):
+        target = torus_target(at, k)
+        pltpu.make_async_remote_copy(
+            src_ref=x_ref.at[target],
+            dst_ref=out_ref.at[me, head],
+            send_sem=send,
+            recv_sem=recv.at[me],
+            device_id={"seq": target},
+        ).start()
+
+    def to_sibling(j):
+        pltpu.make_async_remote_copy(
+            src_ref=out_ref.at[j, head],
+            dst_ref=out_ref.at[j, head],
+            send_sem=pair_send,
+            recv_sem=pair_recv,
+            device_id={"head": 1 - head},
+        ).start()
+
+    own.wait()
+    to_sibling(me)
+
+    @pl.loop(1, 64)
+    def _(k):
+        source = torus_target(at, 64 - k)
+        pltpu.make_async_copy(x_ref.at[0], out_ref.at[source, head], recv.at[source]).wait()
+        to_sibling(source)
+
+    pltpu.make_async_copy(x_ref.at[pl.ds(0, 63)], x_ref.at[pl.ds(0, 63)], send).wait()
+    pltpu.make_async_copy(x_ref, x_ref, pair_send).wait()
+    pltpu.make_async_copy(x_ref, x_ref, pair_recv).wait()
+
+
+def dispatch(x, collective):
+    return pl.pallas_call(
+        dispatch_kernel,
+        out_shape=jax.ShapeDtypeStruct((64, 2) + x.shape[1:], x.dtype),
+        in_specs=[pl.BlockSpec(memory_space=pl.ANY)],
+        out_specs=pl.BlockSpec(memory_space=pl.ANY),
+        scratch_shapes=[
+            pltpu.SemaphoreType.DMA,
+            pltpu.SemaphoreType.DMA,
+            pltpu.SemaphoreType.DMA((64,)),
+            pltpu.SemaphoreType.DMA,
+            pltpu.SemaphoreType.DMA,
+        ],
+        compiler_params=params(collective),
+        name="dispatch",
+    )(x)
+
+
+def bring_home_kernel(x_ref, out_ref, theirs, sums, local_sem, send, recv, pair_send, pair_recv):
+    me, at = coordinates()
+    head = lax.axis_index("head")
+    greet_all_and_sibling(me)
+
+    @pl.loop(0, 64)
+    def _(k):
+        j = torus_target(at, k)
+        pltpu.make_async_remote_copy(
+            src_ref=x_ref.at[j, 1 - head],
+            dst_ref=theirs.at[j],
+            send_sem=pair_send,
+            recv_sem=pair_recv.at[j],
+            device_id={"head": 1 - head},
+        ).start()
+
+    def both(j):
+        pltpu.make_async_copy(theirs.at[j], theirs.at[j], pair_recv.at[j]).wait()
+        total = x_ref[j, head].astype(jnp.float32) + theirs[j].astype(jnp.float32)
+        sums[j] = total.astype(sums.dtype)
+
+    @pl.loop(1, 64)
+    def _(k):
+        j = torus_target(at, k)
+        both(j)
+        pltpu.make_async_remote_copy(
+            src_ref=sums.at[j],
+            dst_ref=out_ref.at[me],
+            send_sem=send,
+            recv_sem=recv,
+            device_id={"seq": j},
+        ).start()
+
+    both(me)
+    own = pltpu.make_async_copy(sums.at[me], out_ref.at[me], local_sem)
+    own.start()
+    own.wait()
+    pltpu.make_async_copy(theirs, theirs, pair_send).wait()
+    pltpu.make_async_copy(sums.at[pl.ds(0, 63)], sums.at[pl.ds(0, 63)], send).wait()
+    pltpu.make_async_copy(sums.at[pl.ds(0, 63)], sums.at[pl.ds(0, 63)], recv).wait()
+
+
+def bring_home(x, collective):
+    shape = (x.shape[0],) + x.shape[2:]
+    return pl.pallas_call(
+        bring_home_kernel,
+        out_shape=jax.ShapeDtypeStruct(shape, x.dtype),
+        in_specs=[pl.BlockSpec(memory_space=pltpu.VMEM)],
+        out_specs=pl.BlockSpec(memory_space=pl.ANY),
+        scratch_shapes=[
+            pltpu.VMEM(shape, x.dtype),
+            pltpu.VMEM(shape, x.dtype),
+            pltpu.SemaphoreType.DMA,
+            pltpu.SemaphoreType.DMA,
+            pltpu.SemaphoreType.DMA,
+            pltpu.SemaphoreType.DMA,
+            pltpu.SemaphoreType.DMA((64,)),
+        ],
+        compiler_params=params(collective, vmem_limit_bytes=40 * MIB),
+        name="bring_home",
+    )(x)
+
+
+def scan_kernel(reverse, x_ref, out_ref, got, made, send, recv, back_send, back_recv):
+    me, at = coordinates()
+    greet_all(me)
+    got[me] = x_ref[me]
+
+    @pl.loop(1, 64)
+    def _(k):
+        target = torus_target(at, k)
+        pltpu.make_async_remote_copy(
+            src_ref=x_ref.at[target],
+            dst_ref=got.at[me],
+            send_sem=send,
+            recv_sem=recv,
+            device_id={"seq": target},
+        ).start()
+
+    some = pl.ds(0, 63)
+    pltpu.make_async_copy(x_ref.at[some], x_ref.at[some], send).wait()
+    pltpu.make_async_copy(got.at[some], got.at[some], recv).wait()
+    heads, width = made.shape[1:]
+    chosen = lax.broadcasted_iota(jnp.int32, (heads, width), 0) == lax.broadcasted_iota(
+        jnp.int32, (heads, width), 1
+    )
+
+    def step(k, state):
+        at_k = 63 - k if reverse else k
+        made[at_k] = state
+        row = got[at_k, heads : heads + 8, :][0:1, :]
+        decay = jnp.sum(jnp.where(chosen, row, 0.0), axis=1, keepdims=True)
+        return decay * state + got[at_k, 0:heads, :]
+
+    lax.fori_loop(0, 64, step, jnp.zeros((heads, width), jnp.float32))
+    out_ref[me] = made[me]
+
+    @pl.loop(1, 64)
+    def _(k):
+        target = torus_target(at, k)
+        pltpu.make_async_remote_copy(
+            src_ref=made.at[target],
+            dst_ref=out_ref.at[me],
+            send_sem=back_send,
+            recv_sem=back_recv,
+            device_id={"seq": target},
+        ).start()
+
+    pltpu.make_async_copy(made.at[some], made.at[some], back_send).wait()
+    pltpu.make_async_copy(made.at[some], made.at[some], back_recv).wait()
+
+
+def carried(decay, state, reverse, collective):
+    heads, size, width = state.shape
+    rows = jnp.broadcast_to(jnp.pad(decay, (0, width - heads))[None, None, :], (size, 8, width))
+    sent = jnp.concatenate([state.transpose(1, 0, 2), rows], axis=1)
+    out = pl.pallas_call(
+        functools.partial(scan_kernel, reverse),
+        out_shape=jax.ShapeDtypeStruct((size, heads, width), jnp.float32),
+        in_specs=[pl.BlockSpec(memory_space=pltpu.VMEM)],
+        out_specs=pl.BlockSpec(memory_space=pltpu.VMEM),
+        scratch_shapes=[
+            pltpu.VMEM(sent.shape, jnp.float32),
+            pltpu.VMEM((size, heads, width), jnp.float32),
+        ]
+        + [pltpu.SemaphoreType.DMA] * 4,
+        compiler_params=params(collective),
+        name="carried_back" if reverse else "carried",
+    )(sent)
+    return out.transpose(1, 0, 2)
+
+
+def pair_kernel(x_ref, out_ref, theirs, send, recv):
+    greet_sibling()
+    copy = pltpu.make_async_remote_copy(
+        src_ref=x_ref,
+        dst_ref=theirs,
+        send_sem=send,
+        recv_sem=recv,
+        device_id={"head": 1 - lax.axis_index("head")},
+    )
+    copy.start()
+    copy.wait()
+    rows = x_ref.shape[0]
+    step = min(rows, 16)
+
+    @pl.loop(0, rows // step)
+    def _(i):
+        here = pl.ds(pl.multiple_of(i * step, step), step)
+        out_ref[here] = x_ref[here] + theirs[here]
+
+
+def pair_total(x, collective):
+    return pl.pallas_call(
+        pair_kernel,
+        out_shape=jax.ShapeDtypeStruct(x.shape, x.dtype),
+        in_specs=[pl.BlockSpec(memory_space=pltpu.VMEM)],
+        out_specs=pl.BlockSpec(memory_space=pltpu.VMEM),
+        scratch_shapes=[
+            pltpu.VMEM(x.shape, x.dtype),
+            pltpu.SemaphoreType.DMA,
+            pltpu.SemaphoreType.DMA,
+        ],
+        compiler_params=params(collective),
+        name="pair_total",
+    )(x)
+
+
+def small_kernel(x_ref, out_ref, got, send, recv, back_send, back_recv):
+    me, at = coordinates()
+    greet_all(me)
+    got[me] = x_ref[me]
+
+    @pl.loop(1, 64)
+    def _(k):
+        target = torus_target(at, k)
+        pltpu.make_async_remote_copy(
+            src_ref=x_ref.at[target],
+            dst_ref=got.at[me],
+            send_sem=send,
+            recv_sem=recv,
+            device_id={"seq": target},
+        ).start()
+
+    some = pl.ds(0, 63)
+    pltpu.make_async_copy(x_ref.at[some], x_ref.at[some], send).wait()
+    pltpu.make_async_copy(got.at[some], got.at[some], recv).wait()
+    out_ref[me] = lax.fori_loop(
+        1, 64, lambda k, total: total + got[k], got[0]
+    )
+
+    @pl.loop(1, 64)
+    def _(k):
+        target = torus_target(at, k)
+        pltpu.make_async_remote_copy(
+            src_ref=out_ref.at[me],
+            dst_ref=out_ref.at[me],
+            send_sem=back_send,
+            recv_sem=back_recv,
+            device_id={"seq": target},
+        ).start()
+
+    pltpu.make_async_copy(got.at[some], got.at[some], back_send).wait()
+    pltpu.make_async_copy(got.at[some], got.at[some], back_recv).wait()
+
+
+def small_totals(parts, collective):
+    flat = jnp.concatenate([part.reshape(-1) for part in parts])
+    size = flat.shape[0]
+    each = -(-size // (64 * 1024)) * 1024
+    sent = jnp.pad(flat, (0, 64 * each - size)).reshape(64, each // 128, 128)
+    out = pl.pallas_call(
+        small_kernel,
+        out_shape=jax.ShapeDtypeStruct(sent.shape, jnp.float32),
+        in_specs=[pl.BlockSpec(memory_space=pltpu.VMEM)],
+        out_specs=pl.BlockSpec(memory_space=pltpu.VMEM),
+        scratch_shapes=[pltpu.VMEM(sent.shape, jnp.float32)] + [pltpu.SemaphoreType.DMA] * 4,
+        compiler_params=params(collective),
+        name="small_totals",
+    )(sent).reshape(-1)
+    result, start = [], 0
+    for part in parts:
+        result.append(out[start : start + part.size].reshape(part.shape))
+        start += part.size
+    return result
+
+
+def routing_kernel(routes_ref, weights_ref, position_ref, weight_ref):
+    experts, tokens = position_ref.shape
+    expert = lax.broadcasted_iota(jnp.int32, (experts, tokens), 0)
+    named = jnp.zeros((experts, tokens), jnp.float32)
+    weight = jnp.zeros((experts, tokens), jnp.float32)
+    for k in range(routes_ref.shape[0]):
+        hit = expert == routes_ref[k : k + 1, :]
+        named = named + jnp.where(hit, 1.0, 0.0)
+        weight = weight + jnp.where(hit, weights_ref[k : k + 1, :], 0.0)
+    earlier = jnp.where(
+        lax.broadcasted_iota(jnp.int32, (tokens, tokens), 0)
+        < lax.broadcasted_iota(jnp.int32, (tokens, tokens), 1),
+        1.0,
+        0.0,
+    ).astype(jnp.bfloat16)
+    count = jnp.dot(named.astype(jnp.bfloat16), earlier, preferred_element_type=jnp.float32)
+    position_ref[...] = jnp.where(named > 0.0, count, -1.0)
+    weight_ref[...] = weight
+
+
+def routing(routes, route_weights, experts):
+    tokens = routes.shape[0]
+    return pl.pallas_call(
+        routing_kernel,
+        out_shape=[jax.ShapeDtypeStruct((experts, tokens), jnp.float32)] * 2,
+        name="routing",
+    )(routes.T, route_weights.T)
+
+
+def chosen_slots(position, first, count, slots):
+    tokens = position.shape[1]
+    number = lax.broadcasted_iota(jnp.int32, (count, slots, tokens), 1)
+    number = (number + slots * lax.axis_index("head")).astype(jnp.float32)
+    return jnp.where(position[:, None, :] == number, 1.0, 0.0).reshape(count * slots, tokens)
+
+
+def send_kernel(slots, position_ref, weight_ref, rows_ref, grads_ref, out_ref, grad_ref):
+    position, weight = position_ref[...], weight_ref[...]
+    count = position.shape[0]
+    tokens = position.shape[1]
+    chosen = chosen_slots(position, 0, count, slots)
+    weighted = chosen.reshape(count, slots, tokens) * weight[:, None, :]
+    slot_weight = jnp.sum(weighted.reshape(count * slots, tokens), axis=1, keepdims=True)
+    chosen = chosen.astype(jnp.bfloat16)
+    rows = jnp.dot(chosen, rows_ref[...], preferred_element_type=jnp.float32)
+    out_ref[...] = rows.astype(jnp.bfloat16).reshape(out_ref.shape)
+    grads = jnp.dot(chosen, grads_ref[...], preferred_element_type=jnp.float32) * slot_weight
+    grad_ref[...] = grads.astype(jnp.bfloat16).reshape(grad_ref.shape)
+
+
+def send_rows(position, weight, rows, grads, slots):
+    experts, tokens = position.shape
+    width = rows.shape[1]
+    step = 8
+    whole = pl.BlockSpec((tokens, width), lambda i: (0, 0))
+    mine = pl.BlockSpec((step, tokens), lambda i: (i, 0))
+    out = pl.BlockSpec((step, slots, width), lambda i: (i, 0, 0))
+    return pl.pallas_call(
+        functools.partial(send_kernel, slots),
+        grid=(experts // step,),
+        out_shape=[jax.ShapeDtypeStruct((experts, slots, width), jnp.bfloat16)] * 2,
+        in_specs=[mine, mine, whole, whole],
+        out_specs=[out, out],
+        name="send_rows",
+    )(position, weight, rows, grads)
+
+
+def combine_kernel(slots, position_ref, weight_ref, res_ref, grad_ref, mix_ref, sum_ref):
+    position, weight = position_ref[...], weight_ref[...]
+    count, tokens = position.shape
+    chosen = chosen_slots(position, 0, count, slots)
+    weighted = (chosen.reshape(count, slots, tokens) * weight[:, None, :]).reshape(chosen.shape)
+    high = weighted.astype(jnp.bfloat16)
+    less = (weighted - high.astype(jnp.float32)).astype(jnp.bfloat16)
+    rows = res_ref[...].reshape(count * slots, res_ref.shape[2])
+    grads = grad_ref[...].reshape(count * slots, grad_ref.shape[2])
+
+    def over_slots(picked, values):
+        return lax.dot_general(
+            picked, values, (((0,), (0,)), ((), ())), preferred_element_type=jnp.float32
+        )
+
+    @pl.when(pl.program_id(0) == 0)
+    def _():
+        mix_ref[...] = jnp.zeros_like(mix_ref)
+        sum_ref[...] = jnp.zeros_like(sum_ref)
+
+    mix_ref[...] += over_slots(high, rows) + over_slots(less, rows)
+    sum_ref[...] += over_slots(chosen.astype(jnp.bfloat16), grads)
+
+
+def combine(position, weight, res, grad):
+    experts, tokens = position.shape
+    _, slots, width = res.shape
+    step = 16
+    mine = pl.BlockSpec((step, tokens), lambda i: (i, 0))
+    rows = pl.BlockSpec((step, slots, width), lambda i: (i, 0, 0))
+    out = pl.BlockSpec((tokens, width), lambda i: (0, 0))
+    return pl.pallas_call(
+        functools.partial(combine_kernel, slots),
+        grid=(experts // step,),
+        out_shape=[jax.ShapeDtypeStruct((tokens, width), jnp.float32)] * 2,
+        in_specs=[mine, mine, rows, rows],
+        out_specs=[out, out],
+        compiler_params=pltpu.CompilerParams(vmem_limit_bytes=40 * MIB),
+        name="combine",
+    )(position, weight, res, grad)
+
 
 HIGHEST = lax.Precision.HIGHEST
 EPSILON = 1e-05
@@ -11,24 +694,6 @@
     count = lax.axis_size(axis)
     leading, last = (max(0, -steps), min(count, count - steps))
     return lax.ppermute(value, axis, [(source, source + steps) for source in range(leading, last)])
-
-
-def carried_in(array, axis, combine, identity, reverse):
-    peers, here = (lax.axis_size(axis), lax.axis_index(axis))
-    everything = jax.tree.map(lambda part: lax.all_gather(part, axis), array)
-    start = jax.tree.map(
-        lambda part, zero: jnp.broadcast_to(jnp.asarray(zero, part.dtype), part.shape),
-        array,
-        identity,
-    )
-
-    def step(k, before):
-        at = peers - 1 - k if reverse else k
-        reached = at > here if reverse else at < here
-        new = combine(before, jax.tree.map(lambda part: part[at], everything))
-        return jax.tree.map(lambda a, b: jnp.where(reached, a, b), new, before)
-
-    return lax.fori_loop(0, peers, step, start)
 
 
 def product(left_side, right_side):
@@ -87,28 +752,6 @@
         "tn,hpn->thp", state_read, state_start, precision=HIGHEST
     )
     return within_part + carried_part + skip_gain[None, :, None] * heads_x
-
-
-def combine_states(earlier, following):
-    first_decay, first_state = earlier
-    next_decay, next_state = following
-    return (first_decay * next_decay, next_decay[:, None, None] * first_state + next_state)
-
-
-def head_total(operand):
-    return lax.psum(operand, "head")
-
-
-def gate_stat(operand):
-    return lax.psum(operand, "head")
-
-
-def to_experts(operand):
-    return lax.all_to_all(operand, "seq", split_axis=1, concat_axis=1, tiled=True)
-
-
-def to_home(operand):
-    return lax.all_to_all(operand, "seq", split_axis=1, concat_axis=1, tiled=True)
 
 
 def per_device(
@@ -148,19 +791,33 @@
     choices_per = routes.shape[1]
     capacity = max(2, tokens * choices_per * 4 // (3 * experts_all))
     slot_count = local_experts * seq_devices * capacity
-    gathered = (
-        lax.all_gather(mixer_in, "seq", axis=0, tiled=True),
-        lax.all_gather(state_proj, "seq", axis=0, tiled=True),
-        lax.all_gather(step_proj, "seq", axis=0, tiled=True),
-        lax.all_gather(mixer_out, "seq", axis=0, tiled=True),
-        lax.all_gather(shared_gate_up, "seq", axis=0, tiled=True),
-        lax.all_gather(shared_down, "seq", axis=0, tiled=True),
-    )
-    full_in, full_state, full_step, full_out, full_shared, full_down = gathered
+    gathered = gather_rows(
+        jnp.concatenate(
+            [
+                mixer_in.reshape(-1, 2 * inner_dev),
+                state_proj,
+                jnp.pad(step_proj, ((0, 0), (0, 128 - heads_dev))),
+            ],
+            axis=1,
+        ),
+        0,
+    ).reshape(model_width, -1)
+    full_in = gathered[:, : 2 * inner_dev]
+    full_state = gathered[:, 2 * inner_dev : 2 * inner_dev + 2 * state_size]
+    full_step = gathered[:, 2 * inner_dev + 2 * state_size :][:, :heads_dev]
+    gathered = gather_rows(
+        jnp.concatenate(
+            [mixer_out, shared_gate_up.reshape(-1, 2 * shared_dev), shared_down], axis=1
+        ),
+        1,
+    ).reshape(model_width, -1)
+    full_out = gathered[:, :inner_dev]
+    shared_flat = gathered[:, inner_dev : inner_dev + 2 * shared_dev]
+    full_down = gathered[:, inner_dev + 2 * shared_dev :]
     resid_in = layer_in.astype(jnp.float32)
     scale_first = rms_scale(resid_in)
     normed = (resid_in * scale_first * norm_first).astype(jnp.bfloat16)
-    zx_both = product(normed, full_in.reshape(model_width, 2 * inner_dev))
+    zx_both = product(normed, full_in)
     gate_z = zx_both[:, :inner_dev]
     pre_x = zx_both[:, inner_dev:]
     pre_bc = product(normed, full_state)
@@ -178,48 +835,32 @@
     state_read = active[:, inner_dev + state_size :]
     step_size = jax.nn.softplus(step_raw)
     decay_total, state_local = group_state(heads_x, state_in, step_size, decay_rate)
-    identity = (jnp.ones_like(decay_total), jnp.zeros_like(state_local))
-    prefix = carried_in((decay_total, state_local), "seq", combine_states, identity, False)
-    state_start = prefix[1]
+    state_start = carried(decay_total, state_local, False, 2)
     ssd = group_out(
         heads_x, state_in, state_read, step_size, decay_rate, state_start, skip_gain
     ).reshape(tokens, inner_dev)
     gate_act = silu(gate_z)
     gated_ssd = ssd * gate_act
-    gate_scale = lax.rsqrt(gate_stat(jnp.sum(gated_ssd * gated_ssd, axis=1)) / inner_all + EPSILON)[
+    gate_scale = lax.rsqrt(pair_total(jnp.sum(gated_ssd * gated_ssd, axis=1).reshape(-1, 128), 4).reshape(-1) / inner_all + EPSILON)[
         :, None
     ]
     normed_gate = (gated_ssd * gate_scale * gate_gain).astype(jnp.bfloat16)
-    mixer_sum = head_total(product_nt(normed_gate, full_out))
+    mixer_sum = pair_total(product_nt(normed_gate, full_out), 6)
     residual = resid_in + mixer_sum
     scale_second = rms_scale(residual)
     normed_second = (residual * scale_second * norm_second).astype(jnp.bfloat16)
-    shared_flat = full_shared.reshape(model_width, 2 * shared_dev)
     shared_both = product(normed_second, shared_flat)
     shared_gate = shared_both[:, :shared_dev]
     shared_up = shared_both[:, shared_dev:]
     shared_hid = (silu(shared_gate) * shared_up).astype(jnp.bfloat16)
     shared_part = product_nt(shared_hid, full_down)
-    flat_routes = routes.reshape(-1)
-    one_hot = (flat_routes[:, None] == jnp.arange(experts_all, dtype=jnp.int32)[None, :]).astype(
-        jnp.int32
-    )
-    position = jnp.sum((jnp.cumsum(one_hot, axis=0) - one_hot) * one_hot, axis=1)
-    slot_row = (
-        flat_routes % local_experts * (seq_devices * capacity)
-        + flat_routes // local_experts * capacity
-        + position
-    )
-    owner_mask = (slot_row[None, :] == jnp.arange(slot_count, dtype=jnp.int32)[:, None]).reshape(
-        slot_count, tokens, choices_per
-    )
-    picker = jnp.any(owner_mask, axis=2).astype(jnp.bfloat16)
-    send_rows = (
-        product(picker, normed_second)
-        .astype(jnp.bfloat16)
-        .reshape(local_experts, seq_devices * capacity, model_width)
-    )
-    slot_in = to_experts(send_rows)
+    position, slot_weight = routing(routes, route_weights, experts_all)
+    rows_out, grads_out = send_rows(
+        position, slot_weight, normed_second, grad_out, capacity // lax.axis_size("head")
+    )
+    slot_shape = (local_experts, seq_devices * capacity, model_width)
+    slot_in = dispatch(rows_out, 11).reshape(slot_shape)
+    grad_slots = dispatch(grads_out, 12).reshape(slot_shape)
     gate_up_res = jnp.einsum(
         "erd,edkf->erkf", slot_in, expert_gate_up, preferred_element_type=jnp.float32
     )
@@ -229,25 +870,9 @@
     expert_res = jnp.einsum(
         "erf,efd->erd", expert_hid, expert_down, preferred_element_type=jnp.float32
     ).astype(jnp.bfloat16)
-    home_rows = to_home(expert_res).reshape(slot_count, model_width)
-    picked = home_rows[slot_row].astype(jnp.float32).reshape(tokens, choices_per, model_width)
-    expert_mix = jnp.sum(picked * route_weights[:, :, None], axis=1)
-    branch_sum = head_total(shared_part + expert_mix)
-    layer_out = (residual + branch_sum).astype(jnp.bfloat16)
-    gathered = (
-        lax.all_gather(mixer_in, "seq", axis=0, tiled=True),
-        lax.all_gather(state_proj, "seq", axis=0, tiled=True),
-        lax.all_gather(step_proj, "seq", axis=0, tiled=True),
-        lax.all_gather(mixer_out, "seq", axis=0, tiled=True),
-        lax.all_gather(shared_gate_up, "seq", axis=0, tiled=True),
-        lax.all_gather(shared_down, "seq", axis=0, tiled=True),
-    )
-    full_in, full_state, full_step, full_out, full_shared, full_down = gathered
-    shared_flat = full_shared.reshape(model_width, 2 * shared_dev)
+    home_shape = (seq_devices, 2, capacity // 2, model_width)
+    home_rows = bring_home(expert_res.reshape(home_shape), 13)
     grad_float = grad_out.astype(jnp.float32)
-    slot_weight = jnp.zeros((slot_count,), jnp.float32).at[slot_row].set(route_weights.reshape(-1))
-    grad_send = (product(picker, grad_out) * slot_weight[:, None]).astype(jnp.bfloat16)
-    grad_slots = to_experts(grad_send.reshape(local_experts, seq_devices * capacity, model_width))
     grad_hid = jnp.einsum(
         "erd,efd->erf", grad_slots, expert_down, preferred_element_type=jnp.float32
     )
@@ -263,10 +888,10 @@
     grad_slot_in = jnp.einsum(
         "erkf,edkf->erd", grad_gate_up, expert_gate_up, preferred_element_type=jnp.float32
     ).astype(jnp.bfloat16)
-    grad_home = to_home(grad_slot_in).reshape(slot_count, model_width)
-    expert_grad_rows = jnp.sum(
-        grad_home[slot_row].astype(jnp.float32).reshape(tokens, choices_per, model_width), axis=1
-    )
+    grad_home = bring_home(grad_slot_in.reshape(home_shape), 14)
+    expert_mix, expert_grad_rows = combine(position, slot_weight, home_rows, grad_home)
+    branch_sum = pair_total(shared_part + expert_mix, 7)
+    layer_out = (residual + branch_sum).astype(jnp.bfloat16)
     grad_shared_hid = product(grad_out, full_down)
     grad_shared_gate = grad_shared_hid * shared_up * silu_slope(shared_gate)
     grad_shared_up = grad_shared_hid * silu(shared_gate)
@@ -274,10 +899,8 @@
         jnp.bfloat16
     )
     shared_down_grad = product_tn(grad_out, shared_hid)
-    shared_gate_up_grad = product_tn(normed_second, grad_shared_both).reshape(
-        model_width, 2, shared_dev
-    )
-    grad_normed_second = head_total(product_nt(grad_shared_both, shared_flat) + expert_grad_rows)
+    shared_gate_up_grad = product_tn(normed_second, grad_shared_both)
+    grad_normed_second = pair_total(product_nt(grad_shared_both, shared_flat) + expert_grad_rows, 8)
     norm_second_grad, grad_resid_norm = norm_back(
         residual, scale_second, norm_second, grad_normed_second
     )
@@ -286,7 +909,7 @@
     mixer_out_grad = product_tn(grad_mix, normed_gate)
     grad_normed_gate = product(grad_mix, full_out)
     weighted = grad_normed_gate * gate_gain
-    inner_dot = gate_stat(jnp.sum(weighted * gated_ssd, axis=1))[:, None]
+    inner_dot = pair_total(jnp.sum(weighted * gated_ssd, axis=1).reshape(-1, 128), 5).reshape(-1)[:, None]
     grad_gated = gate_scale * weighted - gated_ssd * gate_scale**3 * inner_dot / inner_all
     gate_gain_grad = jnp.sum(grad_normed_gate * gated_ssd * gate_scale, axis=0)
     grad_ssd = grad_gated * gate_act
@@ -303,18 +926,16 @@
         grad_start,
         skip_gain_grad,
     ) = pull_out(grad_ssd.reshape(tokens, heads_dev, head_size))
-    suffix = carried_in((decay_total, grad_start), "seq", combine_states, identity, True)
-    grad_next = suffix[1]
+    grad_next = carried(decay_total, grad_start, True, 3)
     grad_decay = jnp.sum(grad_next * state_start, axis=(1, 2))
     _, pull_state = jax.vjp(group_state, heads_x, state_in, step_size, decay_rate)
     grad_x_second, grad_in_second, grad_step_second, grad_rate_second = pull_state(
         (grad_decay, grad_next)
     )
     decay_rate_grad = grad_rate_first + grad_rate_second
-    grad_bc = lax.psum(
-        jnp.concatenate([grad_in_first + grad_in_second, grad_read], axis=1).astype(jnp.bfloat16),
-        "head",
-    ).astype(jnp.float32)
+    grad_bc = pair_total(
+        jnp.concatenate([grad_in_first + grad_in_second, grad_read], axis=1), 10
+    )
     grad_active = jnp.concatenate(
         [(grad_x_first + grad_x_second).reshape(tokens, inner_dev), grad_bc], axis=1
     )
@@ -341,24 +962,33 @@
     grad_zx = jnp.concatenate([grad_gate_z, grad_pre[:, :inner_dev]], axis=1).astype(jnp.bfloat16)
     grad_bc_low = grad_pre[:, inner_dev:].astype(jnp.bfloat16)
     grad_step_low = grad_step_raw.astype(jnp.bfloat16)
-    in_partial = product_nt(grad_zx, full_in.reshape(model_width, 2 * inner_dev)) + product_nt(
+    in_partial = product_nt(grad_zx, full_in) + product_nt(
         grad_step_low, full_step
     )
-    grad_normed = head_total(in_partial) + product_nt(grad_bc_low, full_state)
-    mixer_in_grad = product_tn(normed, grad_zx).reshape(model_width, 2, inner_dev)
+    grad_normed = pair_total(in_partial, 9) + product_nt(grad_bc_low, full_state)
+    mixer_in_grad = product_tn(normed, grad_zx)
     state_proj_grad = product_tn(normed, grad_bc_low)
     step_proj_grad = product_tn(normed, grad_step_low)
     norm_first_grad, grad_in_norm = norm_back(resid_in, scale_first, norm_first, grad_normed)
     input_grad = grad_resid + grad_in_norm
+    low = lambda *parts: jnp.concatenate(
+        [part.astype(jnp.bfloat16) for part in parts], axis=1
+    ).reshape(4, 4, 4, model_width // 64, -1)
+    summed = scatter_rows(
+        low(mixer_in_grad, state_proj_grad, jnp.pad(step_proj_grad, ((0, 0), (0, 128 - heads_dev)))),
+        15,
+    )
+    summed_late = scatter_rows(low(mixer_out_grad, shared_gate_up_grad, shared_down_grad), 16)
+    wide = 2 * inner_dev + 2 * state_size
     weight_sums = (
-        lax.psum_scatter(mixer_in_grad, "seq", scatter_dimension=0, tiled=True),
-        lax.psum_scatter(state_proj_grad, "seq", scatter_dimension=0, tiled=True),
-        lax.psum_scatter(step_proj_grad, "seq", scatter_dimension=0, tiled=True),
-        lax.psum_scatter(mixer_out_grad, "seq", scatter_dimension=0, tiled=True),
-        lax.psum_scatter(shared_gate_up_grad, "seq", scatter_dimension=0, tiled=True),
-        lax.psum_scatter(shared_down_grad, "seq", scatter_dimension=0, tiled=True),
-    )
-    small_sums = lax.psum(
+        summed[:, : 2 * inner_dev].reshape(-1, 2, inner_dev),
+        summed[:, 2 * inner_dev : wide],
+        summed[:, wide : wide + heads_dev],
+        summed_late[:, :inner_dev],
+        summed_late[:, inner_dev : inner_dev + 2 * shared_dev].reshape(-1, 2, shared_dev),
+        summed_late[:, inner_dev + 2 * shared_dev :],
+    )
+    small_sums = small_totals(
         (
             norm_first_grad,
             norm_second_grad,
@@ -369,7 +999,7 @@
             skip_gain_grad,
             gate_gain_grad,
         ),
-        "seq",
+        17,
     )
     return (
         layer_out,

time: 3480 us -> 881 us (0.25)
  waiting for transfers between devices: 1150 us -> 0.01 us
  blocking collectives: 896 us -> 0 us
  local copies, waits for them, and re-layouts: 749 us -> 73 us
  Pallas kernels: 0 us -> 593 us
  other arithmetic: 435 us -> 68.4 us
  starting transfers between devices: 50.2 us -> 5.76 us
    pallas_call x0 -> x21, Pallas kernels: none -> 593 us  [the longest x2 117 us: bring_home(): pl.pallas_call(bring_home_kernel, out_shape=jax.ShapeDtypeStruct(shape, x...]
    all_gather x3 -> x0, blocking collectives: 523 us -> none  [the longest x1 223 us: carried_in(): everything = jax.tree.map(lambda part: lax.all_gather(part, axis), array)]
    reduce_scatter x2 -> x0, waiting for transfers between devices: 451 us -> none  [the longest x1 230 us: per_device(): lax.psum_scatter(mixer_out_grad, 'seq', scatter_dimension=0, tiled=True)]
    psum x3 -> x0, blocking collectives: 373 us -> none  [the longest x1 297 us: per_device(): lax.psum((norm_first_grad, norm_second_grad, step_bias_grad, kernel_grad[...]
    unnamed x18 -> x0, waiting for transfers between devices: 338 us -> none
    unnamed x269 -> x242, local copies, waits for them, and re-layouts: 276 us -> 22.4 us
    all_to_all x4 -> x0, waiting for transfers between devices: 183 us -> none  [the longest x2 138 us: to_home(): lax.all_to_all(operand, 'seq', split_axis=1, concat_axis=1, tiled=True)]
    reshape x6 -> x7, local copies, waits for them, and re-layouts: 176 us -> 4.32 us  [the longest x2 1.22 us: small_totals(): result.append(out[start:start + part.size].reshape(part.shape))]
  transfers between devices with their start and end apart: 21 -> 2, of which waited for: 12 -> 0; matrix products, arithmetic and copies ran while one was open for 30% -> 6% of each run, Pallas kernels for 0% -> 11%
where the time goes in v1:
time: 881 us; the launch traced here: 876 us
  Pallas kernels  593 us (67%)
  matrix products  133 us (15%)
  local copies, waits for them, and re-layouts  73 us (8%)
  other arithmetic  68.4 us (8%)
    pallas_call x2, Pallas kernels, bring_home(): pl.pallas_call(bring_home_kernel, out_shape=jax.ShapeDtypeStruct(shape, x...  117 us
    pallas_call x2, Pallas kernels, dispatch(): pl.pallas_call(dispatch_kernel, out_shape=jax.ShapeDtypeStruct((64, 2) +...  116 us
    pallas_call x2, Pallas kernels, scatter_rows(): pl.pallas_call(functools.partial(scatter_kernel, columns), out_shape=jax....  98.6 us
    pallas_call x2, Pallas kernels, gather_rows(): pl.pallas_call(functools.partial(gather_kernel, columns), out_shape=jax.S...  97.6 us
    pallas_call x2, Pallas kernels, carried(): pl.pallas_call(functools.partial(scan_kernel, reverse), out_shape=jax.Sha...  76.3 us
    pallas_call x7, Pallas kernels, pair_total(): pl.pallas_call(pair_kernel, out_shape=jax.ShapeDtypeStruct(x.shape, x.dty...  54.2 us
    dot_general x3, matrix products, group_out(): within_part = jnp.einsum('tsh,shp->thp', mixing, heads_x, precision=HIGHEST)  27.8 us
    unnamed x242, local copies, waits for them, and re-layouts  22.4 us
  transfers between devices with their start and end apart: 2, of which 0 were waited for; matrix products, arithmetic and copies ran while one was open for 6% of the time, Pallas kernels for 11%

profile of v1, /device:TPU:1, one launch (start us, length us, event | category | flops | bytes accessed | tf_op | source)
XLA Modules:
  0.0 875.5 jit_solution(4556621751189421609)
XLA Ops:
  3.1 52.6 %gather_rows.2 = bf16[4,4,4,24,3456]{4,3,2,1,0:T(8,128)(2,1)} custom-call(bf16[24,3456]{1,0:T(8,128)(2,1)} %fusion.105.x_ref), custom_call_target="tpu_custom_call" | custom-call | tf_op jit(solution)/shard_map/gather_rows/pallas_call | solution.py:111
  74.6 44.9 %gather_rows.3 = bf16[4,4,4,24,3072]{4,3,2,1,0:T(8,128)(2,1)} custom-call(bf16[24,3072]{1,0:T(8,128)(2,1)} %pad_maximum_fusion.14.x_ref), custom_call_target="tpu_custom_call" | custom-call | tf_op jit(solution)/shard_map/gather_rows/pallas_call | solution.py:111
  140.0 31.0 %carried.1 = f32[64,24,128]{2,1,0:T(8,128)} custom-call(f32[64,32,128]{2,1,0:T(8,128)} %pad_maximum_fusion.5.x_ref), custom_call_target="tpu_custom_call" | custom-call | tf_op jit(solution)/shard_map/carried/pallas_call | solution.py:469
  173.9 8.8 %fusion.57 = f32[256,24,64]{0,2,1:T(8,128)} fusion(f32[256,24,64]{0,2,1:T(8,128)S(1)} %bitcast.262, f32[256,24,64]{0,2,1:T(8,128)S(1)} %fusion.93, f32[256,24]{0,1:T(8,128)S(1)} %copy-done.89, f32[256,256]{1,0:T(8,128)S(1)} %copy-done.64, f32[256,24]{0,1:T(8,128)S(1)} %copy-done.87, pred[256,256]{1,0:T(8,128)(4,1)S(1)} %copy-done.76, ...), kind=kOutput, calls=%fused_computation.105 | convolution fusion | flops 1217396736 | bytes 5120096 | tf_op jit(solution)/shard_map/tsh,shp->thp/dot_general | solution.py:750
  189.8 12.9 %pair_total.7 = f32[2,128]{1,0:T(2,128)} custom-call(f32[2,128]{1,0:T(2,128)} %bitcast.312), custom_call_target="tpu_custom_call" | custom-call | tf_op jit(solution)/shard_map/pair_total/pallas_call | solution.py:506
  210.1 6.2 pair_total.8
  223.3 6.9 send_rows.1
  230.2 54.8 %dispatch.2 = bf16[64,2,16,1536]{3,2,1,0:T(8,128)(2,1)} custom-call(bf16[64,16,1536]{2,1,0:T(8,128)(2,1)} %get-tuple-element.26.x_ref), custom_call_target="tpu_custom_call" | custom-call | tf_op jit(solution)/shard_map/dispatch/pallas_call | solution.py:336
  295.5 57.8 %bring_home.2.res_ref = bf16[64,16,1536]{2,1,0:T(8,128)(2,1)S(1)} custom-call(bf16[64,2,16,1536]{3,2,1,0:T(8,128)(2,1)S(1)} %bitcast.253), custom_call_target="tpu_custom_call" | custom-call | tf_op jit(solution)/shard_map/bring_home/pallas_call | solution.py:397
  354.9 61.2 %dispatch.3 = bf16[64,2,16,1536]{3,2,1,0:T(8,128)(2,1)} custom-call(bf16[64,16,1536]{2,1,0:T(8,128)(2,1)} %get-tuple-element.27.x_ref), custom_call_target="tpu_custom_call" | custom-call | tf_op jit(solution)/shard_map/dispatch/pallas_call | solution.py:336
  416.1 6.7 fusion.84
  426.7 59.1 %bring_home.3.grad_ref = bf16[64,16,1536]{2,1,0:T(8,128)(2,1)S(1)} custom-call(bf16[64,2,16,1536]{3,2,1,0:T(8,128)(2,1)S(1)} %bitcast.254), custom_call_target="tpu_custom_call" | custom-call | tf_op jit(solution)/shard_map/bring_home/pallas_call | solution.py:397
  494.2 6.8 pair_total.10
  507.7 6.3 pair_total.9
  545.3 45.3 %carried_back.1 = f32[64,24,128]{2,1,0:T(8,128)} custom-call(f32[64,32,128]{2,1,0:T(8,128)} %pad_maximum_fusion.4.x_ref), custom_call_target="tpu_custom_call" | custom-call | tf_op jit(solution)/shard_map/carried_back/pallas_call | solution.py:469
  598.6 10.8 %fusion.19 = (f32[256,24]{0,1:T(8,128)}, f32[256,24]{0,1:T(8,128)}, f32[256,24]{0,1:T(8,128)}, f32[256,256]{1,0:T(8,128)S(1)}) fusion(f32[256,24]{0,1:T(8,128)S(1)} %copy-done.90, f32[256,256]{1,0:T(8,128)S(1)} %copy-done.65, f32[256,24]{0,1:T(8,128)S(1)} %copy-done.88, pred[256,256]{1,0:T(8,128)(4,1)S(1)} %copy-done.77, f32[24,64,256]{2,1,0:T(8,128)S(1)} %bitcast.288, ...), kind=kOutput, calls=%fused_computation.35 | convolution fusion | flops 1231468544 | bytes 3858432 | tf_op jit(solution)/shard_map/transpose(jvp(tsh,shp->thp))/dot_general | solution.py:750
  618.6 8.3 fusion.56
  670.2 7.4 pad_maximum_fusion
  677.7 12.7 %copy.212 = bf16[1536,3072]{1,0:T(8,128)(2,1)} copy(bf16[1536,3072]{0,1:T(8,128)(2,1)} %pad_maximum_fusion) | data formatting | bytes 18874368 | tf_op jit(solution)/shard_map/concatenate | solution.py:974
  690.4 49.2 %scatter_rows.3 = f32[24,3072]{1,0:T(8,128)} custom-call(bf16[4,4,4,24,3072]{4,3,2,1,0:T(8,128)(2,1)} %bitcast.260), custom_call_target="tpu_custom_call" | custom-call | tf_op jit(solution)/shard_map/scatter_rows/pallas_call | solution.py:247
  747.5 7.2 copy.214
  771.4 49.4 %scatter_rows.2 = f32[24,3456]{1,0:T(8,128)} custom-call(bf16[4,4,4,24,3456]{4,3,2,1,0:T(8,128)(2,1)} %bitcast.259), custom_call_target="tpu_custom_call" | custom-call | tf_op jit(solution)/shard_map/scatter_rows/pallas_call | solution.py:247
  826.0 14.0 %pair_total.13 = f32[256,1536]{1,0:T(8,128)} custom-call(f32[256,1536]{1,0:T(8,128)} %convolution_add_fusion.2.x_ref), custom_call_target="tpu_custom_call" | custom-call | tf_op jit(solution)/shard_map/pair_total/pallas_call | solution.py:506
  844.4 20.4 %small_totals.1 = f32[64,8,128]{2,1,0:T(8,128)} custom-call(f32[64,8,128]{2,1,0:T(8,128)} %pad_bitcast_fusion.x_ref), custom_call_target="tpu_custom_call" | custom-call | tf_op jit(solution)/shard_map/small_totals/pallas_call | solution.py:564
  (398 shorter events, 231.8 us)
Async XLA Ops:
  0.7 284.4 %copy-start = (bf16[1,1536,2,256]{3,2,1,0:T(2,128)(2,1)S(1)}, bf16[1,1536,2,256]{3,2,1,0:T(2,128)(2,1)}, u32[]{:S(2)}) copy-start(bf16[1,1536,2,256]{3,2,1,0:T(2,128)(2,1)} %param.35) | copy-start | bytes 4718596
  3.1 52.7 %copy-start.17 = (bf16[256,1536]{1,0:T(8,128)(2,1)S(1)}, bf16[256,1536]{1,0:T(8,128)(2,1)}, u32[]{:S(2)}) copy-start(bf16[256,1536]{1,0:T(8,128)(2,1)} %param.20) | copy-start | bytes 2359300
  3.1 53.5 %copy-start.66 = (f32[1536]{0:T(1024)S(1)}, f32[1536]{0:T(1024)}, u32[]{:S(2)}) copy-start(f32[1536]{0:T(1024)} %param.21) | copy-start | bytes 18436
  56.6 13.0 %copy-start.84 = (f32[256]{0:T(256)}, f32[256]{0:T(256)S(1)}, u32[]{:S(2)}) copy-start(f32[256]{0:T(256)S(1)} %get-tuple-element.179) | copy-start | bytes 3076
  65.3 57.2 %collective-permute-start = (f32[3,1792]{1,0:T(4,128)S(1)}, f32[3,1792]{1,0:T(4,128)}, u32[]{:S(2)}, u32[]{:S(2)}) collective-permute-start(f32[3,1792]{1,0:T(4,128)S(1)} %fusion.136), channel_id=1, source_target_pairs={{0,2},{2,4},{4,6},{6,8},{8,10},{10,12},{12,14},{14,16},{16,18},{18... | collective-permute-start | bytes 64520 | tf_op jit(solution)/shard_map/ppermute | solution.py:696
  71.1 48.4 %copy-start.54 = (f32[256,24]{1,0:T(8,128)}, f32[256,24]{1,0:T(8,128)S(1)}, u32[]{:S(2)}) copy-start(f32[256,24]{1,0:T(8,128)S(1)} %get-tuple-element.183) | copy-start | bytes 73732
  72.2 47.3 %copy-start.45 = (f32[24,2,128]{0,2,1:T(8,128)}, f32[24,2,128]{0,2,1:T(8,128)S(1)}, u32[]{:S(2)}) copy-start(f32[24,2,128]{0,2,1:T(8,128)S(1)} %copy.179) | copy-start | bytes 73732
  72.2 47.3 %copy-start.97 = (f32[24]{0:T(128)}, f32[24]{0:T(128)S(1)}, u32[]{:S(2)}) copy-start(f32[24]{0:T(128)S(1)} %slice_bitcast_fusion) | copy-start | bytes 292
  72.4 51.8 %copy-start.70 = (f32[1792]{0:T(1024)}, f32[1792]{0:T(1024)S(1)}, u32[]{:S(2)}) copy-start(f32[1792]{0:T(1024)S(1)} %get-tuple-element.137) | copy-start | bytes 21508
  72.4 51.8 %copy-start.72 = (f32[1792]{0:T(1024)}, f32[1792]{0:T(1024)S(1)}, u32[]{:S(2)}) copy-start(f32[1792]{0:T(1024)S(1)} %get-tuple-element.138) | copy-start | bytes 21508
  72.4 51.8 %copy-start.74 = (f32[1792]{0:T(1024)}, f32[1792]{0:T(1024)S(1)}, u32[]{:S(2)}) copy-start(f32[1792]{0:T(1024)S(1)} %get-tuple-element.139) | copy-start | bytes 21508
  140.0 33.8 %copy-start.87 = (f32[256,24]{0,1:T(8,128)S(1)}, f32[256,24]{0,1:T(8,128)}, u32[]{:S(2)}) copy-start(f32[256,24]{0,1:T(8,128)} %copy.180) | copy-start | bytes 73732
  185.7 18.9 %copy-start.81 = (f32[1536]{0:T(1024)S(1)}, f32[1536]{0:T(1024)}, u32[]{:S(2)}) copy-start(f32[1536]{0:T(1024)} %param.30) | copy-start | bytes 18436
  203.4 322.9 %copy-start.94 = (f32[256]{0:T(256)}, f32[256]{0:T(256)S(1)}, u32[]{:S(2)}) copy-start(f32[256]{0:T(256)S(1)} %rsqrt_bitcast_fusion) | copy-start | bytes 3076
  416.1 69.7 %slice-start.2 = ((s8[9437184]{0:T(1024)(128)(4,1)}), s8[4194304]{0:T(1024)(128)(4,1)S(1)}, s32[]{:S(2)}) async-start(s8[9437184]{0:T(1024)(128)(4,1)} %bitcast.275), calls=%async_computation.2 | async-start | bytes 8388608
  416.1 69.7 %slice-start.3 = ((s8[9437184]{0:T(1024)(128)(4,1)}), s8[4194304]{0:T(1024)(128)(4,1)S(1)}, s32[]{:S(2)}) async-start(s8[9437184]{0:T(1024)(128)(4,1)} %bitcast.275), calls=%async_computation.3 | async-start | bytes 8388608
  422.9 63.0 %slice-start.4 = ((s8[9437184]{0:T(1024)(128)(4,1)}), s8[1048576]{0:T(1024)(128)(4,1)S(1)}, s32[]{:S(2)}) async-start(s8[9437184]{0:T(1024)(128)(4,1)} %bitcast.275), calls=%async_computation.4 | async-start | bytes 2097152
  426.7 59.2 %copy-start.39 = (bf16[256,1536]{1,0:T(8,128)(2,1)S(1)}, bf16[256,1536]{1,0:T(8,128)(2,1)}, u32[]{:S(2)}) copy-start(bf16[256,1536]{1,0:T(8,128)(2,1)} %grads_ref.1) | copy-start | bytes 2359300
  426.7 59.2 %copy-start.106 = (f32[256,1024]{1,0:T(8,128)S(1)}, f32[256,1024]{1,0:T(8,128)}, u32[]{:S(2)}) copy-start(f32[256,1024]{1,0:T(8,128)} %fusion.33) | copy-start | bytes 3145732
  545.3 49.6 %copy-start.29 = (f32[256,1536]{0,1:T(8,128)S(1)}, f32[256,1536]{0,1:T(8,128)}, u32[]{:S(2)}) copy-start(f32[256,1536]{0,1:T(8,128)} %copy.176) | copy-start | bytes 4718596
  656.2 98.5 %collective-permute-start.1 = (f32[3,1792]{1,0:T(4,128)}, f32[3,1792]{1,0:T(4,128)}, u32[]{:S(2)}, u32[]{:S(2)}) collective-permute-start(f32[3,1792]{1,0:T(4,128)} %pad_add_fusion.2), channel_id=1, source_target_pairs={{2,0},{4,2},{6,4},{8,6},{10,8},{12,10},{14,12},{16,14},{18,16},{20... | collective-permute-start | bytes 64520 | tf_op jit(solution)/shard_map/ppermute | solution.py:696
  840.1 29.1 %slice-start.7 = ((f32[24,3456]{1,0:T(8,128)}), f32[24,3072]{1,0:T(8,128)S(1)}, s32[]{:S(2)}) async-start(f32[24,3456]{1,0:T(8,128)} %scatter_rows.2), calls=%async_computation.7 | async-start | bytes 589824 | tf_op jit(solution)/shard_map/slice | solution.py:984
  840.1 31.3 %copy-start.101 = (f32[256]{0:T(256)S(1)}, f32[256]{0:T(256)}, u32[]{:S(2)}) copy-start(f32[256]{0:T(256)} %get-tuple-element.178) | copy-start | bytes 3076
  843.5 27.8 %copy-start.19 = (bf16[256,1536]{1,0:T(8,128)(2,1)S(1)}, bf16[256,1536]{1,0:T(8,128)(2,1)}, u32[]{:S(2)}) copy-start(bf16[256,1536]{1,0:T(8,128)(2,1)} %param.20) | copy-start | bytes 2359300
  (98 other events, 424.2 us)

commit v2 on v0

v2 whole, which is shorter than its diff:
```python
import functools
import jax
import jax.numpy as jnp
from jax import lax
from jax.experimental import pallas as pl
from jax.experimental.pallas import tpu as pltpu
from jax.sharding import PartitionSpec as P

ORDERS = ((0, 1, 2), (1, 2, 0), (2, 0, 1))
MIB = 1 << 20


def coordinates():
    me = lax.axis_index("seq")
    return me, [me // 16, (me // 4) % 4, me % 4]


def seq_of(at):
    return at[0] * 16 + at[1] * 4 + at[2]


def moved(at, axis, by):
    return [(c + by) % 4 if i == axis else c for i, c in enumerate(at)]


def greet_neighbours(at):
    barrier = pltpu.get_barrier_semaphore()
    for axis in range(3):
        for by in (1, 3):
            pl.semaphore_signal(barrier, inc=1, device_id={"seq": seq_of(moved(at, axis, by))})
    pl.semaphore_wait(barrier, 6)


def greet_all(me):
    barrier = pltpu.get_barrier_semaphore()

    @pl.loop(1, 64)
    def _(k):
        pl.semaphore_signal(barrier, inc=1, device_id={"seq": (me + k) % 64})

    pl.semaphore_wait(barrier, 63)


def parts_of(columns):
    third = columns // 3
    tiles = third // 128
    half = tiles // 2 * 128
    return third, half


def region(at, order, phase, value, cols):
    index = [None] * 3
    for i in range(3):
        if i < phase:
            index[order[i]] = slice(None)
        elif i == phase:
            index[order[i]] = value
        else:
            index[order[i]] = at[order[i]]
    return tuple(index) + (slice(None), cols)


def gather_kernel(columns, x_ref, out_ref, local_sem, send, recv):
    me, at = coordinates()
    third, half = parts_of(columns)
    own = pltpu.make_async_copy(x_ref, out_ref.at[at[0], at[1], at[2]], local_sem)
    own.start()
    greet_neighbours(at)
    for phase in range(3):
        firsts, seconds = [], []
        for p, order in enumerate(ORDERS):
            axis = order[phase]
            cols = pl.ds(p * third, third)
            here = region(at, order, phase, at[axis], cols)
            source = x_ref.at[:, cols] if phase == 0 else out_ref.at[here]
            for kind, by in enumerate((1, 3)):
                copy = pltpu.make_async_remote_copy(
                    src_ref=source,
                    dst_ref=out_ref.at[here],
                    send_sem=send.at[phase, p, kind],
                    recv_sem=recv.at[phase, p, kind],
                    device_id={"seq": seq_of(moved(at, axis, by))},
                )
                copy.start()
                firsts.append(copy)
        if phase == 0:
            own.wait()
        for p, order in enumerate(ORDERS):
            axis = order[phase]
            for kind, by in enumerate((1, 3)):
                cols = pl.ds(p * third, half) if kind == 0 else pl.ds(p * third + half, third - half)
                there = region(at, order, phase, (at[axis] - by) % 4, cols)
                firsts[p * 2 + kind].wait_recv()
                copy = pltpu.make_async_remote_copy(
                    src_ref=out_ref.at[there],
                    dst_ref=out_ref.at[there],
                    send_sem=send.at[phase, p, 2 + kind],
                    recv_sem=recv.at[phase, p, 2 + kind],
                    device_id={"seq": seq_of(moved(at, axis, by))},
                )
                copy.start()
                seconds.append(copy)
        for copy in seconds:
            copy.wait_recv()
        for copy in firsts + seconds:
            copy.wait_send()


def gather_rows(x, collective):
    rows, columns = x.shape
    out = pl.pallas_call(
        functools.partial(gather_kernel, columns),
        out_shape=jax.ShapeDtypeStruct((4, 4, 4, rows, columns), x.dtype),
        in_specs=[pl.BlockSpec(memory_space=pl.ANY)],
        out_specs=pl.BlockSpec(memory_space=pl.ANY),
        scratch_shapes=[
            pltpu.SemaphoreType.DMA,
            pltpu.SemaphoreType.DMA((3, 3, 4)),
            pltpu.SemaphoreType.DMA((3, 3, 4)),
        ],
        compiler_params=pltpu.CompilerParams(collective_id=collective, has_side_effects=True),
        name="gather_rows",
    )(x)
    return out


def torus_target(at, k):
    return ((at[0] + k // 16) % 4) * 16 + ((at[1] + k // 4) % 4) * 4 + (at[2] + k) % 4


def params(collective, **more):
    return pltpu.CompilerParams(collective_id=collective, has_side_effects=True, **more)


def greet_all_and_sibling(me):
    barrier = pltpu.get_barrier_semaphore()

    @pl.loop(1, 64)
    def _(k):
        pl.semaphore_signal(barrier, inc=1, device_id={"seq": (me + k) % 64})

    pl.semaphore_signal(barrier, inc=1, device_id={"head": 1 - lax.axis_index("head")})
    pl.semaphore_wait(barrier, 64)


def greet_sibling():
    barrier = pltpu.get_barrier_semaphore()
    pl.semaphore_signal(barrier, inc=1, device_id={"head": 1 - lax.axis_index("head")})
    pl.semaphore_wait(barrier, 1)


def experts_kernel(
    rows_ref,
    grads_ref,
    gate_up_ref,
    down_ref,
    home_ref,
    res_ref,
    gate_up_grad_ref,
    down_grad_ref,
    slot_in,
    grad_slots,
    theirs_x,
    theirs_y,
    sums,
    wide_grad,
    send,
    home_send,
    home_recv,
    sems,
):
    me, at = coordinates()
    head = lax.axis_index("head")
    sibling = {"head": 1 - head}
    mine, place = me // 8, me % 8
    names = ("recv", "fwd_send", "fwd_recv", "kept", "given_send", "given_recv")
    names += ("x_send", "x_recv", "y_send", "y_recv")
    sem = {name: sems.at[n] for n, name in enumerate(names)}
    greet_all_and_sibling(me)

    def group(c):
        return pl.ds(pl.multiple_of(c * 8, 8), 8)

    own = pltpu.make_async_copy(rows_ref.at[me], slot_in.at[me, head], sem["recv"].at[mine])
    own.start()

    @pl.loop(0, 64)
    def _(k):
        j = ((mine - k // 8) % 8) * 8 + (place + k) % 8

        @pl.when(k > 0)
        def _():
            pltpu.make_async_remote_copy(
                src_ref=rows_ref.at[j],
                dst_ref=slot_in.at[me, head],
                send_sem=send,
                recv_sem=sem["recv"].at[mine],
                device_id={"seq": j},
            ).start()

    def given(c):
        return pltpu.make_async_remote_copy(
            src_ref=grads_ref.at[group(c)],
            dst_ref=grad_slots.at[group(c), head],
            send_sem=sem["given_send"].at[c],
            recv_sem=sem["given_recv"].at[c],
            device_id=sibling,
        )

    def kept(c):
        return pltpu.make_async_copy(
            grads_ref.at[group(c)], grad_slots.at[group(c), head], sem["kept"].at[c]
        )

    def forward(c):
        return pltpu.make_async_remote_copy(
            src_ref=slot_in.at[group(c), head],
            dst_ref=slot_in.at[group(c), head],
            send_sem=sem["fwd_send"].at[c],
            recv_sem=sem["fwd_recv"].at[c],
            device_id=sibling,
        )

    def swap(c, source, target, name):
        return pltpu.make_async_remote_copy(
            src_ref=source.at[group(c), 1 - head],
            dst_ref=target.at[group(c)],
            send_sem=sem[name + "_send"].at[c],
            recv_sem=sem[name + "_recv"].at[c],
            device_id=sibling,
        )

    @pl.loop(0, 8)
    def _(i):
        c = (mine + i) % 8
        kept(c).start()
        given(c).start()

    wide_grad[...] = jnp.zeros_like(wide_grad)
    down_grad_ref[...] = jnp.zeros_like(down_grad_ref)
    hidden = down_ref.shape[0]
    width = down_ref.shape[1]

    def nt(left, right):
        return lax.dot_general(
            left, right, (((1,), (1,)), ((), ())), preferred_element_type=jnp.float32
        )

    def tn(left, right):
        return lax.dot_general(
            left, right, (((0,), (0,)), ((), ())), preferred_element_type=jnp.float32
        )

    @pl.loop(0, 10)
    def _(i):
        @pl.when(i < 8)
        def _():
            c = (mine + i) % 8
            pltpu.make_async_copy(
                rows_ref.at[group(c)], slot_in.at[group(c), head], sem["recv"].at[c]
            ).wait()
            forward(c).start()

        @pl.when((i >= 1) & (i < 9))
        def _():
            c = (mine + i + 7) % 8
            forward(c).wait()
            kept(c).wait()
            given(c).wait()
            rows = slot_in[group(c)].reshape(256, width)
            grads = grad_slots[group(c)].reshape(256, width)
            both = jnp.dot(rows, gate_up_ref[...], preferred_element_type=jnp.float32)
            gate, up = both[:, :hidden], both[:, hidden:]
            sig = jax.nn.sigmoid(gate)
            act = gate * sig
            hid = (act * up).astype(jnp.bfloat16)
            grad_hid = nt(grads, down_ref[...])
            grad_gate = grad_hid * up * (sig * (1.0 + gate * (1.0 - sig)))
            grad_both = jnp.concatenate([grad_gate, grad_hid * act], axis=1).astype(jnp.bfloat16)
            wide_grad[...] += tn(rows, grad_both)
            down_grad_ref[...] += tn(hid, grads)
            back = nt(grad_both, gate_up_ref[...]).astype(jnp.bfloat16)
            slot_in[group(c)] = back.reshape(8, 2, 16, width)
            res = jnp.dot(hid, down_ref[...], preferred_element_type=jnp.float32)
            grad_slots[group(c)] = res.astype(jnp.bfloat16).reshape(8, 2, 16, width)
            swap(c, slot_in, theirs_x, "x").start()
            swap(c, grad_slots, theirs_y, "y").start()

        @pl.when(i >= 2)
        def _():
            c = (mine + i + 6) % 8
            swap(c, slot_in, theirs_x, "x").wait()

            @pl.loop(0, 8)
            def _(n):
                j = c * 8 + (place + n) % 8
                total = slot_in[j, head].astype(jnp.float32) + theirs_x[j].astype(jnp.float32)
                sums[j] = total.astype(sums.dtype)

                @pl.when(j != me)
                def _():
                    pltpu.make_async_remote_copy(
                        src_ref=sums.at[j],
                        dst_ref=home_ref.at[me],
                        send_sem=home_send,
                        recv_sem=home_recv,
                        device_id={"seq": j},
                    ).start()

                @pl.when(j == me)
                def _():
                    pltpu.make_async_copy(sums.at[me], home_ref.at[me], home_recv).start()

            swap(c, grad_slots, theirs_y, "y").wait()

            @pl.loop(0, 8)
            def _(n):
                j = c * 8 + n
                total = grad_slots[j, head].astype(jnp.float32) + theirs_y[j].astype(jnp.float32)
                res_ref[j] = total.astype(res_ref.dtype)

    tiles = hidden // 128
    for tile in range(tiles):
        for which in range(2):
            start = which * hidden + tile * 128
            gate_up_grad_ref[pl.ds(tile * 2 + which, width, stride=2 * tiles), :] = wide_grad[
                :, start : start + 128
            ]
    some = pl.ds(0, 63)
    pltpu.make_async_copy(rows_ref.at[some], rows_ref.at[some], send).wait()
    pltpu.make_async_copy(sums.at[some], sums.at[some], home_send).wait()
    pltpu.make_async_copy(sums, home_ref, home_recv).wait()


def experts(rows, grads, gate_up, down, collective):
    hidden, width = down.shape
    half, bf16 = rows.shape, rows.dtype
    whole = (half[0], 2) + half[1:]
    vmem = pl.BlockSpec(memory_space=pltpu.VMEM)
    home, res, wide, down_grad = pl.pallas_call(
        experts_kernel,
        out_shape=[
            jax.ShapeDtypeStruct(half, bf16),
            jax.ShapeDtypeStruct(half, bf16),
            jax.ShapeDtypeStruct((width * 2 * hidden // 128, 128), jnp.float32),
            jax.ShapeDtypeStruct((hidden, width), jnp.float32),
        ],
        in_specs=[vmem] * 4,
        out_specs=[pl.BlockSpec(memory_space=pl.ANY)] + [vmem] * 3,
        scratch_shapes=[
            pltpu.VMEM(whole, bf16),
            pltpu.VMEM(whole, bf16),
            pltpu.VMEM(half, bf16),
            pltpu.VMEM(half, bf16),
            pltpu.VMEM(half, bf16),
            pltpu.VMEM((width, 2 * hidden), jnp.float32),
            pltpu.SemaphoreType.DMA,
            pltpu.SemaphoreType.DMA,
            pltpu.SemaphoreType.DMA,
            pltpu.SemaphoreType.DMA((10, 8)),
        ],
        compiler_params=params(collective, vmem_limit_bytes=58 * MIB),
        name="experts",
    )(rows, grads, gate_up, down)
    wide = wide.reshape(width, hidden // 128, 2, 128).transpose(0, 2, 1, 3)
    return home, res, wide.reshape(1, width, 2, hidden), down_grad[None]


class Scan:
    def __init__(self, reverse, at, me, x_ref, out_ref, got, made, sems):
        self.reverse, self.at, self.me = reverse, at, me
        self.x_ref, self.out_ref, self.got, self.made = x_ref, out_ref, got, made
        self.send, self.recv, self.back_send, self.back_recv = [sems.at[n] for n in range(4)]

    def spread(self, source, target_ref, send, recv):
        @pl.loop(1, 64)
        def _(k):
            target = torus_target(self.at, k)
            pltpu.make_async_remote_copy(
                src_ref=source.at[target],
                dst_ref=target_ref.at[self.me],
                send_sem=send,
                recv_sem=recv,
                device_id={"seq": target},
            ).start()

    def begin(self):
        self.got[self.me] = self.x_ref[self.me]
        self.spread(self.x_ref, self.got, self.send, self.recv)

    def middle(self):
        some = pl.ds(0, 63)
        x_ref, got, made = self.x_ref, self.got, self.made
        pltpu.make_async_copy(x_ref.at[some], x_ref.at[some], self.send).wait()
        pltpu.make_async_copy(got.at[some], got.at[some], self.recv).wait()
        heads, width = made.shape[1:]
        chosen = lax.broadcasted_iota(jnp.int32, (heads, width), 0) == lax.broadcasted_iota(
            jnp.int32, (heads, width), 1
        )

        def step(k, state):
            at_k = 63 - k if self.reverse else k
            made[at_k] = state
            row = got[at_k, heads : heads + 8, :][0:1, :]
            decay = jnp.sum(jnp.where(chosen, row, 0.0), axis=1, keepdims=True)
            return decay * state + got[at_k, 0:heads, :]

        lax.fori_loop(0, 64, step, jnp.zeros((heads, width), jnp.float32))
        self.out_ref[self.me] = made[self.me]
        self.spread(made, self.out_ref, self.back_send, self.back_recv)

    def end(self):
        some = pl.ds(0, 63)
        made = self.made
        pltpu.make_async_copy(made.at[some], made.at[some], self.back_send).wait()
        pltpu.make_async_copy(made.at[some], made.at[some], self.back_recv).wait()


def scan_shapes(size, heads, width):
    return [
        pltpu.VMEM((size, heads + 8, width), jnp.float32),
        pltpu.VMEM((size, heads, width), jnp.float32),
        pltpu.SemaphoreType.DMA((4,)),
    ]


def scan_kernel(reverse, x_ref, out_ref, got, made, sems):
    me, at = coordinates()
    greet_all(me)
    scan = Scan(reverse, at, me, x_ref, out_ref, got, made, sems)
    scan.begin()
    scan.middle()
    scan.end()


def scan_message(decay, state):
    heads, size, width = state.shape
    rows = jnp.broadcast_to(jnp.pad(decay, (0, width - heads))[None, None, :], (size, 8, width))
    return jnp.concatenate([state.transpose(1, 0, 2), rows], axis=1)


def carried(decay, state, collective):
    heads, size, width = state.shape
    out = pl.pallas_call(
        functools.partial(scan_kernel, False),
        out_shape=jax.ShapeDtypeStruct((size, heads, width), jnp.float32),
        in_specs=[pl.BlockSpec(memory_space=pltpu.VMEM)],
        out_specs=pl.BlockSpec(memory_space=pltpu.VMEM),
        scratch_shapes=scan_shapes(size, heads, width),
        compiler_params=params(collective),
        name="carried",
    )(scan_message(decay, state))
    return out.transpose(1, 0, 2)


class Small:
    def __init__(self, at, me, x_ref, out_ref, got, sems):
        self.at, self.me = at, me
        self.x_ref, self.out_ref, self.got = x_ref, out_ref, got
        self.send, self.recv, self.back_send, self.back_recv = [sems.at[n] for n in range(4)]

    def begin(self):
        self.got[self.me] = self.x_ref[self.me]

        @pl.loop(1, 64)
        def _(k):
            target = torus_target(self.at, k)
            pltpu.make_async_remote_copy(
                src_ref=self.x_ref.at[target],
                dst_ref=self.got.at[self.me],
                send_sem=self.send,
                recv_sem=self.recv,
                device_id={"seq": target},
            ).start()

    def middle(self):
        some = pl.ds(0, 63)
        x_ref, got, out_ref, me = self.x_ref, self.got, self.out_ref, self.me
        pltpu.make_async_copy(x_ref.at[some], x_ref.at[some], self.send).wait()
        pltpu.make_async_copy(got.at[some], got.at[some], self.recv).wait()
        out_ref[me] = lax.fori_loop(1, 64, lambda k, total: total + got[k], got[0])

        @pl.loop(1, 64)
        def _(k):
            target = torus_target(self.at, k)
            pltpu.make_async_remote_copy(
                src_ref=out_ref.at[me],
                dst_ref=out_ref.at[me],
                send_sem=self.back_send,
                recv_sem=self.back_recv,
                device_id={"seq": target},
            ).start()

    def end(self):
        some = pl.ds(0, 63)
        got = self.got
        pltpu.make_async_copy(got.at[some], got.at[some], self.back_send).wait()
        pltpu.make_async_copy(got.at[some], got.at[some], self.back_recv).wait()


class Scatter:
    def __init__(self, at, plan, lefts, right, out_ref, buf, rest, send, recv):
        self.at, self.plan, self.lefts, self.right = at, plan, lefts, right
        self.out_ref, self.buf, self.rest, self.send, self.recv = out_ref, buf, rest, send, recv
        self.third, self.half = parts_of(buf.shape[4])
        self.copies = {}

    def spans(self, p):
        start, third, half = p * self.third, self.third, self.half
        return pl.ds(start, half), pl.ds(start + half, third - half)

    def product(self, p):
        buf, right = self.buf, self.right
        rows = buf.shape[3]
        for which, start, length in self.plan[p]:
            left = self.lefts[which]

            @pl.loop(0, 4)
            def _(x):
                across = pl.ds(pl.multiple_of(x * 16 * rows, 128), 16 * rows)
                total = lax.dot_general(
                    left[:, across],
                    right[:, start : start + length],
                    (((0,), (0,)), ((), ())),
                    preferred_element_type=jnp.float32,
                )
                total = total.reshape(4, 4, rows, length).astype(jnp.bfloat16)
                buf[x, :, :, :, start : start + length] = total

    def send_to(self, phase, p, by, value, cols, slot, kind):
        order = ORDERS[p]
        axis = order[phase]
        lead = (slice(None),) * phase
        copy = pltpu.make_async_remote_copy(
            src_ref=self.buf.at[region(self.at, order, phase, value, cols)],
            dst_ref=self.rest[phase].at[(slot,) + lead + (slice(None), cols)],
            send_sem=self.send.at[phase, p, kind],
            recv_sem=self.recv.at[phase, p, kind],
            device_id={"seq": seq_of(moved(self.at, axis, by))},
        )
        copy.start()
        self.copies[phase, p, kind] = copy

    def added(self, phase, p, value, cols, slots):
        order, buf, room = ORDERS[p], self.buf, self.rest[phase]

        @pl.loop(0, 4**phase)
        def _(i):
            free = ((), (i,), (i // 4, i % 4))[phase]
            index = list(region(self.at, order, phase, value, cols))
            for n, axis in enumerate(sorted(order[:phase])):
                index[axis] = free[n]
            index = tuple(index)
            total = buf[index].astype(jnp.float32)
            for slot in slots:
                total = total + room[(slot,) + free + (slice(None), cols)].astype(jnp.float32)
            if phase == 0 and len(slots) == 2:
                self.out_ref[:, cols] = total
            else:
                buf[index] = total.astype(jnp.bfloat16)

    def first(self, phase, p):
        c = self.at[ORDERS[p][phase]]
        low, high = self.spans(p)
        self.send_to(phase, p, 1, (c + 2) % 4, low, 2, 0)
        self.send_to(phase, p, 3, (c + 2) % 4, high, 2, 1)
        self.send_to(phase, p, 1, (c + 1) % 4, high, 0, 2)
        self.send_to(phase, p, 3, (c + 3) % 4, low, 1, 3)

    def second(self, phase, p):
        c = self.at[ORDERS[p][phase]]
        low, high = self.spans(p)
        self.copies[phase, p, 0].wait_recv()
        self.added(phase, p, (c + 1) % 4, low, (2,))
        self.send_to(phase, p, 1, (c + 1) % 4, low, 0, 4)
        self.copies[phase, p, 1].wait_recv()
        self.added(phase, p, (c + 3) % 4, high, (2,))
        self.send_to(phase, p, 3, (c + 3) % 4, high, 1, 5)

    def third_step(self, phase, p):
        c = self.at[ORDERS[p][phase]]
        low, high = self.spans(p)
        self.copies[phase, p, 2].wait_recv()
        self.copies[phase, p, 5].wait_recv()
        self.added(phase, p, c, high, (0, 1))
        self.copies[phase, p, 3].wait_recv()
        self.copies[phase, p, 4].wait_recv()
        self.added(phase, p, c, low, (0, 1))

    def finish(self, phase):
        for p in range(3):
            self.third_step(phase, p)
            if phase > 0:
                self.first(phase - 1, p)

    def end(self):
        for copy in self.copies.values():
            copy.wait_send()


def scatter_shapes(rows, columns):
    return [
        pltpu.VMEM((4, 4, 4, rows, columns), jnp.bfloat16),
        [pltpu.VMEM((3,) + (4,) * phase + (rows, columns), jnp.bfloat16) for phase in range(3)],
        pltpu.SemaphoreType.DMA((3, 3, 6)),
        pltpu.SemaphoreType.DMA((3, 3, 6)),
    ]


def scatter_kernel(
    plan, lefts, right, scanned, small, out_ref, scan_out, small_out, buf, rest, send, recv, scan_scratch, small_scratch
):
    me, at = coordinates()
    greet_all(me)
    sums = Scatter(at, plan, lefts, right, out_ref, buf, rest, send, recv)
    others = []
    if scanned is not None:
        got, made, sems = scan_scratch
        others.append(Scan(True, at, me, scanned, scan_out, got, made, sems))
    if small is not None:
        got, sems = small_scratch
        others.append(Small(at, me, small, small_out, got, sems))
    for other in others:
        other.begin()
    for p in range(3):
        sums.product(p)
        sums.first(2, p)
    for other in others:
        other.middle()
    for phase in (2, 1, 0):
        for p in range(3):
            sums.second(phase, p)
        sums.finish(phase)
    for other in others:
        other.end()
    sums.end()


def scatter_rows(lefts, right, plan, collective, scanned=None, small=None):
    model, columns = lefts[0].shape[1], right.shape[1]
    rows = model // 64
    vmem = pl.BlockSpec(memory_space=pltpu.VMEM)
    scan_scratch = small_scratch = None
    out_shape = [jax.ShapeDtypeStruct((rows, columns), jnp.float32), None, None]
    if scanned is not None:
        size, heads, width = scanned.shape
        scan_scratch = scan_shapes(size, heads - 8, width)
        out_shape[1] = jax.ShapeDtypeStruct((size, heads - 8, width), jnp.float32)
    if small is not None:
        small_scratch = [pltpu.VMEM(small.shape, jnp.float32), pltpu.SemaphoreType.DMA((4,))]
        out_shape[2] = jax.ShapeDtypeStruct(small.shape, jnp.float32)
    spec = lambda tree: jax.tree.map(lambda _: vmem, tree)
    return pl.pallas_call(
        functools.partial(scatter_kernel, plan),
        out_shape=out_shape,
        in_specs=spec([lefts, right, scanned, small]),
        out_specs=spec(out_shape),
        scratch_shapes=scatter_shapes(rows, columns) + [scan_scratch, small_scratch],
        compiler_params=params(collective, vmem_limit_bytes=60 * MIB),
        name="scatter_rows",
    )(lefts, right, scanned, small)


def pair_kernel(x_ref, out_ref, theirs, send, recv):
    greet_sibling()
    copy = pltpu.make_async_remote_copy(
        src_ref=x_ref,
        dst_ref=theirs,
        send_sem=send,
        recv_sem=recv,
        device_id={"head": 1 - lax.axis_index("head")},
    )
    copy.start()
    copy.wait()
    rows = x_ref.shape[0]
    step = min(rows, 16)

    @pl.loop(0, rows // step)
    def _(i):
        here = pl.ds(pl.multiple_of(i * step, step), step)
        out_ref[here] = x_ref[here] + theirs[here]


def pair_total(x, collective):
    return pl.pallas_call(
        pair_kernel,
        out_shape=jax.ShapeDtypeStruct(x.shape, x.dtype),
        in_specs=[pl.BlockSpec(memory_space=pltpu.VMEM)],
        out_specs=pl.BlockSpec(memory_space=pltpu.VMEM),
        scratch_shapes=[
            pltpu.VMEM(x.shape, x.dtype),
            pltpu.SemaphoreType.DMA,
            pltpu.SemaphoreType.DMA,
        ],
        compiler_params=params(collective),
        name="pair_total",
    )(x)


def small_message(parts):
    flat = jnp.concatenate([part.reshape(-1) for part in parts])
    size = flat.shape[0]
    each = -(-size // (64 * 1024)) * 1024
    return jnp.pad(flat, (0, 64 * each - size)).reshape(64, each // 128, 128)


def small_parts(parts, out):
    out, result, start = out.reshape(-1), [], 0
    for part in parts:
        result.append(out[start : start + part.size].reshape(part.shape))
        start += part.size
    return result


def routing_kernel(routes_ref, weights_ref, position_ref, weight_ref):
    experts, tokens = position_ref.shape
    expert = lax.broadcasted_iota(jnp.int32, (experts, tokens), 0)
    named = jnp.zeros((experts, tokens), jnp.float32)
    weight = jnp.zeros((experts, tokens), jnp.float32)
    for k in range(routes_ref.shape[0]):
        hit = expert == routes_ref[k : k + 1, :]
        named = named + jnp.where(hit, 1.0, 0.0)
        weight = weight + jnp.where(hit, weights_ref[k : k + 1, :], 0.0)
    earlier = jnp.where(
        lax.broadcasted_iota(jnp.int32, (tokens, tokens), 0)
        < lax.broadcasted_iota(jnp.int32, (tokens, tokens), 1),
        1.0,
        0.0,
    ).astype(jnp.bfloat16)
    count = jnp.dot(named.astype(jnp.bfloat16), earlier, preferred_element_type=jnp.float32)
    position_ref[...] = jnp.where(named > 0.0, count, -1.0)
    weight_ref[...] = weight


def routing(routes, route_weights, experts):
    tokens = routes.shape[0]
    return pl.pallas_call(
        routing_kernel,
        out_shape=[jax.ShapeDtypeStruct((experts, tokens), jnp.float32)] * 2,
        name="routing",
    )(routes.T, route_weights.T)


def chosen_slots(position, first, count, slots):
    tokens = position.shape[1]
    number = lax.broadcasted_iota(jnp.int32, (count, slots, tokens), 1)
    number = (number + slots * lax.axis_index("head")).astype(jnp.float32)
    return jnp.where(position[:, None, :] == number, 1.0, 0.0).reshape(count * slots, tokens)


def send_kernel(slots, weigh, position_ref, weight_ref, rows_ref, out_ref):
    position = position_ref[...]
    chosen = chosen_slots(position, 0, position.shape[0], slots)
    rows = jnp.dot(
        chosen.astype(jnp.bfloat16), rows_ref[...], preferred_element_type=jnp.float32
    )
    if weigh:
        weighted = chosen.reshape(-1, slots, chosen.shape[1]) * weight_ref[...][:, None, :]
        rows = rows * jnp.sum(weighted.reshape(chosen.shape), axis=1, keepdims=True)
    out_ref[...] = rows.astype(jnp.bfloat16).reshape(out_ref.shape)


def send_rows(position, weight, rows, slots, weigh):
    experts, tokens = position.shape
    width = rows.shape[1]
    step = 16
    whole = pl.BlockSpec((tokens, width), lambda i: (0, 0))
    mine = pl.BlockSpec((step, tokens), lambda i: (i, 0))
    out = pl.BlockSpec((step, slots, width), lambda i: (i, 0, 0))
    return pl.pallas_call(
        functools.partial(send_kernel, slots, weigh),
        grid=(experts // step,),
        out_shape=jax.ShapeDtypeStruct((experts, slots, width), jnp.bfloat16),
        in_specs=[mine, mine, whole],
        out_specs=out,
        compiler_params=pltpu.CompilerParams(vmem_limit_bytes=40 * MIB),
        name="send_grads" if weigh else "send_rows",
    )(position, weight, rows)


def combine_kernel(slots, weigh, position_ref, weight_ref, rows_ref, out_ref):
    position = position_ref[...]
    count = position.shape[0]
    chosen = chosen_slots(position, 0, count, slots)
    rows = rows_ref[...].reshape(count * slots, rows_ref.shape[2])

    def over_slots(picked):
        return lax.dot_general(
            picked, rows, (((0,), (0,)), ((), ())), preferred_element_type=jnp.float32
        )

    @pl.when(pl.program_id(0) == 0)
    def _():
        out_ref[...] = jnp.zeros_like(out_ref)

    if weigh:
        weighted = chosen.reshape(count, slots, -1) * weight_ref[...][:, None, :]
        weighted = weighted.reshape(chosen.shape)
        high = weighted.astype(jnp.bfloat16)
        less = (weighted - high.astype(jnp.float32)).astype(jnp.bfloat16)
        out_ref[...] += over_slots(high) + over_slots(less)
    else:
        out_ref[...] += over_slots(chosen.astype(jnp.bfloat16))


def combine(position, weight, home, weigh):
    experts, tokens = position.shape
    _, slots, width = home.shape
    step = 16
    mine = pl.BlockSpec((step, tokens), lambda i: (i, 0))
    rows = pl.BlockSpec((step, slots, width), lambda i: (i, 0, 0))
    out = pl.BlockSpec((tokens, width), lambda i: (0, 0))
    return pl.pallas_call(
        functools.partial(combine_kernel, slots, weigh),
        grid=(experts // step,),
        out_shape=jax.ShapeDtypeStruct((tokens, width), jnp.float32),
        in_specs=[mine, mine, rows],
        out_specs=out,
        compiler_params=pltpu.CompilerParams(vmem_limit_bytes=40 * MIB),
        name="combine_mix" if weigh else "combine_grads",
    )(position, weight, home)


HIGHEST = lax.Precision.HIGHEST
EPSILON = 1e-05


def shifted(value, axis, steps):
    count = lax.axis_size(axis)
    leading, last = (max(0, -steps), min(count, count - steps))
    return lax.ppermute(value, axis, [(source, source + steps) for source in range(leading, last)])


def product(left_side, right_side):
    return jnp.dot(left_side, right_side, preferred_element_type=jnp.float32)


def product_nt(left_side, right_side):
    return lax.dot_general(
        left_side, right_side, (((1,), (1,)), ((), ())), preferred_element_type=jnp.float32
    )


def product_tn(left_side, right_side):
    return lax.dot_general(
        left_side, right_side, (((0,), (0,)), ((), ())), preferred_element_type=jnp.float32
    )


def silu(operand):
    return operand * jax.nn.sigmoid(operand)


def silu_slope(operand):
    sig_part = jax.nn.sigmoid(operand)
    return sig_part * (1.0 + operand * (1.0 - sig_part))


def rms_scale(operand):
    return lax.rsqrt(jnp.mean(operand * operand, axis=-1, keepdims=True) + EPSILON)


def norm_back(operand, row_scale, gain_vec, grad_rows):
    gain_grad = jnp.sum(grad_rows * operand * row_scale, axis=0)
    inner_mean = jnp.mean(operand * gain_vec * grad_rows, axis=-1, keepdims=True)
    return (gain_grad, row_scale * gain_vec * grad_rows - operand * row_scale**3 * inner_mean)


def group_state(heads_x, state_in, step_size, decay_rate):
    cum_decay = jnp.cumsum(-step_size * decay_rate[None, :], axis=0)
    tail_decay = cum_decay[-1]
    tok_weight = jnp.exp(tail_decay[None, :] - cum_decay) * step_size
    state_new = jnp.einsum("th,thp,tn->hpn", tok_weight, heads_x, state_in, precision=HIGHEST)
    return (jnp.exp(tail_decay), state_new)


def group_out(heads_x, state_in, state_read, step_size, decay_rate, state_start, skip_gain):
    length_rows = heads_x.shape[0]
    cum_decay = jnp.cumsum(-step_size * decay_rate[None, :], axis=0)
    causal = (jnp.arange(length_rows)[:, None] >= jnp.arange(length_rows)[None, :])[:, :, None]
    gap_decay = cum_decay[:, None, :] - cum_decay[None, :, :]
    decay_mat = jnp.where(causal, jnp.exp(jnp.where(causal, gap_decay, 0.0)), 0.0)
    scores = jnp.dot(state_read, state_in.T, precision=HIGHEST)
    mixing = decay_mat * scores[:, :, None] * step_size[None, :, :]
    within_part = jnp.einsum("tsh,shp->thp", mixing, heads_x, precision=HIGHEST)
    carried_part = jnp.exp(cum_decay)[:, :, None] * jnp.einsum(
        "tn,hpn->thp", state_read, state_start, precision=HIGHEST
    )
    return within_part + carried_part + skip_gain[None, :, None] * heads_x


def per_device(
    layer_in,
    norm_first,
    mixer_in,
    state_proj,
    step_proj,
    step_bias,
    conv_main,
    conv_state,
    decay_rate,
    skip_gain,
    gate_gain,
    mixer_out,
    norm_second,
    shared_gate_up,
    shared_down,
    expert_gate_up,
    expert_down,
    routes,
    route_weights,
    grad_out,
):
    tokens = layer_in.shape[0]
    model_width = layer_in.shape[1]
    inner_dev = mixer_in.shape[2]
    inner_all = inner_dev * lax.axis_size("head")
    state_size = state_proj.shape[1] // 2
    heads_dev = step_proj.shape[1]
    head_size = inner_dev // heads_dev
    conv_taps = conv_main.shape[0]
    shared_dev = shared_down.shape[1]
    local_experts = expert_gate_up.shape[0]
    seq_devices = lax.axis_size("seq")
    experts_all = local_experts * seq_devices
    choices_per = routes.shape[1]
    capacity = max(2, tokens * choices_per * 4 // (3 * experts_all))
    slot_count = local_experts * seq_devices * capacity
    gathered = gather_rows(
        jnp.concatenate(
            [
                mixer_in.reshape(-1, 2 * inner_dev),
                state_proj,
                jnp.pad(step_proj, ((0, 0), (0, 128 - heads_dev))),
            ],
            axis=1,
        ),
        0,
    ).reshape(model_width, -1)
    full_in = gathered[:, : 2 * inner_dev]
    full_state = gathered[:, 2 * inner_dev : 2 * inner_dev + 2 * state_size]
    full_step = gathered[:, 2 * inner_dev + 2 * state_size :][:, :heads_dev]
    late_rows = jnp.concatenate(
        [mixer_out, shared_gate_up.reshape(-1, 2 * shared_dev), shared_down], axis=1
    )
    full_in, late_rows, grad_out_late = lax.optimization_barrier((full_in, late_rows, grad_out))
    gathered = lax.all_gather(late_rows, "seq", axis=0, tiled=True)
    full_out = gathered[:, :inner_dev]
    shared_flat = gathered[:, inner_dev : inner_dev + 2 * shared_dev]
    full_down = gathered[:, inner_dev + 2 * shared_dev :]
    slots_dev = capacity // lax.axis_size("head")
    position, slot_weight = routing(routes, route_weights, experts_all)
    grads_out = send_rows(position, slot_weight, grad_out_late, slots_dev, True)
    grads_in = lax.all_to_all(grads_out, "seq", split_axis=0, concat_axis=0, tiled=True)
    resid_in = layer_in.astype(jnp.float32)
    scale_first = rms_scale(resid_in)
    normed = (resid_in * scale_first * norm_first).astype(jnp.bfloat16)
    zx_both = product(normed, full_in)
    gate_z = zx_both[:, :inner_dev]
    pre_x = zx_both[:, inner_dev:]
    pre_bc = product(normed, full_state)
    step_raw = product(normed, full_step) + step_bias
    conv_input = jnp.concatenate([pre_x, pre_bc], axis=1)
    edge_rows = shifted(conv_input[tokens - (conv_taps - 1) :], "seq", 1)
    padded = jnp.concatenate([edge_rows, conv_input], axis=0)
    kernel = jnp.concatenate([conv_main, conv_state], axis=1)
    conv_sum = kernel[0] * padded[0:tokens]
    for tap_index in range(1, conv_taps):
        conv_sum = conv_sum + kernel[tap_index] * padded[tap_index : tap_index + tokens]
    active = silu(conv_sum)
    heads_x = active[:, :inner_dev].reshape(tokens, heads_dev, head_size)
    state_in = active[:, inner_dev : inner_dev + state_size]
    state_read = active[:, inner_dev + state_size :]
    step_size = jax.nn.softplus(step_raw)
    decay_total, state_local = group_state(heads_x, state_in, step_size, decay_rate)
    state_start = carried(decay_total, state_local, 2)
    ssd = group_out(
        heads_x, state_in, state_read, step_size, decay_rate, state_start, skip_gain
    ).reshape(tokens, inner_dev)
    gate_act = silu(gate_z)
    gated_ssd = ssd * gate_act
    gate_scale = lax.rsqrt(pair_total(jnp.sum(gated_ssd * gated_ssd, axis=1).reshape(-1, 128), 4).reshape(-1) / inner_all + EPSILON)[
        :, None
    ]
    normed_gate = (gated_ssd * gate_scale * gate_gain).astype(jnp.bfloat16)
    mixer_sum = pair_total(product_nt(normed_gate, full_out), 6)
    residual = resid_in + mixer_sum
    scale_second = rms_scale(residual)
    normed_second = (residual * scale_second * norm_second).astype(jnp.bfloat16)
    shared_both = product(normed_second, shared_flat)
    shared_gate = shared_both[:, :shared_dev]
    shared_up = shared_both[:, shared_dev:]
    shared_hid = (silu(shared_gate) * shared_up).astype(jnp.bfloat16)
    shared_part = product_nt(shared_hid, full_down)
    rows_out = send_rows(position, slot_weight, normed_second, slots_dev, False)
    grad_home, res_sums, expert_gate_up_grad, expert_down_grad = experts(
        rows_out,
        grads_in,
        expert_gate_up.reshape(model_width, -1),
        expert_down.reshape(-1, model_width),
        11,
    )
    grad_float = grad_out.astype(jnp.float32)
    home_rows = lax.all_to_all(res_sums, "seq", split_axis=0, concat_axis=0, tiled=True)
    expert_grad_rows = combine(position, slot_weight, grad_home, False)
    grad_shared_hid = product(grad_out, full_down)
    grad_shared_gate = grad_shared_hid * shared_up * silu_slope(shared_gate)
    grad_shared_up = grad_shared_hid * silu(shared_gate)
    grad_shared_both = jnp.concatenate([grad_shared_gate, grad_shared_up], axis=1).astype(
        jnp.bfloat16
    )
    grad_normed_second = pair_total(product_nt(grad_shared_both, shared_flat) + expert_grad_rows, 8)
    norm_second_grad, grad_resid_norm = norm_back(
        residual, scale_second, norm_second, grad_normed_second
    )
    grad_resid = grad_float + grad_resid_norm
    grad_mix = grad_resid.astype(jnp.bfloat16)
    grad_normed_gate = product(grad_mix, full_out)
    weighted = grad_normed_gate * gate_gain
    inner_dot = pair_total(jnp.sum(weighted * gated_ssd, axis=1).reshape(-1, 128), 5).reshape(-1)[:, None]
    grad_gated = gate_scale * weighted - gated_ssd * gate_scale**3 * inner_dot / inner_all
    gate_gain_grad = jnp.sum(grad_normed_gate * gated_ssd * gate_scale, axis=0)
    grad_ssd = grad_gated * gate_act
    grad_gate_z = grad_gated * ssd * silu_slope(gate_z)
    _, pull_out = jax.vjp(
        group_out, heads_x, state_in, state_read, step_size, decay_rate, state_start, skip_gain
    )
    (
        grad_x_first,
        grad_in_first,
        grad_read,
        grad_step_first,
        grad_rate_first,
        grad_start,
        skip_gain_grad,
    ) = pull_out(grad_ssd.reshape(tokens, heads_dev, head_size))
    late_plan = (
        ((0, 0, 1024),),
        ((0, 1024, 512), (1, 1536, 512)),
        ((1, 2048, 512), (2, 2560, 512)),
    )
    summed_late, grad_next, _ = scatter_rows(
        [grad_mix, normed_second, grad_out],
        jnp.concatenate([normed_gate, grad_shared_both, shared_hid], axis=1),
        late_plan,
        3,
        scanned=scan_message(decay_total, grad_start),
    )
    grad_next = grad_next.transpose(1, 0, 2)
    grad_decay = jnp.sum(grad_next * state_start, axis=(1, 2))
    _, pull_state = jax.vjp(group_state, heads_x, state_in, step_size, decay_rate)
    grad_x_second, grad_in_second, grad_step_second, grad_rate_second = pull_state(
        (grad_decay, grad_next)
    )
    decay_rate_grad = grad_rate_first + grad_rate_second
    grad_bc = pair_total(
        jnp.concatenate([grad_in_first + grad_in_second, grad_read], axis=1), 10
    )
    grad_active = jnp.concatenate(
        [(grad_x_first + grad_x_second).reshape(tokens, inner_dev), grad_bc], axis=1
    )
    grad_conv = grad_active * silu_slope(conv_sum)
    grad_padded = jnp.pad(kernel[0] * grad_conv, ((0, conv_taps - 1), (0, 0)))
    for tap_index in range(1, conv_taps):
        grad_padded = grad_padded + jnp.pad(
            kernel[tap_index] * grad_conv, ((tap_index, conv_taps - 1 - tap_index), (0, 0))
        )
    kernel_grad = jnp.stack(
        [
            jnp.sum(grad_conv * padded[tap_index : tap_index + tokens], axis=0)
            for tap_index in range(conv_taps)
        ]
    )
    spill_rows = shifted(grad_padded[: conv_taps - 1], "seq", -1)
    grad_pre = grad_padded[conv_taps - 1 :]
    grad_pre = jnp.concatenate(
        [grad_pre[: tokens - (conv_taps - 1)], grad_pre[tokens - (conv_taps - 1) :] + spill_rows],
        axis=0,
    )
    grad_step_raw = (grad_step_first + grad_step_second) * jax.nn.sigmoid(step_raw)
    step_bias_grad = jnp.sum(grad_step_raw, axis=0)
    grad_zx = jnp.concatenate([grad_gate_z, grad_pre[:, :inner_dev]], axis=1).astype(jnp.bfloat16)
    grad_bc_low = grad_pre[:, inner_dev:].astype(jnp.bfloat16)
    grad_step_low = grad_step_raw.astype(jnp.bfloat16)
    in_partial = product_nt(grad_zx, full_in) + product_nt(
        grad_step_low, full_step
    )
    grad_normed = pair_total(in_partial, 9) + product_nt(grad_bc_low, full_state)
    norm_first_grad, grad_in_norm = norm_back(resid_in, scale_first, norm_first, grad_normed)
    input_grad = grad_resid + grad_in_norm
    small = (
        norm_first_grad,
        norm_second_grad,
        step_bias_grad,
        kernel_grad[:, :inner_dev],
        kernel_grad[:, inner_dev:],
        decay_rate_grad,
        skip_gain_grad,
        gate_gain_grad,
    )
    summed, _, small_sums = scatter_rows(
        [normed],
        jnp.concatenate(
            [grad_zx, grad_bc_low, jnp.pad(grad_step_low, ((0, 0), (0, 128 - heads_dev)))], axis=1
        ),
        tuple(((0, start, 1152),) for start in (0, 1152, 2304)),
        15,
        small=small_message(small),
    )
    small_sums = small_parts(small, small_sums)
    expert_mix = combine(position, slot_weight, home_rows, True)
    branch_sum = pair_total(shared_part + expert_mix, 7)
    layer_out = (residual + branch_sum).astype(jnp.bfloat16)
    wide = 2 * inner_dev + 2 * state_size
    weight_sums = (
        summed[:, : 2 * inner_dev].reshape(-1, 2, inner_dev),
        summed[:, 2 * inner_dev : wide],
        summed[:, wide : wide + heads_dev],
        summed_late[:, :inner_dev],
        summed_late[:, inner_dev : inner_dev + 2 * shared_dev].reshape(-1, 2, shared_dev),
        summed_late[:, inner_dev + 2 * shared_dev :],
    )
    return (
        layer_out,
        input_grad,
        small_sums[0],
        weight_sums[0],
        weight_sums[1],
        weight_sums[2],
        small_sums[2],
        small_sums[3],
        small_sums[4],
        small_sums[5],
        small_sums[6],
        small_sums[7],
        weight_sums[3],
        small_sums[1],
        weight_sums[4],
        weight_sums[5],
        expert_gate_up_grad,
        expert_down_grad,
    )


def solution(mesh):
    placed = (
        P("seq", None),
        P(),
        P("seq", None, "head"),
        P("seq", None),
        P("seq", "head"),
        P("head"),
        P(None, "head"),
        P(),
        P("head"),
        P("head"),
        P("head"),
        P("seq", "head"),
        P(),
        P("seq", None, "head"),
        P("seq", "head"),
        P("seq", None, None, "head"),
        P("seq", "head", None),
        P("seq", None),
        P("seq", None),
        P("seq", None),
    )
    return jax.shard_map(
        per_device,
        mesh=mesh,
        in_specs=placed,
        out_specs=(
            P("seq", None),
            P("seq", None),
            P(),
            P("seq", None, "head"),
            P("seq", None),
            P("seq", "head"),
            P("head"),
            P(None, "head"),
            P(),
            P("head"),
            P("head"),
            P("head"),
            P("seq", "head"),
            P(),
            P("seq", None, "head"),
            P("seq", "head"),
            P("seq", None, None, "head"),
            P("seq", "head", None),
        ),
        check_vma=False,
    )
```

time: 3480 us -> 694 us (0.20)
  waiting for transfers between devices: 1150 us -> 10.5 us
  blocking collectives: 896 us -> 0 us
  local copies, waits for them, and re-layouts: 749 us -> 64.1 us
  Pallas kernels: 0 us -> 424 us
  other arithmetic: 435 us -> 55.4 us
  matrix products: 149 us -> 85.6 us
    all_gather x3 -> x0, blocking collectives: 523 us -> none  [the longest x1 223 us: carried_in(): everything = jax.tree.map(lambda part: lax.all_gather(part, axis), array)]
    reduce_scatter x2 -> x0, waiting for transfers between devices: 451 us -> none  [the longest x1 230 us: per_device(): lax.psum_scatter(mixer_out_grad, 'seq', scatter_dimension=0, tiled=True)]
    pallas_call x0 -> x17, Pallas kernels: none -> 424 us  [the longest x2 142 us: scatter_rows(): pl.pallas_call(functools.partial(scatter_kernel, plan), out_shape=out_sha...]
    psum x3 -> x0, blocking collectives: 373 us -> none  [the longest x1 297 us: per_device(): lax.psum((norm_first_grad, norm_second_grad, step_bias_grad, kernel_grad[...]
    unnamed x18 -> x1, waiting for transfers between devices: 338 us -> 0.02 us
    unnamed x269 -> x241, local copies, waits for them, and re-layouts: 276 us -> 22.8 us
    all_to_all x4 -> x2, waiting for transfers between devices: 183 us -> 9.38 us  [the longest x1 9.37 us: per_device(): lax.all_to_all(res_sums, 'seq', split_axis=0, concat_axis=0, tiled=True)]
    reshape x6 -> x7, local copies, waits for them, and re-layouts: 176 us -> 3.72 us  [the longest x2 1.22 us: small_parts(): result.append(out[start:start + part.size].reshape(part.shape))]
  transfers between devices with their start and end apart: 21 -> 5, of which waited for: 12 -> 2; matrix products, arithmetic and copies ran while one was open for 30% -> 12% of each run, Pallas kernels for 0% -> 12%
where the time goes in v2:
time: 694 us; the launch traced here: 681 us
  Pallas kernels  424 us (61%)
  matrix products  85.6 us (12%)
  local copies, waits for them, and re-layouts  64.1 us (9%)
  other arithmetic  55.4 us (8%)
  starting transfers between devices  25.3 us (4%)
  between operations  16.1 us (2%)
  waiting for transfers between devices  10.5 us (2%)
    pallas_call x2, Pallas kernels, scatter_rows(): pl.pallas_call(functools.partial(scatter_kernel, plan), out_shape=out_sha...  142 us
    pallas_call x1, Pallas kernels, experts(): pl.pallas_call(experts_kernel, out_shape=[jax.ShapeDtypeStruct(half, bf16...  116 us
    pallas_call x1, Pallas kernels, gather_rows(): pl.pallas_call(functools.partial(gather_kernel, columns), out_shape=jax.S...  52.6 us
    pallas_call x1, Pallas kernels, carried(): pl.pallas_call(functools.partial(scan_kernel, False), out_shape=jax.Shape...  50.9 us
    pallas_call x7, Pallas kernels, pair_total(): pl.pallas_call(pair_kernel, out_shape=jax.ShapeDtypeStruct(x.shape, x.dty...  50.4 us
    dot_general x3, matrix products, group_out(): within_part = jnp.einsum('tsh,shp->thp', mixing, heads_x, precision=HIGHEST)  26 us
    unnamed x241, local copies, waits for them, and re-layouts  22.8 us
    dot_general x6, matrix products, product_nt(): lax.dot_general(left_side, right_side, (((1,), (1,)), ((), ())), preferre...  22.3 us
  transfers between devices with their start and end apart: 5, of which 2 were waited for; matrix products, arithmetic and copies ran while one was open for 12% of the time, Pallas kernels for 12%

profile of v2, /device:TPU:1, one launch (start us, length us, event | category | flops | bytes accessed | tf_op | source)
XLA Modules:
  0.0 680.5 jit_solution(4188481174115455954)
XLA Ops:
  9.6 52.6 %gather_rows.1 = bf16[4,4,4,24,3456]{4,3,2,1,0:T(8,128)(2,1)} custom-call(bf16[24,3456]{1,0:T(8,128)(2,1)} %fusion.87.x_ref), custom_call_target="tpu_custom_call" | custom-call | tf_op jit(solution)/shard_map/gather_rows/pallas_call | solution.py:111
  62.3 8.1 %slice.213 = bf16[1536,3072]{1,0:T(8,128)(2,1)} slice(bf16[1536,3456]{1,0:T(8,128)(2,1)} %bitcast.185), slice={[0:1536], [0:3072]} | slice | bytes 18874368 | tf_op jit(solution)/shard_map/slice | solution.py:940
  72.3 5.4 fusion.131
  91.9 8.2 %all-to-all-start = ((bf16[64,16,1536]{2,1,0:T(8,128)(2,1)}), bf16[64,16,1536]{2,1,0:T(8,128)(2,1)}, u32[]{:S(2)}, u32[]{:S(2)}) async-start(bf16[64,16,1536]{2,1,0:T(8,128)(2,1)} %send_grads.1), calls=%async_computation | async-start | bytes 6291456 | tf_op jit(solution)/shard_map/all_to_all | solution.py:954
  121.2 50.9 %carried.1 = f32[64,24,128]{2,1,0:T(8,128)} custom-call(f32[64,32,128]{2,1,0:T(8,128)} %pad_maximum_fusion.3.x_ref), custom_call_target="tpu_custom_call" | custom-call | tf_op jit(solution)/shard_map/carried/pallas_call | solution.py:444
  175.3 7.3 %fusion.47 = f32[256,24,64]{0,2,1:T(8,128)S(1)} fusion(f32[256,24,64]{0,2,1:T(8,128)S(1)} %bitcast.191, f32[256,24,64]{0,2,1:T(8,128)S(1)} %fusion.74, f32[256,24]{0,1:T(8,128)S(1)} %copy-done.90, f32[256,256]{1,0:T(8,128)S(1)} %fusion.110, f32[256,24]{0,1:T(8,128)S(1)} %copy-done.88, pred[256,256]{1,0:T(8,128)(4,1)S(1)} %copy-done.77, ...), kind=kOutput, calls=%fused_computation.77 | convolution fusion | flops 1217396736 | bytes 5120096 | tf_op jit(solution)/shard_map/tsh,shp->thp/dot_general | solution.py:885
  186.3 10.3 %pair_total.7 = f32[2,128]{1,0:T(2,128)} custom-call(f32[2,128]{1,0:T(2,128)} %bitcast.228), custom_call_target="tpu_custom_call" | custom-call | tf_op jit(solution)/shard_map/pair_total/pallas_call | solution.py:685
  198.5 4.9 fusion.10.x_ref
  203.4 6.4 pair_total.8
  217.1 116.4 %experts.1 = (bf16[64,16,1536]{2,1,0:T(8,128)(2,1)}, bf16[64,16,1536]{2,1,0:T(8,128)(2,1)}, f32[6144,128]{1,0:T(8,128)}, f32[256,1536]{1,0:T(8,128)}) custom-call(bf16[64,16,1536]{2,1,0:T(8,128)(2,1)} %copy-done, bf16[64,16,1536]{2,1,0:T(8,128)(2,1)} %all-to-all-done.grads_ref, bf16[1536,512]{1,0:T(8,128)(2,1)} %bitcast.202, bf16[256,1536]{1,0:T(8,128)(2,1)} %bitcast.212), custom_call_target="tpu_custom_call" | custom-call | tf_op jit(solution)/shard_map/experts/pallas_call | solution.py:340
  333.5 11.6 %all-to-all-start.1 = ((bf16[64,16,1536]{2,1,0:T(8,128)(2,1)}), bf16[64,16,1536]{2,1,0:T(8,128)(2,1)S(1)}, u32[]{:S(2)}, u32[]{:S(2)}) async-start(bf16[64,16,1536]{2,1,0:T(8,128)(2,1)} %get-tuple-element.36), calls=%async_computation.1 | async-start | bytes 6291456 | tf_op jit(solution)/shard_map/all_to_all | solution.py:1004
  355.6 4.1 convolution_add_fusion.x_ref
  359.7 8.2 %pair_total.10 = f32[256,1536]{1,0:T(8,128)} custom-call(f32[256,1536]{1,0:T(8,128)} %convolution_add_fusion.x_ref), custom_call_target="tpu_custom_call" | custom-call | tf_op jit(solution)/shard_map/pair_total/pallas_call | solution.py:685
  372.8 9.4 %all-to-all-done.1.rows_ref = bf16[64,16,1536]{2,1,0:T(8,128)(2,1)S(1)} async-done(((bf16[64,16,1536]{2,1,0:T(8,128)(2,1)}), bf16[64,16,1536]{2,1,0:T(8,128)(2,1)S(1)}, u32[]{:S(2)}, u32[]{:S(2)}) %all-to-all-start.1) | async-done | bytes 3145760 | tf_op jit(solution)/shard_map/all_to_all | solution.py:1004
  388.3 11.3 %pair_total.9 = f32[256,1536]{1,0:T(8,128)} custom-call(f32[256,1536]{1,0:T(8,128)} %convolution_add_fusion.3.x_ref), custom_call_target="tpu_custom_call" | custom-call | tf_op jit(solution)/shard_map/pair_total/pallas_call | solution.py:685
  403.7 5.8 multiply_reduce_fusion.6
  412.0 5.5 multiply_reduce_fusion.7
  428.5 76.8 %scatter_rows.2 = (f32[24,3072]{1,0:T(8,128)}, f32[64,24,128]{2,1,0:T(8,128)}) custom-call(bf16[256,1536]{1,0:T(8,128)(2,1)} %copy-done.46, bf16[256,1536]{1,0:T(8,128)(2,1)} %copy-done.4, bf16[256,1536]{1,0:T(8,128)(2,1)} %lefts_2_.1, bf16[256,3072]{1,0:T(8,128)(2,1)} %pad_maximum_fusion.1.right, f32[64,32,128]{2,1,0:T(8,128)} %pad_maximum_fusion.2.scanned), custom_call_target="tpu_custom_call" | custom-call | tf_op jit(solution)/shard_map/scatter_rows/pallas_call | solution.py:653
  511.9 10.5 %fusion.14 = (f32[256,24]{0,1:T(8,128)}, f32[256,24]{0,1:T(8,128)}, f32[256,24]{0,1:T(8,128)}, f32[256,256]{1,0:T(8,128)S(1)}) fusion(f32[256,24]{0,1:T(8,128)S(1)} %copy-done.91, f32[256,256]{1,0:T(8,128)S(1)} %copy-done.61, f32[256,24]{0,1:T(8,128)S(1)} %copy-done.89, pred[256,256]{1,0:T(8,128)(4,1)S(1)} %copy-done.78, f32[24,64,256]{2,1,0:T(8,128)S(1)} %bitcast.199, ...), kind=kOutput, calls=%fused_computation.24 | convolution fusion | flops 1231468544 | bytes 3858432 | tf_op jit(solution)/shard_map/transpose(jvp(tsh,shp->thp))/dot_general | solution.py:885
  524.1 5.5 pair_total.12
  529.6 8.2 %fusion.46 = f32[256,24,64]{0,2,1:T(8,128)} fusion(f32[256,24,64]{0,2,1:T(8,128)} %get-tuple-element.109, f32[256,24,64]{0,2,1:T(8,128)S(1)} %bitcast.200, f32[24,64,256]{2,1,0:T(8,128)S(1)} %bitcast.201, f32[256,24]{0,1:T(8,128)S(1)} %copy-done.91, f32[256,256]{1,0:T(8,128)} %copy-done.60, f32[256,24]{0,1:T(8,128)S(1)} %copy-done.89, ...), kind=kOutput, calls=%fused_computation.75 | convolution fusion | flops 1217396736 | bytes 6692960 | tf_op jit(solution)/shard_map/transpose(jvp(tsh,shp->thp))/dot_general | solution.py:885
  572.0 5.2 fusion.42
  581.1 6.3 pair_total.13
  590.7 65.5 %scatter_rows.3 = (f32[24,3456]{1,0:T(8,128)}, f32[64,8,128]{2,1,0:T(8,128)}) custom-call(bf16[256,1536]{1,0:T(8,128)(2,1)} %copy-done.48, bf16[256,3456]{1,0:T(8,128)(2,1)} %fusion.31.right, f32[64,8,128]{2,1,0:T(8,128)} %pad_bitcast_fusion.small), custom_call_target="tpu_custom_call" | custom-call | tf_op jit(solution)/shard_map/scatter_rows/pallas_call | solution.py:653
  (384 shorter events, 159.8 us)
Async XLA Ops:
  7.2 191.3 %all-gather.2.cloned.1.call-start = ((), (), s32[]{:S(2)}) async-start(), calls=%async_computation.2 | async-start | bytes 9584640 | tf_op jit(solution)/shard_map/all_gather | solution.py:947
  72.3 27.9 %copy-start.48 = (bf16[256,1536]{1,0:T(8,128)(2,1)}, bf16[256,1536]{1,0:T(8,128)(2,1)S(1)}, u32[]{:S(2)}) copy-start(bf16[256,1536]{1,0:T(8,128)(2,1)S(1)} %fusion.34.lefts_0_) | copy-start | bytes 2359300
  79.4 29.6 %copy-start.13 = (f32[256,1536]{1,0:T(8,128)}, f32[256,1536]{1,0:T(8,128)S(1)}, u32[]{:S(2)}) copy-start(f32[256,1536]{1,0:T(8,128)S(1)} %slice.214) | copy-start | bytes 4718596
  81.5 26.5 %copy-start.43 = (f32[256,256]{1,0:T(8,128)}, f32[256,256]{1,0:T(8,128)S(1)}, u32[]{:S(2)}) copy-start(f32[256,256]{1,0:T(8,128)S(1)} %fusion.77) | copy-start | bytes 786436
  81.5 26.5 %collective-permute-start = (f32[3,1792]{1,0:T(4,128)S(1)}, f32[3,1792]{1,0:T(4,128)}, u32[]{:S(2)}, u32[]{:S(2)}) collective-permute-start(f32[3,1792]{1,0:T(4,128)S(1)} %fusion.117), channel_id=1, source_target_pairs={{0,2},{2,4},{4,6},{6,8},{8,10},{10,12},{12,14},{14,16},{16,18},{18... | collective-permute-start | bytes 64520 | tf_op jit(solution)/shard_map/ppermute | solution.py:831
  91.9 125.2 %all-to-all-start = ((bf16[64,16,1536]{2,1,0:T(8,128)(2,1)}), bf16[64,16,1536]{2,1,0:T(8,128)(2,1)}, u32[]{:S(2)}, u32[]{:S(2)}) async-start(bf16[64,16,1536]{2,1,0:T(8,128)(2,1)} %send_grads.1), calls=%async_computation | async-start | bytes 6291456 | tf_op jit(solution)/shard_map/all_to_all | solution.py:954
  104.4 11.4 %copy-start.62 = (f32[256,24]{0,1:T(8,128)}, f32[256,24]{0,1:T(8,128)S(1)}, u32[]{:S(2)}) copy-start(f32[256,24]{0,1:T(8,128)S(1)} %copy.181) | copy-start | bytes 73732
  105.1 70.1 %copy-start.64 = (f32[256,24]{0,1:T(8,128)}, f32[256,24]{0,1:T(8,128)S(1)}, u32[]{:S(2)}) copy-start(f32[256,24]{0,1:T(8,128)S(1)} %copy.180) | copy-start | bytes 73732
  112.3 60.3 %copy-start.20 = (f32[256,1792]{1,0:T(8,128)}, f32[256,1792]{1,0:T(8,128)S(1)}, u32[]{:S(2)}) copy-start(f32[256,1792]{1,0:T(8,128)S(1)} %get-tuple-element.77) | copy-start | bytes 5505028
  115.8 59.5 %copy-start.25 = (f32[256,1536]{0,1:T(8,128)}, f32[256,1536]{0,1:T(8,128)S(1)}, u32[]{:S(2)}) copy-start(f32[256,1536]{0,1:T(8,128)S(1)} %copy.172) | copy-start | bytes 4718596
  183.1 14.1 %copy-start.84 = (f32[1536]{0:T(1024)S(1)}, f32[1536]{0:T(1024)}, u32[]{:S(2)}) copy-start(f32[1536]{0:T(1024)} %param.30) | copy-start | bytes 18436
  186.3 17.1 %copy-start.31 = (f32[256,1536]{1,0:T(8,128)}, f32[256,1536]{1,0:T(8,128)S(1)}, u32[]{:S(2)}) copy-start(f32[256,1536]{1,0:T(8,128)S(1)} %get-tuple-element.76) | copy-start | bytes 4718596
  333.5 11.7 %copy-start.101 = (f32[2,128]{1,0:T(2,128)S(1)}, f32[2,128]{1,0:T(2,128)}, u32[]{:S(2)}) copy-start(f32[2,128]{1,0:T(2,128)} %pair_total.7) | copy-start | bytes 3076
  333.5 48.7 %all-to-all-start.1 = ((bf16[64,16,1536]{2,1,0:T(8,128)(2,1)}), bf16[64,16,1536]{2,1,0:T(8,128)(2,1)S(1)}, u32[]{:S(2)}, u32[]{:S(2)}) async-start(bf16[64,16,1536]{2,1,0:T(8,128)(2,1)} %get-tuple-element.36), calls=%async_computation.1 | async-start | bytes 6291456 | tf_op jit(solution)/shard_map/all_to_all | solution.py:1004
  388.2 11.3 %copy-start.3 = (bf16[256,1536]{1,0:T(8,128)(2,1)S(1)}, bf16[256,1536]{1,0:T(8,128)(2,1)}, u32[]{:S(2)}) copy-start(bf16[256,1536]{1,0:T(8,128)(2,1)} %lefts_2_.1) | copy-start | bytes 2359300
  388.2 11.3 %copy-start.19 = (f32[256,1536]{1,0:T(8,128)S(1)}, f32[256,1536]{1,0:T(8,128)}, u32[]{:S(2)}) copy-start(f32[256,1536]{1,0:T(8,128)} %copy-done.18) | copy-start | bytes 4718596
  388.2 11.3 %copy-start.96 = (f32[256]{0:T(256)S(1)}, f32[256]{0:T(256)}, u32[]{:S(2)}) copy-start(f32[256]{0:T(256)} %copy-done.95) | copy-start | bytes 3076
  388.3 11.3 %copy-start.105 = (f32[256]{0:T(256)S(1)}, f32[256]{0:T(256)}, u32[]{:S(2)}) copy-start(f32[256]{0:T(256)} %get-tuple-element.103) | copy-start | bytes 3076
  388.3 11.4 %copy-start.107 = (f32[256]{0:T(256)S(1)}, f32[256]{0:T(256)}, u32[]{:S(2)}) copy-start(f32[256]{0:T(256)} %broadcast_multiply_fusion.7) | copy-start | bytes 3076
  428.5 76.8 %copy-start.28 = (f32[256,24,64]{0,2,1:T(8,128)S(1)}, f32[256,24,64]{0,2,1:T(8,128)}, u32[]{:S(2)}) copy-start(f32[256,24,64]{0,2,1:T(8,128)} %copy-done.27) | copy-start | bytes 4718596
  529.6 11.3 %copy-start.14 = (f32[256,1536]{1,0:T(8,128)S(1)}, f32[256,1536]{1,0:T(8,128)}, u32[]{:S(2)}) copy-start(f32[256,1536]{1,0:T(8,128)} %copy-done.13) | copy-start | bytes 4718596
  549.4 20.2 %collective-permute-start.1 = (f32[3,1792]{1,0:T(4,128)}, f32[3,1792]{1,0:T(4,128)}, u32[]{:S(2)}, u32[]{:S(2)}) collective-permute-start(f32[3,1792]{1,0:T(4,128)} %pad_add_fusion.2), channel_id=1, source_target_pairs={{2,0},{4,2},{6,4},{8,6},{10,8},{12,10},{14,12},{16,14},{18,16},{20... | collective-permute-start | bytes 64520 | tf_op jit(solution)/shard_map/ppermute | solution.py:831
  550.7 11.1 %copy-start.81 = (f32[1792]{0:T(1024)S(1)}, f32[1792]{0:T(1024)}, u32[]{:S(2)}) copy-start(f32[1792]{0:T(1024)} %get-tuple-element.50) | copy-start | bytes 21508
  590.7 75.7 %copy-start.109 = (f32[256]{0:T(256)S(1)}, f32[256]{0:T(256)}, u32[]{:S(2)}) copy-start(f32[256]{0:T(256)} %get-tuple-element.101) | copy-start | bytes 3076
  (98 other events, 406.1 us)
Sparse Core Ops, SparseCore 0:
  71.3 127.1 all-gather.1

commit v3 on v2

--- a/solution.py
+++ b/solution.py
@@ -8,6 +8,7 @@
 
 ORDERS = ((0, 1, 2), (1, 2, 0), (2, 0, 1))
 MIB = 1 << 20
+EPSILON = 1e-05
 
 
 def coordinates():
@@ -23,12 +24,12 @@
     return [(c + by) % 4 if i == axis else c for i, c in enumerate(at)]
 
 
-def greet_neighbours(at):
+def greet_neighbours(at, count=6):
     barrier = pltpu.get_barrier_semaphore()
     for axis in range(3):
         for by in (1, 3):
             pl.semaphore_signal(barrier, inc=1, device_id={"seq": seq_of(moved(at, axis, by))})
-    pl.semaphore_wait(barrier, 6)
+    pl.semaphore_wait(barrier, count)
 
 
 def greet_all(me):
@@ -58,70 +59,6 @@
         else:
             index[order[i]] = at[order[i]]
     return tuple(index) + (slice(None), cols)
-
-
-def gather_kernel(columns, x_ref, out_ref, local_sem, send, recv):
-    me, at = coordinates()
-    third, half = parts_of(columns)
-    own = pltpu.make_async_copy(x_ref, out_ref.at[at[0], at[1], at[2]], local_sem)
-    own.start()
-    greet_neighbours(at)
-    for phase in range(3):
-        firsts, seconds = [], []
-        for p, order in enumerate(ORDERS):
-            axis = order[phase]
-            cols = pl.ds(p * third, third)
-            here = region(at, order, phase, at[axis], cols)
-            source = x_ref.at[:, cols] if phase == 0 else out_ref.at[here]
-            for kind, by in enumerate((1, 3)):
-                copy = pltpu.make_async_remote_copy(
-                    src_ref=source,
-                    dst_ref=out_ref.at[here],
-                    send_sem=send.at[phase, p, kind],
-                    recv_sem=recv.at[phase, p, kind],
-                    device_id={"seq": seq_of(moved(at, axis, by))},
-                )
-                copy.start()
-                firsts.append(copy)
-        if phase == 0:
-            own.wait()
-        for p, order in enumerate(ORDERS):
-            axis = order[phase]
-            for kind, by in enumerate((1, 3)):
-                cols = pl.ds(p * third, half) if kind == 0 else pl.ds(p * third + half, third - half)
-                there = region(at, order, phase, (at[axis] - by) % 4, cols)
-                firsts[p * 2 + kind].wait_recv()
-                copy = pltpu.make_async_remote_copy(
-                    src_ref=out_ref.at[there],
-                    dst_ref=out_ref.at[there],
-                    send_sem=send.at[phase, p, 2 + kind],
-                    recv_sem=recv.at[phase, p, 2 + kind],
-                    device_id={"seq": seq_of(moved(at, axis, by))},
-                )
-                copy.start()
-                seconds.append(copy)
-        for copy in seconds:
-            copy.wait_recv()
-        for copy in firsts + seconds:
-            copy.wait_send()
-
-
-def gather_rows(x, collective):
-    rows, columns = x.shape
-    out = pl.pallas_call(
-        functools.partial(gather_kernel, columns),
-        out_shape=jax.ShapeDtypeStruct((4, 4, 4, rows, columns), x.dtype),
-        in_specs=[pl.BlockSpec(memory_space=pl.ANY)],
-        out_specs=pl.BlockSpec(memory_space=pl.ANY),
-        scratch_shapes=[
-            pltpu.SemaphoreType.DMA,
-            pltpu.SemaphoreType.DMA((3, 3, 4)),
-            pltpu.SemaphoreType.DMA((3, 3, 4)),
-        ],
-        compiler_params=pltpu.CompilerParams(collective_id=collective, has_side_effects=True),
-        name="gather_rows",
-    )(x)
-    return out
 
 
 def torus_target(at, k):
@@ -394,9 +331,8 @@
         pltpu.make_async_copy(x_ref.at[some], x_ref.at[some], self.send).wait()
         pltpu.make_async_copy(got.at[some], got.at[some], self.recv).wait()
         heads, width = made.shape[1:]
-        chosen = lax.broadcasted_iota(jnp.int32, (heads, width), 0) == lax.broadcasted_iota(
-            jnp.int32, (heads, width), 1
-        )
+        number = lax.broadcasted_iota(jnp.int32, (heads, width), 0) + heads * self.me
+        chosen = number // 64 == lax.broadcasted_iota(jnp.int32, (heads, width), 1)
 
         def step(k, state):
             at_k = 63 - k if self.reverse else k
@@ -414,43 +350,6 @@
         made = self.made
         pltpu.make_async_copy(made.at[some], made.at[some], self.back_send).wait()
         pltpu.make_async_copy(made.at[some], made.at[some], self.back_recv).wait()
-
-
-def scan_shapes(size, heads, width):
-    return [
-        pltpu.VMEM((size, heads + 8, width), jnp.float32),
-        pltpu.VMEM((size, heads, width), jnp.float32),
-        pltpu.SemaphoreType.DMA((4,)),
-    ]
-
-
-def scan_kernel(reverse, x_ref, out_ref, got, made, sems):
-    me, at = coordinates()
-    greet_all(me)
-    scan = Scan(reverse, at, me, x_ref, out_ref, got, made, sems)
-    scan.begin()
-    scan.middle()
-    scan.end()
-
-
-def scan_message(decay, state):
-    heads, size, width = state.shape
-    rows = jnp.broadcast_to(jnp.pad(decay, (0, width - heads))[None, None, :], (size, 8, width))
-    return jnp.concatenate([state.transpose(1, 0, 2), rows], axis=1)
-
-
-def carried(decay, state, collective):
-    heads, size, width = state.shape
-    out = pl.pallas_call(
-        functools.partial(scan_kernel, False),
-        out_shape=jax.ShapeDtypeStruct((size, heads, width), jnp.float32),
-        in_specs=[pl.BlockSpec(memory_space=pltpu.VMEM)],
-        out_specs=pl.BlockSpec(memory_space=pltpu.VMEM),
-        scratch_shapes=scan_shapes(size, heads, width),
-        compiler_params=params(collective),
-        name="carried",
-    )(scan_message(decay, state))
-    return out.transpose(1, 0, 2)
 
 
 class Small:
@@ -607,58 +506,1042 @@
     ]
 
 
-def scatter_kernel(
-    plan, lefts, right, scanned, small, out_ref, scan_out, small_out, buf, rest, send, recv, scan_scratch, small_scratch
+def dot_nn(left, right):
+    return jnp.dot(left, right, preferred_element_type=jnp.float32)
+
+
+def dot_nt(left, right):
+    return lax.dot_general(
+        left, right, (((1,), (1,)), ((), ())), preferred_element_type=jnp.float32
+    )
+
+
+def dot_tn(left, right):
+    return lax.dot_general(
+        left, right, (((0,), (0,)), ((), ())), preferred_element_type=jnp.float32
+    )
+
+
+def low(value):
+    return value.astype(jnp.bfloat16)
+
+
+def split(value, count):
+    parts = []
+    for _ in range(count):
+        parts.append(low(value))
+        value = value - parts[-1].astype(jnp.float32)
+    return parts
+
+
+def dot_split(left, right, count, dot=dot_nn):
+    return sum(dot(left, part) for part in split(right, count))
+
+
+def split_dot(left, right, count):
+    return sum(dot_nn(part, right) for part in split(left, count))
+
+
+def dot_three(left, right, dot=dot_nn):
+    high, less = split(left, 2)
+    other_high, other_less = split(right, 2)
+    return dot(high, other_high) + dot(less, other_high) + dot(high, other_less)
+
+
+def head_spread(lanes, width, size):
+    head = lax.broadcasted_iota(jnp.int32, (lanes, width), 0)
+    column = lax.broadcasted_iota(jnp.int32, (lanes, width), 1)
+    return low(jnp.where(head == column // size, 1.0, 0.0))
+
+
+def head_gather(lanes, width, size):
+    head = lax.broadcasted_iota(jnp.int32, (width, lanes), 1)
+    column = lax.broadcasted_iota(jnp.int32, (width, lanes), 0)
+    return low(jnp.where(head == column // size, 1.0, 0.0))
+
+
+def triangle(rows, keep):
+    first = lax.broadcasted_iota(jnp.int32, (rows, rows), 0)
+    second = lax.broadcasted_iota(jnp.int32, (rows, rows), 1)
+    return keep(first, second)
+
+
+def silu_parts(value):
+    sig = jax.nn.sigmoid(value)
+    return value * sig, sig * (1.0 + value * (1.0 - sig))
+
+
+def mixer_back_kernel(
+    plan,
+    lefts,
+    right,
+    dy_ref,
+    y_ref,
+    x_ref,
+    bc_ref,
+    conv_ref,
+    pre_ref,
+    gate_ref,
+    step_raw_ref,
+    numbers_ref,
+    taps_ref,
+    start_ref,
+    out_ref,
+    grads_ref,
+    taps_grad_ref,
+    heads_grad_ref,
+    message,
+    back,
+    got,
+    made,
+    decayed,
+    q,
+    spread,
+    cum_rows,
+    scores,
+    acc,
+    ext,
+    mine,
+    theirs,
+    buf,
+    rest,
+    send,
+    recv,
+    scan_sems,
+    sems,
 ):
     me, at = coordinates()
-    greet_all(me)
+    head = lax.axis_index("head")
+    tokens, width = x_ref.shape
+    size = start_ref.shape[1]
+    lanes = step_raw_ref.shape[1]
+    each = width // 64
+    mid = tokens // 2
+    cut = 384
+    greet_all_and_sibling(me)
     sums = Scatter(at, plan, lefts, right, out_ref, buf, rest, send, recv)
-    others = []
-    if scanned is not None:
-        got, made, sems = scan_scratch
-        others.append(Scan(True, at, me, scanned, scan_out, got, made, sems))
-    if small is not None:
-        got, sems = small_scratch
-        others.append(Small(at, me, small, small_out, got, sems))
-    for other in others:
-        other.begin()
+    scan = Scan(True, at, me, message, back, got, made, scan_sems)
+
+    rate = numbers_ref[0:1, :]
+    step_raw = step_raw_ref[...]
+    step = jax.nn.softplus(step_raw)
+    earlier = low(triangle(tokens, lambda t, s: jnp.where(t >= s, 1.0, 0.0)))
+    cum = dot_split(earlier, -step * rate, 3)
+    cum_rows[...] = cum.T
+    tail = cum[tokens - 1 : tokens, :]
+    rest_decay = jnp.exp(tail - cum)
+    weight = rest_decay * step
+    spreader = head_spread(lanes, width, 64)
+    gatherer = head_gather(lanes, width, 64)
+    spread[...] = split_dot(jnp.exp(cum), spreader, 2)
+    held_full, read_full = bc_ref[:, :size], bc_ref[:, size:]
+    held, read = low(held_full), low(read_full)
+
+    for c in range(0, width, cut):
+        part = dy_ref[:, c : c + cut] * spread[:, c : c + cut]
+        decayed[:, c : c + cut] = part
+        made_rows = dot_three(part, read_full, dot_tn)
+        message[c // each : (c + cut) // each, 0:each, :] = made_rows.reshape(
+            cut // each, each, size
+        )
+    message[:, each : each + 8, :] = jnp.broadcast_to(jnp.exp(tail)[None], (64, 8, lanes))
+    scan.begin()
+    for p in range(3):
+        sums.product(p)
+    scan.middle()
+    for p in range(3):
+        sums.first(2, p)
+
+    spread[...] = split_dot(step, spreader, 2)
+    blocks = ((0, 0), (0, 1), (1, 1))
+    for n, (s, t) in enumerate(blocks):
+        scores[n] = dot_nt(held[s * mid : (s + 1) * mid], read[t * mid : (t + 1) * mid])
+    acc[...] = jnp.zeros_like(acc)
+    causal = triangle(mid, lambda s, t: s <= t)
+    second_head = lax.broadcasted_iota(jnp.int32, (tokens, 128), 1) >= 64
+
+    @pl.loop(0, width // 128)
+    def _(i):
+        here = pl.ds(pl.multiple_of(i * 128, 128), 128)
+        dy, dy_less = split(dy_ref[:, here], 2)
+        stepped = x_ref[:, here] * spread[:, here]
+        results = []
+        for which in range(2):
+            row = cum_rows[pl.ds(2 * i + which, 1), :]
+            column = jnp.broadcast_to(row, (128, tokens)).T
+            mask = second_head if which else jnp.logical_not(second_head)
+            values, values_less = split(jnp.where(mask, stepped, 0.0), 2)
+            total = [None, None]
+            for n, (s, t) in enumerate(blocks):
+                gap = row[:, t * mid : (t + 1) * mid] - column[s * mid : (s + 1) * mid]
+                decay = jnp.exp(gap)
+                if s == t:
+                    decay = jnp.where(causal, decay, 0.0)
+                later = dy[t * mid : (t + 1) * mid]
+                first, later_less = values[s * mid : (s + 1) * mid], dy_less[t * mid : (t + 1) * mid]
+                pairs = dot_nt(first, later) + dot_nt(first, later_less)
+                pairs = pairs + dot_nt(values_less[s * mid : (s + 1) * mid], later)
+                acc[n] += decay * pairs
+                part = dot_nn(low(decay * scores[n]), later)
+                total[s] = part if total[s] is None else total[s] + part
+            results.append(total)
+        for s in range(2):
+            rows = slice(s * mid, (s + 1) * mid)
+            q[rows, here] = jnp.where(second_head[rows], results[1][s], results[0][s])
+
+    scan.end()
+
+    skip = split_dot(jnp.broadcast_to(numbers_ref[1:2, :], (8, lanes)), spreader, 2)[0:1, :]
+    grad_weight = grad_step = rows_sum = jnp.zeros((tokens, lanes), jnp.float32)
+    skip_grad = jnp.zeros((8, lanes), jnp.float32)
+    state_dot = jnp.zeros((lanes, size), jnp.float32)
+    held_parts = held_full[:mid], held_full[mid:]
+    read_parts = read_full[:mid], read_full[mid:]
+    grad_held = dot_three(acc[0], read_parts[0]) + dot_three(acc[1], read_parts[1])
+    grad_held = jnp.concatenate([grad_held, dot_three(acc[2], read_parts[1])], axis=0)
+    grad_read = dot_three(acc[1], held_parts[0], dot_tn) + dot_three(acc[2], held_parts[1], dot_tn)
+    grad_read = jnp.concatenate([dot_three(acc[0], held_parts[0], dot_tn), grad_read], axis=0)
+    for c in range(0, width, cut):
+        here = slice(c, c + cut)
+        x, dy, inner = x_ref[:, here], dy_ref[:, here], q[:, here]
+        after = back[c // each : (c + cut) // each].reshape(cut, size)
+        start = start_ref[here, :]
+        gather = gatherer[here, :]
+        weights = split_dot(weight, spreader[:, here], 2)
+        through = dot_nt(held, low(after))
+        grad_x = inner * spread[:, here] + skip[:, here] * dy + weights * through
+        grad_step = grad_step + split_dot(x * inner, gather, 2)
+        grad_weight = grad_weight + split_dot(x * through, gather, 2)
+        rows_sum = rows_sum + split_dot(dy * (y_ref[:, here] - skip[:, here] * x), gather, 2)
+        pairs = jnp.sum(dy * x, axis=0, keepdims=True)
+        skip_grad = skip_grad + split_dot(jnp.broadcast_to(pairs, (8, cut)), gather, 2)
+        state_dot = state_dot + dot_split(gather, after * start, 2, dot_tn)
+        grad_held = grad_held + dot_three(weights * x, after)
+        grad_read = grad_read + dot_three(decayed[:, here], start)
+        ext[0:tokens, here] = grad_x * silu_parts(conv_ref[:, here])[1]
+    mine[:, :size] = grad_held
+    mine[:, size:] = grad_read
+    swap = pltpu.make_async_remote_copy(
+        src_ref=mine,
+        dst_ref=theirs,
+        send_sem=sems.at[0],
+        recv_sem=sems.at[1],
+        device_id={"head": 1 - head},
+    )
+    swap.start()
+    for p in range(3):
+        sums.second(2, p)
+
+    ones = jnp.ones((8, size), jnp.bfloat16)
+    state_grad = dot_split(ones, state_dot, 2, dot_nt)[0:1, :]
+    used = grad_weight * weight
+    tail_grad = jnp.sum(used, axis=0, keepdims=True) + jnp.exp(tail) * state_grad
+    grad_cum = rows_sum - step * grad_step - used
+    last = lax.broadcasted_iota(jnp.int32, (tokens, lanes), 0) == tokens - 1
+    grad_cum = grad_cum + jnp.where(last, tail_grad, 0.0)
+    later = low(triangle(tokens, lambda t, s: jnp.where(t <= s, 1.0, 0.0)))
+    grad_log = dot_split(later, grad_cum, 3)
+    grad_step = grad_step + grad_weight * rest_decay - rate * grad_log
+    grad_raw = grad_step * jax.nn.sigmoid(step_raw)
+    heads_grad_ref[...] = jnp.zeros_like(heads_grad_ref)
+    heads_grad_ref[0:1, :] = skip_grad[0:1, :]
+    heads_grad_ref[1:2, :] = -jnp.sum(step * grad_log, axis=0, keepdims=True)
+    heads_grad_ref[2:3, :] = jnp.sum(grad_raw, axis=0, keepdims=True)
+
+    channels = width + 2 * size
+    grads_ref[:, 0:width] = gate_ref[...]
+    grads_ref[:, width + channels : width + channels + lanes] = low(grad_raw)
+    swap.wait()
+    ext[0:tokens, width:channels] = (mine[...] + theirs[...]) * silu_parts(
+        conv_ref[:, width:channels]
+    )[1]
+    edge = pltpu.make_async_remote_copy(
+        src_ref=ext.at[pl.ds(0, 8)],
+        dst_ref=ext.at[pl.ds(tokens, 8)],
+        send_sem=sems.at[2],
+        recv_sem=sems.at[3],
+        device_id={"seq": (me + 63) % 64},
+    )
+    edge.start()
+    sums.finish(2)
+    edge.wait()
+    there = jnp.where(me == 63, 0.0, 1.0)
+    ext[tokens : tokens + 8, :] = ext[tokens : tokens + 8, :] * there
+    taps_grad_ref[...] = jnp.zeros_like(taps_grad_ref)
+
+    @pl.loop(0, channels // 256)
+    def _(i):
+        here = pl.ds(pl.multiple_of(i * 256, 256), 256)
+        grad = ext[0:tokens, here]
+        total = jnp.zeros_like(grad)
+        for j in range(4):
+            total = total + taps_ref[j : j + 1, here] * ext[3 - j : 3 - j + tokens, here]
+            products = grad * pre_ref[5 + j : 5 + j + tokens, here]
+            taps_grad_ref[j : j + 1, here] = jnp.sum(products, axis=0, keepdims=True)
+        grads_ref[:, pl.ds(pl.multiple_of(width + i * 256, 256), 256)] = low(total)
+
+    for phase in (1, 0):
+        for p in range(3):
+            sums.second(phase, p)
+        sums.finish(phase)
+    sums.end()
+
+
+def mixer_back(lefts, right, plan, dy, y, x, bc, conv, pre, gate, step_raw, numbers, taps, start, collective):
+    model, columns = lefts[0].shape[1], right.shape[1]
+    rows = model // 64
+    tokens, width = x.shape
+    size, lanes = start.shape[1], step_raw.shape[1]
+    each, channels, mid = width // 64, width + 2 * size, tokens // 2
+    f32, bf16 = jnp.float32, jnp.bfloat16
+    vmem = pl.BlockSpec(memory_space=pltpu.VMEM)
+    args = (lefts, right, dy, y, x, bc, conv, pre, gate, step_raw, numbers, taps, start)
+    return pl.pallas_call(
+        functools.partial(mixer_back_kernel, plan),
+        out_shape=[
+            jax.ShapeDtypeStruct((rows, columns), f32),
+            jax.ShapeDtypeStruct((tokens, width + channels + lanes), bf16),
+            jax.ShapeDtypeStruct((8, channels), f32),
+            jax.ShapeDtypeStruct((8, lanes), f32),
+        ],
+        in_specs=jax.tree.map(lambda _: vmem, list(args)),
+        out_specs=[vmem] * 4,
+        scratch_shapes=[
+            pltpu.VMEM((64, each + 8, size), f32),
+            pltpu.VMEM((64, each, size), f32),
+            pltpu.VMEM((64, each + 8, size), f32),
+            pltpu.VMEM((64, each, size), f32),
+            pltpu.VMEM((tokens, width), f32),
+            pltpu.VMEM((tokens, width), f32),
+            pltpu.VMEM((tokens, width), f32),
+            pltpu.VMEM((lanes, tokens), f32),
+            pltpu.VMEM((3, mid, mid), f32),
+            pltpu.VMEM((3, mid, mid), f32),
+            pltpu.VMEM((tokens + 8, channels), f32),
+            pltpu.VMEM((tokens, 2 * size), f32),
+            pltpu.VMEM((tokens, 2 * size), f32),
+        ]
+        + scatter_shapes(rows, columns)
+        + [pltpu.SemaphoreType.DMA((4,)), pltpu.SemaphoreType.DMA((4,))],
+        compiler_params=params(collective, vmem_limit_bytes=60 * MIB),
+        name="mixer_back",
+    )(*args)
+
+
+def input_back_kernel(
+    plan,
+    left,
+    right,
+    weights_ref,
+    resid_ref,
+    gain_ref,
+    grad_ref,
+    small_ref,
+    out_ref,
+    input_ref,
+    small_out,
+    weights,
+    mine,
+    theirs,
+    small,
+    small_got,
+    buf,
+    rest,
+    send,
+    recv,
+    small_sems,
+    sems,
+):
+    me, at = coordinates()
+    head = lax.axis_index("head")
+    tokens, model = resid_ref.shape
+    columns = right.shape[1]
+    load = pltpu.make_async_copy(weights_ref, weights, sems.at[0])
+    load.start()
+    greet_all_and_sibling(me)
+    sums = Scatter(at, plan, [left], right, out_ref, buf, rest, send, recv)
+    totals = Small(at, me, small, small_out, small_got, small_sems)
     for p in range(3):
         sums.product(p)
         sums.first(2, p)
-    for other in others:
-        other.middle()
-    for phase in (2, 1, 0):
+    load.wait()
+
+    start = columns - 384
+    other = pl.multiple_of(start + 128 * (1 - head), 128)
+    cut = 256
+    swaps = []
+    for c in range(0, model, cut):
+        rows = slice(c, c + cut)
+        total = dot_nt(right[...], weights[rows, :])
+        total = total - dot_nt(right[:, pl.ds(other, 128)], weights[rows, pl.ds(other, 128)])
+        mine[:, rows] = total
+        swap = pltpu.make_async_remote_copy(
+            src_ref=mine.at[:, pl.ds(c, cut)],
+            dst_ref=theirs.at[:, pl.ds(c, cut)],
+            send_sem=sems.at[1 + c // cut],
+            recv_sem=sems.at[1 + (model + c) // cut],
+            device_id={"head": 1 - head},
+        )
+        swap.start()
+        swaps.append(swap)
+    for p in range(3):
+        sums.second(2, p)
+    square = jnp.zeros((tokens, 1), jnp.float32)
+    inner = jnp.zeros((tokens, 1), jnp.float32)
+    for n, c in enumerate(range(0, model, cut)):
+        rows = slice(c, c + cut)
+        swaps[n].wait()
+        grad = mine[:, rows] + theirs[:, rows]
+        mine[:, rows] = grad
+        resid = resid_ref[:, rows].astype(jnp.float32)
+        square = square + jnp.sum(resid * resid, axis=1, keepdims=True)
+        inner = inner + jnp.sum(resid * gain_ref[:, rows] * grad, axis=1, keepdims=True)
+    scale = lax.rsqrt(square / model + EPSILON)
+    pull = scale * scale * scale * (inner / model)
+    small[...] = small_ref[...]
+    for c in range(0, model, cut):
+        rows = slice(c, c + cut)
+        grad = mine[:, rows]
+        resid = resid_ref[:, rows].astype(jnp.float32)
+        input_ref[:, rows] = grad_ref[:, rows] + scale * gain_ref[:, rows] * grad - resid * pull
+        gain_grad = jnp.sum(grad * resid * scale, axis=0, keepdims=True)
+        for tile in range(c // 128, (c + cut) // 128):
+            at_tile = tile * 128 - c
+            small[tile // 8, tile % 8 : tile % 8 + 1, :] = gain_grad[:, at_tile : at_tile + 128]
+    totals.begin()
+    sums.finish(2)
+    totals.middle()
+    for phase in (1, 0):
         for p in range(3):
             sums.second(phase, p)
         sums.finish(phase)
-    for other in others:
-        other.end()
+    totals.end()
     sums.end()
 
 
-def scatter_rows(lefts, right, plan, collective, scanned=None, small=None):
-    model, columns = lefts[0].shape[1], right.shape[1]
+def input_back(left, right, plan, weights, resid, gain, grad, small, collective):
+    tokens, model = resid.shape
+    columns = right.shape[1]
     rows = model // 64
+    f32 = jnp.float32
     vmem = pl.BlockSpec(memory_space=pltpu.VMEM)
-    scan_scratch = small_scratch = None
-    out_shape = [jax.ShapeDtypeStruct((rows, columns), jnp.float32), None, None]
-    if scanned is not None:
-        size, heads, width = scanned.shape
-        scan_scratch = scan_shapes(size, heads - 8, width)
-        out_shape[1] = jax.ShapeDtypeStruct((size, heads - 8, width), jnp.float32)
-    if small is not None:
-        small_scratch = [pltpu.VMEM(small.shape, jnp.float32), pltpu.SemaphoreType.DMA((4,))]
-        out_shape[2] = jax.ShapeDtypeStruct(small.shape, jnp.float32)
-    spec = lambda tree: jax.tree.map(lambda _: vmem, tree)
     return pl.pallas_call(
-        functools.partial(scatter_kernel, plan),
-        out_shape=out_shape,
-        in_specs=spec([lefts, right, scanned, small]),
-        out_specs=spec(out_shape),
-        scratch_shapes=scatter_shapes(rows, columns) + [scan_scratch, small_scratch],
-        compiler_params=params(collective, vmem_limit_bytes=60 * MIB),
-        name="scatter_rows",
-    )(lefts, right, scanned, small)
+        functools.partial(input_back_kernel, plan),
+        out_shape=[
+            jax.ShapeDtypeStruct((rows, columns), f32),
+            jax.ShapeDtypeStruct((tokens, model), f32),
+            jax.ShapeDtypeStruct(small.shape, f32),
+        ],
+        in_specs=[vmem, vmem, pl.BlockSpec(memory_space=pl.ANY)] + [vmem] * 4,
+        out_specs=[vmem] * 3,
+        scratch_shapes=[
+            pltpu.VMEM(weights.shape, weights.dtype),
+            pltpu.VMEM((tokens, model), f32),
+            pltpu.VMEM((tokens, model), f32),
+            pltpu.VMEM(small.shape, f32),
+            pltpu.VMEM(small.shape, f32),
+        ]
+        + scatter_shapes(rows, columns)
+        + [pltpu.SemaphoreType.DMA((4,)), pltpu.SemaphoreType.DMA((1 + 2 * model // 256,))],
+        compiler_params=params(collective, vmem_limit_bytes=62 * MIB),
+        name="input_back",
+    )(left, right, weights, resid, gain, grad, small)
+
+
+class Gather:
+    def __init__(self, at, x_ref, out_ref, send, recv, local_sem):
+        self.at, self.x_ref, self.out_ref, self.send, self.recv = at, x_ref, out_ref, send, recv
+        self.third, self.half = parts_of(x_ref.shape[1])
+        self.own = pltpu.make_async_copy(x_ref, out_ref.at[at[0], at[1], at[2]], local_sem)
+        self.copies = {}
+
+    def put(self, source, here, phase, p, kind, by):
+        copy = pltpu.make_async_remote_copy(
+            src_ref=source,
+            dst_ref=self.out_ref.at[here],
+            send_sem=self.send.at[phase, p, kind],
+            recv_sem=self.recv.at[phase, p, kind],
+            device_id={"seq": seq_of(moved(self.at, ORDERS[p][phase], by))},
+        )
+        copy.start()
+        self.copies[phase, p, kind] = copy
+
+    def first(self, phase):
+        if phase == 1:
+            self.own.wait()
+        if phase > 0:
+            self.arrived(phase - 1)
+        else:
+            self.own.start()
+        for p, order in enumerate(ORDERS):
+            cols = pl.ds(p * self.third, self.third)
+            here = region(self.at, order, phase, self.at[order[phase]], cols)
+            source = self.x_ref.at[:, cols] if phase == 0 else self.out_ref.at[here]
+            for kind, by in enumerate((1, 3)):
+                self.put(source, here, phase, p, kind, by)
+
+    def second(self, phase):
+        for p, order in enumerate(ORDERS):
+            for kind, by in enumerate((1, 3)):
+                start, length = p * self.third, self.half
+                if kind:
+                    start, length = start + self.half, self.third - self.half
+                there = region(
+                    self.at, order, phase, (self.at[order[phase]] - by) % 4, pl.ds(start, length)
+                )
+                self.copies[phase, p, kind].wait_recv()
+                self.put(self.out_ref.at[there], there, phase, p, 2 + kind, by)
+
+    def arrived(self, phase):
+        for p in range(3):
+            for kind in (2, 3):
+                self.copies[phase, p, kind].wait_recv()
+
+    def end(self):
+        for copy in self.copies.values():
+            copy.wait_send()
+
+
+def gather_shapes():
+    return [
+        pltpu.SemaphoreType.DMA((3, 3, 4)),
+        pltpu.SemaphoreType.DMA((3, 3, 4)),
+        pltpu.SemaphoreType.DMA,
+    ]
+
+
+def gather_kernel(x_ref, edge_ref, out_ref, before_ref, send, recv, local_sem, edge_sems):
+    me, at = coordinates()
+    barrier = pltpu.get_barrier_semaphore()
+    pl.semaphore_signal(barrier, inc=1, device_id={"seq": (me + 63) % 64})
+    greet_neighbours(at, 7)
+    gather = Gather(at, x_ref, out_ref, send, recv, local_sem)
+    edge = pltpu.make_async_remote_copy(
+        src_ref=edge_ref,
+        dst_ref=before_ref,
+        send_sem=edge_sems.at[0],
+        recv_sem=edge_sems.at[1],
+        device_id={"seq": (me + 1) % 64},
+    )
+    edge.start()
+    for phase in range(3):
+        gather.first(phase)
+        gather.second(phase)
+    gather.arrived(2)
+    edge.wait()
+    gather.end()
+
+
+def gather_rows(x, edge, collective):
+    rows, columns = x.shape
+    hbm = pl.BlockSpec(memory_space=pl.ANY)
+    return pl.pallas_call(
+        gather_kernel,
+        out_shape=[
+            jax.ShapeDtypeStruct((4, 4, 4, rows, columns), x.dtype),
+            jax.ShapeDtypeStruct(edge.shape, edge.dtype),
+        ],
+        in_specs=[hbm, hbm],
+        out_specs=[hbm, hbm],
+        scratch_shapes=gather_shapes() + [pltpu.SemaphoreType.DMA((2,))],
+        compiler_params=params(collective),
+        name="gather_rows",
+    )(x, edge)
+
+
+def mixer_kernel(
+    layer_ref,
+    edge_ref,
+    norm_ref,
+    weights_ref,
+    numbers_ref,
+    taps_ref,
+    gain_ref,
+    late_ref,
+    normed_ref,
+    z_ref,
+    x_ref,
+    bc_ref,
+    conv_ref,
+    pre_ref,
+    step_raw_ref,
+    start_ref,
+    y_ref,
+    gated_ref,
+    scale_ref,
+    gathered_ref,
+    weights,
+    normed,
+    message,
+    got,
+    made,
+    spread,
+    cum_rows,
+    scores,
+    mine,
+    theirs,
+    load_sems,
+    scan_sems,
+    pair_sems,
+    send,
+    recv,
+    local_sem,
+):
+    me, at = coordinates()
+    head = lax.axis_index("head")
+    tokens, model = layer_ref.shape
+    width = x_ref.shape[1]
+    size = bc_ref.shape[1] // 2
+    lanes = step_raw_ref.shape[1]
+    each = width // 64
+    mid = tokens // 2
+    cut = 384
+
+    def load(n):
+        cols = pl.ds(pl.multiple_of(n * cut, 128), cut)
+        return pltpu.make_async_copy(weights_ref.at[:, cols], weights.at[:, cols], load_sems.at[n])
+
+    for n in (8, 4, 5, 6, 7, 0, 1, 2, 3):
+        load(n).start()
+    greet_all_and_sibling(me)
+    gather = Gather(at, late_ref, gathered_ref, send, recv, local_sem)
+    gather.first(0)
+
+    def norm(rows):
+        rows = rows.astype(jnp.float32)
+        scale = lax.rsqrt(jnp.mean(rows * rows, axis=1, keepdims=True) + EPSILON)
+        return low(rows * scale * norm_ref[...])
+
+    before = norm(edge_ref[...]).astype(jnp.float32) * jnp.where(me == 0, 0.0, 1.0)
+    normed[0:16, :] = low(before)
+    normed[16 : 16 + tokens, :] = norm(layer_ref[...])
+    normed_ref[...] = normed[16 : 16 + tokens, :]
+    gather.second(0)
+
+    def conv(cols):
+        total = jnp.zeros((tokens, cols.size), jnp.float32)
+        for j in range(4):
+            total = total + taps_ref[j : j + 1, cols] * pre_ref[5 + j : 5 + j + tokens, cols]
+        conv_ref[:, cols] = total
+        return total * jax.nn.sigmoid(total)
+
+    load(8).wait()
+    last = dot_nn(normed[...], weights[:, 8 * cut : 9 * cut])
+    cols = pl.ds(width, 2 * size)
+    pre_ref[:, cols] = last[8:, : 2 * size]
+    bc_ref[...] = conv(cols)
+    step_raw = last[16:, 2 * size :] + numbers_ref[2:3, :]
+    step_raw_ref[...] = step_raw
+    step = jax.nn.softplus(step_raw)
+    earlier = low(triangle(tokens, lambda t, s: jnp.where(t >= s, 1.0, 0.0)))
+    cum = dot_split(earlier, -step * numbers_ref[0:1, :], 3)
+    cum_rows[...] = cum.T
+    tail = cum[tokens - 1 : tokens, :]
+    spreader = head_spread(lanes, width, 64)
+    spread[...] = split_dot(jnp.exp(tail - cum) * step, spreader, 2)
+    held, read = bc_ref[:, :size], bc_ref[:, size:]
+    gather.first(1)
+
+    @pl.loop(0, 4)
+    def _(i):
+        load(4 + i).wait()
+        from_cols = pl.ds(pl.multiple_of((4 + i) * cut, 128), cut)
+        here = pl.ds(pl.multiple_of(i * cut, 128), cut)
+        pre_ref[:, here] = dot_nn(normed[...], weights[:, from_cols])[8:]
+        x = conv(here)
+        x_ref[:, here] = x
+        made_rows = dot_three(x * spread[:, here], held, dot_tn)
+        message[pl.ds(i * (cut // each), cut // each), 0:each, :] = made_rows.reshape(
+            cut // each, each, size
+        )
+
+    message[:, each : each + 8, :] = jnp.broadcast_to(jnp.exp(tail)[None], (64, 8, lanes))
+    scan = Scan(False, at, me, message, start_ref, got, made, scan_sems)
+    scan.begin()
+    gather.second(1)
+
+    @pl.loop(0, 4)
+    def _(i):
+        load(i).wait()
+        here = pl.ds(pl.multiple_of(i * cut, 128), cut)
+        z_ref[:, here] = dot_nn(normed[16 : 16 + tokens, :], weights[:, here])
+
+    scan.middle()
+    gather.first(2)
+
+    spread[...] = split_dot(step, spreader, 2)
+    blocks = ((0, 0), (1, 0), (1, 1))
+    for n, (t, s) in enumerate(blocks):
+        rows, columns = slice(t * mid, (t + 1) * mid), slice(s * mid, (s + 1) * mid)
+        scores[n] = dot_three(read[rows], held[columns], dot_nt)
+    causal = triangle(mid, lambda t, s: t >= s)
+    second_head = lax.broadcasted_iota(jnp.int32, (tokens, 128), 1) >= 64
+
+    @pl.loop(0, width // 128)
+    def _(i):
+        here = pl.ds(pl.multiple_of(i * 128, 128), 128)
+        values, values_less = split(x_ref[:, here] * spread[:, here], 2)
+        results = []
+        for which in range(2):
+            row = cum_rows[pl.ds(2 * i + which, 1), :]
+            column = jnp.broadcast_to(row, (128, tokens)).T
+            total = [None, None]
+            for n, (t, s) in enumerate(blocks):
+                columns = slice(s * mid, (s + 1) * mid)
+                decay = jnp.exp(column[t * mid : (t + 1) * mid] - row[:, columns])
+                if s == t:
+                    decay = jnp.where(causal, decay, 0.0)
+                mixing, mixing_less = split(decay * scores[n], 2)
+                part = dot_nn(mixing, values[columns]) + dot_nn(mixing_less, values[columns])
+                part = part + dot_nn(mixing, values_less[columns])
+                total[t] = part if total[t] is None else total[t] + part
+            results.append(total)
+        for t in range(2):
+            rows = slice(t * mid, (t + 1) * mid)
+            y_ref[rows, here] = jnp.where(second_head[rows], results[1][t], results[0][t])
+
+    scan.end()
+    skip = split_dot(jnp.broadcast_to(numbers_ref[1:2, :], (8, lanes)), spreader, 2)[0:1, :]
+    carry = split_dot(jnp.exp(cum), spreader, 2)
+    square = jnp.zeros((tokens, 1), jnp.float32)
+    for c in range(0, width, cut):
+        here = slice(c, c + cut)
+        start = start_ref[c // each : (c + cut) // each].reshape(cut, size)
+        through = dot_three(read, start, dot_nt)
+        y = y_ref[:, here] + carry[:, here] * through + skip[:, here] * x_ref[:, here]
+        y_ref[:, here] = y
+        z = z_ref[:, here]
+        gated = y * (z * jax.nn.sigmoid(z))
+        spread[:, here] = gated
+        square = square + jnp.sum(gated * gated, axis=1, keepdims=True)
+    mine[...] = jnp.broadcast_to(square, mine.shape)
+    swap = pltpu.make_async_remote_copy(
+        src_ref=mine,
+        dst_ref=theirs,
+        send_sem=pair_sems.at[0],
+        recv_sem=pair_sems.at[1],
+        device_id={"head": 1 - head},
+    )
+    swap.start()
+    gather.second(2)
+    swap.wait()
+    scale = lax.rsqrt((mine[...] + theirs[...]) / (2 * width) + EPSILON)
+    scale_ref[...] = scale
+    for c in range(0, width, cut):
+        here = slice(c, c + cut)
+        gated_ref[:, here] = low(spread[:, here] * scale[:, 0:1] * gain_ref[:, here])
+    gather.arrived(2)
+    gather.end()
+
+
+def mixer(layer_in, edge, norm, weights, numbers, taps, gain, late, collective):
+    tokens, model = layer_in.shape
+    width, channels = gain.shape[1], taps.shape[1]
+    lanes = numbers.shape[1]
+    size = (channels - width) // 2
+    each, mid = width // 64, tokens // 2
+    f32, bf16 = jnp.float32, jnp.bfloat16
+    vmem, hbm = pl.BlockSpec(memory_space=pltpu.VMEM), pl.BlockSpec(memory_space=pl.ANY)
+    out = [
+        ((tokens, model), bf16),
+        ((tokens, width), f32),
+        ((tokens, width), f32),
+        ((tokens, 2 * size), f32),
+        ((tokens, channels), f32),
+        ((tokens + 8, channels), f32),
+        ((tokens, lanes), f32),
+        ((64, each, size), f32),
+        ((tokens, width), f32),
+        ((tokens, width), bf16),
+        ((tokens, lanes), f32),
+        ((4, 4, 4) + late.shape, bf16),
+    ]
+    return pl.pallas_call(
+        mixer_kernel,
+        out_shape=[jax.ShapeDtypeStruct(*shape) for shape in out],
+        in_specs=[vmem, vmem, vmem, hbm, vmem, vmem, vmem, hbm],
+        out_specs=[vmem] * (len(out) - 1) + [hbm],
+        scratch_shapes=[
+            pltpu.VMEM(weights.shape, bf16),
+            pltpu.VMEM((tokens + 16, model), bf16),
+            pltpu.VMEM((64, each + 8, size), f32),
+            pltpu.VMEM((64, each + 8, size), f32),
+            pltpu.VMEM((64, each, size), f32),
+            pltpu.VMEM((tokens, width), f32),
+            pltpu.VMEM((lanes, tokens), f32),
+            pltpu.VMEM((3, mid, mid), f32),
+            pltpu.VMEM((tokens, lanes), f32),
+            pltpu.VMEM((tokens, lanes), f32),
+            pltpu.SemaphoreType.DMA((9,)),
+            pltpu.SemaphoreType.DMA((4,)),
+            pltpu.SemaphoreType.DMA((2,)),
+        ]
+        + gather_shapes(),
+        compiler_params=params(collective, vmem_limit_bytes=56 * MIB),
+        name="mixer",
+    )(layer_in, edge, norm, weights, numbers, taps, gain, late)
+
+
+class PairSum:
+    def __init__(self, mine, theirs, sems, cut):
+        self.mine, self.theirs, self.sems, self.cut = mine, theirs, sems, cut
+        self.count = mine.shape[1] // cut
+
+    def copy(self, n):
+        cols = pl.ds(n * self.cut, self.cut)
+        return pltpu.make_async_remote_copy(
+            src_ref=self.mine.at[:, cols],
+            dst_ref=self.theirs.at[:, cols],
+            send_sem=self.sems.at[0, n],
+            recv_sem=self.sems.at[1, n],
+            device_id={"head": 1 - lax.axis_index("head")},
+        )
+
+
+def residual_kernel(
+    gated_ref,
+    weights_ref,
+    layer_ref,
+    norm_ref,
+    grad_out_ref,
+    position_ref,
+    resid_ref,
+    normed_ref,
+    scale_ref,
+    rows_ref,
+    shared_ref,
+    back_ref,
+    right_ref,
+    weights,
+    mine,
+    theirs,
+    load_sems,
+    sems,
+):
+    tokens, model = layer_ref.shape
+    inner = gated_ref.shape[1]
+    hidden = right_ref.shape[1] // 3
+    cut = 256
+    loads = []
+    for n, (start, length) in enumerate(
+        ((0, inner), (inner + 2 * hidden, hidden), (inner, 2 * hidden))
+    ):
+        cols = pl.ds(start, length)
+        loads.append(
+            pltpu.make_async_copy(weights_ref.at[:, cols], weights.at[:, cols], load_sems.at[n])
+        )
+        loads[-1].start()
+    greet_sibling()
+    pair = PairSum(mine, theirs, sems, cut)
+    loads[0].wait()
+    gated = gated_ref[...]
+    for n in range(pair.count):
+        rows = slice(n * cut, (n + 1) * cut)
+        mine[:, rows] = dot_nt(gated, weights[rows, 0:inner])
+        pair.copy(n).start()
+    loads[1].wait()
+    down = slice(inner + 2 * hidden, inner + 3 * hidden)
+    both = slice(inner, inner + 2 * hidden)
+    grad_hid = dot_nn(grad_out_ref[...], weights[:, down])
+    square = jnp.zeros((tokens, 1), jnp.float32)
+    for n in range(pair.count):
+        rows = slice(n * cut, (n + 1) * cut)
+        pair.copy(n).wait()
+        resid = layer_ref[:, rows].astype(jnp.float32) + (mine[:, rows] + theirs[:, rows])
+        resid_ref[:, rows] = resid
+        square = square + jnp.sum(resid * resid, axis=1, keepdims=True)
+    scale = lax.rsqrt(square / model + EPSILON)
+    scale_ref[...] = jnp.broadcast_to(scale, scale_ref.shape)
+    for n in range(pair.count):
+        rows = slice(n * cut, (n + 1) * cut)
+        normed_ref[:, rows] = low(resid_ref[:, rows] * scale * norm_ref[:, rows])
+    normed = normed_ref[...]
+    slots = rows_ref.shape[1]
+    step = 16
+
+    @pl.loop(0, rows_ref.shape[0] // step)
+    def _(i):
+        here = pl.ds(pl.multiple_of(i * step, step), step)
+        chosen = chosen_slots(position_ref[here, :], 0, step, slots)
+        rows_ref[here] = low(dot_nn(low(chosen), normed)).reshape(step, slots, model)
+
+    loads[2].wait()
+    gate_up = dot_nn(normed, weights[:, both])
+    gate, up = gate_up[:, :hidden], gate_up[:, hidden:]
+    act, slope = silu_parts(gate)
+    hid = low(act * up)
+    right_ref[:, 2 * hidden :] = hid
+    right_ref[:, 0:hidden] = low(grad_hid * up * slope)
+    right_ref[:, hidden : 2 * hidden] = low(grad_hid * act)
+    grads = right_ref[:, 0 : 2 * hidden]
+    for n in range(pair.count):
+        rows = slice(n * cut, (n + 1) * cut)
+        shared_ref[:, rows] = dot_nt(hid, weights[rows, down])
+        back_ref[:, rows] = dot_nt(grads, weights[rows, both])
+
+
+def residual_block(gated, weights, layer_in, norm, grad_out, position, slots, collective):
+    tokens, model = layer_in.shape
+    hidden = (weights.shape[1] - gated.shape[1]) // 3
+    f32, bf16 = jnp.float32, jnp.bfloat16
+    vmem, hbm = pl.BlockSpec(memory_space=pltpu.VMEM), pl.BlockSpec(memory_space=pl.ANY)
+    out = [
+        ((tokens, model), f32),
+        ((tokens, model), bf16),
+        ((tokens, 128), f32),
+        ((position.shape[0], slots, model), bf16),
+        ((tokens, model), f32),
+        ((tokens, model), f32),
+        ((tokens, 3 * hidden), bf16),
+    ]
+    return pl.pallas_call(
+        residual_kernel,
+        out_shape=[jax.ShapeDtypeStruct(*shape) for shape in out],
+        in_specs=[vmem, hbm] + [vmem] * 4,
+        out_specs=[vmem] * len(out),
+        scratch_shapes=[
+            pltpu.VMEM(weights.shape, bf16),
+            pltpu.VMEM((tokens, model), f32),
+            pltpu.VMEM((tokens, model), f32),
+            pltpu.SemaphoreType.DMA((3,)),
+            pltpu.SemaphoreType.DMA((2, model // 256)),
+        ],
+        compiler_params=params(collective, vmem_limit_bytes=48 * MIB),
+        name="residual_block",
+    )(gated, weights, layer_in, norm, grad_out, position)
+
+
+def gate_back_kernel(
+    home_ref,
+    position_ref,
+    back_ref,
+    resid_ref,
+    scale_ref,
+    norm_ref,
+    grad_out_ref,
+    weights_ref,
+    z_ref,
+    y_ref,
+    gate_scale_ref,
+    gain_ref,
+    grad_resid_ref,
+    grad_mix_ref,
+    grad_y_ref,
+    grad_z_ref,
+    norm_grad_ref,
+    gain_grad_ref,
+    weights,
+    mine,
+    theirs,
+    stat,
+    stat_theirs,
+    load_sem,
+    sems,
+    stat_sems,
+):
+    tokens, model = resid_ref.shape
+    inner = z_ref.shape[1]
+    experts, slots = home_ref.shape[:2]
+    cut = 256
+    load = pltpu.make_async_copy(weights_ref.at[:, pl.ds(0, inner)], weights, load_sem)
+    load.start()
+    greet_sibling()
+    pair = PairSum(mine, theirs, sems, cut)
+    mine[...] = back_ref[...]
+    step = 16
+
+    @pl.loop(0, experts // step)
+    def _(i):
+        here = pl.ds(pl.multiple_of(i * step, step), step)
+        chosen = low(chosen_slots(position_ref[here, :], 0, step, slots))
+        rows = home_ref[here].reshape(step * slots, model)
+        mine[...] += dot_tn(chosen, rows)
+
+    for n in range(pair.count):
+        pair.copy(n).start()
+    scale = scale_ref[:, 0:1]
+    inner_sum = jnp.zeros((tokens, 1), jnp.float32)
+    for n in range(pair.count):
+        cols = slice(n * cut, (n + 1) * cut)
+        pair.copy(n).wait()
+        grad = mine[:, cols] + theirs[:, cols]
+        mine[:, cols] = grad
+        resid = resid_ref[:, cols]
+        norm_grad_ref[:, cols] = jnp.sum(grad * resid * scale, axis=0, keepdims=True)
+        inner_sum = inner_sum + jnp.sum(resid * norm_ref[:, cols] * grad, axis=1, keepdims=True)
+    pull = scale * scale * scale * (inner_sum / model)
+    for n in range(pair.count):
+        cols = slice(n * cut, (n + 1) * cut)
+        grad = scale * norm_ref[:, cols] * mine[:, cols] - resid_ref[:, cols] * pull
+        grad = grad_out_ref[:, cols].astype(jnp.float32) + grad
+        grad_resid_ref[:, cols] = grad
+        grad_mix_ref[:, cols] = low(grad)
+    load.wait()
+    grad_mix = grad_mix_ref[...]
+    gate_scale = gate_scale_ref[:, 0:1]
+    wide = 384
+    dots = jnp.zeros((tokens, 1), jnp.float32)
+    for c in range(0, inner, wide):
+        cols = slice(c, c + wide)
+        grad = dot_nn(grad_mix, weights[:, cols])
+        z = z_ref[:, cols]
+        gated = y_ref[:, cols] * (z * jax.nn.sigmoid(z))
+        gain_grad_ref[:, cols] = jnp.sum(grad * gated * gate_scale, axis=0, keepdims=True)
+        weighted = grad * gain_ref[:, cols]
+        grad_y_ref[:, cols] = weighted
+        dots = dots + jnp.sum(weighted * gated, axis=1, keepdims=True)
+    stat[...] = jnp.broadcast_to(dots, stat.shape)
+    swap = pltpu.make_async_remote_copy(
+        src_ref=stat,
+        dst_ref=stat_theirs,
+        send_sem=stat_sems.at[0],
+        recv_sem=stat_sems.at[1],
+        device_id={"head": 1 - lax.axis_index("head")},
+    )
+    swap.start()
+    swap.wait()
+    dots = (stat[...] + stat_theirs[...])[:, 0:1]
+    pull = gate_scale * gate_scale * gate_scale * (dots / (2 * inner))
+    for c in range(0, inner, wide):
+        cols = slice(c, c + wide)
+        z, y = z_ref[:, cols], y_ref[:, cols]
+        act, slope = silu_parts(z)
+        grad = gate_scale * grad_y_ref[:, cols] - y * act * pull
+        grad_y_ref[:, cols] = grad * act
+        grad_z_ref[:, cols] = low(grad * y * slope)
+
+
+def gate_back(home, position, back, resid, scale, norm, grad_out, weights, z, y, gate_scale, gain, collective):
+    tokens, model = resid.shape
+    inner = z.shape[1]
+    f32, bf16 = jnp.float32, jnp.bfloat16
+    vmem, hbm = pl.BlockSpec(memory_space=pltpu.VMEM), pl.BlockSpec(memory_space=pl.ANY)
+    out = [
+        ((tokens, model), f32),
+        ((tokens, model), bf16),
+        ((tokens, inner), f32),
+        ((tokens, inner), bf16),
+        ((1, model), f32),
+        ((1, inner), f32),
+    ]
+    return pl.pallas_call(
+        gate_back_kernel,
+        out_shape=[jax.ShapeDtypeStruct(*shape) for shape in out],
+        in_specs=[vmem] * 7 + [hbm] + [vmem] * 4,
+        out_specs=[vmem] * len(out),
+        scratch_shapes=[
+            pltpu.VMEM((model, inner), bf16),
+            pltpu.VMEM((tokens, model), f32),
+            pltpu.VMEM((tokens, model), f32),
+            pltpu.VMEM((tokens, 128), f32),
+            pltpu.VMEM((tokens, 128), f32),
+            pltpu.SemaphoreType.DMA,
+            pltpu.SemaphoreType.DMA((2, model // 256)),
+            pltpu.SemaphoreType.DMA((2,)),
+        ],
+        compiler_params=params(collective, vmem_limit_bytes=48 * MIB),
+        name="gate_back",
+    )(home, position, back, resid, scale, norm, grad_out, weights, z, y, gate_scale, gain)
 
 
 def pair_kernel(x_ref, out_ref, theirs, send, recv):
@@ -819,74 +1702,6 @@
         compiler_params=pltpu.CompilerParams(vmem_limit_bytes=40 * MIB),
         name="combine_mix" if weigh else "combine_grads",
     )(position, weight, home)
-
-
-HIGHEST = lax.Precision.HIGHEST
-EPSILON = 1e-05
-
-
-def shifted(value, axis, steps):
-    count = lax.axis_size(axis)
-    leading, last = (max(0, -steps), min(count, count - steps))
-    return lax.ppermute(value, axis, [(source, source + steps) for source in range(leading, last)])
-
-
-def product(left_side, right_side):
-    return jnp.dot(left_side, right_side, preferred_element_type=jnp.float32)
-
-
-def product_nt(left_side, right_side):
-    return lax.dot_general(
-        left_side, right_side, (((1,), (1,)), ((), ())), preferred_element_type=jnp.float32
-    )
-
-
-def product_tn(left_side, right_side):
-    return lax.dot_general(
-        left_side, right_side, (((0,), (0,)), ((), ())), preferred_element_type=jnp.float32
-    )
-
-
-def silu(operand):
-    return operand * jax.nn.sigmoid(operand)
-
-
-def silu_slope(operand):
-    sig_part = jax.nn.sigmoid(operand)
-    return sig_part * (1.0 + operand * (1.0 - sig_part))
-
-
-def rms_scale(operand):
-    return lax.rsqrt(jnp.mean(operand * operand, axis=-1, keepdims=True) + EPSILON)
-
-
-def norm_back(operand, row_scale, gain_vec, grad_rows):
-    gain_grad = jnp.sum(grad_rows * operand * row_scale, axis=0)
-    inner_mean = jnp.mean(operand * gain_vec * grad_rows, axis=-1, keepdims=True)
-    return (gain_grad, row_scale * gain_vec * grad_rows - operand * row_scale**3 * inner_mean)
-
-
-def group_state(heads_x, state_in, step_size, decay_rate):
-    cum_decay = jnp.cumsum(-step_size * decay_rate[None, :], axis=0)
-    tail_decay = cum_decay[-1]
-    tok_weight = jnp.exp(tail_decay[None, :] - cum_decay) * step_size
-    state_new = jnp.einsum("th,thp,tn->hpn", tok_weight, heads_x, state_in, precision=HIGHEST)
-    return (jnp.exp(tail_decay), state_new)
-
-
-def group_out(heads_x, state_in, state_read, step_size, decay_rate, state_start, skip_gain):
-    length_rows = heads_x.shape[0]
-    cum_decay = jnp.cumsum(-step_size * decay_rate[None, :], axis=0)
-    causal = (jnp.arange(length_rows)[:, None] >= jnp.arange(length_rows)[None, :])[:, :, None]
-    gap_decay = cum_decay[:, None, :] - cum_decay[None, :, :]
-    decay_mat = jnp.where(causal, jnp.exp(jnp.where(causal, gap_decay, 0.0)), 0.0)
-    scores = jnp.dot(state_read, state_in.T, precision=HIGHEST)
-    mixing = decay_mat * scores[:, :, None] * step_size[None, :, :]
-    within_part = jnp.einsum("tsh,shp->thp", mixing, heads_x, precision=HIGHEST)
-    carried_part = jnp.exp(cum_decay)[:, :, None] * jnp.einsum(
-        "tn,hpn->thp", state_read, state_start, precision=HIGHEST
-    )
-    return within_part + carried_part + skip_gain[None, :, None] * heads_x
 
 
 def per_device(
@@ -911,201 +1726,134 @@
     route_weights,
     grad_out,
 ):
-    tokens = layer_in.shape[0]
-    model_width = layer_in.shape[1]
+    tokens, model_width = layer_in.shape
     inner_dev = mixer_in.shape[2]
-    inner_all = inner_dev * lax.axis_size("head")
     state_size = state_proj.shape[1] // 2
     heads_dev = step_proj.shape[1]
-    head_size = inner_dev // heads_dev
     conv_taps = conv_main.shape[0]
     shared_dev = shared_down.shape[1]
     local_experts = expert_gate_up.shape[0]
-    seq_devices = lax.axis_size("seq")
-    experts_all = local_experts * seq_devices
+    experts_all = local_experts * lax.axis_size("seq")
     choices_per = routes.shape[1]
     capacity = max(2, tokens * choices_per * 4 // (3 * experts_all))
-    slot_count = local_experts * seq_devices * capacity
-    gathered = gather_rows(
+    slots_dev = capacity // lax.axis_size("head")
+    lanes = 128
+    pad_heads = lambda v: jnp.pad(v, ((0, 0), (0, lanes - heads_dev)))
+    gathered, edge = gather_rows(
         jnp.concatenate(
-            [
-                mixer_in.reshape(-1, 2 * inner_dev),
-                state_proj,
-                jnp.pad(step_proj, ((0, 0), (0, 128 - heads_dev))),
-            ],
-            axis=1,
+            [mixer_in.reshape(-1, 2 * inner_dev), state_proj, pad_heads(step_proj)], axis=1
         ),
+        layer_in[tokens - 16 :],
         0,
-    ).reshape(model_width, -1)
-    full_in = gathered[:, : 2 * inner_dev]
-    full_state = gathered[:, 2 * inner_dev : 2 * inner_dev + 2 * state_size]
-    full_step = gathered[:, 2 * inner_dev + 2 * state_size :][:, :heads_dev]
+    )
     late_rows = jnp.concatenate(
         [mixer_out, shared_gate_up.reshape(-1, 2 * shared_dev), shared_down], axis=1
     )
-    full_in, late_rows, grad_out_late = lax.optimization_barrier((full_in, late_rows, grad_out))
-    gathered = lax.all_gather(late_rows, "seq", axis=0, tiled=True)
-    full_out = gathered[:, :inner_dev]
-    shared_flat = gathered[:, inner_dev : inner_dev + 2 * shared_dev]
-    full_down = gathered[:, inner_dev + 2 * shared_dev :]
-    slots_dev = capacity // lax.axis_size("head")
+    weights_in, late_rows, grad_out_late = lax.optimization_barrier(
+        (gathered.reshape(model_width, -1), late_rows, grad_out)
+    )
     position, slot_weight = routing(routes, route_weights, experts_all)
     grads_out = send_rows(position, slot_weight, grad_out_late, slots_dev, True)
     grads_in = lax.all_to_all(grads_out, "seq", split_axis=0, concat_axis=0, tiled=True)
-    resid_in = layer_in.astype(jnp.float32)
-    scale_first = rms_scale(resid_in)
-    normed = (resid_in * scale_first * norm_first).astype(jnp.bfloat16)
-    zx_both = product(normed, full_in)
-    gate_z = zx_both[:, :inner_dev]
-    pre_x = zx_both[:, inner_dev:]
-    pre_bc = product(normed, full_state)
-    step_raw = product(normed, full_step) + step_bias
-    conv_input = jnp.concatenate([pre_x, pre_bc], axis=1)
-    edge_rows = shifted(conv_input[tokens - (conv_taps - 1) :], "seq", 1)
-    padded = jnp.concatenate([edge_rows, conv_input], axis=0)
-    kernel = jnp.concatenate([conv_main, conv_state], axis=1)
-    conv_sum = kernel[0] * padded[0:tokens]
-    for tap_index in range(1, conv_taps):
-        conv_sum = conv_sum + kernel[tap_index] * padded[tap_index : tap_index + tokens]
-    active = silu(conv_sum)
-    heads_x = active[:, :inner_dev].reshape(tokens, heads_dev, head_size)
-    state_in = active[:, inner_dev : inner_dev + state_size]
-    state_read = active[:, inner_dev + state_size :]
-    step_size = jax.nn.softplus(step_raw)
-    decay_total, state_local = group_state(heads_x, state_in, step_size, decay_rate)
-    state_start = carried(decay_total, state_local, 2)
-    ssd = group_out(
-        heads_x, state_in, state_read, step_size, decay_rate, state_start, skip_gain
-    ).reshape(tokens, inner_dev)
-    gate_act = silu(gate_z)
-    gated_ssd = ssd * gate_act
-    gate_scale = lax.rsqrt(pair_total(jnp.sum(gated_ssd * gated_ssd, axis=1).reshape(-1, 128), 4).reshape(-1) / inner_all + EPSILON)[
-        :, None
-    ]
-    normed_gate = (gated_ssd * gate_scale * gate_gain).astype(jnp.bfloat16)
-    mixer_sum = pair_total(product_nt(normed_gate, full_out), 6)
-    residual = resid_in + mixer_sum
-    scale_second = rms_scale(residual)
-    normed_second = (residual * scale_second * norm_second).astype(jnp.bfloat16)
-    shared_both = product(normed_second, shared_flat)
-    shared_gate = shared_both[:, :shared_dev]
-    shared_up = shared_both[:, shared_dev:]
-    shared_hid = (silu(shared_gate) * shared_up).astype(jnp.bfloat16)
-    shared_part = product_nt(shared_hid, full_down)
-    rows_out = send_rows(position, slot_weight, normed_second, slots_dev, False)
+    numbers = jnp.pad(
+        jnp.stack([decay_rate, skip_gain, step_bias]), ((0, 5), (0, lanes - heads_dev))
+    )
+    taps = jnp.pad(jnp.concatenate([conv_main, conv_state], axis=1), ((0, 8 - conv_taps), (0, 0)))
+    (
+        normed,
+        gate_z,
+        heads_x,
+        state_both,
+        conv_sum,
+        pre,
+        step_raw,
+        state_start,
+        ssd,
+        normed_gate,
+        gate_scale,
+        gathered,
+    ) = mixer(
+        layer_in, edge, norm_first[None], weights_in, numbers, taps, gate_gain[None], late_rows, 1
+    )
+    weights_late = gathered.reshape(model_width, -1)
+    residual, normed_second, scale_second, rows_out, shared_part, shared_back, shared_right = (
+        residual_block(
+            normed_gate,
+            weights_late,
+            layer_in,
+            norm_second[None],
+            grad_out,
+            position,
+            slots_dev,
+            2,
+        )
+    )
     grad_home, res_sums, expert_gate_up_grad, expert_down_grad = experts(
         rows_out,
         grads_in,
         expert_gate_up.reshape(model_width, -1),
         expert_down.reshape(-1, model_width),
-        11,
-    )
-    grad_float = grad_out.astype(jnp.float32)
+        3,
+    )
     home_rows = lax.all_to_all(res_sums, "seq", split_axis=0, concat_axis=0, tiled=True)
-    expert_grad_rows = combine(position, slot_weight, grad_home, False)
-    grad_shared_hid = product(grad_out, full_down)
-    grad_shared_gate = grad_shared_hid * shared_up * silu_slope(shared_gate)
-    grad_shared_up = grad_shared_hid * silu(shared_gate)
-    grad_shared_both = jnp.concatenate([grad_shared_gate, grad_shared_up], axis=1).astype(
-        jnp.bfloat16
-    )
-    grad_normed_second = pair_total(product_nt(grad_shared_both, shared_flat) + expert_grad_rows, 8)
-    norm_second_grad, grad_resid_norm = norm_back(
-        residual, scale_second, norm_second, grad_normed_second
-    )
-    grad_resid = grad_float + grad_resid_norm
-    grad_mix = grad_resid.astype(jnp.bfloat16)
-    grad_normed_gate = product(grad_mix, full_out)
-    weighted = grad_normed_gate * gate_gain
-    inner_dot = pair_total(jnp.sum(weighted * gated_ssd, axis=1).reshape(-1, 128), 5).reshape(-1)[:, None]
-    grad_gated = gate_scale * weighted - gated_ssd * gate_scale**3 * inner_dot / inner_all
-    gate_gain_grad = jnp.sum(grad_normed_gate * gated_ssd * gate_scale, axis=0)
-    grad_ssd = grad_gated * gate_act
-    grad_gate_z = grad_gated * ssd * silu_slope(gate_z)
-    _, pull_out = jax.vjp(
-        group_out, heads_x, state_in, state_read, step_size, decay_rate, state_start, skip_gain
-    )
-    (
-        grad_x_first,
-        grad_in_first,
-        grad_read,
-        grad_step_first,
-        grad_rate_first,
-        grad_start,
-        skip_gain_grad,
-    ) = pull_out(grad_ssd.reshape(tokens, heads_dev, head_size))
+    grad_resid, grad_mix, grad_ssd, grad_gate_z, norm_second_grad, gate_gain_grad = gate_back(
+        grad_home,
+        position,
+        shared_back,
+        residual,
+        scale_second,
+        norm_second[None],
+        grad_out,
+        weights_late,
+        gate_z,
+        ssd,
+        gate_scale,
+        gate_gain[None],
+        4,
+    )
     late_plan = (
         ((0, 0, 1024),),
         ((0, 1024, 512), (1, 1536, 512)),
         ((1, 2048, 512), (2, 2560, 512)),
     )
-    summed_late, grad_next, _ = scatter_rows(
+    summed_late, right_grads, taps_grad, heads_grad = mixer_back(
         [grad_mix, normed_second, grad_out],
-        jnp.concatenate([normed_gate, grad_shared_both, shared_hid], axis=1),
+        jnp.concatenate([normed_gate, shared_right], axis=1),
         late_plan,
-        3,
-        scanned=scan_message(decay_total, grad_start),
-    )
-    grad_next = grad_next.transpose(1, 0, 2)
-    grad_decay = jnp.sum(grad_next * state_start, axis=(1, 2))
-    _, pull_state = jax.vjp(group_state, heads_x, state_in, step_size, decay_rate)
-    grad_x_second, grad_in_second, grad_step_second, grad_rate_second = pull_state(
-        (grad_decay, grad_next)
-    )
-    decay_rate_grad = grad_rate_first + grad_rate_second
-    grad_bc = pair_total(
-        jnp.concatenate([grad_in_first + grad_in_second, grad_read], axis=1), 10
-    )
-    grad_active = jnp.concatenate(
-        [(grad_x_first + grad_x_second).reshape(tokens, inner_dev), grad_bc], axis=1
-    )
-    grad_conv = grad_active * silu_slope(conv_sum)
-    grad_padded = jnp.pad(kernel[0] * grad_conv, ((0, conv_taps - 1), (0, 0)))
-    for tap_index in range(1, conv_taps):
-        grad_padded = grad_padded + jnp.pad(
-            kernel[tap_index] * grad_conv, ((tap_index, conv_taps - 1 - tap_index), (0, 0))
-        )
-    kernel_grad = jnp.stack(
-        [
-            jnp.sum(grad_conv * padded[tap_index : tap_index + tokens], axis=0)
-            for tap_index in range(conv_taps)
-        ]
-    )
-    spill_rows = shifted(grad_padded[: conv_taps - 1], "seq", -1)
-    grad_pre = grad_padded[conv_taps - 1 :]
-    grad_pre = jnp.concatenate(
-        [grad_pre[: tokens - (conv_taps - 1)], grad_pre[tokens - (conv_taps - 1) :] + spill_rows],
-        axis=0,
-    )
-    grad_step_raw = (grad_step_first + grad_step_second) * jax.nn.sigmoid(step_raw)
-    step_bias_grad = jnp.sum(grad_step_raw, axis=0)
-    grad_zx = jnp.concatenate([grad_gate_z, grad_pre[:, :inner_dev]], axis=1).astype(jnp.bfloat16)
-    grad_bc_low = grad_pre[:, inner_dev:].astype(jnp.bfloat16)
-    grad_step_low = grad_step_raw.astype(jnp.bfloat16)
-    in_partial = product_nt(grad_zx, full_in) + product_nt(
-        grad_step_low, full_step
-    )
-    grad_normed = pair_total(in_partial, 9) + product_nt(grad_bc_low, full_state)
-    norm_first_grad, grad_in_norm = norm_back(resid_in, scale_first, norm_first, grad_normed)
-    input_grad = grad_resid + grad_in_norm
+        grad_ssd,
+        ssd,
+        heads_x,
+        state_both,
+        conv_sum,
+        pre,
+        grad_gate_z,
+        step_raw,
+        numbers,
+        taps,
+        state_start.reshape(inner_dev, state_size),
+        5,
+    )
+    home_rows, right_grads = lax.optimization_barrier((home_rows, right_grads))
     small = (
-        norm_first_grad,
+        jnp.zeros_like(norm_first),
         norm_second_grad,
-        step_bias_grad,
-        kernel_grad[:, :inner_dev],
-        kernel_grad[:, inner_dev:],
-        decay_rate_grad,
-        skip_gain_grad,
+        heads_grad[2, :heads_dev],
+        taps_grad[:conv_taps, :inner_dev],
+        taps_grad[:conv_taps, inner_dev:],
+        heads_grad[1, :heads_dev],
+        heads_grad[0, :heads_dev],
         gate_gain_grad,
     )
-    summed, _, small_sums = scatter_rows(
-        [normed],
-        jnp.concatenate(
-            [grad_zx, grad_bc_low, jnp.pad(grad_step_low, ((0, 0), (0, 128 - heads_dev)))], axis=1
-        ),
+    summed, input_grad, small_sums = input_back(
+        normed,
+        right_grads,
         tuple(((0, start, 1152),) for start in (0, 1152, 2304)),
-        15,
-        small=small_message(small),
+        weights_in,
+        layer_in,
+        norm_first[None],
+        grad_resid,
+        small_message(small),
+        6,
     )
     small_sums = small_parts(small, small_sums)
     expert_mix = combine(position, slot_weight, home_rows, True)
@@ -1132,9 +1880,9 @@
         small_sums[4],
         small_sums[5],
         small_sums[6],
-        small_sums[7],
+        small_sums[7].reshape(-1),
         weight_sums[3],
-        small_sums[1],
+        small_sums[1].reshape(-1),
         weight_sums[4],
         weight_sums[5],
         expert_gate_up_grad,

time: 694 us -> 561 us (0.81); the launches traced: 681 us -> 558 us
  matrix products: 85.6 us -> 0 us
  Pallas kernels: 424 us -> 485 us
  other arithmetic: 55.4 us -> 9.53 us
  local copies, waits for them, and re-layouts: 64.1 us -> 40.7 us
  between operations: 16.1 us -> 1.17 us
  waiting for transfers between devices: 10.5 us -> 0.01 us
    pallas_call x4 -> x6, Pallas kernels: 246 us -> 345 us  [the longest x1 107 us: mixer(): pl.pallas_call(mixer_kernel, out_shape=[jax.ShapeDtypeStruct(*shape) for...]
    dot_general x24 -> x0, matrix products: 85.6 us -> none  [the longest x3 26 us: group_out(): within_part = jnp.einsum('tsh,shp->thp', mixing, heads_x, precision=HIGHEST)]
    pallas_call x7 -> x1, Pallas kernels: 50.4 us -> 15.1 us  [pair_total(): pl.pallas_call(pair_kernel, out_shape=jax.ShapeDtypeStruct(x.shape, x.dty...]
    reduce_sum x11 -> x0, other arithmetic: 21.4 us -> none  [the longest x2 5.62 us: group_out(): return within_part + carried_part + skip_gain[None, :, None] * heads_x]
    slice x9 -> x2, local copies, waits for them, and re-layouts: 13.1 us -> 2.23 us  [the longest x1 1.43 us: per_device(): layer_in[tokens - 16:]]
    all_to_all x1, waiting for transfers between devices: 9.37 us -> 0.01 us  [per_device(): lax.all_to_all(res_sums, 'seq', split_axis=0, concat_axis=0, tiled=True)]
    unnamed x241 -> x70, local copies, waits for them, and re-layouts: 22.8 us -> 20.9 us
  transfers between devices with their start and end apart: 5 -> 2, of which waited for: 2 -> 0; matrix products, arithmetic and copies ran while one was open for 12% -> 2% of each run, Pallas kernels for 12% -> 41%
where the time goes in v3:
time: 561 us; the launch traced here: 558 us
  Pallas kernels  485 us (86%)
  local copies, waits for them, and re-layouts  40.7 us (7%)
  starting transfers between devices  20.9 us (4%)
  other arithmetic  9.53 us (2%)
    pallas_call x1, Pallas kernels, experts(): pl.pallas_call(experts_kernel, out_shape=[jax.ShapeDtypeStruct(half, bf16...  118 us
    pallas_call x1, Pallas kernels, mixer(): pl.pallas_call(mixer_kernel, out_shape=[jax.ShapeDtypeStruct(*shape) for...  107 us
    pallas_call x1, Pallas kernels, mixer_back(): pl.pallas_call(functools.partial(mixer_back_kernel, plan), out_shape=[jax...  93 us
    pallas_call x1, Pallas kernels, input_back(): pl.pallas_call(functools.partial(input_back_kernel, plan), out_shape=[jax...  64.1 us
    pallas_call x1, Pallas kernels, gather_rows(): pl.pallas_call(gather_kernel, out_shape=[jax.ShapeDtypeStruct((4, 4, 4, r...  50.9 us
    unnamed x70, local copies, waits for them, and re-layouts  20.9 us
    pallas_call x1, Pallas kernels, residual_block(): pl.pallas_call(residual_kernel, out_shape=[jax.ShapeDtypeStruct(*shape) f...  15.7 us
    pallas_call x1, Pallas kernels, pair_total(): pl.pallas_call(pair_kernel, out_shape=jax.ShapeDtypeStruct(x.shape, x.dty...  15.1 us
  transfers between devices with their start and end apart: 2, of which 0 were waited for; matrix products, arithmetic and copies ran while one was open for 2% of the time, Pallas kernels for 41%

profile of v3, /device:TPU:1, one launch (start us, length us, event | category | flops | bytes accessed | tf_op | source)
XLA Modules:
  0.0 557.8 jit_solution(8594381204029363974)
XLA Ops:
  1.7 1.4 slice.60.edge_ref
  3.9 1.4 fusion.1.x_ref
  5.3 50.9 %gather_rows.1 = (bf16[4,4,4,24,3456]{4,3,2,1,0:T(8,128)(2,1)}, bf16[16,1536]{1,0:T(8,128)(2,1)}) custom-call(bf16[24,3456]{1,0:T(8,128)(2,1)} %fusion.1.x_ref, bf16[16,1536]{1,0:T(8,128)(2,1)} %slice.60.edge_ref), custom_call_target="tpu_custom_call" | custom-call | tf_op jit(solution)/shard_map/gather_rows/pallas_call | solution.py:1038
  56.2 1.6 pad_maximum_fusion.1.late_ref
  57.8 1.5 routing.1
  61.0 1.6 send_grads.1
  62.7 1.7 copy-done.1
  64.3 10.2 %all-to-all-start = ((bf16[64,16,1536]{2,1,0:T(8,128)(2,1)}), bf16[64,16,1536]{2,1,0:T(8,128)(2,1)}, u32[]{:S(2)}, u32[]{:S(2)}) async-start(bf16[64,16,1536]{2,1,0:T(8,128)(2,1)} %copy-done.1), calls=%async_computation | async-start | bytes 6291456 | tf_op jit(solution)/shard_map/all_to_all | solution.py:1757
  75.9 1.5 copy.41
  78.6 106.8 %mixer.1 = (bf16[256,1536]{1,0:T(8,128)(2,1)}, f32[256,1536]{1,0:T(8,128)}, f32[256,1536]{1,0:T(8,128)}, f32[256,256]{1,0:T(8,128)}, f32[256,1792]{1,0:T(8,128)}...) custom-call(bf16[256,1536]{1,0:T(8,128)(2,1)} %resid_ref.1, ...), custom_call_target="tpu_custom_call" | custom-call | tf_op jit(solution)/shard_map/mixer/pallas_call | solution.py:1259
  186.6 15.7 %residual_block.1 = (f32[256,1536]{1,0:T(8,128)S(1)}, bf16[256,1536]{1,0:T(8,128)(2,1)S(1)}, f32[256,128]{1,0:T(8,128)S(1)}, bf16[64,16,1536]{2,1,0:T(8,128)(2,1...) custom-call(bf16[256,1536]{1,0:T(8,128)(2,1)S(1)} %copy-done.5, ...), custom_call_target="tpu_custom_call" | custom-call | tf_op jit(solution)/shard_map/residual_block/pallas_call | solution.py:1397
  204.4 117.5 %experts.1 = (bf16[64,16,1536]{2,1,0:T(8,128)(2,1)}, bf16[64,16,1536]{2,1,0:T(8,128)(2,1)}, f32[6144,128]{1,0:T(8,128)}, f32[256,1536]{1,0:T(8,128)}) custom-call(bf16[64,16,1536]{2,1,0:T(8,128)(2,1)} %get-tuple-element.73.rows_ref, bf16[64,16,1536]{2,1,0:T(8,128)(2,1)} %all-to-all-done.grads_ref, bf16[1536,512]{1,0:T(8,128)(2,1)} %bitcast.38, ...), custom_call_target="tpu_custom_call" | custom-call | tf_op jit(solution)/shard_map/experts/pallas_call | solution.py:277
  321.9 10.6 %all-to-all-start.1 = ((bf16[64,16,1536]{2,1,0:T(8,128)(2,1)}), bf16[64,16,1536]{2,1,0:T(8,128)(2,1)}, u32[]{:S(2)}, u32[]{:S(2)}) async-start(bf16[64,16,1536]{2,1,0:T(8,128)(2,1)} %get-tuple-element.75), calls=%async_computation.1 | async-start | bytes 6291456 | tf_op jit(solution)/shard_map/all_to_all | solution.py:1798
  332.6 1.4 pad_maximum_fusion.right
  334.0 14.6 %gate_back.1 = (f32[256,1536]{1,0:T(8,128)S(1)}, bf16[256,1536]{1,0:T(8,128)(2,1)S(1)}, f32[256,1536]{1,0:T(8,128)S(1)}, bf16[256,1536]{1,0:T(8,128)(2,1)S(1)}, ...) custom-call(bf16[64,16,1536]{2,1,0:T(8,128)(2,1)} %get-tuple-element.76.home_ref, f32[64,256]{1,0:T(8,128)S(1)} %copy-done.10, ...), custom_call_target="tpu_custom_call" | custom-call | tf_op jit(solution)/shard_map/gate_back/pallas_call | solution.py:1527
  352.6 93.0 %mixer_back.1 = (f32[24,3072]{1,0:T(8,128)}, bf16[256,3456]{1,0:T(8,128)(2,1)}, f32[8,1792]{1,0:T(8,128)}, f32[8,128]{1,0:T(8,128)}) custom-call(bf16[256,1536]{1,0:T(8,128)(2,1)} %copy-done.12, bf16[256,1536]{1,0:T(8,128)(2,1)} %copy-done.11, bf16[256,1536]{1,0:T(8,128)(2,1)} %lefts_2_.1, bf16[256,3072]{1,0:T(8,128)(2,1)} %pad_maximum_fusion.right, ...), custom_call_target="tpu_custom_call" | custom-call | tf_op jit(solution)/shard_map/mixer_back/pallas_call | solution.py:799
  446.5 1.6 slice.76
  448.1 1.4 slice.79
  453.5 64.1 %input_back.1 = (f32[24,3456]{1,0:T(8,128)}, f32[256,1536]{1,0:T(8,128)}, f32[64,8,128]{2,1,0:T(8,128)}) custom-call(bf16[256,1536]{1,0:T(8,128)(2,1)} %get-tuple-element.95.left, bf16[256,3456]{1,0:T(8,128)(2,1)} %get-tuple-element.96.right, bf16[1536,3456]{1,0:T(8,128)(2,1)} %bitcast.35, bf16[256,1536]{1,0:T(8,128)(2,1)} %resid_ref.1, ...), custom_call_target="tpu_custom_call" | custom-call | tf_op jit(solution)/shard_map/input_back/pallas_call | solution.py:928
  518.4 1.4 fusion.2
  527.8 4.6 combine_mix.1
  533.8 15.1 %pair_total.1 = f32[256,1536]{1,0:T(8,128)} custom-call(f32[256,1536]{1,0:T(8,128)} %add.14.x_ref), custom_call_target="tpu_custom_call" | custom-call | tf_op jit(solution)/shard_map/pair_total/pallas_call | solution.py:1568
  548.9 2.6 add_convert_fusion
  553.9 1.7 copy.47
  (94 shorter events, 32.6 us)
Async XLA Ops:
  0.7 58.7 %copy-start = (bf16[256,1536]{1,0:T(8,128)(2,1)S(1)}, bf16[256,1536]{1,0:T(8,128)(2,1)}, u32[]{:S(2)}) copy-start(bf16[256,1536]{1,0:T(8,128)(2,1)} %lefts_2_.1) | copy-start | bytes 2359300
  62.7 1.7 copy-start.1
  64.3 10.2 %copy-start.24 = (f32[1536]{0:T(1024)S(1)}, f32[1536]{0:T(1024)}, u32[]{:S(2)}) copy-start(f32[1536]{0:T(1024)} %param.21) | copy-start | bytes 18436
  64.3 10.9 %copy-start.25 = (f32[1536]{0:T(1024)S(1)}, f32[1536]{0:T(1024)}, u32[]{:S(2)}) copy-start(f32[1536]{0:T(1024)} %param.30) | copy-start | bytes 18436
  64.3 11.5 %copy-start.26 = (f32[1536]{0:T(1024)S(1)}, f32[1536]{0:T(1024)}, u32[]{:S(2)}) copy-start(f32[1536]{0:T(1024)} %param.32) | copy-start | bytes 18436
  64.3 11.5 %copy-start.19 = (bf16[1,1536,2,256]{3,2,1,0:T(2,128)(2,1)S(1)}, bf16[1,1536,2,256]{3,2,1,0:T(2,128)(2,1)}, u32[]{:S(2)}) copy-start(bf16[1,1536,2,256]{3,2,1,0:T(2,128)(2,1)} %param.35) | copy-start | bytes 4718596
  64.3 140.0 %all-to-all-start = ((bf16[64,16,1536]{2,1,0:T(8,128)(2,1)}), bf16[64,16,1536]{2,1,0:T(8,128)(2,1)}, u32[]{:S(2)}, u32[]{:S(2)}) async-start(bf16[64,16,1536]{2,1,0:T(8,128)(2,1)} %copy-done.1), calls=%async_computation | async-start | bytes 6291456 | tf_op jit(solution)/shard_map/all_to_all | solution.py:1757
  75.8 1.6 copy-start.28
  75.8 1.6 copy-start.29
  75.8 1.6 copy-start.30
  75.8 2.2 copy-start.23
  75.8 2.2 copy-start.27
  78.6 106.8 %copy-start.2 = (bf16[256,1536]{1,0:T(8,128)(2,1)S(1)}, bf16[256,1536]{1,0:T(8,128)(2,1)}, u32[]{:S(2)}) copy-start(bf16[256,1536]{1,0:T(8,128)(2,1)} %resid_ref.1) | copy-start | bytes 2359300
  78.6 106.9 %copy-start.10 = (f32[64,256]{1,0:T(8,128)S(1)}, f32[64,256]{1,0:T(8,128)}, u32[]{:S(2)}) copy-start(f32[64,256]{1,0:T(8,128)} %get-tuple-element.69.position_ref) | copy-start | bytes 196612
  321.9 10.7 %copy-start.6 = (bf16[256,1536]{1,0:T(8,128)(2,1)S(1)}, bf16[256,1536]{1,0:T(8,128)(2,1)}, u32[]{:S(2)}) copy-start(bf16[256,1536]{1,0:T(8,128)(2,1)} %get-tuple-element.67.gated_ref) | copy-start | bytes 2359300
  321.9 131.5 %all-to-all-start.1 = ((bf16[64,16,1536]{2,1,0:T(8,128)(2,1)}), bf16[64,16,1536]{2,1,0:T(8,128)(2,1)}, u32[]{:S(2)}, u32[]{:S(2)}) async-start(bf16[64,16,1536]{2,1,0:T(8,128)(2,1)} %get-tuple-element.75), calls=%async_computation.1 | async-start | bytes 6291456 | tf_op jit(solution)/shard_map/all_to_all | solution.py:1798
  332.6 1.4 copy-start.16
  332.6 1.4 copy-start.17
  453.5 74.3 %copy-start.15 = (f32[64,256]{1,0:T(8,128)S(1)}, f32[64,256]{1,0:T(8,128)}, u32[]{:S(2)}) copy-start(f32[64,256]{1,0:T(8,128)} %get-tuple-element.72.weight_ref) | copy-start | bytes 196612
  527.8 4.6 copy-start.22
  533.8 15.1 %copy-start.4 = (f32[256,1536]{1,0:T(8,128)S(1)}, f32[256,1536]{1,0:T(8,128)}, u32[]{:S(2)}) copy-start(f32[256,1536]{1,0:T(8,128)} %copy-done.3) | copy-start | bytes 4718596
  548.9 2.6 copy-start.21
  551.5 2.5 copy-start.18
  553.9 2.5 copy-start.20
  (9 other events, 9.0 us)

commit v4 on v3

--- a/solution.py
+++ b/solution.py
@@ -24,22 +24,19 @@
     return [(c + by) % 4 if i == axis else c for i, c in enumerate(at)]
 
 
-def greet_neighbours(at, count=6):
-    barrier = pltpu.get_barrier_semaphore()
-    for axis in range(3):
-        for by in (1, 3):
-            pl.semaphore_signal(barrier, inc=1, device_id={"seq": seq_of(moved(at, axis, by))})
-    pl.semaphore_wait(barrier, count)
-
-
-def greet_all(me):
+def announce(me, with_sibling):
     barrier = pltpu.get_barrier_semaphore()
 
     @pl.loop(1, 64)
     def _(k):
-        pl.semaphore_signal(barrier, inc=1, device_id={"seq": (me + k) % 64})
-
-    pl.semaphore_wait(barrier, 63)
+        pl.semaphore_signal(barrier, inc=1, device_id={"seq": lax.rem(me + k, 64)})
+
+    if with_sibling:
+        pl.semaphore_signal(barrier, inc=1, device_id={"head": 1 - lax.axis_index("head")})
+
+
+def await_all(with_sibling):
+    pl.semaphore_wait(pltpu.get_barrier_semaphore(), 64 if with_sibling else 63)
 
 
 def parts_of(columns):
@@ -61,23 +58,31 @@
     return tuple(index) + (slice(None), cols)
 
 
-def torus_target(at, k):
-    return ((at[0] + k // 16) % 4) * 16 + ((at[1] + k // 4) % 4) * 4 + (at[2] + k) % 4
+class Ways:
+    def __init__(self, at):
+        self.at = at
+
+    def group(self, g, back=False):
+        x, z, y = self.at
+        sign, lead = (-1, 8) if back else (1, 0)
+        near, far = lax.rem(g, 4), g // 4
+        xs = [lax.rem(x + lead + sign * a, 4) * 16 for a in range(4)]
+        zs = [lax.rem(z + lead + sign * (near + a), 4) * 4 for a in range(4)]
+        ys = [lax.rem(y + lead + sign * (far + a), 4) for a in range(4)]
+        return [(g * 8 + n, xs[n % 4] + zs[n % 4] + ys[(n % 4 + n // 4 * 2) % 4]) for n in range(8)]
+
+    def each(self, first, last, body, back=False):
+        @pl.loop(first, last)
+        def _(g):
+            for n, (k, device) in enumerate(self.group(g, back)):
+                if n == 0:
+                    pl.when(k > 0)(functools.partial(body, k, device))
+                else:
+                    body(k, device)
 
 
 def params(collective, **more):
     return pltpu.CompilerParams(collective_id=collective, has_side_effects=True, **more)
-
-
-def greet_all_and_sibling(me):
-    barrier = pltpu.get_barrier_semaphore()
-
-    @pl.loop(1, 64)
-    def _(k):
-        pl.semaphore_signal(barrier, inc=1, device_id={"seq": (me + k) % 64})
-
-    pl.semaphore_signal(barrier, inc=1, device_id={"head": 1 - lax.axis_index("head")})
-    pl.semaphore_wait(barrier, 64)
 
 
 def greet_sibling():
@@ -109,31 +114,31 @@
     me, at = coordinates()
     head = lax.axis_index("head")
     sibling = {"head": 1 - head}
-    mine, place = me // 8, me % 8
     names = ("recv", "fwd_send", "fwd_recv", "kept", "given_send", "given_recv")
     names += ("x_send", "x_recv", "y_send", "y_recv")
     sem = {name: sems.at[n] for n, name in enumerate(names)}
-    greet_all_and_sibling(me)
+    announce(me, True)
+    wide_grad[...] = jnp.zeros_like(wide_grad)
+    down_grad_ref[...] = jnp.zeros_like(down_grad_ref)
+    ways = Ways(at)
+    await_all(True)
 
     def group(c):
         return pl.ds(pl.multiple_of(c * 8, 8), 8)
 
-    own = pltpu.make_async_copy(rows_ref.at[me], slot_in.at[me, head], sem["recv"].at[mine])
+    own = pltpu.make_async_copy(rows_ref.at[me], slot_in.at[0, head], sem["recv"].at[0])
     own.start()
 
-    @pl.loop(0, 64)
-    def _(k):
-        j = ((mine - k // 8) % 8) * 8 + (place + k) % 8
-
-        @pl.when(k > 0)
-        def _():
-            pltpu.make_async_remote_copy(
-                src_ref=rows_ref.at[j],
-                dst_ref=slot_in.at[me, head],
-                send_sem=send,
-                recv_sem=sem["recv"].at[mine],
-                device_id={"seq": j},
-            ).start()
+    def put(k, target):
+        pltpu.make_async_remote_copy(
+            src_ref=rows_ref.at[target],
+            dst_ref=slot_in.at[k, head],
+            send_sem=send,
+            recv_sem=sem["recv"].at[k // 8],
+            device_id={"seq": target},
+        ).start()
+
+    ways.each(0, 8, put)
 
     def given(c):
         return pltpu.make_async_remote_copy(
@@ -168,13 +173,10 @@
         )
 
     @pl.loop(0, 8)
-    def _(i):
-        c = (mine + i) % 8
+    def _(c):
         kept(c).start()
         given(c).start()
 
-    wide_grad[...] = jnp.zeros_like(wide_grad)
-    down_grad_ref[...] = jnp.zeros_like(down_grad_ref)
     hidden = down_ref.shape[0]
     width = down_ref.shape[1]
 
@@ -192,7 +194,7 @@
     def _(i):
         @pl.when(i < 8)
         def _():
-            c = (mine + i) % 8
+            c = i
             pltpu.make_async_copy(
                 rows_ref.at[group(c)], slot_in.at[group(c), head], sem["recv"].at[c]
             ).wait()
@@ -200,7 +202,7 @@
 
         @pl.when((i >= 1) & (i < 9))
         def _():
-            c = (mine + i + 7) % 8
+            c = i - 1
             forward(c).wait()
             kept(c).wait()
             given(c).wait()
@@ -225,29 +227,29 @@
 
         @pl.when(i >= 2)
         def _():
-            c = (mine + i + 6) % 8
+            c = i - 2
             swap(c, slot_in, theirs_x, "x").wait()
 
-            @pl.loop(0, 8)
-            def _(n):
-                j = c * 8 + (place + n) % 8
-                total = slot_in[j, head].astype(jnp.float32) + theirs_x[j].astype(jnp.float32)
-                sums[j] = total.astype(sums.dtype)
-
-                @pl.when(j != me)
-                def _():
-                    pltpu.make_async_remote_copy(
-                        src_ref=sums.at[j],
-                        dst_ref=home_ref.at[me],
-                        send_sem=home_send,
-                        recv_sem=home_recv,
-                        device_id={"seq": j},
-                    ).start()
-
-                @pl.when(j == me)
-                def _():
-                    pltpu.make_async_copy(sums.at[me], home_ref.at[me], home_recv).start()
-
+            def add(k):
+                total = slot_in[k, head].astype(jnp.float32) + theirs_x[k].astype(jnp.float32)
+                sums[k] = total.astype(sums.dtype)
+
+            def put_home(k, source):
+                add(k)
+                pltpu.make_async_remote_copy(
+                    src_ref=sums.at[k],
+                    dst_ref=home_ref.at[me],
+                    send_sem=home_send,
+                    recv_sem=home_recv,
+                    device_id={"seq": source},
+                ).start()
+
+            @pl.when(c == 0)
+            def _():
+                add(0)
+                pltpu.make_async_copy(sums.at[0], home_ref.at[me], home_recv).start()
+
+            ways.each(c, c + 1, put_home, back=True)
             swap(c, grad_slots, theirs_y, "y").wait()
 
             @pl.loop(0, 8)
@@ -310,9 +312,7 @@
         self.send, self.recv, self.back_send, self.back_recv = [sems.at[n] for n in range(4)]
 
     def spread(self, source, target_ref, send, recv):
-        @pl.loop(1, 64)
-        def _(k):
-            target = torus_target(self.at, k)
+        def put(_, target):
             pltpu.make_async_remote_copy(
                 src_ref=source.at[target],
                 dst_ref=target_ref.at[self.me],
@@ -320,6 +320,8 @@
                 recv_sem=recv,
                 device_id={"seq": target},
             ).start()
+
+        Ways(self.at).each(0, 8, put)
 
     def begin(self):
         self.got[self.me] = self.x_ref[self.me]
@@ -341,7 +343,7 @@
             decay = jnp.sum(jnp.where(chosen, row, 0.0), axis=1, keepdims=True)
             return decay * state + got[at_k, 0:heads, :]
 
-        lax.fori_loop(0, 64, step, jnp.zeros((heads, width), jnp.float32))
+        lax.fori_loop(0, 64, step, jnp.zeros((heads, width), jnp.float32), unroll=8)
         self.out_ref[self.me] = made[self.me]
         self.spread(made, self.out_ref, self.back_send, self.back_recv)
 
@@ -361,9 +363,7 @@
     def begin(self):
         self.got[self.me] = self.x_ref[self.me]
 
-        @pl.loop(1, 64)
-        def _(k):
-            target = torus_target(self.at, k)
+        def put(_, target):
             pltpu.make_async_remote_copy(
                 src_ref=self.x_ref.at[target],
                 dst_ref=self.got.at[self.me],
@@ -372,16 +372,16 @@
                 device_id={"seq": target},
             ).start()
 
+        Ways(self.at).each(0, 8, put)
+
     def middle(self):
         some = pl.ds(0, 63)
         x_ref, got, out_ref, me = self.x_ref, self.got, self.out_ref, self.me
         pltpu.make_async_copy(x_ref.at[some], x_ref.at[some], self.send).wait()
         pltpu.make_async_copy(got.at[some], got.at[some], self.recv).wait()
-        out_ref[me] = lax.fori_loop(1, 64, lambda k, total: total + got[k], got[0])
-
-        @pl.loop(1, 64)
-        def _(k):
-            target = torus_target(self.at, k)
+        out_ref[me] = lax.fori_loop(1, 64, lambda k, total: total + got[k], got[0], unroll=9)
+
+        def put(_, target):
             pltpu.make_async_remote_copy(
                 src_ref=out_ref.at[me],
                 dst_ref=out_ref.at[me],
@@ -389,6 +389,8 @@
                 recv_sem=self.back_recv,
                 device_id={"seq": target},
             ).start()
+
+        Ways(self.at).each(0, 8, put)
 
     def end(self):
         some = pl.ds(0, 63)
@@ -459,10 +461,18 @@
                 buf[index] = total.astype(jnp.bfloat16)
 
     def first(self, phase, p):
+        self.first_far(phase, p)
+        self.first_near(phase, p)
+
+    def first_far(self, phase, p):
         c = self.at[ORDERS[p][phase]]
         low, high = self.spans(p)
         self.send_to(phase, p, 1, (c + 2) % 4, low, 2, 0)
         self.send_to(phase, p, 3, (c + 2) % 4, high, 2, 1)
+
+    def first_near(self, phase, p):
+        c = self.at[ORDERS[p][phase]]
+        low, high = self.spans(p)
         self.send_to(phase, p, 1, (c + 1) % 4, high, 0, 2)
         self.send_to(phase, p, 3, (c + 3) % 4, low, 1, 3)
 
@@ -618,7 +628,7 @@
     each = width // 64
     mid = tokens // 2
     cut = 384
-    greet_all_and_sibling(me)
+    announce(me, True)
     sums = Scatter(at, plan, lefts, right, out_ref, buf, rest, send, recv)
     scan = Scan(True, at, me, message, back, got, made, scan_sems)
 
@@ -645,12 +655,14 @@
             cut // each, each, size
         )
     message[:, each : each + 8, :] = jnp.broadcast_to(jnp.exp(tail)[None], (64, 8, lanes))
+    await_all(True)
     scan.begin()
     for p in range(3):
         sums.product(p)
+        sums.first_far(2, p)
     scan.middle()
     for p in range(3):
-        sums.first(2, p)
+        sums.first_near(2, p)
 
     spread[...] = split_dot(step, spreader, 2)
     blocks = ((0, 0), (0, 1), (1, 1))
@@ -689,6 +701,8 @@
             rows = slice(s * mid, (s + 1) * mid)
             q[rows, here] = jnp.where(second_head[rows], results[1][s], results[0][s])
 
+    for p in range(3):
+        sums.second(2, p)
     scan.end()
 
     skip = split_dot(jnp.broadcast_to(numbers_ref[1:2, :], (8, lanes)), spreader, 2)[0:1, :]
@@ -729,8 +743,6 @@
         device_id={"head": 1 - head},
     )
     swap.start()
-    for p in range(3):
-        sums.second(2, p)
 
     ones = jnp.ones((8, size), jnp.bfloat16)
     state_grad = dot_split(ones, state_dot, 2, dot_nt)[0:1, :]
@@ -837,12 +849,20 @@
     gain_ref,
     grad_ref,
     small_ref,
+    res_ref,
+    position_ref,
+    weight_ref,
+    shared_ref,
+    block_ref,
     out_ref,
     input_ref,
     small_out,
+    layer_ref,
     weights,
     mine,
     theirs,
+    theirs_mix,
+    home,
     small,
     small_got,
     buf,
@@ -851,6 +871,8 @@
     recv,
     small_sems,
     sems,
+    home_sems,
+    mix_sems,
 ):
     me, at = coordinates()
     head = lax.axis_index("head")
@@ -858,11 +880,26 @@
     columns = right.shape[1]
     load = pltpu.make_async_copy(weights_ref, weights, sems.at[0])
     load.start()
-    greet_all_and_sibling(me)
+    announce(me, True)
     sums = Scatter(at, plan, [left], right, out_ref, buf, rest, send, recv)
     totals = Small(at, me, small, small_out, small_got, small_sems)
+    own = pltpu.make_async_copy(res_ref.at[0], home.at[me], home_sems.at[2])
+    own.start()
+
+    def put(k, source):
+        pltpu.make_async_remote_copy(
+            src_ref=res_ref.at[k],
+            dst_ref=home.at[me],
+            send_sem=home_sems.at[0],
+            recv_sem=home_sems.at[1],
+            device_id={"seq": source},
+        ).start()
+
+    ways = Ways(at)
     for p in range(3):
         sums.product(p)
+        if p == 0:
+            await_all(True)
         sums.first(2, p)
     load.wait()
 
@@ -886,6 +923,7 @@
         swaps.append(swap)
     for p in range(3):
         sums.second(2, p)
+    ways.each(0, 8, put, back=True)
     square = jnp.zeros((tokens, 1), jnp.float32)
     inner = jnp.zeros((tokens, 1), jnp.float32)
     for n, c in enumerate(range(0, model, cut)):
@@ -911,48 +949,81 @@
     totals.begin()
     sums.finish(2)
     totals.middle()
-    for phase in (1, 0):
-        for p in range(3):
-            sums.second(phase, p)
-        sums.finish(phase)
+    for p in range(3):
+        sums.second(1, p)
+
+    own.wait()
+    some = pl.ds(0, 63)
+    pltpu.make_async_copy(home.at[some], home.at[some], home_sems.at[1]).wait()
+    slots, step = home.shape[1], 16
+    mine[...] = shared_ref[...]
+
+    @pl.loop(0, home.shape[0] // step)
+    def _(i):
+        here = pl.ds(pl.multiple_of(i * step, step), step)
+        chosen = chosen_slots(position_ref[here, :], slots)
+        weighted = chosen.reshape(step, slots, -1) * weight_ref[here, :][:, None, :]
+        high, less = split(weighted.reshape(chosen.shape), 2)
+        rows = home[here].reshape(step * slots, model)
+        mine[...] += dot_tn(high, rows) + dot_tn(less, rows)
+
+    pair = PairSum(mine, theirs_mix, mix_sems, cut)
+    for n in range(pair.count):
+        pair.copy(n).start()
+    sums.finish(1)
+    for p in range(3):
+        sums.second(0, p)
+    for n in range(pair.count):
+        cols = slice(n * cut, (n + 1) * cut)
+        pair.copy(n).wait()
+        layer_ref[:, cols] = low(block_ref[:, cols] + (mine[:, cols] + theirs_mix[:, cols]))
+    sums.finish(0)
     totals.end()
     sums.end()
-
-
-def input_back(left, right, plan, weights, resid, gain, grad, small, collective):
+    pltpu.make_async_copy(home.at[some], home.at[some], home_sems.at[0]).wait()
+
+
+def input_back(
+    left, right, plan, weights, resid, gain, grad, small, res, position, weight, shared, block, collective
+):
     tokens, model = resid.shape
     columns = right.shape[1]
     rows = model // 64
     f32 = jnp.float32
-    vmem = pl.BlockSpec(memory_space=pltpu.VMEM)
+    vmem, hbm = pl.BlockSpec(memory_space=pltpu.VMEM), pl.BlockSpec(memory_space=pl.ANY)
     return pl.pallas_call(
         functools.partial(input_back_kernel, plan),
         out_shape=[
             jax.ShapeDtypeStruct((rows, columns), f32),
             jax.ShapeDtypeStruct((tokens, model), f32),
             jax.ShapeDtypeStruct(small.shape, f32),
+            jax.ShapeDtypeStruct((tokens, model), jnp.bfloat16),
         ],
-        in_specs=[vmem, vmem, pl.BlockSpec(memory_space=pl.ANY)] + [vmem] * 4,
-        out_specs=[vmem] * 3,
+        in_specs=[vmem, vmem, hbm] + [vmem] * 4 + [hbm] + [vmem] * 4,
+        out_specs=[vmem] * 4,
         scratch_shapes=[
             pltpu.VMEM(weights.shape, weights.dtype),
             pltpu.VMEM((tokens, model), f32),
             pltpu.VMEM((tokens, model), f32),
+            pltpu.VMEM((tokens, model), f32),
+            pltpu.VMEM(res.shape, res.dtype),
             pltpu.VMEM(small.shape, f32),
             pltpu.VMEM(small.shape, f32),
         ]
         + scatter_shapes(rows, columns)
-        + [pltpu.SemaphoreType.DMA((4,)), pltpu.SemaphoreType.DMA((1 + 2 * model // 256,))],
+        + [pltpu.SemaphoreType.DMA((4,)), pltpu.SemaphoreType.DMA((1 + 2 * model // 256,))]
+        + [pltpu.SemaphoreType.DMA((3,)), pltpu.SemaphoreType.DMA((2, model // 256))],
         compiler_params=params(collective, vmem_limit_bytes=62 * MIB),
         name="input_back",
-    )(left, right, weights, resid, gain, grad, small)
+    )(left, right, weights, resid, gain, grad, small, res, position, weight, shared, block)
 
 
 class Gather:
     def __init__(self, at, x_ref, out_ref, send, recv, local_sem):
         self.at, self.x_ref, self.out_ref, self.send, self.recv = at, x_ref, out_ref, send, recv
-        self.third, self.half = parts_of(x_ref.shape[1])
-        self.own = pltpu.make_async_copy(x_ref, out_ref.at[at[0], at[1], at[2]], local_sem)
+        self.third, self.half = parts_of(out_ref.shape[4])
+        if x_ref is not None:
+            self.own = pltpu.make_async_copy(x_ref, out_ref.at[at[0], at[1], at[2]], local_sem)
         self.copies = {}
 
     def put(self, source, here, phase, p, kind, by):
@@ -969,10 +1040,10 @@
     def first(self, phase):
         if phase == 1:
             self.own.wait()
-        if phase > 0:
+        if phase == 0:
+            self.own.start()
+        elif (phase - 1, 0, 2) in self.copies:
             self.arrived(phase - 1)
-        else:
-            self.own.start()
         for p, order in enumerate(ORDERS):
             cols = pl.ds(p * self.third, self.third)
             here = region(self.at, order, phase, self.at[order[phase]], cols)
@@ -1010,43 +1081,136 @@
     ]
 
 
-def gather_kernel(x_ref, edge_ref, out_ref, before_ref, send, recv, local_sem, edge_sems):
+def slot_tables(routes_ref, weights_ref, position_ref, weight_ref):
+    experts, tokens = position_ref.shape
+    expert = lax.broadcasted_iota(jnp.int32, (experts, tokens), 0)
+    named = jnp.zeros((experts, tokens), jnp.float32)
+    weight = jnp.zeros((experts, tokens), jnp.float32)
+    for k in range(routes_ref.shape[0]):
+        hit = expert == routes_ref[k : k + 1, :]
+        named = named + jnp.where(hit, 1.0, 0.0)
+        weight = weight + jnp.where(hit, weights_ref[k : k + 1, :], 0.0)
+    earlier = low(triangle(tokens, lambda t, s: jnp.where(t < s, 1.0, 0.0)))
+    position_ref[...] = jnp.where(named > 0.0, dot_nn(low(named), earlier), -1.0)
+    weight_ref[...] = weight
+
+
+def chosen_slots(position, slots):
+    count, tokens = position.shape
+    number = lax.broadcasted_iota(jnp.int32, (count, slots, tokens), 1)
+    number = (number + slots * lax.axis_index("head")).astype(jnp.float32)
+    return jnp.where(position[:, None, :] == number, 1.0, 0.0).reshape(count * slots, tokens)
+
+
+def gather_kernel(
+    x_ref,
+    late_ref,
+    layer_ref,
+    routes_ref,
+    weights_ref,
+    grads_ref,
+    out_ref,
+    late_out,
+    before_ref,
+    position_ref,
+    weight_ref,
+    slots_ref,
+    rows,
+    send,
+    recv,
+    local_sem,
+    late_send,
+    late_recv,
+    late_sem,
+    sems,
+):
     me, at = coordinates()
-    barrier = pltpu.get_barrier_semaphore()
-    pl.semaphore_signal(barrier, inc=1, device_id={"seq": (me + 63) % 64})
-    greet_neighbours(at, 7)
+    announce(me, False)
     gather = Gather(at, x_ref, out_ref, send, recv, local_sem)
+    late = Gather(at, late_ref, late_out, late_send, late_recv, late_sem)
+    await_all(False)
+    gather.first(0)
+    late.first(0)
     edge = pltpu.make_async_remote_copy(
-        src_ref=edge_ref,
+        src_ref=layer_ref.at[pl.ds(layer_ref.shape[0] - 16, 16)],
         dst_ref=before_ref,
-        send_sem=edge_sems.at[0],
-        recv_sem=edge_sems.at[1],
+        send_sem=sems.at[0],
+        recv_sem=sems.at[1],
         device_id={"seq": (me + 1) % 64},
     )
     edge.start()
-    for phase in range(3):
-        gather.first(phase)
-        gather.second(phase)
+    slot_tables(routes_ref, weights_ref, position_ref, weight_ref)
+    grads = grads_ref[...]
+    slots, step = rows.shape[1], 16
+
+    @pl.loop(0, rows.shape[0] // step)
+    def _(i):
+        here = pl.ds(pl.multiple_of(i * step, step), step)
+        chosen = chosen_slots(position_ref[here, :], slots)
+        weighted = chosen.reshape(step, slots, -1) * weight_ref[here, :][:, None, :]
+        scale = jnp.sum(weighted.reshape(chosen.shape), axis=1, keepdims=True)
+        rows[here] = low(dot_nn(low(chosen), grads) * scale).reshape(step, slots, -1)
+
+    own = pltpu.make_async_copy(rows.at[me], slots_ref.at[0], sems.at[2])
+    own.start()
+
+    def put(k, target):
+        pltpu.make_async_remote_copy(
+            src_ref=rows.at[target],
+            dst_ref=slots_ref.at[k],
+            send_sem=sems.at[3],
+            recv_sem=sems.at[4],
+            device_id={"seq": target},
+        ).start()
+
+    ways = Ways(at)
+    gather.second(0)
+    late.second(0)
+    ways.each(0, 1, put)
+    gather.first(1)
+    late.first(1)
+    ways.each(1, 2, put)
+    gather.second(1)
+    late.second(1)
+    ways.each(2, 3, put)
+    gather.first(2)
+    ways.each(3, 4, put)
+    gather.second(2)
+    ways.each(4, 8, put)
+    late.arrived(1)
+    late.end()
     gather.arrived(2)
     edge.wait()
     gather.end()
-
-
-def gather_rows(x, edge, collective):
+    own.wait()
+    some = pl.ds(0, 63)
+    pltpu.make_async_copy(rows.at[some], rows.at[some], sems.at[3]).wait()
+    pltpu.make_async_copy(rows.at[some], rows.at[some], sems.at[4]).wait()
+
+
+def gather_rows(x, late, layer_in, routes, route_weights, grads, experts, slots, collective):
     rows, columns = x.shape
-    hbm = pl.BlockSpec(memory_space=pl.ANY)
+    tokens, model = grads.shape
+    hbm, vmem = pl.BlockSpec(memory_space=pl.ANY), pl.BlockSpec(memory_space=pltpu.VMEM)
     return pl.pallas_call(
         gather_kernel,
         out_shape=[
             jax.ShapeDtypeStruct((4, 4, 4, rows, columns), x.dtype),
-            jax.ShapeDtypeStruct(edge.shape, edge.dtype),
+            jax.ShapeDtypeStruct((4, 4, 4) + late.shape, late.dtype),
+            jax.ShapeDtypeStruct((16, model), layer_in.dtype),
+            jax.ShapeDtypeStruct((experts, tokens), jnp.float32),
+            jax.ShapeDtypeStruct((experts, tokens), jnp.float32),
+            jax.ShapeDtypeStruct((experts, slots, model), grads.dtype),
         ],
-        in_specs=[hbm, hbm],
-        out_specs=[hbm, hbm],
-        scratch_shapes=gather_shapes() + [pltpu.SemaphoreType.DMA((2,))],
-        compiler_params=params(collective),
+        in_specs=[hbm, hbm, hbm, vmem, vmem, vmem],
+        out_specs=[hbm, hbm, hbm, vmem, vmem, hbm],
+        scratch_shapes=[pltpu.VMEM((experts, slots, model), grads.dtype)]
+        + gather_shapes()
+        + gather_shapes()
+        + [pltpu.SemaphoreType.DMA((5,))],
+        compiler_params=params(collective, vmem_limit_bytes=60 * MIB),
         name="gather_rows",
-    )(x, edge)
+    )(x, late, layer_in, routes.T, route_weights.T, grads)
 
 
 def mixer_kernel(
@@ -1057,7 +1221,7 @@
     numbers_ref,
     taps_ref,
     gain_ref,
-    late_ref,
+    _,
     normed_ref,
     z_ref,
     x_ref,
@@ -1085,7 +1249,6 @@
     pair_sems,
     send,
     recv,
-    local_sem,
 ):
     me, at = coordinates()
     head = lax.axis_index("head")
@@ -1103,9 +1266,8 @@
 
     for n in (8, 4, 5, 6, 7, 0, 1, 2, 3):
         load(n).start()
-    greet_all_and_sibling(me)
-    gather = Gather(at, late_ref, gathered_ref, send, recv, local_sem)
-    gather.first(0)
+    announce(me, True)
+    gather = Gather(at, None, gathered_ref, send, recv, None)
 
     def norm(rows):
         rows = rows.astype(jnp.float32)
@@ -1116,7 +1278,8 @@
     normed[0:16, :] = low(before)
     normed[16 : 16 + tokens, :] = norm(layer_ref[...])
     normed_ref[...] = normed[16 : 16 + tokens, :]
-    gather.second(0)
+    await_all(True)
+    gather.first(2)
 
     def conv(cols):
         total = jnp.zeros((tokens, cols.size), jnp.float32)
@@ -1140,7 +1303,6 @@
     spreader = head_spread(lanes, width, 64)
     spread[...] = split_dot(jnp.exp(tail - cum) * step, spreader, 2)
     held, read = bc_ref[:, :size], bc_ref[:, size:]
-    gather.first(1)
 
     @pl.loop(0, 4)
     def _(i):
@@ -1158,7 +1320,7 @@
     message[:, each : each + 8, :] = jnp.broadcast_to(jnp.exp(tail)[None], (64, 8, lanes))
     scan = Scan(False, at, me, message, start_ref, got, made, scan_sems)
     scan.begin()
-    gather.second(1)
+    gather.second(2)
 
     @pl.loop(0, 4)
     def _(i):
@@ -1167,7 +1329,6 @@
         z_ref[:, here] = dot_nn(normed[16 : 16 + tokens, :], weights[:, here])
 
     scan.middle()
-    gather.first(2)
 
     spread[...] = split_dot(step, spreader, 2)
     blocks = ((0, 0), (1, 0), (1, 1))
@@ -1223,7 +1384,6 @@
         device_id={"head": 1 - head},
     )
     swap.start()
-    gather.second(2)
     swap.wait()
     scale = lax.rsqrt((mine[...] + theirs[...]) / (2 * width) + EPSILON)
     scale_ref[...] = scale
@@ -1254,7 +1414,7 @@
         ((tokens, width), f32),
         ((tokens, width), bf16),
         ((tokens, lanes), f32),
-        ((4, 4, 4) + late.shape, bf16),
+        (late.shape, bf16),
     ]
     return pl.pallas_call(
         mixer_kernel,
@@ -1276,7 +1436,8 @@
             pltpu.SemaphoreType.DMA((4,)),
             pltpu.SemaphoreType.DMA((2,)),
         ]
-        + gather_shapes(),
+        + gather_shapes()[:2],
+        input_output_aliases={7: len(out) - 1},
         compiler_params=params(collective, vmem_limit_bytes=56 * MIB),
         name="mixer",
     )(layer_in, edge, norm, weights, numbers, taps, gain, late)
@@ -1362,7 +1523,7 @@
     @pl.loop(0, rows_ref.shape[0] // step)
     def _(i):
         here = pl.ds(pl.multiple_of(i * step, step), step)
-        chosen = chosen_slots(position_ref[here, :], 0, step, slots)
+        chosen = chosen_slots(position_ref[here, :], slots)
         rows_ref[here] = low(dot_nn(low(chosen), normed)).reshape(step, slots, model)
 
     loads[2].wait()
@@ -1453,7 +1614,7 @@
     @pl.loop(0, experts // step)
     def _(i):
         here = pl.ds(pl.multiple_of(i * step, step), step)
-        chosen = low(chosen_slots(position_ref[here, :], 0, step, slots))
+        chosen = low(chosen_slots(position_ref[here, :], slots))
         rows = home_ref[here].reshape(step * slots, model)
         mine[...] += dot_tn(chosen, rows)
 
@@ -1544,42 +1705,6 @@
     )(home, position, back, resid, scale, norm, grad_out, weights, z, y, gate_scale, gain)
 
 
-def pair_kernel(x_ref, out_ref, theirs, send, recv):
-    greet_sibling()
-    copy = pltpu.make_async_remote_copy(
-        src_ref=x_ref,
-        dst_ref=theirs,
-        send_sem=send,
-        recv_sem=recv,
-        device_id={"head": 1 - lax.axis_index("head")},
-    )
-    copy.start()
-    copy.wait()
-    rows = x_ref.shape[0]
-    step = min(rows, 16)
-
-    @pl.loop(0, rows // step)
-    def _(i):
-        here = pl.ds(pl.multiple_of(i * step, step), step)
-        out_ref[here] = x_ref[here] + theirs[here]
-
-
-def pair_total(x, collective):
-    return pl.pallas_call(
-        pair_kernel,
-        out_shape=jax.ShapeDtypeStruct(x.shape, x.dtype),
-        in_specs=[pl.BlockSpec(memory_space=pltpu.VMEM)],
-        out_specs=pl.BlockSpec(memory_space=pltpu.VMEM),
-        scratch_shapes=[
-            pltpu.VMEM(x.shape, x.dtype),
-            pltpu.SemaphoreType.DMA,
-            pltpu.SemaphoreType.DMA,
-        ],
-        compiler_params=params(collective),
-        name="pair_total",
-    )(x)
-
-
 def small_message(parts):
     flat = jnp.concatenate([part.reshape(-1) for part in parts])
     size = flat.shape[0]
@@ -1593,115 +1718,6 @@
         result.append(out[start : start + part.size].reshape(part.shape))
         start += part.size
     return result
-
-
-def routing_kernel(routes_ref, weights_ref, position_ref, weight_ref):
-    experts, tokens = position_ref.shape
-    expert = lax.broadcasted_iota(jnp.int32, (experts, tokens), 0)
-    named = jnp.zeros((experts, tokens), jnp.float32)
-    weight = jnp.zeros((experts, tokens), jnp.float32)
-    for k in range(routes_ref.shape[0]):
-        hit = expert == routes_ref[k : k + 1, :]
-        named = named + jnp.where(hit, 1.0, 0.0)
-        weight = weight + jnp.where(hit, weights_ref[k : k + 1, :], 0.0)
-    earlier = jnp.where(
-        lax.broadcasted_iota(jnp.int32, (tokens, tokens), 0)
-        < lax.broadcasted_iota(jnp.int32, (tokens, tokens), 1),
-        1.0,
-        0.0,
-    ).astype(jnp.bfloat16)
-    count = jnp.dot(named.astype(jnp.bfloat16), earlier, preferred_element_type=jnp.float32)
-    position_ref[...] = jnp.where(named > 0.0, count, -1.0)
-    weight_ref[...] = weight
-
-
-def routing(routes, route_weights, experts):
-    tokens = routes.shape[0]
-    return pl.pallas_call(
-        routing_kernel,
-        out_shape=[jax.ShapeDtypeStruct((experts, tokens), jnp.float32)] * 2,
-        name="routing",
-    )(routes.T, route_weights.T)
-
-
-def chosen_slots(position, first, count, slots):
-    tokens = position.shape[1]
-    number = lax.broadcasted_iota(jnp.int32, (count, slots, tokens), 1)
-    number = (number + slots * lax.axis_index("head")).astype(jnp.float32)
-    return jnp.where(position[:, None, :] == number, 1.0, 0.0).reshape(count * slots, tokens)
-
-
-def send_kernel(slots, weigh, position_ref, weight_ref, rows_ref, out_ref):
-    position = position_ref[...]
-    chosen = chosen_slots(position, 0, position.shape[0], slots)
-    rows = jnp.dot(
-        chosen.astype(jnp.bfloat16), rows_ref[...], preferred_element_type=jnp.float32
-    )
-    if weigh:
-        weighted = chosen.reshape(-1, slots, chosen.shape[1]) * weight_ref[...][:, None, :]
-        rows = rows * jnp.sum(weighted.reshape(chosen.shape), axis=1, keepdims=True)
-    out_ref[...] = rows.astype(jnp.bfloat16).reshape(out_ref.shape)
-
-
-def send_rows(position, weight, rows, slots, weigh):
-    experts, tokens = position.shape
-    width = rows.shape[1]
-    step = 16
-    whole = pl.BlockSpec((tokens, width), lambda i: (0, 0))
-    mine = pl.BlockSpec((step, tokens), lambda i: (i, 0))
-    out = pl.BlockSpec((step, slots, width), lambda i: (i, 0, 0))
-    return pl.pallas_call(
-        functools.partial(send_kernel, slots, weigh),
-        grid=(experts // step,),
-        out_shape=jax.ShapeDtypeStruct((experts, slots, width), jnp.bfloat16),
-        in_specs=[mine, mine, whole],
-        out_specs=out,
-        compiler_params=pltpu.CompilerParams(vmem_limit_bytes=40 * MIB),
-        name="send_grads" if weigh else "send_rows",
-    )(position, weight, rows)
-
-
-def combine_kernel(slots, weigh, position_ref, weight_ref, rows_ref, out_ref):
-    position = position_ref[...]
-    count = position.shape[0]
-    chosen = chosen_slots(position, 0, count, slots)
-    rows = rows_ref[...].reshape(count * slots, rows_ref.shape[2])
-
-    def over_slots(picked):
-        return lax.dot_general(
-            picked, rows, (((0,), (0,)), ((), ())), preferred_element_type=jnp.float32
-        )
-
-    @pl.when(pl.program_id(0) == 0)
-    def _():
-        out_ref[...] = jnp.zeros_like(out_ref)
-
-    if weigh:
-        weighted = chosen.reshape(count, slots, -1) * weight_ref[...][:, None, :]
-        weighted = weighted.reshape(chosen.shape)
-        high = weighted.astype(jnp.bfloat16)
-        less = (weighted - high.astype(jnp.float32)).astype(jnp.bfloat16)
-        out_ref[...] += over_slots(high) + over_slots(less)
-    else:
-        out_ref[...] += over_slots(chosen.astype(jnp.bfloat16))
-
-
-def combine(position, weight, home, weigh):
-    experts, tokens = position.shape
-    _, slots, width = home.shape
-    step = 16
-    mine = pl.BlockSpec((step, tokens), lambda i: (i, 0))
-    rows = pl.BlockSpec((step, slots, width), lambda i: (i, 0, 0))
-    out = pl.BlockSpec((tokens, width), lambda i: (0, 0))
-    return pl.pallas_call(
-        functools.partial(combine_kernel, slots, weigh),
-        grid=(experts // step,),
-        out_shape=jax.ShapeDtypeStruct((tokens, width), jnp.float32),
-        in_specs=[mine, mine, rows],
-        out_specs=out,
-        compiler_params=pltpu.CompilerParams(vmem_limit_bytes=40 * MIB),
-        name="combine_mix" if weigh else "combine_grads",
-    )(position, weight, home)
 
 
 def per_device(
@@ -1739,22 +1755,23 @@
     slots_dev = capacity // lax.axis_size("head")
     lanes = 128
     pad_heads = lambda v: jnp.pad(v, ((0, 0), (0, lanes - heads_dev)))
-    gathered, edge = gather_rows(
+    late_rows = jnp.concatenate(
+        [mixer_out, shared_gate_up.reshape(-1, 2 * shared_dev), shared_down], axis=1
+    )
+    gathered, late_rows, edge, position, slot_weight, grads_in = gather_rows(
         jnp.concatenate(
             [mixer_in.reshape(-1, 2 * inner_dev), state_proj, pad_heads(step_proj)], axis=1
         ),
-        layer_in[tokens - 16 :],
+        late_rows,
+        layer_in,
+        routes,
+        route_weights,
+        grad_out,
+        experts_all,
+        slots_dev,
         0,
     )
-    late_rows = jnp.concatenate(
-        [mixer_out, shared_gate_up.reshape(-1, 2 * shared_dev), shared_down], axis=1
-    )
-    weights_in, late_rows, grad_out_late = lax.optimization_barrier(
-        (gathered.reshape(model_width, -1), late_rows, grad_out)
-    )
-    position, slot_weight = routing(routes, route_weights, experts_all)
-    grads_out = send_rows(position, slot_weight, grad_out_late, slots_dev, True)
-    grads_in = lax.all_to_all(grads_out, "seq", split_axis=0, concat_axis=0, tiled=True)
+    weights_in = gathered.reshape(model_width, -1)
     numbers = jnp.pad(
         jnp.stack([decay_rate, skip_gain, step_bias]), ((0, 5), (0, lanes - heads_dev))
     )
@@ -1795,7 +1812,6 @@
         expert_down.reshape(-1, model_width),
         3,
     )
-    home_rows = lax.all_to_all(res_sums, "seq", split_axis=0, concat_axis=0, tiled=True)
     grad_resid, grad_mix, grad_ssd, grad_gate_z, norm_second_grad, gate_gain_grad = gate_back(
         grad_home,
         position,
@@ -1833,7 +1849,6 @@
         state_start.reshape(inner_dev, state_size),
         5,
     )
-    home_rows, right_grads = lax.optimization_barrier((home_rows, right_grads))
     small = (
         jnp.zeros_like(norm_first),
         norm_second_grad,
@@ -1844,7 +1859,7 @@
         heads_grad[0, :heads_dev],
         gate_gain_grad,
     )
-    summed, input_grad, small_sums = input_back(
+    summed, input_grad, small_sums, layer_out = input_back(
         normed,
         right_grads,
         tuple(((0, start, 1152),) for start in (0, 1152, 2304)),
@@ -1853,12 +1868,14 @@
         norm_first[None],
         grad_resid,
         small_message(small),
+        res_sums,
+        position,
+        slot_weight,
+        shared_part,
+        residual,
         6,
     )
     small_sums = small_parts(small, small_sums)
-    expert_mix = combine(position, slot_weight, home_rows, True)
-    branch_sum = pair_total(shared_part + expert_mix, 7)
-    layer_out = (residual + branch_sum).astype(jnp.bfloat16)
     wide = 2 * inner_dev + 2 * state_size
     weight_sums = (
         summed[:, : 2 * inner_dev].reshape(-1, 2, inner_dev),

time: 561 us -> 502 us (0.89)
  the two profiles are of different devices: /device:TPU:1 before, /device:TPU:0 now
where the time goes in v4:
time: 502 us; the launch traced here: 493 us
  Pallas kernels  455 us (91%)
  local copies, waits for them, and re-layouts  30.9 us (6%)
  other arithmetic  5.8 us (1%)
    pallas_call x1, Pallas kernels, input_back(): pl.pallas_call(functools.partial(input_back_kernel, plan), out_shape=[jax...  100 us
    pallas_call x1, Pallas kernels, gather_rows(): pl.pallas_call(gather_kernel, out_shape=[jax.ShapeDtypeStruct((4, 4, 4, r...  97.5 us
    pallas_call x1, Pallas kernels, experts(): pl.pallas_call(experts_kernel, out_shape=[jax.ShapeDtypeStruct(half, bf16...  87.1 us
    pallas_call x1, Pallas kernels, mixer_back(): pl.pallas_call(functools.partial(mixer_back_kernel, plan), out_shape=[jax...  79.6 us
    pallas_call x1, Pallas kernels, mixer(): pl.pallas_call(mixer_kernel, out_shape=[jax.ShapeDtypeStruct(*shape) for...  62.1 us
    unnamed x63, local copies, waits for them, and re-layouts  15 us
    pallas_call x1, Pallas kernels, residual_block(): pl.pallas_call(residual_kernel, out_shape=[jax.ShapeDtypeStruct(*shape) f...  14.2 us
    pallas_call x1, Pallas kernels, gate_back(): pl.pallas_call(gate_back_kernel, out_shape=[jax.ShapeDtypeStruct(*shape)...  14.1 us

profile of v4, /device:TPU:0, one launch (start us, length us, event | category | flops | bytes accessed | tf_op | source)
XLA Modules:
  0.0 492.7 jit_solution(8934168724540815447)
XLA Ops:
  0.7 1.0 copy.40
  1.7 1.4 fusion.1.x_ref
  3.9 1.6 pad_maximum_fusion.1.late_ref
  5.5 97.5 %gather_rows.1 = (bf16[4,4,4,24,3456]{4,3,2,1,0:T(8,128)(2,1)}, bf16[4,4,4,24,3072]{4,3,2,1,0:T(8,128)(2,1)}, bf16[16,1536]{1,0:T(8,128)(2,1)}, f32[64,256]{1,0:...) custom-call(bf16[24,3456]{1,0:T(8,128)(2,1)} %fusion.1.x_ref, bf16[24,3072]{1,0:T(8,128)(2,1)} %pad_maximum_fusion.1.late_ref, ...), custom_call_target="tpu_custom_call" | custom-call | tf_op jit(solution)/shard_map/gather_rows/pallas_call | solution.py:1195
  105.4 62.1 %mixer.1 = (bf16[256,1536]{1,0:T(8,128)(2,1)}, f32[256,1536]{1,0:T(8,128)}, f32[256,1536]{1,0:T(8,128)}, f32[256,256]{1,0:T(8,128)}, f32[256,1792]{1,0:T(8,128)}...) custom-call(bf16[256,1536]{1,0:T(8,128)(2,1)} %resid_ref.1, ...), custom_call_target="tpu_custom_call", output_to_operand_aliasing={{11}: (7, {})} | custom-call | tf_op jit(solution)/shard_map/mixer/pallas_call | solution.py:1419
  167.6 1.1 copy-done.3
  168.7 14.2 %residual_block.1 = (f32[256,1536]{1,0:T(8,128)S(1)}, bf16[256,1536]{1,0:T(8,128)(2,1)S(1)}, f32[256,128]{1,0:T(8,128)S(1)}, bf16[64,16,1536]{2,1,0:T(8,128)(2,1...) custom-call(bf16[256,1536]{1,0:T(8,128)(2,1)S(1)} %copy-done.3, ...), custom_call_target="tpu_custom_call" | custom-call | tf_op jit(solution)/shard_map/residual_block/pallas_call | solution.py:1558
  183.0 1.7 copy.42
  184.9 87.1 %experts.1 = (bf16[64,16,1536]{2,1,0:T(8,128)(2,1)}, bf16[64,16,1536]{2,1,0:T(8,128)(2,1)}, f32[6144,128]{1,0:T(8,128)}, f32[256,1536]{1,0:T(8,128)}) custom-call(bf16[64,16,1536]{2,1,0:T(8,128)(2,1)} %get-tuple-element.68.rows_ref, bf16[64,16,1536]{2,1,0:T(8,128)(2,1)} %get-tuple-element.69.grads_ref, bf16[1536,512]{1,0:T(8,128)(2,1)} %bitcast.38, ...), custom_call_target="tpu_custom_call" | custom-call | tf_op jit(solution)/shard_map/experts/pallas_call | solution.py:279
  272.1 14.1 %gate_back.1 = (f32[256,1536]{1,0:T(8,128)S(1)}, bf16[256,1536]{1,0:T(8,128)(2,1)S(1)}, f32[256,1536]{1,0:T(8,128)S(1)}, bf16[256,1536]{1,0:T(8,128)(2,1)S(1)}, ...) custom-call(bf16[64,16,1536]{2,1,0:T(8,128)(2,1)} %get-tuple-element.70.home_ref, f32[64,256]{1,0:T(8,128)S(1)} %copy-done.10, ...), custom_call_target="tpu_custom_call" | custom-call | tf_op jit(solution)/shard_map/gate_back/pallas_call | solution.py:1688
  287.0 0.9 copy-done.9
  287.9 1.5 pad_maximum_fusion.right
  290.1 79.6 %mixer_back.1 = (f32[24,3072]{1,0:T(8,128)}, bf16[256,3456]{1,0:T(8,128)(2,1)}, f32[8,1792]{1,0:T(8,128)}, f32[8,128]{1,0:T(8,128)}) custom-call(bf16[256,1536]{1,0:T(8,128)(2,1)} %copy-done.8, bf16[256,1536]{1,0:T(8,128)(2,1)} %copy-done.7, bf16[256,1536]{1,0:T(8,128)(2,1)} %lefts_2_.1, bf16[256,3072]{1,0:T(8,128)(2,1)} %pad_maximum_fusion.right, ...), custom_call_target="tpu_custom_call" | custom-call | tf_op jit(solution)/shard_map/mixer_back/pallas_call | solution.py:811
  372.9 100.0 %input_back.1 = (f32[24,3456]{1,0:T(8,128)}, f32[256,1536]{1,0:T(8,128)}, f32[64,8,128]{2,1,0:T(8,128)}, bf16[256,1536]{1,0:T(8,128)(2,1)}) custom-call(bf16[256,1536]{1,0:T(8,128)(2,1)} %get-tuple-element.64.left, bf16[256,3456]{1,0:T(8,128)(2,1)} %get-tuple-element.88.right, bf16[1536,3456]{1,0:T(8,128)(2,1)} %bitcast.37, bf16[256,1536]{1,0:T(8,128)(2,1)} %resid_ref.1, ...), custom_call_target="tpu_custom_call" | custom-call | tf_op jit(solution)/shard_map/input_back/pallas_call | solution.py:994
  472.9 1.1 slice.63
  473.9 1.0 reshape.106
  476.4 1.4 fusion.2
  477.8 1.3 slice.64
  479.1 1.3 slice.65
  481.8 1.3 fusion.3
  486.1 1.1 copy.50
  487.2 1.3 copy-done.13
  488.5 1.7 copy.51
  491.1 1.1 copy.52
  (76 shorter events, 14.8 us)
Async XLA Ops:
  0.7 102.3 %copy-start.19 = (f32[4,1536]{1,0:T(4,128)S(1)}, f32[4,1536]{1,0:T(4,128)}, u32[]{:S(2)}) copy-start(f32[4,1536]{1,0:T(4,128)} %param.26) | copy-start | bytes 73732
  0.7 102.3 %copy-start.23 = (f32[4,256]{1,0:T(4,128)S(1)}, f32[4,256]{1,0:T(4,128)}, u32[]{:S(2)}) copy-start(f32[4,256]{1,0:T(4,128)} %param.27) | copy-start | bytes 12292
  0.7 102.9 %copy-start.20 = (f32[1536]{0:T(1024)S(1)}, f32[1536]{0:T(1024)}, u32[]{:S(2)}) copy-start(f32[1536]{0:T(1024)} %param.21) | copy-start | bytes 18436
  0.7 103.5 %copy-start.21 = (f32[1536]{0:T(1024)S(1)}, f32[1536]{0:T(1024)}, u32[]{:S(2)}) copy-start(f32[1536]{0:T(1024)} %param.30) | copy-start | bytes 18436
  0.7 104.1 %copy-start.26 = (f32[24]{0:T(128)S(1)}, f32[24]{0:T(128)}, u32[]{:S(2)}) copy-start(f32[24]{0:T(128)} %param.28) | copy-start | bytes 292
  0.7 104.1 %copy-start.25 = (f32[24]{0:T(128)S(1)}, f32[24]{0:T(128)}, u32[]{:S(2)}) copy-start(f32[24]{0:T(128)} %param.29) | copy-start | bytes 292
  0.7 104.1 %copy-start.24 = (f32[24]{0:T(128)S(1)}, f32[24]{0:T(128)}, u32[]{:S(2)}) copy-start(f32[24]{0:T(128)} %param.25) | copy-start | bytes 292
  105.4 62.1 %copy-start.22 = (f32[1536]{0:T(1024)S(1)}, f32[1536]{0:T(1024)}, u32[]{:S(2)}) copy-start(f32[1536]{0:T(1024)} %param.32) | copy-start | bytes 18436
  105.4 62.1 %copy-start = (bf16[256,1536]{1,0:T(8,128)(2,1)S(1)}, bf16[256,1536]{1,0:T(8,128)(2,1)}, u32[]{:S(2)}) copy-start(bf16[256,1536]{1,0:T(8,128)(2,1)} %resid_ref.1) | copy-start | bytes 2359300
  105.4 62.1 %copy-start.1 = (bf16[256,1536]{1,0:T(8,128)(2,1)S(1)}, bf16[256,1536]{1,0:T(8,128)(2,1)}, u32[]{:S(2)}) copy-start(bf16[256,1536]{1,0:T(8,128)(2,1)} %lefts_2_.1) | copy-start | bytes 2359300
  105.4 62.1 %copy-start.10 = (f32[64,256]{1,0:T(8,128)S(1)}, f32[64,256]{1,0:T(8,128)}, u32[]{:S(2)}) copy-start(f32[64,256]{1,0:T(8,128)} %get-tuple-element.67.position_ref) | copy-start | bytes 196612
  168.7 14.3 %copy-start.14 = (bf16[1,1536,2,256]{3,2,1,0:T(2,128)(2,1)S(1)}, bf16[1,1536,2,256]{3,2,1,0:T(2,128)(2,1)}, u32[]{:S(2)}) copy-start(bf16[1,1536,2,256]{3,2,1,0:T(2,128)(2,1)} %param.35) | copy-start | bytes 4718596
  183.0 1.7 copy-start.2
  183.0 1.9 copy-start.7
  184.9 87.1 %copy-start.11 = (f32[256,128]{1,0:T(8,128)S(1)}, f32[256,128]{1,0:T(8,128)}, u32[]{:S(2)}) copy-start(f32[256,128]{1,0:T(8,128)} %get-tuple-element.76.gate_scale_ref) | copy-start | bytes 393220
  184.9 87.1 %copy-start.12 = (f32[1,1536]{1,0:T(1,128)S(1)}, f32[1,1536]{1,0:T(1,128)}, u32[]{:S(2)}) copy-start(f32[1,1536]{1,0:T(1,128)} %broadcast_in_dim.19.gain_ref) | copy-start | bytes 18436
  272.1 15.9 %copy-start.4 = (bf16[256,1536]{1,0:T(8,128)(2,1)S(1)}, bf16[256,1536]{1,0:T(8,128)(2,1)}, u32[]{:S(2)}) copy-start(bf16[256,1536]{1,0:T(8,128)(2,1)} %get-tuple-element.65.gated_ref) | copy-start | bytes 2359300
  287.9 1.6 copy-start.5
  287.9 2.2 copy-start.6
  372.9 110.3 %copy-start.18 = (f32[24,3072]{1,0:T(8,128)S(1)}, f32[24,3072]{1,0:T(8,128)}, u32[]{:S(2)}) copy-start(f32[24,3072]{1,0:T(8,128)} %get-tuple-element.101) | copy-start | bytes 884740
  472.9 12.3 %copy-start.17 = (bf16[256,1536]{1,0:T(8,128)(2,1)S(1)}, bf16[256,1536]{1,0:T(8,128)(2,1)}, u32[]{:S(2)}) copy-start(bf16[256,1536]{1,0:T(8,128)(2,1)} %get-tuple-element.131) | copy-start | bytes 2359300
  473.9 12.2 %copy-start.16 = (f32[256,1536]{1,0:T(8,128)S(1)}, f32[256,1536]{1,0:T(8,128)}, u32[]{:S(2)}) copy-start(f32[256,1536]{1,0:T(8,128)} %get-tuple-element.132) | copy-start | bytes 4718596
  486.1 2.5 copy-start.13
  488.5 2.5 copy-start.15
  (3 other events, 2.9 us)

commit v5 on v4

--- a/solution.py
+++ b/solution.py
@@ -7,7 +7,7 @@
 from jax.sharding import PartitionSpec as P
 
 ORDERS = ((0, 1, 2), (1, 2, 0), (2, 0, 1))
-MIB = 1 << 20
+VMEM = 62 << 20
 EPSILON = 1e-05
 
 
@@ -81,31 +81,206 @@
                     body(k, device)
 
 
+class Lazy:
+    def __init__(self, source, ref, sem):
+        self.ref, self.copy = ref, pltpu.make_async_copy(source, ref, sem)
+        self.shape, self.dtype = ref.shape, ref.dtype
+        self.copy.start()
+
+    def ready(self):
+        if self.copy is not None:
+            self.copy.wait()
+            self.copy = None
+        return self.ref
+
+    @property
+    def at(self):
+        return self.ready().at
+
+    def __getitem__(self, index):
+        return self.ready()[index]
+
+
+class Eager:
+    def __init__(self, target, ref, sem):
+        self.ref, self.copy, self.going = ref, pltpu.make_async_copy(ref, target, sem), False
+        self.shape, self.dtype, self.at = ref.shape, ref.dtype, ref.at
+
+    def __getitem__(self, index):
+        return self.ref[index]
+
+    def __setitem__(self, index, value):
+        self.ref[index] = value
+
+    def flush(self):
+        if not self.going:
+            self.going = True
+            self.copy.start()
+
+
+def ready(*refs):
+    for ref in refs:
+        if isinstance(ref, Lazy):
+            ref.ready()
+
+
+def call(kernel, out_shape, in_specs, out_specs, scratch_shapes, **options):
+    def run(*args):
+        leaves, tree = jax.tree.flatten(list(args))
+        specs = tree.flatten_up_to(list(in_specs))
+        shapes, out_tree = jax.tree.flatten(list(out_shape))
+        out_kinds = out_tree.flatten_up_to(list(out_specs))
+        lazy = [n for n, spec in enumerate(specs) if spec is Lazy]
+        eager = [n for n, spec in enumerate(out_kinds) if spec is Eager]
+        hbm = pl.BlockSpec(memory_space=pl.ANY)
+        buffers = [pltpu.VMEM(leaves[n].shape, leaves[n].dtype) for n in lazy]
+        buffers += [pltpu.VMEM(shapes[n].shape, shapes[n].dtype) for n in eager]
+        buffers += [pltpu.SemaphoreType.DMA((max(1, len(lazy)),))]
+        buffers += [pltpu.SemaphoreType.DMA((max(1, len(eager)),))]
+        own = len(scratch_shapes)
+
+        def body(*refs):
+            ins, outs = list(refs[: len(leaves)]), list(refs[len(leaves) :][: len(shapes)])
+            rest = refs[len(leaves) + len(shapes) :]
+            more = rest[own:]
+            for n, index in enumerate(lazy):
+                ins[index] = Lazy(ins[index], more[n], more[-2].at[n])
+            for n, index in enumerate(eager):
+                outs[index] = Eager(outs[index], more[len(lazy) + n], more[-1].at[n])
+            kernel(*tree.unflatten(ins), *out_tree.unflatten(outs), *rest[:own])
+            for index in lazy:
+                ins[index].ready()
+            for index in eager:
+                outs[index].flush()
+            for index in eager:
+                outs[index].copy.wait()
+
+        out = pl.pallas_call(
+            body,
+            out_shape=shapes,
+            in_specs=[hbm if spec is Lazy else spec for spec in specs],
+            out_specs=[hbm if kind is Eager else kind for kind in out_kinds],
+            scratch_shapes=list(scratch_shapes) + buffers,
+            **options,
+        )(*leaves)
+        return out_tree.unflatten(out)
+
+    return run
+
+
+def emit_kernel(*refs):
+    count = len(refs) // 2
+    for n in range(count):
+        refs[count + n][...] = refs[n][...]
+
+
+def emit(arrays):
+    return pl.pallas_call(
+        emit_kernel,
+        out_shape=[jax.ShapeDtypeStruct(array.shape, array.dtype) for array in arrays],
+        name="emit",
+    )(*arrays)
+
+
+class Spread:
+    def __init__(self, at, me, source, target, sems, first, last, back):
+        self.at, self.me, self.source, self.target = at, me, source, target
+        self.sems = sems
+        self.first, self.last, self.back = first, last, back
+
+    def start(self, first=None, last=None):
+        first = self.first if first is None else first
+        last = self.last if last is None else last
+        if first == 0:
+            own = self.source.at[0 if self.back else self.me]
+            pltpu.make_async_copy(own, self.target.at[0], self.sems.at[1]).start()
+
+        def put(k, device):
+            pltpu.make_async_remote_copy(
+                src_ref=self.source.at[k if self.back else device],
+                dst_ref=self.target.at[k - 8 * self.first],
+                send_sem=self.sems.at[0],
+                recv_sem=self.sems.at[1 + k // 8],
+                device_id={"seq": device},
+            ).start()
+
+        Ways(self.at).each(first, last, put, self.back)
+
+    def arrived(self, first, last):
+        for g in range(first, last):
+            here = self.target.at[pl.ds(8 * (g - self.first), 8)]
+            pltpu.make_async_copy(here, here, self.sems.at[1 + g]).wait()
+
+    def sent(self):
+        count = 8 * (self.last - self.first)
+        here = self.target.at[pl.ds(0, count - 1 if self.first == 0 else count)]
+        pltpu.make_async_copy(here, here, self.sems.at[0]).wait()
+
+    def wait(self):
+        self.arrived(self.first, self.last)
+        self.sent()
+
+
+OUT = ((0, 6), (6, 8))
+HOME = ((0, 3), (3, 8))
+
+
+def part_shape(span, rows):
+    return jax.ShapeDtypeStruct((8 * (span[1] - span[0]),) + rows.shape[1:], rows.dtype)
+
+
 def params(collective, **more):
     return pltpu.CompilerParams(collective_id=collective, has_side_effects=True, **more)
 
 
-def greet_sibling():
-    barrier = pltpu.get_barrier_semaphore()
-    pl.semaphore_signal(barrier, inc=1, device_id={"head": 1 - lax.axis_index("head")})
-    pl.semaphore_wait(barrier, 1)
+class PairSum:
+    def __init__(self, mine, theirs, sems, cut):
+        self.mine, self.theirs, self.sems, self.cut = mine, theirs, sems, cut
+        self.count = mine.shape[1] // cut
+
+    def copy(self, n):
+        cols = pl.ds(n * self.cut, self.cut)
+        return pltpu.make_async_remote_copy(
+            src_ref=self.mine.at[:, cols],
+            dst_ref=self.theirs.at[:, cols],
+            send_sem=self.sems.at[0, n],
+            recv_sem=self.sems.at[1, n],
+            device_id={"head": 1 - lax.axis_index("head")},
+        )
 
 
 def experts_kernel(
-    rows_ref,
-    grads_ref,
+    gated_ref,
+    weights_ref,
+    layer_ref,
+    table_ref,
+    position_ref,
+    grads_refs,
     gate_up_ref,
     down_ref,
+    grad_out_ref,
     home_ref,
     res_ref,
     gate_up_grad_ref,
     down_grad_ref,
+    shared_ref,
+    back_ref,
+    right_ref,
+    resid_ref,
+    normed_ref,
+    scale_ref,
+    rows_ref,
+    mine,
+    theirs,
     slot_in,
     grad_slots,
     theirs_x,
     theirs_y,
     sums,
     wide_grad,
+    weights,
+    load_sems,
+    pair_sems,
     send,
     home_send,
     home_recv,
@@ -118,6 +293,16 @@
     names += ("x_send", "x_recv", "y_send", "y_recv")
     sem = {name: sems.at[n] for n, name in enumerate(names)}
     announce(me, True)
+    shared_hidden = right_ref.shape[1] // 3
+    tokens, model = layer_ref.shape
+    inner = gated_ref.shape[1]
+    loads = []
+    for n, cols in enumerate((pl.ds(0, inner), pl.ds(inner, 3 * shared_hidden))):
+        loads.append(
+            pltpu.make_async_copy(weights_ref.at[:, cols], weights.at[:, cols], load_sems.at[n])
+        )
+        loads[n].start()
+    norm_ref = table_ref.at[5:6, 0:model]
     wide_grad[...] = jnp.zeros_like(wide_grad)
     down_grad_ref[...] = jnp.zeros_like(down_grad_ref)
     ways = Ways(at)
@@ -125,6 +310,80 @@
 
     def group(c):
         return pl.ds(pl.multiple_of(c * 8, 8), 8)
+
+    def given(c, source=None):
+        there = grad_slots.at[group(c), head]
+        return pltpu.make_async_remote_copy(
+            src_ref=there if source is None else source,
+            dst_ref=there,
+            send_sem=sem["given_send"].at[c],
+            recv_sem=sem["given_recv"].at[c],
+            device_id=sibling,
+        )
+
+    def kept(c, source=None):
+        there = grad_slots.at[group(c), head]
+        return pltpu.make_async_copy(there if source is None else source, there, sem["kept"].at[c])
+
+    def forward(c):
+        return pltpu.make_async_remote_copy(
+            src_ref=slot_in.at[group(c), head],
+            dst_ref=slot_in.at[group(c), head],
+            send_sem=sem["fwd_send"].at[c],
+            recv_sem=sem["fwd_recv"].at[c],
+            device_id=sibling,
+        )
+
+    def swap(c, source, target, name):
+        return pltpu.make_async_remote_copy(
+            src_ref=source.at[group(c), 1 - head],
+            dst_ref=target.at[group(c)],
+            send_sem=sem[name + "_send"].at[c],
+            recv_sem=sem[name + "_recv"].at[c],
+            device_id=sibling,
+        )
+
+    for (first, last), grads_ref in zip(OUT, grads_refs):
+        for c in range(first, last):
+            source = grads_ref.at[pl.ds(8 * (c - first), 8)]
+            kept(c, source).start()
+            given(c, source).start()
+
+    cut = 256
+    pair = PairSum(mine, theirs, pair_sems, cut)
+    loads[0].wait()
+    gated = gated_ref[...]
+    for n in range(pair.count):
+        rows = slice(n * cut, (n + 1) * cut)
+        mine[:, rows] = dot_nt(gated, weights[rows, 0:inner])
+        pair.copy(n).start()
+    loads[1].wait()
+    both = slice(inner, inner + 2 * shared_hidden)
+    less = slice(inner + 2 * shared_hidden, inner + 3 * shared_hidden)
+    shared_grad_hid = dot_nn(grad_out_ref[...], weights[:, less])
+    square = jnp.zeros((tokens, 1), jnp.float32)
+    for n in range(pair.count):
+        rows = slice(n * cut, (n + 1) * cut)
+        pair.copy(n).wait()
+        resid = layer_ref[:, rows].astype(jnp.float32) + (mine[:, rows] + theirs[:, rows])
+        resid_ref[:, rows] = resid
+        square = square + jnp.sum(resid * resid, axis=1, keepdims=True)
+    scale = lax.rsqrt(square / model + EPSILON)
+    scale_ref[...] = jnp.broadcast_to(scale, scale_ref.shape)
+    for n in range(pair.count):
+        rows = slice(n * cut, (n + 1) * cut)
+        normed_ref[:, rows] = low(resid_ref[:, rows] * scale * norm_ref[:, rows])
+    resid_ref.flush()
+    normed_ref.flush()
+    ready(position_ref)
+    normed = normed_ref[...]
+    slots, step = rows_ref.shape[1], 16
+
+    @pl.loop(0, rows_ref.shape[0] // step)
+    def _(i):
+        here = pl.ds(pl.multiple_of(i * step, step), step)
+        chosen = chosen_slots(position_ref[here, :], slots)
+        rows_ref[here] = low(dot_nn(low(chosen), normed)).reshape(step, slots, model)
 
     own = pltpu.make_async_copy(rows_ref.at[me], slot_in.at[0, head], sem["recv"].at[0])
     own.start()
@@ -140,43 +399,6 @@
 
     ways.each(0, 8, put)
 
-    def given(c):
-        return pltpu.make_async_remote_copy(
-            src_ref=grads_ref.at[group(c)],
-            dst_ref=grad_slots.at[group(c), head],
-            send_sem=sem["given_send"].at[c],
-            recv_sem=sem["given_recv"].at[c],
-            device_id=sibling,
-        )
-
-    def kept(c):
-        return pltpu.make_async_copy(
-            grads_ref.at[group(c)], grad_slots.at[group(c), head], sem["kept"].at[c]
-        )
-
-    def forward(c):
-        return pltpu.make_async_remote_copy(
-            src_ref=slot_in.at[group(c), head],
-            dst_ref=slot_in.at[group(c), head],
-            send_sem=sem["fwd_send"].at[c],
-            recv_sem=sem["fwd_recv"].at[c],
-            device_id=sibling,
-        )
-
-    def swap(c, source, target, name):
-        return pltpu.make_async_remote_copy(
-            src_ref=source.at[group(c), 1 - head],
-            dst_ref=target.at[group(c)],
-            send_sem=sem[name + "_send"].at[c],
-            recv_sem=sem[name + "_recv"].at[c],
-            device_id=sibling,
-        )
-
-    @pl.loop(0, 8)
-    def _(c):
-        kept(c).start()
-        given(c).start()
-
     hidden = down_ref.shape[0]
     width = down_ref.shape[1]
 
@@ -189,6 +411,22 @@
         return lax.dot_general(
             left, right, (((0,), (0,)), ((), ())), preferred_element_type=jnp.float32
         )
+
+    gate_up = dot_nn(normed, weights[:, both])
+    gate, up = gate_up[:, :shared_hidden], gate_up[:, shared_hidden:]
+    act, slope = silu_parts(gate)
+    hid = low(act * up)
+    right_ref[:, 2 * shared_hidden :] = hid
+    right_ref[:, 0:shared_hidden] = low(shared_grad_hid * up * slope)
+    right_ref[:, shared_hidden : 2 * shared_hidden] = low(shared_grad_hid * act)
+    grads = right_ref[:, 0 : 2 * shared_hidden]
+    for c in range(0, width, 256):
+        rows = slice(c, c + 256)
+        shared_ref[:, rows] = dot_nt(hid, weights[rows, less])
+        back_ref[:, rows] = dot_nt(grads, weights[rows, both])
+    for ref in (shared_ref, back_ref, right_ref):
+        ref.flush()
+    ready(gate_up_ref, down_ref)
 
     @pl.loop(0, 10)
     def _(i):
@@ -271,38 +509,54 @@
     pltpu.make_async_copy(sums, home_ref, home_recv).wait()
 
 
-def experts(rows, grads, gate_up, down, collective):
+def experts(
+    gated, weights, layer_in, table, position, grads, gate_up, down, grad_out, slots, collective
+):
+    tokens, model = layer_in.shape
+    shared_hidden = (weights.shape[1] - gated.shape[1]) // 3
     hidden, width = down.shape
-    half, bf16 = rows.shape, rows.dtype
+    half, bf16 = (position.shape[0], slots, model), jnp.bfloat16
     whole = (half[0], 2) + half[1:]
-    vmem = pl.BlockSpec(memory_space=pltpu.VMEM)
-    home, res, wide, down_grad = pl.pallas_call(
+    vmem, hbm = pl.BlockSpec(memory_space=pltpu.VMEM), pl.BlockSpec(memory_space=pl.ANY)
+    home, res, wide, down_grad, *shared = call(
         experts_kernel,
         out_shape=[
             jax.ShapeDtypeStruct(half, bf16),
             jax.ShapeDtypeStruct(half, bf16),
             jax.ShapeDtypeStruct((width * 2 * hidden // 128, 128), jnp.float32),
             jax.ShapeDtypeStruct((hidden, width), jnp.float32),
+            jax.ShapeDtypeStruct((tokens, width), jnp.float32),
+            jax.ShapeDtypeStruct((tokens, width), jnp.float32),
+            jax.ShapeDtypeStruct((tokens, 3 * shared_hidden), bf16),
+            jax.ShapeDtypeStruct((tokens, model), jnp.float32),
+            jax.ShapeDtypeStruct((tokens, model), bf16),
+            jax.ShapeDtypeStruct((tokens, 128), jnp.float32),
         ],
-        in_specs=[vmem] * 4,
-        out_specs=[pl.BlockSpec(memory_space=pl.ANY)] + [vmem] * 3,
+        in_specs=[Lazy, hbm, Lazy, vmem, Lazy, [hbm] * len(grads), Lazy, Lazy, Lazy],
+        out_specs=[hbm] + [vmem] * 3 + [Eager] * 5 + [vmem],
         scratch_shapes=[
+            pltpu.VMEM(half, bf16),
+            pltpu.VMEM((tokens, model), jnp.float32),
+            pltpu.VMEM((tokens, model), jnp.float32),
             pltpu.VMEM(whole, bf16),
             pltpu.VMEM(whole, bf16),
             pltpu.VMEM(half, bf16),
             pltpu.VMEM(half, bf16),
             pltpu.VMEM(half, bf16),
             pltpu.VMEM((width, 2 * hidden), jnp.float32),
+            pltpu.VMEM(weights.shape, bf16),
+            pltpu.SemaphoreType.DMA((2,)),
+            pltpu.SemaphoreType.DMA((2, model // 256)),
             pltpu.SemaphoreType.DMA,
             pltpu.SemaphoreType.DMA,
             pltpu.SemaphoreType.DMA,
             pltpu.SemaphoreType.DMA((10, 8)),
         ],
-        compiler_params=params(collective, vmem_limit_bytes=58 * MIB),
+        compiler_params=params(collective, vmem_limit_bytes=VMEM),
         name="experts",
-    )(rows, grads, gate_up, down)
+    )(gated, weights, layer_in, table, position, grads, gate_up, down, grad_out)
     wide = wide.reshape(width, hidden // 128, 2, 128).transpose(0, 2, 1, 3)
-    return home, res, wide.reshape(1, width, 2, hidden), down_grad[None]
+    return home, res, wide.reshape(1, width, 2, hidden), down_grad[None], *shared
 
 
 class Scan:
@@ -339,9 +593,10 @@
         def step(k, state):
             at_k = 63 - k if self.reverse else k
             made[at_k] = state
-            row = got[at_k, heads : heads + 8, :][0:1, :]
+            rows = got[at_k].astype(jnp.float32)
+            row = jnp.sum(rows[heads:], axis=0, keepdims=True)
             decay = jnp.sum(jnp.where(chosen, row, 0.0), axis=1, keepdims=True)
-            return decay * state + got[at_k, 0:heads, :]
+            return decay * state + rows[:heads]
 
         lax.fori_loop(0, 64, step, jnp.zeros((heads, width), jnp.float32), unroll=8)
         self.out_ref[self.me] = made[self.me]
@@ -352,6 +607,13 @@
         made = self.made
         pltpu.make_async_copy(made.at[some], made.at[some], self.back_send).wait()
         pltpu.make_async_copy(made.at[some], made.at[some], self.back_recv).wait()
+
+
+def scan_rows(states, decay):
+    decays = [part.astype(jnp.float32) for part in split(decay, 3)]
+    decays = jnp.concatenate(decays + [jnp.zeros((5, decay.shape[1]), jnp.float32)], axis=0)
+    decays = jnp.broadcast_to(decays[None], (states.shape[0],) + decays.shape)
+    return low(jnp.concatenate([states, decays], axis=1))
 
 
 class Small:
@@ -400,8 +662,8 @@
 
 
 class Scatter:
-    def __init__(self, at, plan, lefts, right, out_ref, buf, rest, send, recv):
-        self.at, self.plan, self.lefts, self.right = at, plan, lefts, right
+    def __init__(self, at, plan, lefts, rights, out_ref, buf, rest, send, recv):
+        self.at, self.plan, self.lefts, self.rights = at, plan, lefts, rights
         self.out_ref, self.buf, self.rest, self.send, self.recv = out_ref, buf, rest, send, recv
         self.third, self.half = parts_of(buf.shape[4])
         self.copies = {}
@@ -411,17 +673,18 @@
         return pl.ds(start, half), pl.ds(start + half, third - half)
 
     def product(self, p):
-        buf, right = self.buf, self.right
+        buf = self.buf
         rows = buf.shape[3]
-        for which, start, length in self.plan[p]:
-            left = self.lefts[which]
+        for which, other, first, start, length in self.plan[p]:
+            left, right = self.lefts[which], self.rights[other]
+            ready(left, right)
 
             @pl.loop(0, 4)
             def _(x):
                 across = pl.ds(pl.multiple_of(x * 16 * rows, 128), 16 * rows)
                 total = lax.dot_general(
                     left[:, across],
-                    right[:, start : start + length],
+                    right[:, first : first + length],
                     (((0,), (0,)), ((), ())),
                     preferred_element_type=jnp.float32,
                 )
@@ -582,24 +845,40 @@
 
 
 def mixer_back_kernel(
-    plan,
     lefts,
-    right,
-    dy_ref,
+    rights,
+    home_ref,
+    position_ref,
+    add_ref,
+    resid_ref,
+    scale_ref,
+    weights_ref,
+    z_ref,
+    gate_scale_ref,
     y_ref,
     x_ref,
     bc_ref,
     conv_ref,
     pre_ref,
-    gate_ref,
     step_raw_ref,
-    numbers_ref,
-    taps_ref,
+    table_ref,
     start_ref,
-    out_ref,
+    res_ref,
+    mixer_out_ref,
+    gate_up_ref,
+    down_ref,
     grads_ref,
     taps_grad_ref,
     heads_grad_ref,
+    results_ref,
+    grad_resid_ref,
+    norm_grad_ref,
+    gain_grad_ref,
+    weights,
+    grad_mix,
+    dy_ref,
+    stat,
+    stat_theirs,
     message,
     back,
     got,
@@ -613,24 +892,115 @@
     ext,
     mine,
     theirs,
-    buf,
-    rest,
-    send,
-    recv,
+    shared_out,
+    shared_scratch,
+    mix_scratch,
     scan_sems,
     sems,
+    home_sems,
+    load_sem,
+    pair_sems,
+    stat_sems,
 ):
     me, at = coordinates()
     head = lax.axis_index("head")
     tokens, width = x_ref.shape
+    model = resid_ref.shape[1]
     size = start_ref.shape[1]
     lanes = step_raw_ref.shape[1]
     each = width // 64
     mid = tokens // 2
     cut = 384
+    numbers_ref, taps_ref = table_ref.at[8:16, 0:lanes], table_ref
+    norm_ref, gain_ref = table_ref.at[5:6, 0:model], table_ref.at[6:7, 0:width]
     announce(me, True)
-    sums = Scatter(at, plan, lefts, right, out_ref, buf, rest, send, recv)
+    added = pltpu.make_async_copy(add_ref, q, load_sem.at[1])
+    added.start()
+    load = pltpu.make_async_copy(weights_ref.at[:, pl.ds(0, width)], weights, load_sem.at[0])
+    load.start()
+    normed_second, grad_out = lefts
+    normed_gate, shared_right = rights
+    third = width // 3
+    plan = [((n // 2, 0, n * third, n * third, third),) for n in range(3)]
+    shared = Scatter(at, plan, lefts, [shared_right], shared_out, *shared_scratch)
+    plan = [((0, 0, n * third, n * third, third),) for n in range(3)]
+    mix = Scatter(at, plan, [grad_mix], [normed_gate], mixer_out_ref, *mix_scratch)
     scan = Scan(True, at, me, message, back, got, made, scan_sems)
+    results = Spread(at, me, res_ref, results_ref, home_sems, *HOME[0], True)
+
+    gate_cut = 256
+    pair = PairSum(q, decayed, pair_sems, gate_cut)
+    added.wait()
+    ready(home_ref, position_ref)
+    slots, step = home_ref.shape[1], 16
+
+    @pl.loop(0, home_ref.shape[0] // step)
+    def _(i):
+        here = pl.ds(pl.multiple_of(i * step, step), step)
+        chosen = low(chosen_slots(position_ref[here, :], slots))
+        q[...] += dot_tn(chosen, home_ref[here].reshape(step * slots, model))
+
+    await_all(True)
+    for n in range(pair.count):
+        pair.copy(n).start()
+    for p in range(3):
+        shared.product(p)
+        shared.first(2, p)
+    scale = scale_ref[:, 0:1]
+    inner_sum = jnp.zeros((tokens, 1), jnp.float32)
+    for n in range(pair.count):
+        cols = slice(n * gate_cut, (n + 1) * gate_cut)
+        pair.copy(n).wait()
+        grad = q[:, cols] + decayed[:, cols]
+        q[:, cols] = grad
+        resid = resid_ref[:, cols]
+        norm_grad_ref[:, cols] = jnp.sum(grad * resid * scale, axis=0, keepdims=True)
+        inner_sum = inner_sum + jnp.sum(resid * norm_ref[:, cols] * grad, axis=1, keepdims=True)
+    pull = scale * scale * scale * (inner_sum / model)
+    for n in range(pair.count):
+        cols = slice(n * gate_cut, (n + 1) * gate_cut)
+        grad = scale * norm_ref[:, cols] * q[:, cols] - resid_ref[:, cols] * pull
+        grad = grad_out[:, cols].astype(jnp.float32) + grad
+        grad_resid_ref[:, cols] = grad
+        grad_mix[:, cols] = low(grad)
+    grad_resid_ref.flush()
+
+    load.wait()
+    gate_scale = gate_scale_ref[:, 0:1]
+    dots = jnp.zeros((tokens, 1), jnp.float32)
+    for c in range(0, width, cut):
+        cols = slice(c, c + cut)
+        grad = dot_nn(grad_mix[...], weights[:, cols])
+        z = z_ref[:, cols]
+        gated = y_ref[:, cols] * (z * jax.nn.sigmoid(z))
+        gain_grad_ref[:, cols] = jnp.sum(grad * gated * gate_scale, axis=0, keepdims=True)
+        weighted = grad * gain_ref[:, cols]
+        dy_ref[:, cols] = weighted
+        dots = dots + jnp.sum(weighted * gated, axis=1, keepdims=True)
+    stat[...] = jnp.broadcast_to(dots, stat.shape)
+    stat_swap = pltpu.make_async_remote_copy(
+        src_ref=stat,
+        dst_ref=stat_theirs,
+        send_sem=stat_sems.at[0],
+        recv_sem=stat_sems.at[1],
+        device_id={"head": 1 - head},
+    )
+    stat_swap.start()
+    for p in range(3):
+        mix.product(p)
+        mix.first(2, p)
+    for p in range(3):
+        shared.second(2, p)
+    stat_swap.wait()
+    dots = (stat[...] + stat_theirs[...])[:, 0:1]
+    pull = gate_scale * gate_scale * gate_scale * (dots / (2 * width))
+    for c in range(0, width, cut):
+        cols = slice(c, c + cut)
+        z, y = z_ref[:, cols], y_ref[:, cols]
+        act, slope = silu_parts(z)
+        grad = gate_scale * dy_ref[:, cols] - y * act * pull
+        dy_ref[:, cols] = grad * act
+        grads_ref[:, cols] = low(grad * y * slope)
 
     rate = numbers_ref[0:1, :]
     step_raw = step_raw_ref[...]
@@ -651,18 +1021,13 @@
         part = dy_ref[:, c : c + cut] * spread[:, c : c + cut]
         decayed[:, c : c + cut] = part
         made_rows = dot_three(part, read_full, dot_tn)
-        message[c // each : (c + cut) // each, 0:each, :] = made_rows.reshape(
-            cut // each, each, size
-        )
-    message[:, each : each + 8, :] = jnp.broadcast_to(jnp.exp(tail)[None], (64, 8, lanes))
-    await_all(True)
+        made_rows = made_rows.reshape(cut // each, each, size)
+        message[c // each : (c + cut) // each] = scan_rows(made_rows, jnp.exp(tail))
     scan.begin()
     for p in range(3):
-        sums.product(p)
-        sums.first_far(2, p)
+        mix.second(2, p)
+    shared.finish(2)
     scan.middle()
-    for p in range(3):
-        sums.first_near(2, p)
 
     spread[...] = split_dot(step, spreader, 2)
     blocks = ((0, 0), (0, 1), (1, 1))
@@ -670,6 +1035,7 @@
         scores[n] = dot_nt(held[s * mid : (s + 1) * mid], read[t * mid : (t + 1) * mid])
     acc[...] = jnp.zeros_like(acc)
     causal = triangle(mid, lambda s, t: s <= t)
+    ready(x_ref)
     second_head = lax.broadcasted_iota(jnp.int32, (tokens, 128), 1) >= 64
 
     @pl.loop(0, width // 128)
@@ -702,7 +1068,10 @@
             q[rows, here] = jnp.where(second_head[rows], results[1][s], results[0][s])
 
     for p in range(3):
-        sums.second(2, p)
+        shared.second(1, p)
+    shared.finish(1)
+    mix.finish(2)
+    results.start(HOME[0][0], HOME[0][0] + 1)
     scan.end()
 
     skip = split_dot(jnp.broadcast_to(numbers_ref[1:2, :], (8, lanes)), spreader, 2)[0:1, :]
@@ -743,6 +1112,11 @@
         device_id={"head": 1 - head},
     )
     swap.start()
+    for p in range(3):
+        shared.second(0, p)
+    for p in range(3):
+        mix.second(1, p)
+    results.start(HOME[0][0] + 1, HOME[0][0] + 2)
 
     ones = jnp.ones((8, size), jnp.bfloat16)
     state_grad = dot_split(ones, state_dot, 2, dot_nt)[0:1, :]
@@ -761,7 +1135,6 @@
     heads_grad_ref[2:3, :] = jnp.sum(grad_raw, axis=0, keepdims=True)
 
     channels = width + 2 * size
-    grads_ref[:, 0:width] = gate_ref[...]
     grads_ref[:, width + channels : width + channels + lanes] = low(grad_raw)
     swap.wait()
     ext[0:tokens, width:channels] = (mine[...] + theirs[...]) * silu_parts(
@@ -775,11 +1148,14 @@
         device_id={"seq": (me + 63) % 64},
     )
     edge.start()
-    sums.finish(2)
+    shared.finish(0)
+    mix.finish(1)
+    results.start(HOME[0][0] + 2, HOME[0][1])
     edge.wait()
     there = jnp.where(me == 63, 0.0, 1.0)
     ext[tokens : tokens + 8, :] = ext[tokens : tokens + 8, :] * there
     taps_grad_ref[...] = jnp.zeros_like(taps_grad_ref)
+    ready(pre_ref)
 
     @pl.loop(0, channels // 256)
     def _(i):
@@ -792,36 +1168,76 @@
             taps_grad_ref[j : j + 1, here] = jnp.sum(products, axis=0, keepdims=True)
         grads_ref[:, pl.ds(pl.multiple_of(width + i * 256, 256), 256)] = low(total)
 
-    for phase in (1, 0):
-        for p in range(3):
-            sums.second(phase, p)
-        sums.finish(phase)
-    sums.end()
-
-
-def mixer_back(lefts, right, plan, dy, y, x, bc, conv, pre, gate, step_raw, numbers, taps, start, collective):
-    model, columns = lefts[0].shape[1], right.shape[1]
+    for p in range(3):
+        mix.second(0, p)
+    mix.finish(0)
+    hidden = down_ref.shape[1]
+    for n in range(2):
+        gate_up_ref[:, n, :] = shared_out[:, n * hidden : (n + 1) * hidden]
+    down_ref[...] = shared_out[:, 2 * hidden :]
+    shared.end()
+    mix.end()
+    results.wait()
+
+
+def mixer_back(
+    lefts,
+    rights,
+    home,
+    position,
+    add,
+    resid,
+    scale,
+    weights,
+    z,
+    gate_scale,
+    y,
+    x,
+    bc,
+    conv,
+    pre,
+    step_raw,
+    table,
+    start,
+    res,
+    collective,
+):
+    tokens, model = resid.shape
     rows = model // 64
-    tokens, width = x.shape
+    width = x.shape[1]
+    hidden = rights[1].shape[1] // 3
     size, lanes = start.shape[1], step_raw.shape[1]
     each, channels, mid = width // 64, width + 2 * size, tokens // 2
     f32, bf16 = jnp.float32, jnp.bfloat16
-    vmem = pl.BlockSpec(memory_space=pltpu.VMEM)
-    args = (lefts, right, dy, y, x, bc, conv, pre, gate, step_raw, numbers, taps, start)
-    return pl.pallas_call(
-        functools.partial(mixer_back_kernel, plan),
+    vmem, hbm = pl.BlockSpec(memory_space=pltpu.VMEM), pl.BlockSpec(memory_space=pl.ANY)
+    return call(
+        mixer_back_kernel,
         out_shape=[
-            jax.ShapeDtypeStruct((rows, columns), f32),
+            jax.ShapeDtypeStruct((rows, width), f32),
+            jax.ShapeDtypeStruct((rows, 2, hidden), f32),
+            jax.ShapeDtypeStruct((rows, hidden), f32),
             jax.ShapeDtypeStruct((tokens, width + channels + lanes), bf16),
             jax.ShapeDtypeStruct((8, channels), f32),
             jax.ShapeDtypeStruct((8, lanes), f32),
+            part_shape(HOME[0], res),
+            jax.ShapeDtypeStruct((tokens, model), f32),
+            jax.ShapeDtypeStruct((1, model), f32),
+            jax.ShapeDtypeStruct((1, width), f32),
         ],
-        in_specs=jax.tree.map(lambda _: vmem, list(args)),
-        out_specs=[vmem] * 4,
+        in_specs=[[Lazy] * len(lefts), [Lazy] * len(rights)]
+        + [Lazy, Lazy, hbm, Lazy, Lazy, hbm]
+        + [Lazy] * 4
+        + [vmem, Lazy, Lazy, vmem, vmem, Lazy, hbm],
+        out_specs=[vmem] * 6 + [hbm, Eager, vmem, vmem],
         scratch_shapes=[
-            pltpu.VMEM((64, each + 8, size), f32),
+            pltpu.VMEM((model, width), bf16),
+            pltpu.VMEM((tokens, model), bf16),
+            pltpu.VMEM((tokens, width), f32),
+            pltpu.VMEM((tokens, 128), f32),
+            pltpu.VMEM((tokens, 128), f32),
+            pltpu.VMEM((64, each + 8, size), bf16),
             pltpu.VMEM((64, each, size), f32),
-            pltpu.VMEM((64, each + 8, size), f32),
+            pltpu.VMEM((64, each + 8, size), bf16),
             pltpu.VMEM((64, each, size), f32),
             pltpu.VMEM((tokens, width), f32),
             pltpu.VMEM((tokens, width), f32),
@@ -832,12 +1248,22 @@
             pltpu.VMEM((tokens + 8, channels), f32),
             pltpu.VMEM((tokens, 2 * size), f32),
             pltpu.VMEM((tokens, 2 * size), f32),
-        ]
-        + scatter_shapes(rows, columns)
-        + [pltpu.SemaphoreType.DMA((4,)), pltpu.SemaphoreType.DMA((4,))],
-        compiler_params=params(collective, vmem_limit_bytes=60 * MIB),
+            pltpu.VMEM((rows, 3 * hidden), f32),
+            scatter_shapes(rows, 3 * hidden),
+            scatter_shapes(rows, width),
+            pltpu.SemaphoreType.DMA((4,)),
+            pltpu.SemaphoreType.DMA((4,)),
+            pltpu.SemaphoreType.DMA((9,)),
+            pltpu.SemaphoreType.DMA((2,)),
+            pltpu.SemaphoreType.DMA((2, model // 256)),
+            pltpu.SemaphoreType.DMA((2,)),
+        ],
+        compiler_params=params(collective, vmem_limit_bytes=VMEM),
         name="mixer_back",
-    )(*args)
+    )(
+        lefts, rights, home, position, add, resid, scale, weights, z, gate_scale, y, x, bc, conv,
+        pre, step_raw, table, start, res,
+    )
 
 
 def input_back_kernel(
@@ -846,25 +1272,40 @@
     right,
     weights_ref,
     resid_ref,
-    gain_ref,
+    table_ref,
     grad_ref,
-    small_ref,
     res_ref,
+    near_refs,
     position_ref,
     weight_ref,
     shared_ref,
     block_ref,
-    out_ref,
+    taps_ref,
+    heads_ref,
+    norm_ref,
+    gate_gain_ref,
+    mixer_in_ref,
+    state_ref,
+    step_ref,
     input_ref,
-    small_out,
     layer_ref,
+    norm_first_out,
+    norm_second_out,
+    gate_gain_out,
+    conv_main_out,
+    conv_state_out,
+    heads_outs,
     weights,
     mine,
     theirs,
     theirs_mix,
     home,
+    named,
+    weighed,
     small,
     small_got,
+    small_out,
+    out_ref,
     buf,
     rest,
     send,
@@ -878,28 +1319,18 @@
     head = lax.axis_index("head")
     tokens, model = resid_ref.shape
     columns = right.shape[1]
+    gain_ref = table_ref.at[4:5, 0:model]
     load = pltpu.make_async_copy(weights_ref, weights, sems.at[0])
     load.start()
     announce(me, True)
-    sums = Scatter(at, plan, [left], right, out_ref, buf, rest, send, recv)
+    sums = Scatter(at, plan, [left], [right], out_ref, buf, rest, send, recv)
     totals = Small(at, me, small, small_out, small_got, small_sems)
-    own = pltpu.make_async_copy(res_ref.at[0], home.at[me], home_sems.at[2])
-    own.start()
-
-    def put(k, source):
-        pltpu.make_async_remote_copy(
-            src_ref=res_ref.at[k],
-            dst_ref=home.at[me],
-            send_sem=home_sems.at[0],
-            recv_sem=home_sems.at[1],
-            device_id={"seq": source},
-        ).start()
-
-    ways = Ways(at)
+    results = Spread(at, me, res_ref, home, home_sems, *HOME[1], True)
     for p in range(3):
         sums.product(p)
         if p == 0:
             await_all(True)
+            results.start(HOME[1][0], HOME[1][0] + 1)
         sums.first(2, p)
     load.wait()
 
@@ -923,7 +1354,6 @@
         swaps.append(swap)
     for p in range(3):
         sums.second(2, p)
-    ways.each(0, 8, put, back=True)
     square = jnp.zeros((tokens, 1), jnp.float32)
     inner = jnp.zeros((tokens, 1), jnp.float32)
     for n, c in enumerate(range(0, model, cut)):
@@ -936,7 +1366,25 @@
         inner = inner + jnp.sum(resid * gain_ref[:, rows] * grad, axis=1, keepdims=True)
     scale = lax.rsqrt(square / model + EPSILON)
     pull = scale * scale * scale * (inner / model)
-    small[...] = small_ref[...]
+    tiles, inner_tiles = model // 128, gate_gain_ref.shape[1] // 128
+    channel_tiles = taps_ref.shape[1] // 128
+    small[...] = jnp.zeros_like(small)
+
+    def put_small(row, value):
+        small[row // 8, row % 8 : row % 8 + 1, :] = value
+
+    for tile in range(tiles):
+        put_small(tiles + tile, norm_ref[:, tile * 128 : (tile + 1) * 128])
+    for tile in range(inner_tiles):
+        put_small(2 * tiles + tile, gate_gain_ref[:, tile * 128 : (tile + 1) * 128])
+    taps_row = 2 * tiles + inner_tiles
+    for tap in range(4):
+        for tile in range(channel_tiles):
+            row = taps_row + tap * channel_tiles + tile
+            put_small(row, taps_ref[tap : tap + 1, tile * 128 : (tile + 1) * 128])
+    heads_row = taps_row + 4 * channel_tiles
+    for n in range(3):
+        put_small(heads_row + n, heads_ref[n : n + 1, :])
     for c in range(0, model, cut):
         rows = slice(c, c + cut)
         grad = mine[:, rows]
@@ -945,77 +1393,147 @@
         gain_grad = jnp.sum(grad * resid * scale, axis=0, keepdims=True)
         for tile in range(c // 128, (c + cut) // 128):
             at_tile = tile * 128 - c
-            small[tile // 8, tile % 8 : tile % 8 + 1, :] = gain_grad[:, at_tile : at_tile + 128]
+            put_small(tile, gain_grad[:, at_tile : at_tile + 128])
     totals.begin()
+    results.start(HOME[1][0] + 1, HOME[1][0] + 2)
+    input_ref.flush()
     sums.finish(2)
     totals.middle()
+    results.start(HOME[1][0] + 2, HOME[1][0] + 3)
+    mine[...] = shared_ref[...]
+    slots = home.shape[1]
+
+    def mix(span, rows_ref):
+        @pl.loop(*span)
+        def _(g):
+            for n, (_, expert) in enumerate(Ways(at).group(g)):
+                named[n : n + 1, :] = position_ref[pl.ds(expert, 1), :]
+                weighed[n : n + 1, :] = weight_ref[pl.ds(expert, 1), :]
+            chosen = chosen_slots(named[...], slots)
+            weighted = chosen.reshape(8, slots, -1) * weighed[...][:, None, :]
+            high, less = split(weighted.reshape(chosen.shape), 2)
+            here = pl.ds(pl.multiple_of((g - span[0]) * 8, 8), 8)
+            rows = rows_ref[here].reshape(8 * slots, model)
+            mine[...] += dot_tn(high, rows) + dot_tn(less, rows)
+
+    ready(position_ref, weight_ref, *near_refs)
+    for span, near_ref in zip(HOME, near_refs):
+        mix(span, near_ref)
     for p in range(3):
         sums.second(1, p)
-
-    own.wait()
-    some = pl.ds(0, 63)
-    pltpu.make_async_copy(home.at[some], home.at[some], home_sems.at[1]).wait()
-    slots, step = home.shape[1], 16
-    mine[...] = shared_ref[...]
-
-    @pl.loop(0, home.shape[0] // step)
-    def _(i):
-        here = pl.ds(pl.multiple_of(i * step, step), step)
-        chosen = chosen_slots(position_ref[here, :], slots)
-        weighted = chosen.reshape(step, slots, -1) * weight_ref[here, :][:, None, :]
-        high, less = split(weighted.reshape(chosen.shape), 2)
-        rows = home[here].reshape(step * slots, model)
-        mine[...] += dot_tn(high, rows) + dot_tn(less, rows)
-
+    results.start(HOME[1][0] + 3, HOME[1][0] + 4)
+    results.arrived(HOME[1][0], HOME[1][0] + 2)
+    mix((HOME[1][0], HOME[1][0] + 2), home)
+    sums.finish(1)
+    results.start(HOME[1][0] + 4, HOME[1][1])
+    for p in range(3):
+        sums.second(0, p)
+    results.arrived(HOME[1][0] + 2, HOME[1][1])
+    mix((HOME[1][0] + 2, HOME[1][1]), home.at[pl.ds(16, home.shape[0] - 16)])
     pair = PairSum(mine, theirs_mix, mix_sems, cut)
     for n in range(pair.count):
         pair.copy(n).start()
-    sums.finish(1)
-    for p in range(3):
-        sums.second(0, p)
+    sums.finish(0)
     for n in range(pair.count):
         cols = slice(n * cut, (n + 1) * cut)
         pair.copy(n).wait()
         layer_ref[:, cols] = low(block_ref[:, cols] + (mine[:, cols] + theirs_mix[:, cols]))
-    sums.finish(0)
     totals.end()
+
+    def get_small(row):
+        return small_out[row // 8, row % 8 : row % 8 + 1, :]
+
+    for tile in range(tiles):
+        norm_first_out[tile : tile + 1, :] = get_small(tile)
+        norm_second_out[tile : tile + 1, :] = get_small(tiles + tile)
+    for tile in range(inner_tiles):
+        gate_gain_out[tile : tile + 1, :] = get_small(2 * tiles + tile)
+    for tap in range(4):
+        for tile in range(channel_tiles):
+            value = get_small(taps_row + tap * channel_tiles + tile)
+            if tile < inner_tiles:
+                conv_main_out[tap : tap + 1, tile * 128 : (tile + 1) * 128] = value
+            else:
+                start = (tile - inner_tiles) * 128
+                conv_state_out[tap : tap + 1, start : start + 128] = value
+    for n, heads_out in enumerate(heads_outs):
+        heads_out[...] = get_small(heads_row + n)[:, : heads_out.shape[1]]
+    results.sent()
+    inner = mixer_in_ref.shape[2]
+    for n in range(2):
+        mixer_in_ref[:, n, :] = out_ref[:, n * inner : (n + 1) * inner]
+    wide = 2 * inner + state_ref.shape[1]
+    state_ref[...] = out_ref[:, 2 * inner : wide]
+    step_ref[...] = out_ref[:, wide : wide + 128][:, : step_ref.shape[1]]
     sums.end()
-    pltpu.make_async_copy(home.at[some], home.at[some], home_sems.at[0]).wait()
 
 
 def input_back(
-    left, right, plan, weights, resid, gain, grad, small, res, position, weight, shared, block, collective
+    left,
+    right,
+    plan,
+    weights,
+    resid,
+    table,
+    grad,
+    res,
+    near,
+    position,
+    weight,
+    shared,
+    block,
+    taps,
+    heads,
+    norm,
+    gate_gain,
+    heads_dev,
+    collective,
 ):
     tokens, model = resid.shape
     columns = right.shape[1]
     rows = model // 64
+    inner, channels = gate_gain.shape[1], taps.shape[1]
     f32 = jnp.float32
     vmem, hbm = pl.BlockSpec(memory_space=pltpu.VMEM), pl.BlockSpec(memory_space=pl.ANY)
-    return pl.pallas_call(
+    return call(
         functools.partial(input_back_kernel, plan),
         out_shape=[
-            jax.ShapeDtypeStruct((rows, columns), f32),
+            jax.ShapeDtypeStruct((rows, 2, inner), f32),
+            jax.ShapeDtypeStruct((rows, channels - inner), f32),
+            jax.ShapeDtypeStruct((rows, heads_dev), f32),
             jax.ShapeDtypeStruct((tokens, model), f32),
-            jax.ShapeDtypeStruct(small.shape, f32),
             jax.ShapeDtypeStruct((tokens, model), jnp.bfloat16),
+            jax.ShapeDtypeStruct((model // 128, 128), f32),
+            jax.ShapeDtypeStruct((model // 128, 128), f32),
+            jax.ShapeDtypeStruct((inner // 128, 128), f32),
+            jax.ShapeDtypeStruct((4, inner), f32),
+            jax.ShapeDtypeStruct((4, channels - inner), f32),
+            [jax.ShapeDtypeStruct((1, heads_dev), f32)] * 3,
         ],
-        in_specs=[vmem, vmem, hbm] + [vmem] * 4 + [hbm] + [vmem] * 4,
-        out_specs=[vmem] * 4,
+        in_specs=[vmem, vmem, hbm, Lazy, vmem, Lazy] + [hbm, [Lazy] * len(near)] + [Lazy] * 8,
+        out_specs=[vmem] * 3 + [Eager] * 2 + [vmem] * 5 + [[vmem] * 3],
         scratch_shapes=[
             pltpu.VMEM(weights.shape, weights.dtype),
             pltpu.VMEM((tokens, model), f32),
             pltpu.VMEM((tokens, model), f32),
             pltpu.VMEM((tokens, model), f32),
-            pltpu.VMEM(res.shape, res.dtype),
-            pltpu.VMEM(small.shape, f32),
-            pltpu.VMEM(small.shape, f32),
+            pltpu.VMEM(part_shape(HOME[1], res).shape, res.dtype),
+            pltpu.VMEM((8, tokens), f32),
+            pltpu.VMEM((8, tokens), f32),
+            pltpu.VMEM((64, 8, 128), f32),
+            pltpu.VMEM((64, 8, 128), f32),
+            pltpu.VMEM((64, 8, 128), f32),
+            pltpu.VMEM((rows, columns), f32),
         ]
         + scatter_shapes(rows, columns)
         + [pltpu.SemaphoreType.DMA((4,)), pltpu.SemaphoreType.DMA((1 + 2 * model // 256,))]
-        + [pltpu.SemaphoreType.DMA((3,)), pltpu.SemaphoreType.DMA((2, model // 256))],
-        compiler_params=params(collective, vmem_limit_bytes=62 * MIB),
+        + [pltpu.SemaphoreType.DMA((9,)), pltpu.SemaphoreType.DMA((2, model // 256))],
+        compiler_params=params(collective, vmem_limit_bytes=VMEM),
         name="input_back",
-    )(left, right, weights, resid, gain, grad, small, res, position, weight, shared, block)
+    )(
+        left, right, weights, resid, table, grad, res, near, position, weight, shared, block,
+        taps, heads, norm, gate_gain,
+    )
 
 
 class Gather:
@@ -1109,13 +1627,15 @@
     routes_ref,
     weights_ref,
     grads_ref,
+    vectors,
     out_ref,
     late_out,
     before_ref,
     position_ref,
     weight_ref,
+    rows,
     slots_ref,
-    rows,
+    table_ref,
     send,
     recv,
     local_sem,
@@ -1123,11 +1643,34 @@
     late_recv,
     late_sem,
     sems,
+    out_sems,
 ):
     me, at = coordinates()
     announce(me, False)
     gather = Gather(at, x_ref, out_ref, send, recv, local_sem)
     late = Gather(at, late_ref, late_out, late_send, late_recv, late_sem)
+    conv_main, conv_state, gains, numbers = vectors
+    width, heads = conv_main.shape[1], numbers[0].shape[1]
+    table_ref[...] = jnp.zeros_like(table_ref)
+    table_ref[0:4, 0:width] = conv_main[...]
+    table_ref[0:4, width:] = conv_state[...]
+    for n, gain in enumerate(gains):
+        for tile in range(gain.shape[0]):
+            table_ref[4 + n : 5 + n, tile * 128 : (tile + 1) * 128] = gain[tile : tile + 1, :]
+    for n, number in enumerate(numbers):
+        table_ref[8 + n : 9 + n, 0:heads] = number[...]
+    slot_tables(routes_ref, weights_ref, position_ref, weight_ref)
+    grads = grads_ref[...]
+    slots, step = rows.shape[1], 16
+
+    @pl.loop(0, rows.shape[0] // step)
+    def _(i):
+        here = pl.ds(pl.multiple_of(i * step, step), step)
+        chosen = chosen_slots(position_ref[here, :], slots)
+        weighted = chosen.reshape(step, slots, -1) * weight_ref[here, :][:, None, :]
+        scale = jnp.sum(weighted.reshape(chosen.shape), axis=1, keepdims=True)
+        rows[here] = low(dot_nn(low(chosen), grads) * scale).reshape(step, slots, -1)
+
     await_all(False)
     gather.first(0)
     late.first(0)
@@ -1139,60 +1682,34 @@
         device_id={"seq": (me + 1) % 64},
     )
     edge.start()
-    slot_tables(routes_ref, weights_ref, position_ref, weight_ref)
-    grads = grads_ref[...]
-    slots, step = rows.shape[1], 16
-
-    @pl.loop(0, rows.shape[0] // step)
-    def _(i):
-        here = pl.ds(pl.multiple_of(i * step, step), step)
-        chosen = chosen_slots(position_ref[here, :], slots)
-        weighted = chosen.reshape(step, slots, -1) * weight_ref[here, :][:, None, :]
-        scale = jnp.sum(weighted.reshape(chosen.shape), axis=1, keepdims=True)
-        rows[here] = low(dot_nn(low(chosen), grads) * scale).reshape(step, slots, -1)
-
-    own = pltpu.make_async_copy(rows.at[me], slots_ref.at[0], sems.at[2])
-    own.start()
-
-    def put(k, target):
-        pltpu.make_async_remote_copy(
-            src_ref=rows.at[target],
-            dst_ref=slots_ref.at[k],
-            send_sem=sems.at[3],
-            recv_sem=sems.at[4],
-            device_id={"seq": target},
-        ).start()
-
-    ways = Ways(at)
+    out = Spread(at, me, rows, slots_ref, out_sems, *OUT[0], False)
     gather.second(0)
     late.second(0)
-    ways.each(0, 1, put)
+    out.start(0, 1)
     gather.first(1)
     late.first(1)
-    ways.each(1, 2, put)
+    out.start(1, 2)
     gather.second(1)
     late.second(1)
-    ways.each(2, 3, put)
+    out.start(2, 3)
     gather.first(2)
-    ways.each(3, 4, put)
     gather.second(2)
-    ways.each(4, 8, put)
+    out.start(3, OUT[0][1])
     late.arrived(1)
     late.end()
     gather.arrived(2)
     edge.wait()
     gather.end()
-    own.wait()
-    some = pl.ds(0, 63)
-    pltpu.make_async_copy(rows.at[some], rows.at[some], sems.at[3]).wait()
-    pltpu.make_async_copy(rows.at[some], rows.at[some], sems.at[4]).wait()
-
-
-def gather_rows(x, late, layer_in, routes, route_weights, grads, experts, slots, collective):
+    out.wait()
+
+
+def gather_rows(x, late, layer_in, routes, route_weights, grads, vectors, experts, slots, collective):
     rows, columns = x.shape
+    channels = vectors[0].shape[1] + vectors[1].shape[1]
     tokens, model = grads.shape
+    grad_rows = jax.ShapeDtypeStruct((experts, slots, model), grads.dtype)
     hbm, vmem = pl.BlockSpec(memory_space=pl.ANY), pl.BlockSpec(memory_space=pltpu.VMEM)
-    return pl.pallas_call(
+    return call(
         gather_kernel,
         out_shape=[
             jax.ShapeDtypeStruct((4, 4, 4, rows, columns), x.dtype),
@@ -1200,28 +1717,26 @@
             jax.ShapeDtypeStruct((16, model), layer_in.dtype),
             jax.ShapeDtypeStruct((experts, tokens), jnp.float32),
             jax.ShapeDtypeStruct((experts, tokens), jnp.float32),
-            jax.ShapeDtypeStruct((experts, slots, model), grads.dtype),
+            grad_rows,
+            part_shape(OUT[0], grad_rows),
+            jax.ShapeDtypeStruct((16, channels), jnp.float32),
         ],
-        in_specs=[hbm, hbm, hbm, vmem, vmem, vmem],
-        out_specs=[hbm, hbm, hbm, vmem, vmem, hbm],
-        scratch_shapes=[pltpu.VMEM((experts, slots, model), grads.dtype)]
-        + gather_shapes()
-        + gather_shapes()
-        + [pltpu.SemaphoreType.DMA((5,))],
-        compiler_params=params(collective, vmem_limit_bytes=60 * MIB),
+        in_specs=[hbm, hbm, hbm, vmem, vmem, Lazy, [vmem, vmem, [vmem] * 3, [vmem] * 3]],
+        out_specs=[hbm, hbm, hbm, vmem, vmem, vmem, hbm, vmem],
+        scratch_shapes=gather_shapes() + gather_shapes() + [pltpu.SemaphoreType.DMA((2,))]
+        + [pltpu.SemaphoreType.DMA((9,))],
+        compiler_params=params(collective, vmem_limit_bytes=VMEM),
         name="gather_rows",
-    )(x, late, layer_in, routes.T, route_weights.T, grads)
+    )(x, late, layer_in, routes.T, route_weights.T, grads, vectors)
 
 
 def mixer_kernel(
     layer_ref,
     edge_ref,
-    norm_ref,
+    table_ref,
     weights_ref,
-    numbers_ref,
-    taps_ref,
-    gain_ref,
     _,
+    rows_ref,
     normed_ref,
     z_ref,
     x_ref,
@@ -1234,6 +1749,7 @@
     gated_ref,
     scale_ref,
     gathered_ref,
+    slots_ref,
     weights,
     normed,
     message,
@@ -1249,6 +1765,7 @@
     pair_sems,
     send,
     recv,
+    slot_sems,
 ):
     me, at = coordinates()
     head = lax.axis_index("head")
@@ -1259,6 +1776,8 @@
     each = width // 64
     mid = tokens // 2
     cut = 384
+    norm_ref, gain_ref = table_ref.at[4:5, 0:model], table_ref.at[6:7, 0:width]
+    numbers_ref, taps_ref = table_ref.at[8:16, 0:lanes], table_ref
 
     def load(n):
         cols = pl.ds(pl.multiple_of(n * cut, 128), cut)
@@ -1278,6 +1797,7 @@
     normed[0:16, :] = low(before)
     normed[16 : 16 + tokens, :] = norm(layer_ref[...])
     normed_ref[...] = normed[16 : 16 + tokens, :]
+    normed_ref.flush()
     await_all(True)
     gather.first(2)
 
@@ -1293,6 +1813,7 @@
     cols = pl.ds(width, 2 * size)
     pre_ref[:, cols] = last[8:, : 2 * size]
     bc_ref[...] = conv(cols)
+    bc_ref.flush()
     step_raw = last[16:, 2 * size :] + numbers_ref[2:3, :]
     step_raw_ref[...] = step_raw
     step = jax.nn.softplus(step_raw)
@@ -1313,14 +1834,13 @@
         x = conv(here)
         x_ref[:, here] = x
         made_rows = dot_three(x * spread[:, here], held, dot_tn)
-        message[pl.ds(i * (cut // each), cut // each), 0:each, :] = made_rows.reshape(
-            cut // each, each, size
-        )
-
-    message[:, each : each + 8, :] = jnp.broadcast_to(jnp.exp(tail)[None], (64, 8, lanes))
+        made_rows = made_rows.reshape(cut // each, each, size)
+        message[pl.ds(i * (cut // each), cut // each)] = scan_rows(made_rows, jnp.exp(tail))
+
+    for ref in (x_ref, pre_ref, conv_ref):
+        ref.flush()
     scan = Scan(False, at, me, message, start_ref, got, made, scan_sems)
     scan.begin()
-    gather.second(2)
 
     @pl.loop(0, 4)
     def _(i):
@@ -1328,7 +1848,11 @@
         here = pl.ds(pl.multiple_of(i * cut, 128), cut)
         z_ref[:, here] = dot_nn(normed[16 : 16 + tokens, :], weights[:, here])
 
+    z_ref.flush()
     scan.middle()
+    out = Spread(at, me, rows_ref, slots_ref, slot_sems, *OUT[1], False)
+    gather.second(2)
+    out.start()
 
     spread[...] = split_dot(step, spreader, 2)
     blocks = ((0, 0), (1, 0), (1, 1))
@@ -1375,6 +1899,7 @@
         gated = y * (z * jax.nn.sigmoid(z))
         spread[:, here] = gated
         square = square + jnp.sum(gated * gated, axis=1, keepdims=True)
+    y_ref.flush()
     mine[...] = jnp.broadcast_to(square, mine.shape)
     swap = pltpu.make_async_remote_copy(
         src_ref=mine,
@@ -1392,12 +1917,12 @@
         gated_ref[:, here] = low(spread[:, here] * scale[:, 0:1] * gain_ref[:, here])
     gather.arrived(2)
     gather.end()
-
-
-def mixer(layer_in, edge, norm, weights, numbers, taps, gain, late, collective):
+    out.wait()
+
+
+def mixer(layer_in, edge, table, weights, width, late, grad_rows, collective):
     tokens, model = layer_in.shape
-    width, channels = gain.shape[1], taps.shape[1]
-    lanes = numbers.shape[1]
+    channels, lanes = table.shape[1], 128
     size = (channels - width) // 2
     each, mid = width // 64, tokens // 2
     f32, bf16 = jnp.float32, jnp.bfloat16
@@ -1415,17 +1940,18 @@
         ((tokens, width), bf16),
         ((tokens, lanes), f32),
         (late.shape, bf16),
+        (part_shape(OUT[1], grad_rows).shape, bf16),
     ]
-    return pl.pallas_call(
+    return call(
         mixer_kernel,
         out_shape=[jax.ShapeDtypeStruct(*shape) for shape in out],
-        in_specs=[vmem, vmem, vmem, hbm, vmem, vmem, vmem, hbm],
-        out_specs=[vmem] * (len(out) - 1) + [hbm],
+        in_specs=[vmem, vmem, vmem, hbm, hbm, hbm],
+        out_specs=[Eager] * 6 + [vmem] * 2 + [Eager] * 2 + [vmem] + [hbm] * 2,
         scratch_shapes=[
             pltpu.VMEM(weights.shape, bf16),
             pltpu.VMEM((tokens + 16, model), bf16),
-            pltpu.VMEM((64, each + 8, size), f32),
-            pltpu.VMEM((64, each + 8, size), f32),
+            pltpu.VMEM((64, each + 8, size), bf16),
+            pltpu.VMEM((64, each + 8, size), bf16),
             pltpu.VMEM((64, each, size), f32),
             pltpu.VMEM((tokens, width), f32),
             pltpu.VMEM((lanes, tokens), f32),
@@ -1436,288 +1962,12 @@
             pltpu.SemaphoreType.DMA((4,)),
             pltpu.SemaphoreType.DMA((2,)),
         ]
-        + gather_shapes()[:2],
-        input_output_aliases={7: len(out) - 1},
-        compiler_params=params(collective, vmem_limit_bytes=56 * MIB),
+        + gather_shapes()[:2]
+        + [pltpu.SemaphoreType.DMA((9,))],
+        input_output_aliases={4: len(out) - 2},
+        compiler_params=params(collective, vmem_limit_bytes=VMEM),
         name="mixer",
-    )(layer_in, edge, norm, weights, numbers, taps, gain, late)
-
-
-class PairSum:
-    def __init__(self, mine, theirs, sems, cut):
-        self.mine, self.theirs, self.sems, self.cut = mine, theirs, sems, cut
-        self.count = mine.shape[1] // cut
-
-    def copy(self, n):
-        cols = pl.ds(n * self.cut, self.cut)
-        return pltpu.make_async_remote_copy(
-            src_ref=self.mine.at[:, cols],
-            dst_ref=self.theirs.at[:, cols],
-            send_sem=self.sems.at[0, n],
-            recv_sem=self.sems.at[1, n],
-            device_id={"head": 1 - lax.axis_index("head")},
-        )
-
-
-def residual_kernel(
-    gated_ref,
-    weights_ref,
-    layer_ref,
-    norm_ref,
-    grad_out_ref,
-    position_ref,
-    resid_ref,
-    normed_ref,
-    scale_ref,
-    rows_ref,
-    shared_ref,
-    back_ref,
-    right_ref,
-    weights,
-    mine,
-    theirs,
-    load_sems,
-    sems,
-):
-    tokens, model = layer_ref.shape
-    inner = gated_ref.shape[1]
-    hidden = right_ref.shape[1] // 3
-    cut = 256
-    loads = []
-    for n, (start, length) in enumerate(
-        ((0, inner), (inner + 2 * hidden, hidden), (inner, 2 * hidden))
-    ):
-        cols = pl.ds(start, length)
-        loads.append(
-            pltpu.make_async_copy(weights_ref.at[:, cols], weights.at[:, cols], load_sems.at[n])
-        )
-        loads[-1].start()
-    greet_sibling()
-    pair = PairSum(mine, theirs, sems, cut)
-    loads[0].wait()
-    gated = gated_ref[...]
-    for n in range(pair.count):
-        rows = slice(n * cut, (n + 1) * cut)
-        mine[:, rows] = dot_nt(gated, weights[rows, 0:inner])
-        pair.copy(n).start()
-    loads[1].wait()
-    down = slice(inner + 2 * hidden, inner + 3 * hidden)
-    both = slice(inner, inner + 2 * hidden)
-    grad_hid = dot_nn(grad_out_ref[...], weights[:, down])
-    square = jnp.zeros((tokens, 1), jnp.float32)
-    for n in range(pair.count):
-        rows = slice(n * cut, (n + 1) * cut)
-        pair.copy(n).wait()
-        resid = layer_ref[:, rows].astype(jnp.float32) + (mine[:, rows] + theirs[:, rows])
-        resid_ref[:, rows] = resid
-        square = square + jnp.sum(resid * resid, axis=1, keepdims=True)
-    scale = lax.rsqrt(square / model + EPSILON)
-    scale_ref[...] = jnp.broadcast_to(scale, scale_ref.shape)
-    for n in range(pair.count):
-        rows = slice(n * cut, (n + 1) * cut)
-        normed_ref[:, rows] = low(resid_ref[:, rows] * scale * norm_ref[:, rows])
-    normed = normed_ref[...]
-    slots = rows_ref.shape[1]
-    step = 16
-
-    @pl.loop(0, rows_ref.shape[0] // step)
-    def _(i):
-        here = pl.ds(pl.multiple_of(i * step, step), step)
-        chosen = chosen_slots(position_ref[here, :], slots)
-        rows_ref[here] = low(dot_nn(low(chosen), normed)).reshape(step, slots, model)
-
-    loads[2].wait()
-    gate_up = dot_nn(normed, weights[:, both])
-    gate, up = gate_up[:, :hidden], gate_up[:, hidden:]
-    act, slope = silu_parts(gate)
-    hid = low(act * up)
-    right_ref[:, 2 * hidden :] = hid
-    right_ref[:, 0:hidden] = low(grad_hid * up * slope)
-    right_ref[:, hidden : 2 * hidden] = low(grad_hid * act)
-    grads = right_ref[:, 0 : 2 * hidden]
-    for n in range(pair.count):
-        rows = slice(n * cut, (n + 1) * cut)
-        shared_ref[:, rows] = dot_nt(hid, weights[rows, down])
-        back_ref[:, rows] = dot_nt(grads, weights[rows, both])
-
-
-def residual_block(gated, weights, layer_in, norm, grad_out, position, slots, collective):
-    tokens, model = layer_in.shape
-    hidden = (weights.shape[1] - gated.shape[1]) // 3
-    f32, bf16 = jnp.float32, jnp.bfloat16
-    vmem, hbm = pl.BlockSpec(memory_space=pltpu.VMEM), pl.BlockSpec(memory_space=pl.ANY)
-    out = [
-        ((tokens, model), f32),
-        ((tokens, model), bf16),
-        ((tokens, 128), f32),
-        ((position.shape[0], slots, model), bf16),
-        ((tokens, model), f32),
-        ((tokens, model), f32),
-        ((tokens, 3 * hidden), bf16),
-    ]
-    return pl.pallas_call(
-        residual_kernel,
-        out_shape=[jax.ShapeDtypeStruct(*shape) for shape in out],
-        in_specs=[vmem, hbm] + [vmem] * 4,
-        out_specs=[vmem] * len(out),
-        scratch_shapes=[
-            pltpu.VMEM(weights.shape, bf16),
-            pltpu.VMEM((tokens, model), f32),
-            pltpu.VMEM((tokens, model), f32),
-            pltpu.SemaphoreType.DMA((3,)),
-            pltpu.SemaphoreType.DMA((2, model // 256)),
-        ],
-        compiler_params=params(collective, vmem_limit_bytes=48 * MIB),
-        name="residual_block",
-    )(gated, weights, layer_in, norm, grad_out, position)
-
-
-def gate_back_kernel(
-    home_ref,
-    position_ref,
-    back_ref,
-    resid_ref,
-    scale_ref,
-    norm_ref,
-    grad_out_ref,
-    weights_ref,
-    z_ref,
-    y_ref,
-    gate_scale_ref,
-    gain_ref,
-    grad_resid_ref,
-    grad_mix_ref,
-    grad_y_ref,
-    grad_z_ref,
-    norm_grad_ref,
-    gain_grad_ref,
-    weights,
-    mine,
-    theirs,
-    stat,
-    stat_theirs,
-    load_sem,
-    sems,
-    stat_sems,
-):
-    tokens, model = resid_ref.shape
-    inner = z_ref.shape[1]
-    experts, slots = home_ref.shape[:2]
-    cut = 256
-    load = pltpu.make_async_copy(weights_ref.at[:, pl.ds(0, inner)], weights, load_sem)
-    load.start()
-    greet_sibling()
-    pair = PairSum(mine, theirs, sems, cut)
-    mine[...] = back_ref[...]
-    step = 16
-
-    @pl.loop(0, experts // step)
-    def _(i):
-        here = pl.ds(pl.multiple_of(i * step, step), step)
-        chosen = low(chosen_slots(position_ref[here, :], slots))
-        rows = home_ref[here].reshape(step * slots, model)
-        mine[...] += dot_tn(chosen, rows)
-
-    for n in range(pair.count):
-        pair.copy(n).start()
-    scale = scale_ref[:, 0:1]
-    inner_sum = jnp.zeros((tokens, 1), jnp.float32)
-    for n in range(pair.count):
-        cols = slice(n * cut, (n + 1) * cut)
-        pair.copy(n).wait()
-        grad = mine[:, cols] + theirs[:, cols]
-        mine[:, cols] = grad
-        resid = resid_ref[:, cols]
-        norm_grad_ref[:, cols] = jnp.sum(grad * resid * scale, axis=0, keepdims=True)
-        inner_sum = inner_sum + jnp.sum(resid * norm_ref[:, cols] * grad, axis=1, keepdims=True)
-    pull = scale * scale * scale * (inner_sum / model)
-    for n in range(pair.count):
-        cols = slice(n * cut, (n + 1) * cut)
-        grad = scale * norm_ref[:, cols] * mine[:, cols] - resid_ref[:, cols] * pull
-        grad = grad_out_ref[:, cols].astype(jnp.float32) + grad
-        grad_resid_ref[:, cols] = grad
-        grad_mix_ref[:, cols] = low(grad)
-    load.wait()
-    grad_mix = grad_mix_ref[...]
-    gate_scale = gate_scale_ref[:, 0:1]
-    wide = 384
-    dots = jnp.zeros((tokens, 1), jnp.float32)
-    for c in range(0, inner, wide):
-        cols = slice(c, c + wide)
-        grad = dot_nn(grad_mix, weights[:, cols])
-        z = z_ref[:, cols]
-        gated = y_ref[:, cols] * (z * jax.nn.sigmoid(z))
-        gain_grad_ref[:, cols] = jnp.sum(grad * gated * gate_scale, axis=0, keepdims=True)
-        weighted = grad * gain_ref[:, cols]
-        grad_y_ref[:, cols] = weighted
-        dots = dots + jnp.sum(weighted * gated, axis=1, keepdims=True)
-    stat[...] = jnp.broadcast_to(dots, stat.shape)
-    swap = pltpu.make_async_remote_copy(
-        src_ref=stat,
-        dst_ref=stat_theirs,
-        send_sem=stat_sems.at[0],
-        recv_sem=stat_sems.at[1],
-        device_id={"head": 1 - lax.axis_index("head")},
-    )
-    swap.start()
-    swap.wait()
-    dots = (stat[...] + stat_theirs[...])[:, 0:1]
-    pull = gate_scale * gate_scale * gate_scale * (dots / (2 * inner))
-    for c in range(0, inner, wide):
-        cols = slice(c, c + wide)
-        z, y = z_ref[:, cols], y_ref[:, cols]
-        act, slope = silu_parts(z)
-        grad = gate_scale * grad_y_ref[:, cols] - y * act * pull
-        grad_y_ref[:, cols] = grad * act
-        grad_z_ref[:, cols] = low(grad * y * slope)
-
-
-def gate_back(home, position, back, resid, scale, norm, grad_out, weights, z, y, gate_scale, gain, collective):
-    tokens, model = resid.shape
-    inner = z.shape[1]
-    f32, bf16 = jnp.float32, jnp.bfloat16
-    vmem, hbm = pl.BlockSpec(memory_space=pltpu.VMEM), pl.BlockSpec(memory_space=pl.ANY)
-    out = [
-        ((tokens, model), f32),
-        ((tokens, model), bf16),
-        ((tokens, inner), f32),
-        ((tokens, inner), bf16),
-        ((1, model), f32),
-        ((1, inner), f32),
-    ]
-    return pl.pallas_call(
-        gate_back_kernel,
-        out_shape=[jax.ShapeDtypeStruct(*shape) for shape in out],
-        in_specs=[vmem] * 7 + [hbm] + [vmem] * 4,
-        out_specs=[vmem] * len(out),
-        scratch_shapes=[
-            pltpu.VMEM((model, inner), bf16),
-            pltpu.VMEM((tokens, model), f32),
-            pltpu.VMEM((tokens, model), f32),
-            pltpu.VMEM((tokens, 128), f32),
-            pltpu.VMEM((tokens, 128), f32),
-            pltpu.SemaphoreType.DMA,
-            pltpu.SemaphoreType.DMA((2, model // 256)),
-            pltpu.SemaphoreType.DMA((2,)),
-        ],
-        compiler_params=params(collective, vmem_limit_bytes=48 * MIB),
-        name="gate_back",
-    )(home, position, back, resid, scale, norm, grad_out, weights, z, y, gate_scale, gain)
-
-
-def small_message(parts):
-    flat = jnp.concatenate([part.reshape(-1) for part in parts])
-    size = flat.shape[0]
-    each = -(-size // (64 * 1024)) * 1024
-    return jnp.pad(flat, (0, 64 * each - size)).reshape(64, each // 128, 128)
-
-
-def small_parts(parts, out):
-    out, result, start = out.reshape(-1), [], 0
-    for part in parts:
-        result.append(out[start : start + part.size].reshape(part.shape))
-        start += part.size
-    return result
+    )(layer_in, edge, table, weights, late, grad_rows)
 
 
 def per_device(
@@ -1758,7 +2008,13 @@
     late_rows = jnp.concatenate(
         [mixer_out, shared_gate_up.reshape(-1, 2 * shared_dev), shared_down], axis=1
     )
-    gathered, late_rows, edge, position, slot_weight, grads_in = gather_rows(
+    vectors = [
+        conv_main,
+        conv_state,
+        [gain.reshape(-1, 128) for gain in (norm_first, norm_second, gate_gain)],
+        [number[None] for number in (decay_rate, skip_gain, step_bias)],
+    ]
+    gathered, late_rows, edge, position, slot_weight, grads_out, grads_first, table = gather_rows(
         jnp.concatenate(
             [mixer_in.reshape(-1, 2 * inner_dev), state_proj, pad_heads(step_proj)], axis=1
         ),
@@ -1767,15 +2023,12 @@
         routes,
         route_weights,
         grad_out,
+        vectors,
         experts_all,
         slots_dev,
         0,
     )
     weights_in = gathered.reshape(model_width, -1)
-    numbers = jnp.pad(
-        jnp.stack([decay_rate, skip_gain, step_bias]), ((0, 5), (0, lanes - heads_dev))
-    )
-    taps = jnp.pad(jnp.concatenate([conv_main, conv_state], axis=1), ((0, 8 - conv_taps), (0, 0)))
     (
         normed,
         gate_z,
@@ -1789,119 +2042,158 @@
         normed_gate,
         gate_scale,
         gathered,
+        grads_second,
     ) = mixer(
-        layer_in, edge, norm_first[None], weights_in, numbers, taps, gate_gain[None], late_rows, 1
+        layer_in,
+        edge,
+        table,
+        weights_in,
+        inner_dev,
+        late_rows,
+        grads_out,
+        1,
     )
     weights_late = gathered.reshape(model_width, -1)
-    residual, normed_second, scale_second, rows_out, shared_part, shared_back, shared_right = (
-        residual_block(
-            normed_gate,
-            weights_late,
-            layer_in,
-            norm_second[None],
-            grad_out,
-            position,
-            slots_dev,
-            2,
-        )
-    )
-    grad_home, res_sums, expert_gate_up_grad, expert_down_grad = experts(
-        rows_out,
-        grads_in,
+    (
+        grad_home,
+        res_sums,
+        expert_gate_up_grad,
+        expert_down_grad,
+        shared_part,
+        shared_back,
+        shared_right,
+        residual,
+        normed_second,
+        scale_second,
+    ) = experts(
+        normed_gate,
+        weights_late,
+        layer_in,
+        table,
+        position,
+        [grads_first, grads_second],
         expert_gate_up.reshape(model_width, -1),
         expert_down.reshape(-1, model_width),
-        3,
+        grad_out,
+        slots_dev,
+        2,
     )
-    grad_resid, grad_mix, grad_ssd, grad_gate_z, norm_second_grad, gate_gain_grad = gate_back(
+    (
+        mixer_out_grad,
+        shared_gate_up_grad,
+        shared_down_grad,
+        right_grads,
+        taps_grad,
+        heads_grad,
+        home_near,
+        grad_resid,
+        norm_second_grad,
+        gate_gain_grad,
+    ) = mixer_back(
+        [normed_second, grad_out],
+        [normed_gate, shared_right],
         grad_home,
         position,
         shared_back,
         residual,
         scale_second,
-        norm_second[None],
-        grad_out,
         weights_late,
         gate_z,
-        ssd,
         gate_scale,
-        gate_gain[None],
-        4,
-    )
-    late_plan = (
-        ((0, 0, 1024),),
-        ((0, 1024, 512), (1, 1536, 512)),
-        ((1, 2048, 512), (2, 2560, 512)),
-    )
-    summed_late, right_grads, taps_grad, heads_grad = mixer_back(
-        [grad_mix, normed_second, grad_out],
-        jnp.concatenate([normed_gate, shared_right], axis=1),
-        late_plan,
-        grad_ssd,
         ssd,
         heads_x,
         state_both,
         conv_sum,
         pre,
-        grad_gate_z,
         step_raw,
-        numbers,
-        taps,
+        table,
         state_start.reshape(inner_dev, state_size),
-        5,
+        res_sums,
+        3,
     )
-    small = (
-        jnp.zeros_like(norm_first),
-        norm_second_grad,
-        heads_grad[2, :heads_dev],
-        taps_grad[:conv_taps, :inner_dev],
-        taps_grad[:conv_taps, inner_dev:],
-        heads_grad[1, :heads_dev],
-        heads_grad[0, :heads_dev],
-        gate_gain_grad,
-    )
-    summed, input_grad, small_sums, layer_out = input_back(
+    (
+        mixer_in_grad,
+        state_proj_grad,
+        step_proj_grad,
+        input_grad,
+        layer_out,
+        norm_first_sum,
+        norm_second_sum,
+        gate_gain_sum,
+        conv_main_grad,
+        conv_state_grad,
+        (skip_gain_grad, decay_rate_grad, step_bias_grad),
+    ) = input_back(
         normed,
         right_grads,
-        tuple(((0, start, 1152),) for start in (0, 1152, 2304)),
+        tuple(((0, 0, start, start, 1152),) for start in (0, 1152, 2304)),
         weights_in,
         layer_in,
-        norm_first[None],
+        table,
         grad_resid,
-        small_message(small),
         res_sums,
+        [home_near],
         position,
         slot_weight,
         shared_part,
         residual,
-        6,
+        taps_grad,
+        heads_grad,
+        norm_second_grad,
+        gate_gain_grad,
+        heads_dev,
+        4,
     )
-    small_sums = small_parts(small, small_sums)
-    wide = 2 * inner_dev + 2 * state_size
-    weight_sums = (
-        summed[:, : 2 * inner_dev].reshape(-1, 2, inner_dev),
-        summed[:, 2 * inner_dev : wide],
-        summed[:, wide : wide + heads_dev],
-        summed_late[:, :inner_dev],
-        summed_late[:, inner_dev : inner_dev + 2 * shared_dev].reshape(-1, 2, shared_dev),
-        summed_late[:, inner_dev + 2 * shared_dev :],
+    (
+        mixer_in_grad,
+        state_proj_grad,
+        step_proj_grad,
+        norm_first_sum,
+        norm_second_sum,
+        gate_gain_sum,
+        conv_main_grad,
+        conv_state_grad,
+        skip_gain_grad,
+        decay_rate_grad,
+        step_bias_grad,
+        mixer_out_grad,
+        shared_gate_up_grad,
+        shared_down_grad,
+    ) = emit(
+        [
+            mixer_in_grad,
+            state_proj_grad,
+            step_proj_grad,
+            norm_first_sum,
+            norm_second_sum,
+            gate_gain_sum,
+            conv_main_grad,
+            conv_state_grad,
+            skip_gain_grad,
+            decay_rate_grad,
+            step_bias_grad,
+            mixer_out_grad,
+            shared_gate_up_grad,
+            shared_down_grad,
+        ]
     )
     return (
         layer_out,
         input_grad,
-        small_sums[0],
-        weight_sums[0],
-        weight_sums[1],
-        weight_sums[2],
-        small_sums[2],
-        small_sums[3],
-        small_sums[4],
-        small_sums[5],
-        small_sums[6],
-        small_sums[7].reshape(-1),
-        weight_sums[3],
-        small_sums[1].reshape(-1),
-        weight_sums[4],
-        weight_sums[5],
+        norm_first_sum.reshape(-1),
+        mixer_in_grad,
+        state_proj_grad,
+        step_proj_grad,
+        step_bias_grad.reshape(-1),
+        conv_main_grad,
+        conv_state_grad,
+        decay_rate_grad.reshape(-1),
+        skip_gain_grad.reshape(-1),
+        gate_gain_sum.reshape(-1),
+        mixer_out_grad,
+        norm_second_sum.reshape(-1),
+        shared_gate_up_grad,
+        shared_down_grad,
         expert_gate_up_grad,
         expert_down_grad,
     )

time: 502 us -> 462 us (0.920)
  the two profiles are of different devices: /device:TPU:0 before, /device:TPU:1 now
where the time goes in v5:
time: 462 us; the launch traced here: 453 us
  Pallas kernels  436 us (94%)
  local copies, waits for them, and re-layouts  12.8 us (3%)
    pallas_call x5, Pallas kernels, run(): pl.pallas_call(body, out_shape=shapes, in_specs=[hbm if spec is Lazy else...  434 us
    unnamed x13, local copies, waits for them, and re-layouts  12.8 us

profile of v5, /device:TPU:1, one launch (start us, length us, event | category | flops | bytes accessed | tf_op | source)
XLA Modules:
  0.0 453.3 jit_solution(1292038499162043241)
XLA Ops:
  0.7 0.8 copy.41
  1.5 1.6 pad_maximum_fusion.refs_1_
  3.0 0.9 copy.40
  4.0 1.4 fusion.1.refs_0_
  5.4 2.9 copy.42
  8.2 90.3 %gather_rows.1 = (bf16[4,4,4,24,3456]{4,3,2,1,0:T(8,128)(2,1)}, bf16[4,4,4,24,3072]{4,3,2,1,0:T(8,128)(2,1)}, bf16[16,1536]{1,0:T(8,128)(2,1)}, f32[64,256]{1,0:...) custom-call(bf16[24,3456]{1,0:T(8,128)(2,1)} %fusion.1.refs_0_, ...), custom_call_target="tpu_custom_call" | custom-call | tf_op jit(solution)/shard_map/gather_rows/pallas_call | solution.py:158
  98.5 62.7 %mixer.1 = (bf16[256,1536]{1,0:T(8,128)(2,1)}, f32[256,1536]{1,0:T(8,128)}, f32[256,1536]{1,0:T(8,128)}, f32[256,256]{1,0:T(8,128)}, f32[256,1792]{1,0:T(8,128)}...) custom-call(bf16[256,1536]{1,0:T(8,128)(2,1)} %refs_3_.1, ...), custom_call_target="tpu_custom_call", output_to_operand_aliasing={{11}: (4, {})} | custom-call | tf_op jit(solution)/shard_map/mixer/pallas_call | solution.py:158
  161.2 96.7 %experts.1 = (bf16[64,16,1536]{2,1,0:T(8,128)(2,1)}, bf16[64,16,1536]{2,1,0:T(8,128)(2,1)}, f32[6144,128]{1,0:T(8,128)}, f32[256,1536]{1,0:T(8,128)}, f32[256,15...) custom-call(bf16[256,1536]{1,0:T(8,128)(2,1)} %get-tuple-element.92., ...), custom_call_target="tpu_custom_call" | custom-call | tf_op jit(solution)/shard_map/experts/pallas_call | solution.py:158
  257.9 92.3 %mixer_back.1 = (f32[24,1536]{1,0:T(8,128)}, f32[24,2,512]{2,1,0:T(2,128)}, f32[24,512]{1,0:T(8,128)}, bf16[256,3456]{1,0:T(8,128)(2,1)}, f32[8,1792]{1,0:T(8,12...) custom-call(bf16[256,1536]{1,0:T(8,128)(2,1)} %get-tuple-element.97., ...), custom_call_target="tpu_custom_call" | custom-call | tf_op jit(solution)/shard_map/mixer_back/pallas_call | solution.py:158
  350.3 92.2 %input_back.1 = (f32[24,2,1536]{2,1,0:T(2,128)}, f32[24,256]{1,0:T(8,128)}, f32[24,24]{1,0:T(8,128)}, f32[256,1536]{1,0:T(8,128)}, bf16[256,1536]{1,0:T(8,128)(2...) custom-call(bf16[256,1536]{1,0:T(8,128)(2,1)} %get-tuple-element.91., ...), custom_call_target="tpu_custom_call" | custom-call | tf_op jit(solution)/shard_map/input_back/pallas_call | solution.py:158
  442.5 0.0 copy-start.2
  442.5 2.1 emit.1
  444.6 2.1 copy.48
  446.7 0.0 copy-done.2
  446.7 0.0 copy-start
  446.7 1.1 copy.49
  447.8 1.3 copy-done
  449.2 0.0 copy-start.1
  449.2 1.7 copy.50
  450.8 0.9 copy-done.1
  451.7 1.1 copy.51
Async XLA Ops:
  442.5 4.2 copy-start.2
  446.7 2.5 copy-start
  449.2 2.5 copy-start.1

commit v6 on v5

--- a/solution.py
+++ b/solution.py
@@ -168,16 +168,41 @@
     return run
 
 
-def emit_kernel(*refs):
-    count = len(refs) // 2
-    for n in range(count):
-        refs[count + n][...] = refs[n][...]
-
-
-def emit(arrays):
+def emit_kernel(large, *refs):
+    count = (len(refs) - large - 1) // 2
+    sources, targets = refs[:count], refs[count : 2 * count]
+    buffers, sems = refs[2 * count : -1], refs[-1]
+    pieces = []
+    for n in range(large):
+        rows = sources[n].shape[0] // 4
+        for part in range(4):
+            here = pl.ds(part * rows, rows)
+            place = buffers[n].at[here]
+            come = pltpu.make_async_copy(sources[n].at[here], place, sems.at[0, n, part])
+            go = pltpu.make_async_copy(place, targets[n].at[here], sems.at[1, n, part])
+            come.start()
+            pieces.append((come, go))
+    for n in range(large, count):
+        targets[n][...] = sources[n][...]
+    for come, go in pieces:
+        come.wait()
+        go.start()
+    for _, go in pieces:
+        go.wait()
+
+
+def emit(large, small):
+    arrays = list(large) + list(small)
+    specs = [pl.BlockSpec(memory_space=pl.ANY)] * len(large)
+    specs += [pl.BlockSpec(memory_space=pltpu.VMEM)] * len(small)
     return pl.pallas_call(
-        emit_kernel,
+        functools.partial(emit_kernel, len(large)),
         out_shape=[jax.ShapeDtypeStruct(array.shape, array.dtype) for array in arrays],
+        in_specs=specs,
+        out_specs=specs,
+        scratch_shapes=[pltpu.VMEM(array.shape, array.dtype) for array in large]
+        + [pltpu.SemaphoreType.DMA((2, len(large), 4))],
+        compiler_params=pltpu.CompilerParams(vmem_limit_bytes=VMEM),
         name="emit",
     )(*arrays)
 
@@ -221,8 +246,8 @@
         self.sent()
 
 
-OUT = ((0, 6), (6, 8))
-HOME = ((0, 3), (3, 8))
+OUT = ((0, 4), (4, 5), (5, 8))
+HOME = ((0, 4), (4, 8))
 
 
 def part_shape(span, rows):
@@ -256,6 +281,7 @@
     table_ref,
     position_ref,
     grads_refs,
+    grad_rows_ref,
     gate_up_ref,
     down_ref,
     grad_out_ref,
@@ -270,6 +296,7 @@
     normed_ref,
     scale_ref,
     rows_ref,
+    grads_here,
     mine,
     theirs,
     slot_in,
@@ -281,6 +308,7 @@
     weights,
     load_sems,
     pair_sems,
+    out_sems,
     send,
     home_send,
     home_recv,
@@ -307,6 +335,7 @@
     down_grad_ref[...] = jnp.zeros_like(down_grad_ref)
     ways = Ways(at)
     await_all(True)
+    out = Spread(at, me, grad_rows_ref, grads_here, out_sems, *OUT[2], False)
 
     def group(c):
         return pl.ds(pl.multiple_of(c * 8, 8), 8)
@@ -348,6 +377,8 @@
             source = grads_ref.at[pl.ds(8 * (c - first), 8)]
             kept(c, source).start()
             given(c, source).start()
+
+    out.start()
 
     cut = 256
     pair = PairSum(mine, theirs, pair_sems, cut)
@@ -438,6 +469,15 @@
             ).wait()
             forward(c).start()
 
+        for late in range(*OUT[2]):
+
+            @pl.when(i == late - 2)
+            def _():
+                out.arrived(late, late + 1)
+                source = grads_here.at[pl.ds(8 * (late - OUT[2][0]), 8)]
+                kept(late, source).start()
+                given(late, source).start()
+
         @pl.when((i >= 1) & (i < 9))
         def _():
             c = i - 1
@@ -496,6 +536,7 @@
                 total = grad_slots[j, head].astype(jnp.float32) + theirs_y[j].astype(jnp.float32)
                 res_ref[j] = total.astype(res_ref.dtype)
 
+    out.sent()
     tiles = hidden // 128
     for tile in range(tiles):
         for which in range(2):
@@ -510,7 +551,7 @@
 
 
 def experts(
-    gated, weights, layer_in, table, position, grads, gate_up, down, grad_out, slots, collective
+    gated, weights, layer_in, table, position, grads, grad_rows, gate_up, down, grad_out, slots, collective
 ):
     tokens, model = layer_in.shape
     shared_hidden = (weights.shape[1] - gated.shape[1]) // 3
@@ -532,10 +573,11 @@
             jax.ShapeDtypeStruct((tokens, model), bf16),
             jax.ShapeDtypeStruct((tokens, 128), jnp.float32),
         ],
-        in_specs=[Lazy, hbm, Lazy, vmem, Lazy, [hbm] * len(grads), Lazy, Lazy, Lazy],
+        in_specs=[Lazy, hbm, Lazy, vmem, Lazy, [hbm] * len(grads), hbm, Lazy, Lazy, Lazy],
         out_specs=[hbm] + [vmem] * 3 + [Eager] * 5 + [vmem],
         scratch_shapes=[
             pltpu.VMEM(half, bf16),
+            pltpu.VMEM(part_shape(OUT[2], grad_rows).shape, bf16),
             pltpu.VMEM((tokens, model), jnp.float32),
             pltpu.VMEM((tokens, model), jnp.float32),
             pltpu.VMEM(whole, bf16),
@@ -547,6 +589,7 @@
             pltpu.VMEM(weights.shape, bf16),
             pltpu.SemaphoreType.DMA((2,)),
             pltpu.SemaphoreType.DMA((2, model // 256)),
+            pltpu.SemaphoreType.DMA((9,)),
             pltpu.SemaphoreType.DMA,
             pltpu.SemaphoreType.DMA,
             pltpu.SemaphoreType.DMA,
@@ -554,9 +597,8 @@
         ],
         compiler_params=params(collective, vmem_limit_bytes=VMEM),
         name="experts",
-    )(gated, weights, layer_in, table, position, grads, gate_up, down, grad_out)
-    wide = wide.reshape(width, hidden // 128, 2, 128).transpose(0, 2, 1, 3)
-    return home, res, wide.reshape(1, width, 2, hidden), down_grad[None], *shared
+    )(gated, weights, layer_in, table, position, grads, grad_rows, gate_up, down, grad_out)
+    return home, res, wide, down_grad, *shared
 
 
 class Scan:
@@ -943,6 +985,7 @@
     await_all(True)
     for n in range(pair.count):
         pair.copy(n).start()
+    results.start(HOME[0][0], HOME[0][0] + 1)
     for p in range(3):
         shared.product(p)
         shared.first(2, p)
@@ -1071,7 +1114,7 @@
         shared.second(1, p)
     shared.finish(1)
     mix.finish(2)
-    results.start(HOME[0][0], HOME[0][0] + 1)
+    results.start(HOME[0][0] + 1, HOME[0][0] + 2)
     scan.end()
 
     skip = split_dot(jnp.broadcast_to(numbers_ref[1:2, :], (8, lanes)), spreader, 2)[0:1, :]
@@ -1116,7 +1159,7 @@
         shared.second(0, p)
     for p in range(3):
         mix.second(1, p)
-    results.start(HOME[0][0] + 1, HOME[0][0] + 2)
+    results.start(HOME[0][0] + 2, HOME[0][0] + 3)
 
     ones = jnp.ones((8, size), jnp.bfloat16)
     state_grad = dot_split(ones, state_dot, 2, dot_nt)[0:1, :]
@@ -1150,7 +1193,7 @@
     edge.start()
     shared.finish(0)
     mix.finish(1)
-    results.start(HOME[0][0] + 2, HOME[0][1])
+    results.start(HOME[0][0] + 3, HOME[0][1])
     edge.wait()
     there = jnp.where(me == 63, 0.0, 1.0)
     ext[tokens : tokens + 8, :] = ext[tokens : tokens + 8, :] * there
@@ -1421,11 +1464,10 @@
         mix(span, near_ref)
     for p in range(3):
         sums.second(1, p)
-    results.start(HOME[1][0] + 3, HOME[1][0] + 4)
+    results.start(HOME[1][0] + 3, HOME[1][1])
     results.arrived(HOME[1][0], HOME[1][0] + 2)
     mix((HOME[1][0], HOME[1][0] + 2), home)
     sums.finish(1)
-    results.start(HOME[1][0] + 4, HOME[1][1])
     for p in range(3):
         sums.second(0, p)
     results.arrived(HOME[1][0] + 2, HOME[1][1])
@@ -1621,8 +1663,9 @@
 
 
 def gather_kernel(
-    x_ref,
-    late_ref,
+    early_refs,
+    late_refs,
+    wide_in,
     layer_ref,
     routes_ref,
     weights_ref,
@@ -1636,6 +1679,9 @@
     rows,
     slots_ref,
     table_ref,
+    wide_ref,
+    x_ref,
+    late_ref,
     send,
     recv,
     local_sem,
@@ -1647,6 +1693,23 @@
 ):
     me, at = coordinates()
     announce(me, False)
+    def beside(target, sources):
+        column = 0
+        for source in sources:
+            value = source[...]
+            if value.ndim == 3:
+                value = value.astype(jnp.float32)
+                halves = [low(value[:, n, :]) for n in range(2)]
+            else:
+                halves = [value]
+            for half in halves:
+                target[:, column : column + half.shape[1]] = half
+                column = column + half.shape[1]
+
+    rows_step = x_ref.shape[1] - 128
+    x_ref[:, rows_step:] = jnp.zeros((x_ref.shape[0], 128), x_ref.dtype)
+    beside(x_ref, early_refs)
+    beside(late_ref, late_refs)
     gather = Gather(at, x_ref, out_ref, send, recv, local_sem)
     late = Gather(at, late_ref, late_out, late_send, late_recv, late_sem)
     conv_main, conv_state, gains, numbers = vectors
@@ -1695,6 +1758,16 @@
     gather.first(2)
     gather.second(2)
     out.start(3, OUT[0][1])
+    ready(wide_in)
+    hidden = wide_in.shape[2]
+
+    @pl.loop(0, wide_in.shape[0] // 64)
+    def _(i):
+        here = pl.ds(pl.multiple_of(i * 64, 64), 64)
+        value = wide_in[here].astype(jnp.float32)
+        for n in range(2):
+            wide_ref[here, n * hidden : (n + 1) * hidden] = low(value[:, n, :])
+
     late.arrived(1)
     late.end()
     gather.arrived(2)
@@ -1703,8 +1776,13 @@
     out.wait()
 
 
-def gather_rows(x, late, layer_in, routes, route_weights, grads, vectors, experts, slots, collective):
-    rows, columns = x.shape
+def gather_rows(
+    early, late, wide, layer_in, routes, route_weights, grads, vectors, experts, slots, collective
+):
+    rows = early[0].shape[0]
+    bf16 = early[0].dtype
+    count = lambda arrays: sum(array.size // rows for array in arrays)
+    columns = -(-count(early) // 128) * 128
     channels = vectors[0].shape[1] + vectors[1].shape[1]
     tokens, model = grads.shape
     grad_rows = jax.ShapeDtypeStruct((experts, slots, model), grads.dtype)
@@ -1712,22 +1790,25 @@
     return call(
         gather_kernel,
         out_shape=[
-            jax.ShapeDtypeStruct((4, 4, 4, rows, columns), x.dtype),
-            jax.ShapeDtypeStruct((4, 4, 4) + late.shape, late.dtype),
+            jax.ShapeDtypeStruct((4, 4, 4, rows, columns), bf16),
+            jax.ShapeDtypeStruct((4, 4, 4, rows, count(late)), bf16),
             jax.ShapeDtypeStruct((16, model), layer_in.dtype),
             jax.ShapeDtypeStruct((experts, tokens), jnp.float32),
             jax.ShapeDtypeStruct((experts, tokens), jnp.float32),
             grad_rows,
             part_shape(OUT[0], grad_rows),
             jax.ShapeDtypeStruct((16, channels), jnp.float32),
+            jax.ShapeDtypeStruct((wide.shape[0], 2 * wide.shape[2]), bf16),
         ],
-        in_specs=[hbm, hbm, hbm, vmem, vmem, Lazy, [vmem, vmem, [vmem] * 3, [vmem] * 3]],
-        out_specs=[hbm, hbm, hbm, vmem, vmem, vmem, hbm, vmem],
-        scratch_shapes=gather_shapes() + gather_shapes() + [pltpu.SemaphoreType.DMA((2,))]
+        in_specs=[[vmem] * len(early), [vmem] * len(late), Lazy, hbm, vmem, vmem, Lazy, [vmem, vmem, [vmem] * 3, [vmem] * 3]],
+        out_specs=[hbm, hbm, hbm, vmem, vmem, vmem, hbm, vmem, vmem],
+        scratch_shapes=[pltpu.VMEM((rows, columns), bf16), pltpu.VMEM((rows, count(late)), bf16)]
+        + gather_shapes()
+        + gather_shapes() + [pltpu.SemaphoreType.DMA((2,))]
         + [pltpu.SemaphoreType.DMA((9,))],
         compiler_params=params(collective, vmem_limit_bytes=VMEM),
         name="gather_rows",
-    )(x, late, layer_in, routes.T, route_weights.T, grads, vectors)
+    )(early, late, wide, layer_in, routes.T, route_weights.T, grads, vectors)
 
 
 def mixer_kernel(
@@ -2004,21 +2085,16 @@
     capacity = max(2, tokens * choices_per * 4 // (3 * experts_all))
     slots_dev = capacity // lax.axis_size("head")
     lanes = 128
-    pad_heads = lambda v: jnp.pad(v, ((0, 0), (0, lanes - heads_dev)))
-    late_rows = jnp.concatenate(
-        [mixer_out, shared_gate_up.reshape(-1, 2 * shared_dev), shared_down], axis=1
-    )
     vectors = [
         conv_main,
         conv_state,
         [gain.reshape(-1, 128) for gain in (norm_first, norm_second, gate_gain)],
         [number[None] for number in (decay_rate, skip_gain, step_bias)],
     ]
-    gathered, late_rows, edge, position, slot_weight, grads_out, grads_first, table = gather_rows(
-        jnp.concatenate(
-            [mixer_in.reshape(-1, 2 * inner_dev), state_proj, pad_heads(step_proj)], axis=1
-        ),
-        late_rows,
+    gathered, late_rows, edge, position, slot_weight, grads_out, grads_first, table, gate_up = gather_rows(
+        [mixer_in, state_proj, step_proj],
+        [mixer_out, shared_gate_up, shared_down],
+        expert_gate_up.reshape(expert_gate_up.shape[1:]),
         layer_in,
         routes,
         route_weights,
@@ -2072,7 +2148,8 @@
         table,
         position,
         [grads_first, grads_second],
-        expert_gate_up.reshape(model_width, -1),
+        grads_out,
+        gate_up,
         expert_down.reshape(-1, model_width),
         grad_out,
         slots_dev,
@@ -2145,6 +2222,10 @@
         4,
     )
     (
+        layer_out,
+        input_grad,
+        expert_gate_up_grad,
+        expert_down_grad,
         mixer_in_grad,
         state_proj_grad,
         step_proj_grad,
@@ -2160,6 +2241,7 @@
         shared_gate_up_grad,
         shared_down_grad,
     ) = emit(
+        [layer_out, input_grad, expert_gate_up_grad, expert_down_grad],
         [
             mixer_in_grad,
             state_proj_grad,
@@ -2175,8 +2257,10 @@
             mixer_out_grad,
             shared_gate_up_grad,
             shared_down_grad,
-        ]
+        ],
     )
+    expert_gate_up_grad = expert_gate_up_grad.reshape(model_width, -1, 2, lanes)
+    expert_gate_up_grad = expert_gate_up_grad.transpose(0, 2, 1, 3).reshape(expert_gate_up.shape)
     return (
         layer_out,
         input_grad,
@@ -2195,7 +2279,7 @@
         shared_gate_up_grad,
         shared_down_grad,
         expert_gate_up_grad,
-        expert_down_grad,
+        expert_down_grad[None],
     )
 
 

time: 462 us -> 435 us (0.942)
  local copies, waits for them, and re-layouts: 12.8 us -> 0 us
  Pallas kernels: 436 us -> 427 us
    pallas_call x5, Pallas kernels: 434 us -> 419 us  [run(): pl.pallas_call(body, out_shape=shapes, in_specs=[hbm if spec is Lazy else...]
    unnamed x13 -> x0, local copies, waits for them, and re-layouts: 12.8 us -> none
    pallas_call x1, Pallas kernels: 2.12 us -> 7.76 us  [emit(): pl.pallas_call(functools.partial(emit_kernel, len(large)), out_shape=[jax...]
where the time goes in v6:
time: 435 us; the launch traced here: 428 us
  Pallas kernels  427 us (98%)
    pallas_call x5, Pallas kernels, run(): pl.pallas_call(body, out_shape=shapes, in_specs=[hbm if spec is Lazy else...  419 us

profile of v6, /device:TPU:1, one launch (start us, length us, event | category | flops | bytes accessed | tf_op | source)
XLA Modules:
  0.0 428.0 jit_solution(211993049367509156)
XLA Ops:
  0.7 84.1 %gather_rows.1 = (bf16[4,4,4,24,3456]{4,3,2,1,0:T(8,128)(2,1)}, bf16[4,4,4,24,3072]{4,3,2,1,0:T(8,128)(2,1)}, bf16[16,1536]{1,0:T(8,128)(2,1)}, f32[64,256]{1,0:...) custom-call(bf16[24,2,1536]{2,1,0:T(2,128)(2,1)} %refs_0_.2, ...), custom_call_target="tpu_custom_call" | custom-call | tf_op jit(solution)/shard_map/gather_rows/pallas_call | solution.py:158
  84.8 58.2 %mixer.1 = (bf16[256,1536]{1,0:T(8,128)(2,1)}, f32[256,1536]{1,0:T(8,128)}, f32[256,1536]{1,0:T(8,128)}, f32[256,256]{1,0:T(8,128)}, f32[256,1792]{1,0:T(8,128)}...) custom-call(bf16[256,1536]{1,0:T(8,128)(2,1)} %refs_3_.3, ...), custom_call_target="tpu_custom_call", output_to_operand_aliasing={{11}: (4, {})} | custom-call | tf_op jit(solution)/shard_map/mixer/pallas_call | solution.py:158
  143.0 99.5 %experts.1 = (bf16[64,16,1536]{2,1,0:T(8,128)(2,1)}, bf16[64,16,1536]{2,1,0:T(8,128)(2,1)}, f32[6144,128]{1,0:T(8,128)}, f32[256,1536]{1,0:T(8,128)}, f32[256,15...) custom-call(bf16[256,1536]{1,0:T(8,128)(2,1)} %get-tuple-element.97., ...), custom_call_target="tpu_custom_call" | custom-call | tf_op jit(solution)/shard_map/experts/pallas_call | solution.py:158
  242.4 91.6 %mixer_back.1 = (f32[24,1536]{1,0:T(8,128)}, f32[24,2,512]{2,1,0:T(2,128)}, f32[24,512]{1,0:T(8,128)}, bf16[256,3456]{1,0:T(8,128)(2,1)}, f32[8,1792]{1,0:T(8,12...) custom-call(bf16[256,1536]{1,0:T(8,128)(2,1)} %get-tuple-element.103, ...), custom_call_target="tpu_custom_call" | custom-call | tf_op jit(solution)/shard_map/mixer_back/pallas_call | solution.py:158
  334.0 86.0 %input_back.1 = (f32[24,2,1536]{2,1,0:T(2,128)}, f32[24,256]{1,0:T(8,128)}, f32[24,24]{1,0:T(8,128)}, f32[256,1536]{1,0:T(8,128)}, bf16[256,1536]{1,0:T(8,128)(2...) custom-call(bf16[256,1536]{1,0:T(8,128)(2,1)} %get-tuple-element.96., ...), custom_call_target="tpu_custom_call" | custom-call | tf_op jit(solution)/shard_map/input_back/pallas_call | solution.py:158
  420.0 7.8 %emit.1 = (bf16[256,1536]{1,0:T(8,128)(2,1)}, f32[256,1536]{1,0:T(8,128)}, f32[6144,128]{1,0:T(8,128)}, f32[256,1536]{1,0:T(8,128)}, f32[24,2,1536]{2,1,0:T(2,12...) custom-call(bf16[256,1536]{1,0:T(8,128)(2,1)} %get-tuple-element.128, ...), custom_call_target="tpu_custom_call" | custom-call | tf_op jit(solution)/shard_map/emit/pallas_call | solution.py:198

commit v7 on v6

--- a/solution.py
+++ b/solution.py
@@ -168,22 +168,20 @@
     return run
 
 
-def emit_kernel(large, *refs):
-    count = (len(refs) - large - 1) // 2
-    sources, targets = refs[:count], refs[count : 2 * count]
-    buffers, sems = refs[2 * count : -1], refs[-1]
+def emit_kernel(*refs):
+    count = (len(refs) - 1) // 3
+    sources, targets, buffers, sems = refs[:count], refs[count : 2 * count], refs[2 * count : -1], refs[-1]
     pieces = []
-    for n in range(large):
-        rows = sources[n].shape[0] // 4
-        for part in range(4):
-            here = pl.ds(part * rows, rows)
+    for n in range(count):
+        rows = sources[n].shape[0]
+        parts = 4 if rows >= 256 else 1
+        for part in range(parts):
+            here = pl.ds(part * (rows // parts), rows // parts)
             place = buffers[n].at[here]
             come = pltpu.make_async_copy(sources[n].at[here], place, sems.at[0, n, part])
             go = pltpu.make_async_copy(place, targets[n].at[here], sems.at[1, n, part])
             come.start()
             pieces.append((come, go))
-    for n in range(large, count):
-        targets[n][...] = sources[n][...]
     for come, go in pieces:
         come.wait()
         go.start()
@@ -191,17 +189,15 @@
         go.wait()
 
 
-def emit(large, small):
-    arrays = list(large) + list(small)
-    specs = [pl.BlockSpec(memory_space=pl.ANY)] * len(large)
-    specs += [pl.BlockSpec(memory_space=pltpu.VMEM)] * len(small)
+def emit(arrays):
+    hbm = [pl.BlockSpec(memory_space=pl.ANY)] * len(arrays)
     return pl.pallas_call(
-        functools.partial(emit_kernel, len(large)),
+        emit_kernel,
         out_shape=[jax.ShapeDtypeStruct(array.shape, array.dtype) for array in arrays],
-        in_specs=specs,
-        out_specs=specs,
-        scratch_shapes=[pltpu.VMEM(array.shape, array.dtype) for array in large]
-        + [pltpu.SemaphoreType.DMA((2, len(large), 4))],
+        in_specs=hbm,
+        out_specs=hbm,
+        scratch_shapes=[pltpu.VMEM(array.shape, array.dtype) for array in arrays]
+        + [pltpu.SemaphoreType.DMA((2, len(arrays), 4))],
         compiler_params=pltpu.CompilerParams(vmem_limit_bytes=VMEM),
         name="emit",
     )(*arrays)
@@ -247,7 +243,7 @@
 
 
 OUT = ((0, 4), (4, 5), (5, 8))
-HOME = ((0, 4), (4, 8))
+HOME = ((0, 5), (5, 8))
 
 
 def part_shape(span, rows):
@@ -1145,6 +1141,12 @@
         grad_held = grad_held + dot_three(weights * x, after)
         grad_read = grad_read + dot_three(decayed[:, here], start)
         ext[0:tokens, here] = grad_x * silu_parts(conv_ref[:, here])[1]
+        if c == cut:
+            for p in range(3):
+                shared.second(0, p)
+            for p in range(3):
+                mix.second(1, p)
+            results.start(HOME[0][0] + 2, HOME[0][0] + 3)
     mine[:, :size] = grad_held
     mine[:, size:] = grad_read
     swap = pltpu.make_async_remote_copy(
@@ -1155,11 +1157,8 @@
         device_id={"head": 1 - head},
     )
     swap.start()
-    for p in range(3):
-        shared.second(0, p)
-    for p in range(3):
-        mix.second(1, p)
-    results.start(HOME[0][0] + 2, HOME[0][0] + 3)
+    mix.finish(1)
+    results.start(HOME[0][0] + 3, HOME[0][0] + 4)
 
     ones = jnp.ones((8, size), jnp.bfloat16)
     state_grad = dot_split(ones, state_dot, 2, dot_nt)[0:1, :]
@@ -1192,8 +1191,9 @@
     )
     edge.start()
     shared.finish(0)
-    mix.finish(1)
-    results.start(HOME[0][0] + 3, HOME[0][1])
+    for p in range(3):
+        mix.second(0, p)
+    results.start(HOME[0][0] + 4, HOME[0][1])
     edge.wait()
     there = jnp.where(me == 63, 0.0, 1.0)
     ext[tokens : tokens + 8, :] = ext[tokens : tokens + 8, :] * there
@@ -1211,8 +1211,6 @@
             taps_grad_ref[j : j + 1, here] = jnp.sum(products, axis=0, keepdims=True)
         grads_ref[:, pl.ds(pl.multiple_of(width + i * 256, 256), 256)] = low(total)
 
-    for p in range(3):
-        mix.second(0, p)
     mix.finish(0)
     hidden = down_ref.shape[1]
     for n in range(2):
@@ -1440,9 +1438,6 @@
     totals.begin()
     results.start(HOME[1][0] + 1, HOME[1][0] + 2)
     input_ref.flush()
-    sums.finish(2)
-    totals.middle()
-    results.start(HOME[1][0] + 2, HOME[1][0] + 3)
     mine[...] = shared_ref[...]
     slots = home.shape[1]
 
@@ -1462,16 +1457,19 @@
     ready(position_ref, weight_ref, *near_refs)
     for span, near_ref in zip(HOME, near_refs):
         mix(span, near_ref)
+    first = HOME[1][0]
+    sums.finish(2)
     for p in range(3):
         sums.second(1, p)
-    results.start(HOME[1][0] + 3, HOME[1][1])
-    results.arrived(HOME[1][0], HOME[1][0] + 2)
-    mix((HOME[1][0], HOME[1][0] + 2), home)
+    results.start(first + 2, HOME[1][1])
+    totals.middle()
     sums.finish(1)
+    results.arrived(first, first + 2)
+    mix((first, first + 2), home)
     for p in range(3):
         sums.second(0, p)
-    results.arrived(HOME[1][0] + 2, HOME[1][1])
-    mix((HOME[1][0] + 2, HOME[1][1]), home.at[pl.ds(16, home.shape[0] - 16)])
+    results.arrived(first + 2, HOME[1][1])
+    mix((first + 2, HOME[1][1]), home.at[pl.ds(16, home.shape[0] - 16)])
     pair = PairSum(mine, theirs_mix, mix_sems, cut)
     for n in range(pair.count):
         pair.copy(n).start()
@@ -1552,7 +1550,7 @@
             jax.ShapeDtypeStruct((4, channels - inner), f32),
             [jax.ShapeDtypeStruct((1, heads_dev), f32)] * 3,
         ],
-        in_specs=[vmem, vmem, hbm, Lazy, vmem, Lazy] + [hbm, [Lazy] * len(near)] + [Lazy] * 8,
+        in_specs=[Lazy, Lazy, hbm, Lazy, vmem, Lazy] + [hbm, [Lazy] * len(near)] + [Lazy] * 8,
         out_specs=[vmem] * 3 + [Eager] * 2 + [vmem] * 5 + [[vmem] * 3],
         scratch_shapes=[
             pltpu.VMEM(weights.shape, weights.dtype),
@@ -2241,8 +2239,11 @@
         shared_gate_up_grad,
         shared_down_grad,
     ) = emit(
-        [layer_out, input_grad, expert_gate_up_grad, expert_down_grad],
         [
+            layer_out,
+            input_grad,
+            expert_gate_up_grad,
+            expert_down_grad,
             mixer_in_grad,
             state_proj_grad,
             step_proj_grad,
@@ -2257,7 +2258,7 @@
             mixer_out_grad,
             shared_gate_up_grad,
             shared_down_grad,
-        ],
+        ]
     )
     expert_gate_up_grad = expert_gate_up_grad.reshape(model_width, -1, 2, lanes)
     expert_gate_up_grad = expert_gate_up_grad.transpose(0, 2, 1, 3).reshape(expert_gate_up.shape)

time: 435 us -> 429 us (0.986)
  Pallas kernels: 427 us -> 421 us
    pallas_call x5, Pallas kernels: 419 us -> 414 us  [run(): pl.pallas_call(body, out_shape=shapes, in_specs=[hbm if spec is Lazy else...]
where the time goes in v7:
time: 429 us; the launch traced here: 422 us
  Pallas kernels  421 us (98%)
    pallas_call x5, Pallas kernels, run(): pl.pallas_call(body, out_shape=shapes, in_specs=[hbm if spec is Lazy else...  414 us

profile of v7, /device:TPU:1, one launch (start us, length us, event | category | flops | bytes accessed | tf_op | source)
XLA Modules:
  0.0 422.3 jit_solution(6857424044496664582)
XLA Ops:
  0.7 84.1 %gather_rows.1 = (bf16[4,4,4,24,3456]{4,3,2,1,0:T(8,128)(2,1)}, bf16[4,4,4,24,3072]{4,3,2,1,0:T(8,128)(2,1)}, bf16[16,1536]{1,0:T(8,128)(2,1)}, f32[64,256]{1,0:...) custom-call(bf16[24,2,1536]{2,1,0:T(2,128)(2,1)} %refs_0_.2, ...), custom_call_target="tpu_custom_call" | custom-call | tf_op jit(solution)/shard_map/gather_rows/pallas_call | solution.py:158
  84.8 58.1 %mixer.1 = (bf16[256,1536]{1,0:T(8,128)(2,1)}, f32[256,1536]{1,0:T(8,128)}, f32[256,1536]{1,0:T(8,128)}, f32[256,256]{1,0:T(8,128)}, f32[256,1792]{1,0:T(8,128)}...) custom-call(bf16[256,1536]{1,0:T(8,128)(2,1)} %refs_3_.3, ...), custom_call_target="tpu_custom_call", output_to_operand_aliasing={{11}: (4, {})} | custom-call | tf_op jit(solution)/shard_map/mixer/pallas_call | solution.py:158
  142.9 99.9 %experts.1 = (bf16[64,16,1536]{2,1,0:T(8,128)(2,1)}, bf16[64,16,1536]{2,1,0:T(8,128)(2,1)}, f32[6144,128]{1,0:T(8,128)}, f32[256,1536]{1,0:T(8,128)}, f32[256,15...) custom-call(bf16[256,1536]{1,0:T(8,128)(2,1)} %get-tuple-element.97., ...), custom_call_target="tpu_custom_call" | custom-call | tf_op jit(solution)/shard_map/experts/pallas_call | solution.py:158
  242.9 94.0 %mixer_back.1 = (f32[24,1536]{1,0:T(8,128)}, f32[24,2,512]{2,1,0:T(2,128)}, f32[24,512]{1,0:T(8,128)}, bf16[256,3456]{1,0:T(8,128)(2,1)}, f32[8,1792]{1,0:T(8,12...) custom-call(bf16[256,1536]{1,0:T(8,128)(2,1)} %get-tuple-element.103, ...), custom_call_target="tpu_custom_call" | custom-call | tf_op jit(solution)/shard_map/mixer_back/pallas_call | solution.py:158
  336.9 77.6 %input_back.1 = (f32[24,2,1536]{2,1,0:T(2,128)}, f32[24,256]{1,0:T(8,128)}, f32[24,24]{1,0:T(8,128)}, f32[256,1536]{1,0:T(8,128)}, bf16[256,1536]{1,0:T(8,128)(2...) custom-call(bf16[256,1536]{1,0:T(8,128)(2,1)} %get-tuple-element.96., ...), custom_call_target="tpu_custom_call" | custom-call | tf_op jit(solution)/shard_map/input_back/pallas_call | solution.py:158
  414.5 7.3 %emit.1 = (bf16[256,1536]{1,0:T(8,128)(2,1)}, f32[256,1536]{1,0:T(8,128)}, f32[6144,128]{1,0:T(8,128)}, f32[256,1536]{1,0:T(8,128)}, f32[24,2,1536]{2,1,0:T(2,12...) custom-call(bf16[256,1536]{1,0:T(8,128)(2,1)} %get-tuple-element.128, ...), custom_call_target="tpu_custom_call" | custom-call | tf_op jit(solution)/shard_map/emit/pallas_call | solution.py:194

commit v8 on v7

--- a/solution.py
+++ b/solution.py
@@ -243,7 +243,7 @@
 
 
 OUT = ((0, 4), (4, 5), (5, 8))
-HOME = ((0, 5), (5, 8))
+HOME = ((0, 6), (6, 8))
 
 
 def part_shape(span, rows):
@@ -1457,19 +1457,15 @@
     ready(position_ref, weight_ref, *near_refs)
     for span, near_ref in zip(HOME, near_refs):
         mix(span, near_ref)
-    first = HOME[1][0]
     sums.finish(2)
     for p in range(3):
         sums.second(1, p)
-    results.start(first + 2, HOME[1][1])
     totals.middle()
     sums.finish(1)
-    results.arrived(first, first + 2)
-    mix((first, first + 2), home)
+    results.arrived(*HOME[1])
+    mix(HOME[1], home)
     for p in range(3):
         sums.second(0, p)
-    results.arrived(first + 2, HOME[1][1])
-    mix((first + 2, HOME[1][1]), home.at[pl.ds(16, home.shape[0] - 16)])
     pair = PairSum(mine, theirs_mix, mix_sems, cut)
     for n in range(pair.count):
         pair.copy(n).start()

time: 429 us -> 432 us (level)
  no operation moved by 1% of the time
where the time goes in v8:
time: 432 us; the launch traced here: 426 us
  Pallas kernels  425 us (98%)
    pallas_call x5, Pallas kernels, run(): pl.pallas_call(body, out_shape=shapes, in_specs=[hbm if spec is Lazy else...  418 us

profile of v8, /device:TPU:1, one launch (start us, length us, event | category | flops | bytes accessed | tf_op | source)
XLA Modules:
  0.0 426.1 jit_solution(6141588157797870373)
XLA Ops:
  0.7 84.1 %gather_rows.1 = (bf16[4,4,4,24,3456]{4,3,2,1,0:T(8,128)(2,1)}, bf16[4,4,4,24,3072]{4,3,2,1,0:T(8,128)(2,1)}, bf16[16,1536]{1,0:T(8,128)(2,1)}, f32[64,256]{1,0:...) custom-call(bf16[24,2,1536]{2,1,0:T(2,128)(2,1)} %refs_0_.2, ...), custom_call_target="tpu_custom_call" | custom-call | tf_op jit(solution)/shard_map/gather_rows/pallas_call | solution.py:158
  84.8 58.1 %mixer.1 = (bf16[256,1536]{1,0:T(8,128)(2,1)}, f32[256,1536]{1,0:T(8,128)}, f32[256,1536]{1,0:T(8,128)}, f32[256,256]{1,0:T(8,128)}, f32[256,1792]{1,0:T(8,128)}...) custom-call(bf16[256,1536]{1,0:T(8,128)(2,1)} %refs_3_.3, ...), custom_call_target="tpu_custom_call", output_to_operand_aliasing={{11}: (4, {})} | custom-call | tf_op jit(solution)/shard_map/mixer/pallas_call | solution.py:158
  142.9 99.9 %experts.1 = (bf16[64,16,1536]{2,1,0:T(8,128)(2,1)}, bf16[64,16,1536]{2,1,0:T(8,128)(2,1)}, f32[6144,128]{1,0:T(8,128)}, f32[256,1536]{1,0:T(8,128)}, f32[256,15...) custom-call(bf16[256,1536]{1,0:T(8,128)(2,1)} %get-tuple-element.97., ...), custom_call_target="tpu_custom_call" | custom-call | tf_op jit(solution)/shard_map/experts/pallas_call | solution.py:158
  242.9 96.8 %mixer_back.1 = (f32[24,1536]{1,0:T(8,128)}, f32[24,2,512]{2,1,0:T(2,128)}, f32[24,512]{1,0:T(8,128)}, bf16[256,3456]{1,0:T(8,128)(2,1)}, f32[8,1792]{1,0:T(8,12...) custom-call(bf16[256,1536]{1,0:T(8,128)(2,1)} %get-tuple-element.103, ...), custom_call_target="tpu_custom_call" | custom-call | tf_op jit(solution)/shard_map/mixer_back/pallas_call | solution.py:158
  339.7 78.6 %input_back.1 = (f32[24,2,1536]{2,1,0:T(2,128)}, f32[24,256]{1,0:T(8,128)}, f32[24,24]{1,0:T(8,128)}, f32[256,1536]{1,0:T(8,128)}, bf16[256,1536]{1,0:T(8,128)(2...) custom-call(bf16[256,1536]{1,0:T(8,128)(2,1)} %get-tuple-element.96., ...), custom_call_target="tpu_custom_call" | custom-call | tf_op jit(solution)/shard_map/input_back/pallas_call | solution.py:158
  418.3 7.3 %emit.1 = (bf16[256,1536]{1,0:T(8,128)(2,1)}, f32[256,1536]{1,0:T(8,128)}, f32[6144,128]{1,0:T(8,128)}, f32[256,1536]{1,0:T(8,128)}, f32[24,2,1536]{2,1,0:T(2,12...) custom-call(bf16[256,1536]{1,0:T(8,128)(2,1)} %get-tuple-element.128, ...), custom_call_target="tpu_custom_call" | custom-call | tf_op jit(solution)/shard_map/emit/pallas_call | solution.py:194
